TPU v7x, 256 devices: a whole 4x4x8 slice. The times are simulated.
256 devices in a mesh: die: 2 (over x_lo), row: 16 (over x_hi, y, core), col: 8 (over z).
Axes of the slice: x: 4 (x_hi: 2, x_lo: 2; x = x_hi * 2 + x_lo), y: 4, z: 8, core: 2. Of those that a mesh axis runs over, the one named last changes fastest.
Arguments:
- sheet_res: float32 [4, 2, 1024, 2048], P('die', None, 'row', 'col'), may hold values from 0.5 to 2
- capacity: float32 [4, 1024, 2048], P('die', 'row', 'col'), may hold values from 0.05 to 0.5
- drop_start: float32 [4, 2, 1024, 2048], P('die', None, 'row', 'col'), may hold values from 0 to 1
- load_cell: int32 [4, 128, 256], P('die', 'row', 'col'), may hold values from 0 to 63
- load_current: float32 [2, 4, 2, 128, 256], P(None, 'die', None, 'row', 'col'), may hold values from 1 to 4
- via_cell: int32 [4, 32, 128, 256], P('die', None, 'row', 'col'), may hold values from 0 to 63
- via_current: float32 [2, 4, 2, 32, 128, 256], P(None, 'die', None, None, 'row', 'col'), may hold values from 0.01 to 0.1
- base_sheet: float32 [2, 128, 256], P(None, 'row', 'col'), may hold values from 0.05 to 0.2
- base_start: float32 [2, 128, 256], P(None, 'row', 'col'), may hold values from 0 to 1
- bump_cell: int32 [16, 32], P('row', 'col'), may hold values from 0 to 63
Outputs:
- die_drop: float32 [4, 2, 1024, 2048], P('die', None, 'row', 'col')
- base_drop: float32 [2, 128, 256], P(None, 'row', 'col')
Inputs may be any that keep to these rules, and one draw needn't show every extreme that they name: `load_cell`: offset of a cell within its 8 x 8 tile, row-major. `via_cell`: offset of a cell within its 8 x 8 tile, row-major; two vias may share a cell. `bump_cell`: offset of a cell within its 8 x 8 interposer tile, row-major.
All inputs are finite; a program needn't handle non-finite values.
Results may differ from a plain program's by a relative error of at most 0.0003.
Values sent between devices are 32-bit elements; how exact they have to be, the bound alone decides.
No kernel may reach another device: no remote copies, remote signals or barrier semaphores. Data moves between devices by JAX's collectives and lax.ppermute only.
A program may use at most 64 MiB of HBM per device.

v0:
```python
import jax
import jax.numpy as jnp
from jax import lax
from jax.sharding import PartitionSpec as P

SWEEPS = 6
STEPS = 2


VIA_CONDUCT = 1.0
VIA_RESIST = 4.0
BUMP_CONDUCT = 50.0
BASE_CAPACITY = 0.1
LOWER_BOUND = 0.1
UPPER_BOUND = 1.9


def with_halo(block, sides, width):
    for axis, dim in sides:
        count = lax.axis_size(axis)
        forward = [(i, i + 1) for i in range(count - 1)]
        backward = [(target, source) for source, target in forward]
        low = lax.ppermute(
            lax.slice_in_dim(block, block.shape[dim] - width, None, axis=dim), axis, forward
        )
        high = lax.ppermute(lax.slice_in_dim(block, 0, width, axis=dim), axis, backward)
        block = jnp.concatenate([low, block, high], axis=dim)
    return block


def prefix(part, axis, combine, identity, reverse):
    count = lax.axis_size(axis)
    place = lax.axis_index(axis)
    ahead = count - 1 - place if reverse else place
    gathered = lax.all_gather(part, axis)
    state = jnp.zeros_like(part) + jnp.asarray(identity, part.dtype)

    def one(lap, state):
        source = count - 1 - lap if reverse else lap
        return combine(state, lax.dynamic_index_in_dim(gathered, source, 0, False))

    return lax.fori_loop(0, ahead, one, state)


def tile_offsets(height, breadth):
    row_part = lax.broadcasted_iota(jnp.int32, (height, breadth), 0) % 8
    col_part = lax.broadcasted_iota(jnp.int32, (height, breadth), 1) % 8
    return row_part * 8 + col_part


def place_cells(values, positions, offsets):
    tiles_down, tiles_across = (values.shape[-2], values.shape[-1])
    grid = offsets.reshape(tiles_down, 8, tiles_across, 8)
    hit = positions[..., :, None, :, None] == grid
    placed = jnp.where(hit, values[..., :, None, :, None], 0.0)
    return placed.reshape(placed.shape[:-4] + (tiles_down * 8, tiles_across * 8))


def place_sum(values, positions, offsets):
    tiles_down, tiles_across = (values.shape[-2], values.shape[-1])
    grid = offsets.reshape(tiles_down, 8, tiles_across, 8)
    hit = positions[..., :, None, :, None] == grid
    placed = jnp.sum(jnp.where(hit, values[..., :, None, :, None], 0.0), axis=2)
    return placed.reshape(placed.shape[:-4] + (tiles_down * 8, tiles_across * 8))


def fine_pad(values):
    return with_halo(values, (("row", 2), ("col", 3)), 1)


def coarse_pad(values):
    return with_halo(values, (("row", 1), ("col", 2)), 1)


def link_terms(center, padded):

    def connect(neighbour):
        return jnp.where(neighbour > 0.0, 2.0 / (center + neighbour), 0.0)

    return (
        connect(padded[..., :-2, 1:-1]),
        connect(padded[..., 2:, 1:-1]),
        connect(padded[..., 1:-1, :-2]),
        connect(padded[..., 1:-1, 2:]),
    )


def operate(padded, iterate, couplings):
    link_up, link_down, link_left, link_right, diagonal = couplings
    coupled = link_up * padded[..., :-2, 1:-1] + link_down * padded[..., 2:, 1:-1]
    coupled = coupled + link_left * padded[..., 1:-1, :-2] + link_right * padded[..., 1:-1, 2:]
    return diagonal * iterate - coupled


def chebyshev(initial, source, couplings, inverse, padder):
    middle = 0.5 * (UPPER_BOUND + LOWER_BOUND)
    half_width = 0.5 * (UPPER_BOUND - LOWER_BOUND)
    scaled = middle / half_width
    residual = inverse * (source - operate(padder(initial), initial, couplings))
    update = residual / middle
    iterate = initial
    ratio_now = 1.0 / scaled
    for sweep_index in range(SWEEPS):
        iterate = iterate + update
        if sweep_index + 1 < SWEEPS:
            residual = residual - inverse * operate(padder(update), update, couplings)
            ratio_next = 1.0 / (2.0 * scaled - ratio_now)
            update = ratio_next * ratio_now * update + 2.0 * ratio_next / half_width * residual
            ratio_now = ratio_next
    return iterate


def add_terms(earlier, later):
    return earlier + later


def per_device(
    sheet_res,
    capacity,
    drop_start,
    load_cell,
    load_current,
    via_cell,
    via_current,
    base_sheet,
    base_start,
    bump_cell,
):
    offsets = tile_offsets(sheet_res.shape[2], sheet_res.shape[3])
    base_offsets = tile_offsets(base_sheet.shape[1], base_sheet.shape[2])
    links = link_terms(sheet_res, fine_pad(sheet_res))
    counts = place_sum(jnp.ones(via_current.shape[1:], jnp.float32), via_cell[:, None], offsets)
    diagonal = capacity[:, None] + links[0] + links[1] + links[2] + links[3] + VIA_CONDUCT * counts
    couplings = links + (diagonal,)
    inverse = 1.0 / diagonal
    base_links = link_terms(base_sheet, coarse_pad(base_sheet))
    bumps = place_cells(jnp.ones(bump_cell.shape, jnp.float32), bump_cell, base_offsets)
    base_diagonal = (
        BASE_CAPACITY
        + base_links[0]
        + base_links[1]
        + base_links[2]
        + base_links[3]
        + BUMP_CONDUCT * bumps
    )
    base_couplings = base_links + (base_diagonal,)
    base_inverse = 1.0 / base_diagonal
    device_draw = jnp.sum(via_current, axis=1)
    earlier_sum = prefix(device_draw, "die", add_terms, jnp.zeros_like(device_draw), False)
    through = earlier_sum[:, None] + jnp.cumsum(via_current, axis=1)
    device_through = jnp.sum(through, axis=1)
    later_sum = prefix(device_through, "die", add_terms, jnp.zeros_like(device_through), True)
    beneath = later_sum[:, None] + jnp.flip(jnp.cumsum(jnp.flip(through, 1), axis=1), 1)
    arriving = lax.psum(jnp.sum(device_draw, axis=2), "die")
    die_state, base_state = (drop_start, base_start)
    for step_index in range(STEPS):
        base_source = BASE_CAPACITY * base_state + arriving[step_index]
        base_state = chebyshev(base_state, base_source, base_couplings, base_inverse, coarse_pad)
        bound = base_state[None, :, None] + VIA_RESIST * beneath[step_index]
        loads = place_cells(load_current[step_index], load_cell[:, None], offsets)
        source = (
            capacity[:, None] * die_state
            + loads
            + VIA_CONDUCT * place_sum(bound, via_cell[:, None], offsets)
        )
        die_state = chebyshev(die_state, source, couplings, inverse, fine_pad)
    return (die_state, base_state)


def solution(mesh):
    in_specs = (
        P("die", None, "row", "col"),
        P("die", "row", "col"),
        P("die", None, "row", "col"),
        P("die", "row", "col"),
        P(None, "die", None, "row", "col"),
        P("die", None, "row", "col"),
        P(None, "die", None, None, "row", "col"),
        P(None, "row", "col"),
        P(None, "row", "col"),
        P("row", "col"),
    )
    out_specs = (P("die", None, "row", "col"), P(None, "row", "col"))
    return jax.shard_map(
        per_device, mesh=mesh, in_specs=in_specs, out_specs=out_specs, check_vma=False
    )
```

profile of v0, /device:TPU:102, one launch (start us, length us, event | category | flops | bytes accessed | tf_op | source)
XLA Modules:
  0.0 607.2 jit_solution(572152844453002233)
XLA Ops:
  11.2 7.3 %collective-permute-start.9 = (f32[2,1,32]{2,1,0:T(1,128)S(1)}, f32[2,1,32]{2,1,0:T(1,128)S(1)}, u32[]{:S(2)}, u32[]{:S(2)}) collective-permute-start(f32[2,1,32]{2,1,0:T(1,128)S(1)} %get-tuple-element.242), channel_id=1, source_target_pairs={{8,0},{16,8},{24,16},{32,24},{40,32},{48,40},{56,48},{64,56},{72,6... | collective-permute-start | bytes 776 | tf_op jit(solution)/shard_map/ppermute | solution.py:26
  26.0 14.5 %all-gather = f32[4,2,32,8,32]{4,3,2,1,0:T(8,128)S(1)} all-gather(f32[2,2,32,8,32]{4,3,2,1,0:T(8,128)S(1)} %get-tuple-element.86), channel_id=2, replica_groups=mesh['die'=2,'row'=16,'col'=8] {'die'}, dimensions={0}, use_global_device_ids=true | all-gather | bytes 393216 | tf_op jit(solution)/shard_map/all_gather | solution.py:35
  42.9 13.7 %all-gather.1 = f32[4,2,32,8,32]{4,3,2,1,0:T(8,128)S(1)} all-gather(f32[2,2,32,8,32]{4,3,2,1,0:T(8,128)S(1)} %get-tuple-element.243), channel_id=3, replica_groups=mesh['die'=2,'row'=16,'col'=8] {'die'}, dimensions={0}, use_global_device_ids=true | all-gather | bytes 393216 | tf_op jit(solution)/shard_map/all_gather | solution.py:35
  62.2 7.3 %psum.7 = f32[2,2,8,32]{3,2,1,0:T(8,128)S(1)} all-reduce(f32[2,2,8,32]{3,2,1,0:T(8,128)S(1)} %get-tuple-element.85), channel_id=1, replica_groups=mesh['die'=2,'row'=16,'col'=8] {'die'}, use_global_device_ids=true, to_apply=%region_2.3 | all-reduce | flops 1024 | bytes 8192 | tf_op jit(solution)/shard_map/psum | solution.py:154
  93.1 7.3 %collective-permute-start.13 = (f32[2,1,32]{2,1,0:T(1,128)S(1)}, f32[2,1,32]{2,1,0:T(1,128)S(1)}, u32[]{:S(2)}, u32[]{:S(2)}) collective-permute-start(f32[2,1,32]{2,1,0:T(1,128)S(1)} %get-tuple-element.238), channel_id=1, source_target_pairs={{8,0},{16,8},{24,16},{32,24},{40,32},{48,40},{56,48},{64,56},{72,6... | collective-permute-start | bytes 776 | tf_op jit(solution)/shard_map/ppermute | solution.py:26
  115.2 7.3 %collective-permute-start.17 = (f32[2,1,32]{2,1,0:T(1,128)S(1)}, f32[2,1,32]{2,1,0:T(1,128)S(1)}, u32[]{:S(2)}, u32[]{:S(2)}) collective-permute-start(f32[2,1,32]{2,1,0:T(1,128)S(1)} %get-tuple-element.236), channel_id=1, source_target_pairs={{8,0},{16,8},{24,16},{32,24},{40,32},{48,40},{56,48},{64,56},{72,6... | collective-permute-start | bytes 776 | tf_op jit(solution)/shard_map/ppermute | solution.py:26
  140.5 7.3 %collective-permute-start.21 = (f32[2,1,32]{2,1,0:T(1,128)S(1)}, f32[2,1,32]{2,1,0:T(1,128)S(1)}, u32[]{:S(2)}, u32[]{:S(2)}) collective-permute-start(f32[2,1,32]{2,1,0:T(1,128)S(1)} %get-tuple-element.234), channel_id=1, source_target_pairs={{8,0},{16,8},{24,16},{32,24},{40,32},{48,40},{56,48},{64,56},{72,6... | collective-permute-start | bytes 776 | tf_op jit(solution)/shard_map/ppermute | solution.py:26
  159.9 7.3 %collective-permute-start.25 = (f32[2,1,32]{2,1,0:T(1,128)S(1)}, f32[2,1,32]{2,1,0:T(1,128)S(1)}, u32[]{:S(2)}, u32[]{:S(2)}) collective-permute-start(f32[2,1,32]{2,1,0:T(1,128)S(1)} %get-tuple-element.232), channel_id=1, source_target_pairs={{8,0},{16,8},{24,16},{32,24},{40,32},{48,40},{56,48},{64,56},{72,6... | collective-permute-start | bytes 776 | tf_op jit(solution)/shard_map/ppermute | solution.py:26
  179.3 7.3 %collective-permute-start.29 = (f32[2,1,32]{2,1,0:T(1,128)S(1)}, f32[2,1,32]{2,1,0:T(1,128)S(1)}, u32[]{:S(2)}, u32[]{:S(2)}) collective-permute-start(f32[2,1,32]{2,1,0:T(1,128)S(1)} %get-tuple-element.230), channel_id=1, source_target_pairs={{8,0},{16,8},{24,16},{32,24},{40,32},{48,40},{56,48},{64,56},{72,6... | collective-permute-start | bytes 776 | tf_op jit(solution)/shard_map/ppermute | solution.py:26
  198.7 7.3 %collective-permute-start.57 = (f32[2,1,32]{2,1,0:T(1,128)S(1)}, f32[2,1,32]{2,1,0:T(1,128)S(1)}, u32[]{:S(2)}, u32[]{:S(2)}) collective-permute-start(f32[2,1,32]{2,1,0:T(1,128)S(1)} %get-tuple-element.228), channel_id=1, source_target_pairs={{8,0},{16,8},{24,16},{32,24},{40,32},{48,40},{56,48},{64,56},{72,6... | collective-permute-start | bytes 776 | tf_op jit(solution)/shard_map/ppermute | solution.py:26
  218.2 7.3 %collective-permute-start.61 = (f32[2,1,32]{2,1,0:T(1,128)S(1)}, f32[2,1,32]{2,1,0:T(1,128)S(1)}, u32[]{:S(2)}, u32[]{:S(2)}) collective-permute-start(f32[2,1,32]{2,1,0:T(1,128)S(1)} %get-tuple-element.226), channel_id=1, source_target_pairs={{8,0},{16,8},{24,16},{32,24},{40,32},{48,40},{56,48},{64,56},{72,6... | collective-permute-start | bytes 776 | tf_op jit(solution)/shard_map/ppermute | solution.py:26
  237.6 7.3 %collective-permute-start.65 = (f32[2,1,32]{2,1,0:T(1,128)S(1)}, f32[2,1,32]{2,1,0:T(1,128)S(1)}, u32[]{:S(2)}, u32[]{:S(2)}) collective-permute-start(f32[2,1,32]{2,1,0:T(1,128)S(1)} %get-tuple-element.224), channel_id=1, source_target_pairs={{8,0},{16,8},{24,16},{32,24},{40,32},{48,40},{56,48},{64,56},{72,6... | collective-permute-start | bytes 776 | tf_op jit(solution)/shard_map/ppermute | solution.py:26
  257.4 7.4 %collective-permute-start.69 = (f32[2,1,32]{2,1,0:T(1,128)S(1)}, f32[2,1,32]{2,1,0:T(1,128)S(1)}, u32[]{:S(2)}, u32[]{:S(2)}) collective-permute-start(f32[2,1,32]{2,1,0:T(1,128)S(1)} %get-tuple-element.222), channel_id=1, source_target_pairs={{8,0},{16,8},{24,16},{32,24},{40,32},{48,40},{56,48},{64,56},{72,6... | collective-permute-start | bytes 776 | tf_op jit(solution)/shard_map/ppermute | solution.py:26
  276.8 7.3 %collective-permute-start.73 = (f32[2,1,32]{2,1,0:T(1,128)S(1)}, f32[2,1,32]{2,1,0:T(1,128)S(1)}, u32[]{:S(2)}, u32[]{:S(2)}) collective-permute-start(f32[2,1,32]{2,1,0:T(1,128)S(1)} %get-tuple-element.220), channel_id=1, source_target_pairs={{8,0},{16,8},{24,16},{32,24},{40,32},{48,40},{56,48},{64,56},{72,6... | collective-permute-start | bytes 776 | tf_op jit(solution)/shard_map/ppermute | solution.py:26
  296.2 7.3 %collective-permute-start.77 = (f32[2,1,32]{2,1,0:T(1,128)S(1)}, f32[2,1,32]{2,1,0:T(1,128)S(1)}, u32[]{:S(2)}, u32[]{:S(2)}) collective-permute-start(f32[2,1,32]{2,1,0:T(1,128)S(1)} %get-tuple-element.218), channel_id=1, source_target_pairs={{8,0},{16,8},{24,16},{32,24},{40,32},{48,40},{56,48},{64,56},{72,6... | collective-permute-start | bytes 776 | tf_op jit(solution)/shard_map/ppermute | solution.py:26
  335.2 10.2 %select_reduce_fusion = (f32[2,2,8,8,32,8]{4,5,3,2,1,0:T(8,128)}, f32[2,2,8,8,32,8]{4,5,3,2,1,0:T(8,128)S(1)}) fusion(f32[2,2,32,8,32]{4,3,2,1,0:T(8,128)S(1)} %get-tuple-element.136, pred[2,32,8,8,32,8]{4,5,3,2,1,0:T(8,128)(4,1)S(1)} %copy-done.2, f32[2,2,32,8,32]{4,3,2,1,0:T(8,128)S(1)} %get-tuple-element.135), kind=kLoop, calls=%fused_computation.2 | loop fusion | flops 8257536 | bytes 1835008 | tf_op jit(solution)/shard_map/reduce_sum | solution.py:63
  355.8 7.3 %collective-permute-start.37 = (f32[2,2,1,256]{3,2,1,0:T(1,128)S(1)}, f32[2,2,1,256]{3,2,1,0:T(1,128)S(1)}, u32[]{:S(2)}, u32[]{:S(2)}) collective-permute-start(f32[2,2,1,256]{3,2,1,0:T(1,128)S(1)} %get-tuple-element.184), channel_id=1, source_target_pairs={{8,0},{16,8},{24,16},{32,24},{40,32},{48,40},{56,48},{64,56},{72,6... | collective-permute-start | bytes 12296 | tf_op jit(solution)/shard_map/ppermute | solution.py:26
  378.3 7.3 %collective-permute-start.41 = (f32[2,2,1,256]{3,2,1,0:T(1,128)S(1)}, f32[2,2,1,256]{3,2,1,0:T(1,128)S(1)}, u32[]{:S(2)}, u32[]{:S(2)}) collective-permute-start(f32[2,2,1,256]{3,2,1,0:T(1,128)S(1)} %get-tuple-element.182), channel_id=1, source_target_pairs={{8,0},{16,8},{24,16},{32,24},{40,32},{48,40},{56,48},{64,56},{72,6... | collective-permute-start | bytes 12296 | tf_op jit(solution)/shard_map/ppermute | solution.py:26
  399.6 7.3 %collective-permute-start.45 = (f32[2,2,1,256]{3,2,1,0:T(1,128)S(1)}, f32[2,2,1,256]{3,2,1,0:T(1,128)S(1)}, u32[]{:S(2)}, u32[]{:S(2)}) collective-permute-start(f32[2,2,1,256]{3,2,1,0:T(1,128)S(1)} %get-tuple-element.180), channel_id=1, source_target_pairs={{8,0},{16,8},{24,16},{32,24},{40,32},{48,40},{56,48},{64,56},{72,6... | collective-permute-start | bytes 12296 | tf_op jit(solution)/shard_map/ppermute | solution.py:26
  420.9 7.3 %collective-permute-start.49 = (f32[2,2,1,256]{3,2,1,0:T(1,128)S(1)}, f32[2,2,1,256]{3,2,1,0:T(1,128)S(1)}, u32[]{:S(2)}, u32[]{:S(2)}) collective-permute-start(f32[2,2,1,256]{3,2,1,0:T(1,128)S(1)} %get-tuple-element.178), channel_id=1, source_target_pairs={{8,0},{16,8},{24,16},{32,24},{40,32},{48,40},{56,48},{64,56},{72,6... | collective-permute-start | bytes 12296 | tf_op jit(solution)/shard_map/ppermute | solution.py:26
  498.7 7.3 %collective-permute-start.85 = (f32[2,2,1,256]{3,2,1,0:T(1,128)S(1)}, f32[2,2,1,256]{3,2,1,0:T(1,128)S(1)}, u32[]{:S(2)}, u32[]{:S(2)}) collective-permute-start(f32[2,2,1,256]{3,2,1,0:T(1,128)S(1)} %get-tuple-element.172), channel_id=1, source_target_pairs={{8,0},{16,8},{24,16},{32,24},{40,32},{48,40},{56,48},{64,56},{72,6... | collective-permute-start | bytes 12296 | tf_op jit(solution)/shard_map/ppermute | solution.py:26
  521.2 7.3 %collective-permute-start.89 = (f32[2,2,1,256]{3,2,1,0:T(1,128)S(1)}, f32[2,2,1,256]{3,2,1,0:T(1,128)S(1)}, u32[]{:S(2)}, u32[]{:S(2)}) collective-permute-start(f32[2,2,1,256]{3,2,1,0:T(1,128)S(1)} %get-tuple-element.170), channel_id=1, source_target_pairs={{8,0},{16,8},{24,16},{32,24},{40,32},{48,40},{56,48},{64,56},{72,6... | collective-permute-start | bytes 12296 | tf_op jit(solution)/shard_map/ppermute | solution.py:26
  542.5 7.3 %collective-permute-start.93 = (f32[2,2,1,256]{3,2,1,0:T(1,128)S(1)}, f32[2,2,1,256]{3,2,1,0:T(1,128)S(1)}, u32[]{:S(2)}, u32[]{:S(2)}) collective-permute-start(f32[2,2,1,256]{3,2,1,0:T(1,128)S(1)} %get-tuple-element.168), channel_id=1, source_target_pairs={{8,0},{16,8},{24,16},{32,24},{40,32},{48,40},{56,48},{64,56},{72,6... | collective-permute-start | bytes 12296 | tf_op jit(solution)/shard_map/ppermute | solution.py:26
  585.6 7.3 %collective-permute-start.101 = (f32[2,2,1,256]{3,2,1,0:T(1,128)S(1)}, f32[2,2,1,256]{3,2,1,0:T(1,128)S(1)}, u32[]{:S(2)}, u32[]{:S(2)}) collective-permute-start(f32[2,2,1,256]{3,2,1,0:T(1,128)S(1)} %get-tuple-element.164), channel_id=1, source_target_pairs={{8,0},{16,8},{24,16},{32,24},{40,32},{48,40},{56,48},{64,56},{72,6... | collective-permute-start | bytes 12296 | tf_op jit(solution)/shard_map/ppermute | solution.py:26
  (383 shorter events, 413.7 us)
Async XLA Ops:
  1.4 68.1 %collective-permute-start.5 = (f32[2,1,32]{2,1,0:T(1,128)S(1)}, f32[2,1,32]{2,1,0:T(1,128)S(1)}, u32[]{:S(2)}, u32[]{:S(2)}) collective-permute-start(f32[2,1,32]{2,1,0:T(1,128)S(1)} %get-tuple-element.239), channel_id=1, source_target_pairs={{8,0},{16,8},{24,16},{32,24},{40,32},{48,40},{56,48},{64,56},{72,6... | collective-permute-start | bytes 776 | tf_op jit(solution)/shard_map/ppermute | solution.py:26
  6.6 64.8 %collective-permute-start.4 = (f32[2,1,32]{2,1,0:T(1,128)S(1)}, f32[2,1,32]{2,1,0:T(1,128)S(1)}, u32[]{:S(2)}, u32[]{:S(2)}) collective-permute-start(f32[2,1,32]{2,1,0:T(1,128)S(1)} %get-tuple-element.240), channel_id=1, source_target_pairs={{0,8},{8,16},{16,24},{24,32},{32,40},{40,48},{48,56},{56,64},{64,7... | collective-permute-start | bytes 776 | tf_op jit(solution)/shard_map/ppermute | solution.py:23
  9.3 64.1 %collective-permute-start.8 = (f32[2,1,32]{2,1,0:T(1,128)S(1)}, f32[2,1,32]{2,1,0:T(1,128)S(1)}, u32[]{:S(2)}, u32[]{:S(2)}) collective-permute-start(f32[2,1,32]{2,1,0:T(1,128)S(1)} %get-tuple-element.241), channel_id=1, source_target_pairs={{0,8},{8,16},{16,24},{24,32},{32,40},{40,48},{48,56},{56,64},{64,7... | collective-permute-start | bytes 776 | tf_op jit(solution)/shard_map/ppermute | solution.py:23
  11.2 62.2 %collective-permute-start.9 = (f32[2,1,32]{2,1,0:T(1,128)S(1)}, f32[2,1,32]{2,1,0:T(1,128)S(1)}, u32[]{:S(2)}, u32[]{:S(2)}) collective-permute-start(f32[2,1,32]{2,1,0:T(1,128)S(1)} %get-tuple-element.242), channel_id=1, source_target_pairs={{8,0},{16,8},{24,16},{32,24},{40,32},{48,40},{56,48},{64,56},{72,6... | collective-permute-start | bytes 776 | tf_op jit(solution)/shard_map/ppermute | solution.py:26
  19.9 308.0 %collective-permute-start.1 = (f32[2,2,1,256]{3,2,1,0:T(1,128)}, f32[2,2,1,256]{3,2,1,0:T(1,128)S(1)}, u32[]{:S(2)}, u32[]{:S(2)}) collective-permute-start(f32[2,2,1,256]{3,2,1,0:T(1,128)} %get-tuple-element.185), channel_id=1, source_target_pairs={{8,0},{16,8},{24,16},{32,24},{40,32},{48,40},{56,48},{64,56},{72,6... | collective-permute-start | bytes 12296 | tf_op jit(solution)/shard_map/ppermute | solution.py:26
  69.5 258.4 %collective-permute-start = (f32[2,2,1,256]{3,2,1,0:T(1,128)}, f32[2,2,1,256]{3,2,1,0:T(1,128)S(1)}, u32[]{:S(2)}, u32[]{:S(2)}) collective-permute-start(f32[2,2,1,256]{3,2,1,0:T(1,128)} %get-tuple-element.186), channel_id=1, source_target_pairs={{0,8},{8,16},{16,24},{24,32},{32,40},{40,48},{48,56},{56,64},{64,7... | collective-permute-start | bytes 12296 | tf_op jit(solution)/shard_map/ppermute | solution.py:23
  71.4 249.5 %collective-permute-start.32 = (f32[2,2,1,256]{3,2,1,0:T(1,128)}, f32[2,2,1,256]{3,2,1,0:T(1,128)}, u32[]{:S(2)}, u32[]{:S(2)}) collective-permute-start(f32[2,2,1,256]{3,2,1,0:T(1,128)} %get-tuple-element.187), channel_id=1, source_target_pairs={{0,8},{8,16},{16,24},{24,32},{32,40},{40,48},{48,56},{56,64},{64,7... | collective-permute-start | bytes 12296 | tf_op jit(solution)/shard_map/ppermute | solution.py:23
  91.2 11.7 %collective-permute-start.12 = (f32[2,1,32]{2,1,0:T(1,128)S(1)}, f32[2,1,32]{2,1,0:T(1,128)S(1)}, u32[]{:S(2)}, u32[]{:S(2)}) collective-permute-start(f32[2,1,32]{2,1,0:T(1,128)S(1)} %get-tuple-element.237), channel_id=1, source_target_pairs={{0,8},{8,16},{16,24},{24,32},{32,40},{40,48},{48,56},{56,64},{64,7... | collective-permute-start | bytes 776 | tf_op jit(solution)/shard_map/ppermute | solution.py:23
  93.1 9.8 %collective-permute-start.13 = (f32[2,1,32]{2,1,0:T(1,128)S(1)}, f32[2,1,32]{2,1,0:T(1,128)S(1)}, u32[]{:S(2)}, u32[]{:S(2)}) collective-permute-start(f32[2,1,32]{2,1,0:T(1,128)S(1)} %get-tuple-element.238), channel_id=1, source_target_pairs={{8,0},{16,8},{24,16},{32,24},{40,32},{48,40},{56,48},{64,56},{72,6... | collective-permute-start | bytes 776 | tf_op jit(solution)/shard_map/ppermute | solution.py:26
  113.3 16.3 %collective-permute-start.16 = (f32[2,1,32]{2,1,0:T(1,128)S(1)}, f32[2,1,32]{2,1,0:T(1,128)S(1)}, u32[]{:S(2)}, u32[]{:S(2)}) collective-permute-start(f32[2,1,32]{2,1,0:T(1,128)S(1)} %get-tuple-element.235), channel_id=1, source_target_pairs={{0,8},{8,16},{16,24},{24,32},{32,40},{40,48},{48,56},{56,64},{64,7... | collective-permute-start | bytes 776 | tf_op jit(solution)/shard_map/ppermute | solution.py:23
  115.2 14.4 %collective-permute-start.17 = (f32[2,1,32]{2,1,0:T(1,128)S(1)}, f32[2,1,32]{2,1,0:T(1,128)S(1)}, u32[]{:S(2)}, u32[]{:S(2)}) collective-permute-start(f32[2,1,32]{2,1,0:T(1,128)S(1)} %get-tuple-element.236), channel_id=1, source_target_pairs={{8,0},{16,8},{24,16},{32,24},{40,32},{48,40},{56,48},{64,56},{72,6... | collective-permute-start | bytes 776 | tf_op jit(solution)/shard_map/ppermute | solution.py:26
  138.6 10.4 %collective-permute-start.20 = (f32[2,1,32]{2,1,0:T(1,128)S(1)}, f32[2,1,32]{2,1,0:T(1,128)S(1)}, u32[]{:S(2)}, u32[]{:S(2)}) collective-permute-start(f32[2,1,32]{2,1,0:T(1,128)S(1)} %get-tuple-element.233), channel_id=1, source_target_pairs={{0,8},{8,16},{16,24},{24,32},{32,40},{40,48},{48,56},{56,64},{64,7... | collective-permute-start | bytes 776 | tf_op jit(solution)/shard_map/ppermute | solution.py:23
  235.7 10.8 %collective-permute-start.64 = (f32[2,1,32]{2,1,0:T(1,128)S(1)}, f32[2,1,32]{2,1,0:T(1,128)S(1)}, u32[]{:S(2)}, u32[]{:S(2)}) collective-permute-start(f32[2,1,32]{2,1,0:T(1,128)S(1)} %get-tuple-element.223), channel_id=1, source_target_pairs={{0,8},{8,16},{16,24},{24,32},{32,40},{40,48},{48,56},{56,64},{64,7... | collective-permute-start | bytes 776 | tf_op jit(solution)/shard_map/ppermute | solution.py:23
  255.5 9.4 %collective-permute-start.68 = (f32[2,1,32]{2,1,0:T(1,128)S(1)}, f32[2,1,32]{2,1,0:T(1,128)S(1)}, u32[]{:S(2)}, u32[]{:S(2)}) collective-permute-start(f32[2,1,32]{2,1,0:T(1,128)S(1)} %get-tuple-element.221), channel_id=1, source_target_pairs={{0,8},{8,16},{16,24},{24,32},{32,40},{40,48},{48,56},{56,64},{64,7... | collective-permute-start | bytes 776 | tf_op jit(solution)/shard_map/ppermute | solution.py:23
  274.9 9.8 %collective-permute-start.72 = (f32[2,1,32]{2,1,0:T(1,128)S(1)}, f32[2,1,32]{2,1,0:T(1,128)S(1)}, u32[]{:S(2)}, u32[]{:S(2)}) collective-permute-start(f32[2,1,32]{2,1,0:T(1,128)S(1)} %get-tuple-element.219), channel_id=1, source_target_pairs={{0,8},{8,16},{16,24},{24,32},{32,40},{40,48},{48,56},{56,64},{64,7... | collective-permute-start | bytes 776 | tf_op jit(solution)/shard_map/ppermute | solution.py:23
  294.3 17.2 %collective-permute-start.76 = (f32[2,1,32]{2,1,0:T(1,128)S(1)}, f32[2,1,32]{2,1,0:T(1,128)S(1)}, u32[]{:S(2)}, u32[]{:S(2)}) collective-permute-start(f32[2,1,32]{2,1,0:T(1,128)S(1)} %get-tuple-element.217), channel_id=1, source_target_pairs={{0,8},{8,16},{16,24},{24,32},{32,40},{40,48},{48,56},{56,64},{64,7... | collective-permute-start | bytes 776 | tf_op jit(solution)/shard_map/ppermute | solution.py:23
  296.2 15.3 %collective-permute-start.77 = (f32[2,1,32]{2,1,0:T(1,128)S(1)}, f32[2,1,32]{2,1,0:T(1,128)S(1)}, u32[]{:S(2)}, u32[]{:S(2)}) collective-permute-start(f32[2,1,32]{2,1,0:T(1,128)S(1)} %get-tuple-element.218), channel_id=1, source_target_pairs={{8,0},{16,8},{24,16},{32,24},{40,32},{48,40},{56,48},{64,56},{72,6... | collective-permute-start | bytes 776 | tf_op jit(solution)/shard_map/ppermute | solution.py:26
  322.0 30.1 %collective-permute-start.34 = (f32[2,2,66,1]{3,2,1,0:T(8,128)S(1)}, f32[2,2,66,1]{3,2,1,0:T(8,128)S(1)}, u32[]{:S(2)}, u32[]{:S(2)}) collective-permute-start(f32[2,2,66,1]{3,2,1,0:T(8,128)S(1)} %get-tuple-element.161), channel_id=1, source_target_pairs={{0,1},{1,2},{2,3},{3,4},{4,5},{5,6},{6,7},{8,9},{9,10},{10,11},{11... | collective-permute-start | bytes 3176 | tf_op jit(solution)/shard_map/ppermute | solution.py:23
  325.2 27.0 %collective-permute-start.35 = (f32[2,2,66,1]{3,2,1,0:T(8,128)S(1)}, f32[2,2,66,1]{3,2,1,0:T(8,128)}, u32[]{:S(2)}, u32[]{:S(2)}) collective-permute-start(f32[2,2,66,1]{3,2,1,0:T(8,128)S(1)} %get-tuple-element.162), channel_id=1, source_target_pairs={{1,0},{2,1},{3,2},{4,3},{5,4},{6,5},{7,6},{9,8},{10,9},{11,10},{12... | collective-permute-start | bytes 3176 | tf_op jit(solution)/shard_map/ppermute | solution.py:26
  328.1 24.1 %collective-permute-start.3 = (f32[2,2,66,1]{3,2,1,0:T(8,128)S(1)}, f32[2,2,66,1]{3,2,1,0:T(8,128)}, u32[]{:S(2)}, u32[]{:S(2)}) collective-permute-start(f32[2,2,66,1]{3,2,1,0:T(8,128)S(1)} %get-tuple-element.159), channel_id=1, source_target_pairs={{1,0},{2,1},{3,2},{4,3},{5,4},{6,5},{7,6},{9,8},{10,9},{11,10},{12... | collective-permute-start | bytes 3176 | tf_op jit(solution)/shard_map/ppermute | solution.py:26
  330.8 21.4 %collective-permute-start.2 = (f32[2,2,66,1]{3,2,1,0:T(8,128)S(1)}, f32[2,2,66,1]{3,2,1,0:T(8,128)}, u32[]{:S(2)}, u32[]{:S(2)}) collective-permute-start(f32[2,2,66,1]{3,2,1,0:T(8,128)S(1)} %get-tuple-element.160), channel_id=1, source_target_pairs={{0,1},{1,2},{2,3},{3,4},{4,5},{5,6},{6,7},{8,9},{9,10},{10,11},{11... | collective-permute-start | bytes 3176 | tf_op jit(solution)/shard_map/ppermute | solution.py:23
  440.3 9.4 %collective-permute-start.52 = (f32[2,2,1,256]{3,2,1,0:T(1,128)S(1)}, f32[2,2,1,256]{3,2,1,0:T(1,128)S(1)}, u32[]{:S(2)}, u32[]{:S(2)}) collective-permute-start(f32[2,2,1,256]{3,2,1,0:T(1,128)S(1)} %get-tuple-element.175), channel_id=1, source_target_pairs={{0,8},{8,16},{16,24},{24,32},{32,40},{40,48},{48,56},{56,64},{64,7... | collective-permute-start | bytes 12296 | tf_op jit(solution)/shard_map/ppermute | solution.py:23
  473.5 21.6 %collective-permute-start.82 = (f32[2,2,66,1]{3,2,1,0:T(8,128)}, f32[2,2,66,1]{3,2,1,0:T(8,128)}, u32[]{:S(2)}, u32[]{:S(2)}) collective-permute-start(f32[2,2,66,1]{3,2,1,0:T(8,128)} %get-tuple-element.147), channel_id=1, source_target_pairs={{0,1},{1,2},{2,3},{3,4},{4,5},{5,6},{6,7},{8,9},{9,10},{10,11},{11... | collective-permute-start | bytes 3176 | tf_op jit(solution)/shard_map/ppermute | solution.py:23
  475.4 19.7 %collective-permute-start.83 = (f32[2,2,66,1]{3,2,1,0:T(8,128)}, f32[2,2,66,1]{3,2,1,0:T(8,128)}, u32[]{:S(2)}, u32[]{:S(2)}) collective-permute-start(f32[2,2,66,1]{3,2,1,0:T(8,128)} %get-tuple-element.148), channel_id=1, source_target_pairs={{1,0},{2,1},{3,2},{4,3},{5,4},{6,5},{7,6},{9,8},{10,9},{11,10},{12... | collective-permute-start | bytes 3176 | tf_op jit(solution)/shard_map/ppermute | solution.py:26
  (103 other events, 1437.5 us)
where the time goes:
time: 615 us; the launch traced here: 607 us
  starting transfers between devices  379 us (62%)
  waiting for transfers between devices  105 us (17%)
  local copies, waits for them, and re-layouts  43 us (7%)
  other arithmetic  41.8 us (7%)
  blocking collectives  35.4 us (6%)
    ppermute x52, starting transfers between devices, with_halo(): lax.ppermute(lax.slice_in_dim(block, 0, width, axis=dim), axis, backward)  268 us
    ppermute x52, starting transfers between devices, with_halo(): lax.ppermute(lax.slice_in_dim(block, block.shape[dim] - width, None, axis...  111 us
    ppermute x52, waiting for transfers between devices, with_halo(): lax.ppermute(lax.slice_in_dim(block, 0, width, axis=dim), axis, backward)  89.5 us
    all_gather x2, blocking collectives, prefix(): gathered = lax.all_gather(part, axis)  28.2 us
    ppermute x52, waiting for transfers between devices, with_halo(): lax.ppermute(lax.slice_in_dim(block, block.shape[dim] - width, None, axis...  15.3 us
    broadcast_in_dim x5, local copies, waits for them, and re-layouts, place_cells(): placed = jnp.where(hit, values[..., :, None, :, None], 0.0)  14.1 us
    reduce_sum x2, other arithmetic, place_sum(): placed = jnp.sum(jnp.where(hit, values[..., :, None, :, None], 0.0), axis=2)  12.6 us
  transfers between devices with their start and end apart: 104, of which 51 were waited for; matrix products, arithmetic and copies ran while one was open for 11% of the time, Pallas kernels for 0%

commit v1 on v0

v1 whole, which is shorter than its diff:
```python
import jax
import jax.numpy as jnp
from jax import lax
from jax.experimental import pallas as pl
from jax.experimental.pallas import tpu as pltpu
from jax.sharding import PartitionSpec as P

SWEEPS = 6
STEPS = 2
VIAS = 32

VIA_CONDUCT = 1.0
VIA_RESIST = 4.0
BUMP_CONDUCT = 50.0
BASE_CAPACITY = 0.1
LOWER_BOUND = 0.1
UPPER_BOUND = 1.9

MIDDLE = 0.5 * (UPPER_BOUND + LOWER_BOUND)
HALF = 0.5 * (UPPER_BOUND - LOWER_BOUND)

GROUPS = 12
F32 = jnp.float32


def sweep_weights():
    scaled = MIDDLE / HALF
    ratio = 1.0 / scaled
    pairs = []
    for _ in range(SWEEPS - 1):
        following = 1.0 / (2.0 * scaled - ratio)
        pairs.append((following * ratio, 2.0 * following / HALF))
        ratio = following
    return pairs


WEIGHTS = sweep_weights()


def lane_iota():
    return lax.broadcasted_iota(jnp.int32, (8, 128), 1)


def sub_iota(width=128):
    return lax.broadcasted_iota(jnp.int32, (8, width), 0)


def roll(x, shift, axis):
    shift = shift % x.shape[axis]
    return pltpu.roll(x, shift, axis) if shift else x


def rows(g):
    return pl.ds(8 * g, 8)


def pack_kernel(die_ref, via_ref, cell_ref, load_ref, load_cell_ref, packed_ref, cells_ref, loads_ref, send_ref):
    later = die_ref[0].astype(F32)

    def one(v, total):
        parts = []
        for d in range(2):
            part = jnp.concatenate([via_ref[t, d, n, v] for t in range(2) for n in range(2)], axis=1)
            packed_ref[d, v] = part
            parts.append(part)
        both = parts[0] + parts[1]
        send_ref[v] = both + later * parts[0]
        return total + both

    send_ref[VIAS] = lax.fori_loop(0, VIAS, one, jnp.zeros((8, 128), F32))

    def four(q, carry):
        for d in range(2):
            cells_ref[d, q] = jnp.concatenate([cell_ref[d, 4 * q + k] for k in range(4)], axis=1)
        return carry

    lax.fori_loop(0, VIAS // 4, four, 0)
    for d in range(2):
        loads_ref[d] = jnp.concatenate([load_ref[t, d, n] for t in range(2) for n in range(2)], axis=1)
    loads_ref[2] = jnp.concatenate([load_cell_ref[0].astype(F32), load_cell_ref[1].astype(F32)] * 2, axis=1)


def shared(first, second, shift):
    return jnp.where(sub_iota() < shift, first, roll(second, shift, 0))


def shared_low(first, second, shift):
    return jnp.where(sub_iota() >= shift, first, roll(second, shift, 0))


def place_kernel(
    die_ref, bump_ref, packed_ref, cells_ref, loads_ref, send_ref, got_ref, sheet_ref, cap_ref, drop_ref, base_sheet_ref,
    base_start_ref, counts_ref, field_ref, up_ref, down_ref, base_ref,
):
    lane = lane_iota()
    sub = sub_iota()
    later = die_ref[0].astype(F32)
    weights = (
        (VIA_RESIST * (4.0 - 2.0 * later), VIA_RESIST * (3.0 - 2.0 * later), VIA_RESIST * (1.0 + later)),
        (VIA_RESIST * (3.0 - 2.0 * later), VIA_RESIST * (3.0 - 2.0 * later), VIA_RESIST),
    )
    within = lane % 8
    for d in range(2):
        for half in range(2):
            spread = half * 16 + lane // 8

            def add(state, cell, values, count):
                code = cell - within
                out = []
                for oi in range(8):
                    hit = code == 8 * oi
                    base = oi * 5
                    for m in range(4):
                        out.append(state[base + m] + jnp.where(hit, values[m], 0.0))
                    out.append(state[base + 4] + jnp.where(hit, 1.0, 0.0) if count else state[base + 4])
                return tuple(out)

            def four(q, state):
                cells = cells_ref[d, q]
                for k in range(4):
                    v = 4 * q + k
                    cell = jnp.take_along_axis(cells, spread + 32 * k, axis=1)
                    mixed = (
                        weights[d][0] * packed_ref[0, v] + weights[d][1] * packed_ref[1, v] + weights[d][2] * got_ref[v]
                    )
                    values = [jnp.take_along_axis(mixed, spread + 32 * m, axis=1) for m in range(4)]
                    state = add(state, cell, values, True)
                return state

            state = tuple(jnp.zeros((8, 128), F32) for _ in range(40))
            state = lax.fori_loop(0, VIAS // 4, four, state)
            load_cell = jnp.take_along_axis(loads_ref[2], spread + 32 * d, axis=1).astype(jnp.int32)
            load = loads_ref[d]
            state = add(
                state, load_cell, [jnp.take_along_axis(load, spread + 32 * m, axis=1) for m in range(4)], False
            )
            for oi in range(8):
                for m in range(4):
                    field_ref[m // 2, d, m % 2, half, pl.ds(oi, 8, stride=8), :] = state[oi * 5 + m]
                counts_ref[d, half, pl.ds(oi, 8, stride=8), :] = state[oi * 5 + 4]

    place = 0

    def put(up, down):
        nonlocal place
        up_ref[rows(place), :] = up
        down_ref[rows(place), :] = down
        place += 1

    def pair(first, second):
        put(first(0), first(7))
        put(second(0), second(7))
        put(shared(first(1), second(1), 4), shared_low(first(6), second(6), 4))

    for d in range(2):
        for half in range(2):
            lanes = pl.ds(half * 128, 128)
            for n in range(2):
                pair(lambda g: sheet_ref[d, n, rows(g), lanes], lambda g: drop_ref[d, n, rows(g), lanes])
                one = lambda g: field_ref[0, d, n, half, rows(g), :]
                two = lambda g: field_ref[1, d, n, half, rows(g), :]
                put(one(0), one(7))
                put(shared(one(1), two(0), 3), shared_low(one(6), two(7), 5))
            pair(lambda g: cap_ref[d, rows(g), lanes], lambda g: counts_ref[d, half, rows(g), :])

    own = (lane % 64 >= 16) & (lane % 64 < 48)
    zeros32 = jnp.zeros((8, 16), F32)

    def spread_nets(first, second):
        return jnp.concatenate([zeros32, first, zeros32, zeros32, second, zeros32], axis=1)

    arriving = send_ref[VIAS] + got_ref[VIAS]
    bump = jnp.zeros((8, 128), F32)
    column = lane % 64 - 16
    for k in range(4):
        bump = jnp.where((column // 8 == k) & (sub * 8 + column % 8 == bump_ref[0, k]), 1.0, bump)
    parts = [
        spread_nets(base_sheet_ref[0], base_sheet_ref[1]),
        spread_nets(base_start_ref[0], base_start_ref[1]),
    ]
    for t in range(2):
        moved = jnp.where(lane < 64, roll(arriving, 16 - 64 * t, 1), roll(arriving, 48 - 64 * t, 1))
        parts.append(jnp.where(own, moved, 0.0))
    parts.append(jnp.where(own, bump, 0.0))
    for part in range(5):
        base_ref[rows(part), :] = parts[part]
        put(parts[part], parts[part])


ROW_GROUPS = 57


def row_place(d, half, n, kind):
    start = (d * 2 + half) * 13
    return start + 10 if kind == 2 else start + 5 * n + 3 * kind


def below_rows(ref, d, half, n, kind, second):
    start = row_place(d, half, n, kind)
    if kind == 1:
        if second:
            return roll(ref[rows(start + 1), :], -3, 0), None
        return ref[rows(start), :], ref[rows(start + 1), :]
    last = ref[rows(start + 2), :]
    if second:
        return ref[rows(start + 1), :], roll(last, -4, 0)
    return ref[rows(start), :], last


def above_rows(ref, d, half, n, kind, second):
    start = row_place(d, half, n, kind)
    if kind == 1:
        if second:
            return roll(ref[rows(start + 1), :], -5, 0), None
        return ref[rows(start), :], ref[rows(start + 1), :]
    last = ref[rows(start + 2), :]
    if second:
        return ref[rows(start + 1), :], roll(last, -4, 0)
    return ref[rows(start), :], last


def column_groups(own, below, above, d, half, n, kind, second):
    low = below_rows(below, d, half, n, kind, second)
    high = above_rows(above, d, half, n, kind, second)
    return [own(g) for g in range(8)] + [low[0], low[1], high[1], high[0]]


BASE_ROWS = (0, 1, 2, 3, 4)


def base_groups(base_ref, below_ref, above_ref, below2_ref, above2_ref, field):
    start = ROW_GROUPS - 5 + field
    return [
        base_ref[rows(field), :], below_ref[rows(start), :], below2_ref[rows(field), :],
        above2_ref[rows(field), :], above_ref[rows(start), :],
    ]


COL_GROUPS = 2 * GROUPS + 10


def strip_kernel(
    sheet_ref, cap_ref, drop_ref, counts_ref, field_ref, base_ref, below_ref, above_ref, below2_ref, above2_ref,
    left_ref, right_ref,
):
    lane = lane_iota()
    within = lane % 16

    def fields(half):
        lanes = pl.ds(half * 128, 128)
        first, second = [], []
        for d in range(2):
            for n in range(2):
                first.append(column_groups(
                    lambda g: sheet_ref[d, n, rows(g), lanes], below_ref, above_ref, d, half, n, 0, False))
        for d in range(2):
            for n in range(2):
                first.append(column_groups(
                    lambda g: drop_ref[d, n, rows(g), lanes], below_ref, above_ref, d, half, n, 0, True))
        for d in range(2):
            second.append(column_groups(
                lambda g: cap_ref[d, rows(g), lanes], below_ref, above_ref, d, half, 0, 2, False))
        for d in range(2):
            second.append(column_groups(
                lambda g: counts_ref[d, half, rows(g), :], below_ref, above_ref, d, half, 0, 2, True))
        for d in range(2):
            for n in range(2):
                one = column_groups(
                    lambda g: field_ref[0, d, n, half, rows(g), :], below_ref, above_ref, d, half, n, 1, False)
                two = column_groups(
                    lambda g: field_ref[1, d, n, half, rows(g), :], below_ref, above_ref, d, half, n, 1, True)
                merged = []
                for a, b in zip(one, two):
                    if b is None:
                        merged.append(a)
                    elif half == 0:
                        merged.append(jnp.where(within < 11, a, roll(b, 11, 1)))
                    else:
                        merged.append(jnp.where(within >= 5, a, roll(b, -11, 1)))
                second.append(merged)
        return first, second

    def join(chunks, origin):
        out = roll(chunks[0], -origin, 1)
        for k in range(1, 8):
            out = jnp.where(lane // 16 == k, roll(chunks[k], 16 * k - origin, 1), out)
        return out

    for half, ref, origin in ((0, left_ref, 0), (1, right_ref, 112)):
        for part, chunks in enumerate(fields(half)):
            for g in range(GROUPS):
                ref[rows(part * GROUPS + g), :] = join([chunk[g] for chunk in chunks], origin)

    start = 2 * GROUPS
    groups = [
        base_groups(base_ref, below_ref, above_ref, below2_ref, above2_ref, field) for field in range(5)
    ]
    quarter = (lane % 64) // 16
    for g in range(5):
        sheet, drop, one, two, bump = [groups[field][g] for field in range(5)]
        left = jnp.where(
            quarter == 1, sheet,
            jnp.where(quarter == 2, roll(drop, 16, 1), jnp.where(quarter == 3, roll(one, 32, 1), roll(two, -16, 1))),
        )
        right = jnp.where(
            quarter == 2, sheet,
            jnp.where(quarter == 3, roll(drop, 16, 1), jnp.where(quarter == 1, roll(two, -16, 1), roll(one, -32, 1))),
        )
        left_ref[rows(start + g), :] = left
        right_ref[rows(start + g), :] = right
        left_ref[rows(start + 5 + g), :] = bump
        right_ref[rows(start + 5 + g), :] = bump


def connect(center, neighbour):
    return jnp.where(neighbour > 0.0, 2.0 / (center + neighbour), 0.0)


def base_solve(fields):
    sheet, start, arriving, bump = fields
    steps = [(1, 0), (-1, 0), (1, 1), (-1, 1)]
    inside = sheet > 0.0
    links = [jnp.where(inside, connect(sheet, roll(sheet, s, a)), 0.0) for s, a in steps]
    diagonal = BASE_CAPACITY + links[0] + links[1] + links[2] + links[3] + BUMP_CONDUCT * bump
    inverse = 1.0 / diagonal
    links = [inverse * link for link in links]

    def coupled(v):
        return (links[0] * roll(v, 1, 0) + links[1] * roll(v, -1, 0)) + (
            links[2] * roll(v, 1, 1) + links[3] * roll(v, -1, 1)
        )

    state, results = start, []
    for t in range(STEPS):
        source = BASE_CAPACITY * state + arriving[t]
        residual = inverse * source - (state - coupled(state))
        update = residual / MIDDLE
        for k in range(SWEEPS):
            state = state + update
            if k + 1 < SWEEPS:
                residual = residual - (update - coupled(update))
                update = WEIGHTS[k][0] * update + WEIGHTS[k][1] * residual
        results.append(state)
    return results


def needed(halo):
    if halo > 8:
        return list(range(GROUPS))
    return list(range(8)) + ([8, 11] if halo > 0 else [])


def solve_kernel(
    sheet_ref, cap_ref, drop_ref, counts_ref, field_ref, base_ref, below_ref, above_ref, below2_ref, above2_ref,
    fromleft_ref, fromright_ref, out_ref, base_out_ref,
    s_ext, x_ext, c_ext, k_ext, f_ext, base_ext, link_up, link_down, link_left, link_right, inv_ext, res, upd,
):
    lane = lane_iota()

    groups = [
        base_groups(base_ref, below_ref, above_ref, below2_ref, above2_ref, field) for field in range(5)
    ]
    start = 2 * GROUPS
    quarter = (lane % 64) // 16
    from_left = [fromleft_ref[rows(start + g), :] for g in range(10)]
    from_right = [fromright_ref[rows(start + g), :] for g in range(10)]
    fields = []
    for field in range(5):
        out = []
        for g in range(5):
            right_shift = (32, 16, 0, 48, 32)[field]
            left_shift = (-32, -48, 0, -16, -32)[field]
            group = g + 5 * (field == 4)
            value = jnp.where(quarter == 3, roll(from_right[group], right_shift, 1), groups[field][g])
            out.append(jnp.where(quarter == 0, roll(from_left[group], left_shift, 1), value))
        fields.append(jnp.concatenate(out, axis=0))
    solved = base_solve((fields[0], fields[1], (fields[2], fields[3]), fields[4]))
    for t in range(STEPS):
        base_ext[t] = solved[t]
    for n in range(2):
        base_out_ref[n] = roll(solved[1][0:8], -(64 * n + 16), 1)[:, 0:32]

    def third(part, chunk, g):
        right = fromright_ref[rows(part * GROUPS + g), :]
        left = fromleft_ref[rows(part * GROUPS + g), :]
        value = jnp.where(lane < 16, roll(right, -16 * chunk, 1), 0.0)
        return jnp.where(lane >= 112, roll(left, 112 - 16 * chunk, 1), value)

    def fill(target, index, own, d, n, kind, second, part, chunk, shift=0):
        for half in range(2):
            for g, value in enumerate(
                column_groups(lambda g: own(half, g), below_ref, above_ref, d, half, n, kind, second)
            ):
                if value is not None:
                    target[index, rows(g), pl.ds(half * 128, 128)] = value
        for g in range(GROUPS):
            if shift and g in (9, 10):
                continue
            value = third(part, chunk, g)
            if shift:
                value = jnp.where(lane < 64, roll(value, -shift, 1), roll(value, shift, 1))
            target[index, rows(g), pl.ds(256, 128)] = value

    for d in range(2):
        fill(c_ext, d, lambda half, g: cap_ref[d, rows(g), pl.ds(half * 128, 128)], d, 0, 2, False, 1, d)
        fill(k_ext, d, lambda half, g: counts_ref[d, half, rows(g), :], d, 0, 2, True, 1, 2 + d)
        for n in range(2):
            i = 2 * d + n
            fill(s_ext, i, lambda half, g: sheet_ref[d, n, rows(g), pl.ds(half * 128, 128)], d, n, 0, False, 0, i)
            fill(x_ext, i, lambda half, g: drop_ref[d, n, rows(g), pl.ds(half * 128, 128)], d, n, 0, True, 0, 4 + i)
            fill(f_ext, i, lambda half, g: field_ref[0, d, n, half, rows(g), :], d, n, 1, False, 1, 4 + i)
            fill(f_ext, 4 + i, lambda half, g: field_ref[1, d, n, half, rows(g), :], d, n, 1, True, 1, 4 + i, 11)

    sub = sub_iota(384)
    tile = [lane // 8 + 16, lane // 8 + 32, jnp.where(lane < 64, lane // 8 + 48, lane // 8 + 14 - 14)]

    def image(i, carry):
        d = i // 2
        n = i % 2

        def get(ref, g):
            return ref[rows(g % GROUPS), :]

        def above(value, before):
            return jnp.where(sub == 0, roll(before, 1, 0), roll(value, 1, 0))

        def below(value, after):
            return jnp.where(sub == 7, roll(after, -1, 0), roll(value, -1, 0))

        for g in range(GROUPS):
            here = s_ext[i, rows(g), :]
            after = s_ext[i, rows((g + 1) % GROUPS), :]
            inside = here > 0.0
            down = jnp.where(inside, connect(here, below(here, after)), 0.0)
            right = jnp.where(inside, connect(here, roll(here, -1, 1)), 0.0)
            link_down[rows(g), :] = down
            link_right[rows(g), :] = right
            link_left[rows(g), :] = roll(right, 1, 1)
        for g in range(GROUPS):
            link_up[rows(g), :] = above(get(link_down, g), get(link_down, g - 1))
        for g in range(GROUPS):
            ups, downs = get(link_up, g), get(link_down, g)
            lefts, rights = get(link_left, g), get(link_right, g)
            diagonal = c_ext[d, rows(g), :] + ups + downs + lefts + rights + VIA_CONDUCT * k_ext[d, rows(g), :]
            inverse = jnp.where(diagonal > 0.0, 1.0 / diagonal, 0.0)
            inv_ext[rows(g), :] = inverse
            link_up[rows(g), :] = inverse * ups
            link_left[rows(g), :] = inverse * lefts
            link_right[rows(g), :] = inverse * rights
        for g in range(GROUPS):
            link_down[rows(g), :] = get(inv_ext, g) * get(link_down, g)

        def apply(read, groups, use):
            values = {}
            for g in groups:
                for near in (g - 1, g, g + 1):
                    if near % GROUPS not in values:
                        values[near % GROUPS] = read(near % GROUPS)
                value = values[g]
                total = get(link_up, g) * above(value, values[(g - 1) % GROUPS])
                total = total + get(link_down, g) * below(value, values[(g + 1) % GROUPS])
                total = total + get(link_left, g) * roll(value, 1, 1) + get(link_right, g) * roll(value, -1, 1)
                use(g, value, total)

        for t in range(STEPS):
            halo = 11 - 6 * t

            def begin(g, value, total):
                row = 2 * n
                spread = base_ext[t, pl.ds(base_row(g), 1), :]
                spread = jnp.broadcast_to(spread, (8, 128))
                pieces = [jnp.take_along_axis(spread, index + 32 * row, axis=1) for index in tile]
                bound = jnp.concatenate(pieces, axis=1)
                source = c_ext[d, rows(g), :] * value + f_ext[4 * t + i, rows(g), :] + k_ext[d, rows(g), :] * bound
                residual = get(inv_ext, g) * source - (value - total)
                res[rows(g), :] = residual
                upd[0, rows(g), :] = residual / MIDDLE

            apply(lambda g: x_ext[i, rows(g), :], needed(halo), begin)
            last = needed(6 - 6 * t)
            for k in range(SWEEPS):
                if k + 1 == SWEEPS:
                    for g in last:
                        value = x_ext[i, rows(g), :] + upd[k % 2, rows(g), :]
                        x_ext[i, rows(g), :] = value
                    break

                def advance(g, value, total):
                    if g in last:
                        x_ext[i, rows(g), :] = x_ext[i, rows(g), :] + value
                    residual = res[rows(g), :] - (value - total)
                    res[rows(g), :] = residual
                    upd[(k + 1) % 2, rows(g), :] = WEIGHTS[k][0] * value + WEIGHTS[k][1] * residual

                apply(lambda g: upd[k % 2, rows(g), :], needed(halo - 1 - k), advance)
        for g in range(8):
            out_ref[d, n, rows(g), :] = x_ext[i, rows(g), pl.ds(0, 256)]
        return carry

    lax.fori_loop(0, 4, image, 0)


def base_row(g):
    return g if g < 10 else 28 + g


def spec(count):
    return [pl.BlockSpec(memory_space=pltpu.VMEM)] * count


def smem():
    return pl.BlockSpec(memory_space=pltpu.SMEM)


def call(kernel, name, outs, ins, scratch=(), limit=24):
    return pl.pallas_call(
        kernel,
        out_shape=outs,
        in_specs=ins,
        out_specs=spec(len(outs)),
        scratch_shapes=list(scratch),
        compiler_params=pltpu.CompilerParams(vmem_limit_bytes=limit * 1024 * 1024),
        name=name,
    )


def arr(*shape, dtype=F32):
    return jax.ShapeDtypeStruct(shape, dtype)


def per_device(
    sheet_res, capacity, drop_start, load_cell, load_current, via_cell, via_current, base_sheet, base_start, bump_cell
):
    die = lax.axis_index("die").astype(jnp.int32).reshape(1)
    row_count = lax.axis_size("row")
    col_count = lax.axis_size("col")

    packed, cells, loads, send = call(
        pack_kernel, "pack_vias",
        (arr(2, VIAS, 8, 128), arr(2, VIAS // 4, 8, 128, dtype=jnp.int32), arr(3, 8, 128), arr(VIAS + 1, 8, 128)),
        [smem()] + spec(4),
    )(die, via_current, via_cell, load_current, load_cell)
    got = lax.ppermute(send, "die", [(0, 1), (1, 0)])

    rows_shape = arr(8 * ROW_GROUPS, 128)
    counts, field, up, down, base = call(
        place_kernel, "place_vias",
        (arr(2, 2, 64, 128), arr(2, 2, 2, 2, 64, 128), rows_shape, rows_shape, arr(40, 128)),
        [smem(), smem()] + spec(10),
    )(die, bump_cell, packed, cells, loads, send, got, sheet_res, capacity, drop_start, base_sheet, base_start)

    below = lax.ppermute(up, "row", [(i + 1, i) for i in range(row_count - 1)])
    above = lax.ppermute(down, "row", [(i, i + 1) for i in range(row_count - 1)])
    below2 = lax.ppermute(base, "row", [(i + 2, i) for i in range(row_count - 2)])
    above2 = lax.ppermute(base, "row", [(i, i + 2) for i in range(row_count - 2)])

    strip_shape = arr(8 * COL_GROUPS, 128)
    left, right = call(strip_kernel, "column_strips", (strip_shape, strip_shape), spec(10))(
        sheet_res, capacity, drop_start, counts, field, base, below, above, below2, above2
    )
    from_right = lax.ppermute(left, "col", [(i + 1, i) for i in range(col_count - 1)])
    from_left = lax.ppermute(right, "col", [(i, i + 1) for i in range(col_count - 1)])

    ext = (96, 384)
    scratch = [
        pltpu.VMEM((4,) + ext, F32), pltpu.VMEM((4,) + ext, F32), pltpu.VMEM((2,) + ext, F32),
        pltpu.VMEM((2,) + ext, F32), pltpu.VMEM((8,) + ext, F32), pltpu.VMEM((2, 40, 128), F32),
    ] + [pltpu.VMEM(ext, F32)] * 6 + [pltpu.VMEM((2,) + ext, F32)]
    return call(
        solve_kernel, "solve", (arr(2, 2, 64, 256), arr(2, 8, 32)), spec(12), scratch,
    )(sheet_res, capacity, drop_start, counts, field, base, below, above, below2, above2, from_left, from_right)


def solution(mesh):
    in_specs = (
        P("die", None, "row", "col"),
        P("die", "row", "col"),
        P("die", None, "row", "col"),
        P("die", "row", "col"),
        P(None, "die", None, "row", "col"),
        P("die", None, "row", "col"),
        P(None, "die", None, None, "row", "col"),
        P(None, "row", "col"),
        P(None, "row", "col"),
        P("row", "col"),
    )
    out_specs = (P("die", None, "row", "col"), P(None, "row", "col"))
    return jax.shard_map(
        per_device, mesh=mesh, in_specs=in_specs, out_specs=out_specs, check_vma=False
    )
```

time: 615 us -> 61.8 us (0.10)
  the two profiles are of different devices: /device:TPU:102 before, /device:TPU:120 now
where the time goes in v1:
time: 61.8 us; the launch traced here: 61.4 us
  starting transfers between devices  20.4 us (33%)
  Pallas kernels  18.6 us (30%)
  waiting for transfers between devices  17.4 us (28%)
  local copies, waits for them, and re-layouts  4.26 us (7%)
  between operations  0.77 us (1%)
    pallas_call x1, Pallas kernels, per_device(): call(solve_kernel, 'solve', (arr(2, 2, 64, 256), arr(2, 8, 32)), spec(12)...  9.65 us
    ppermute x1, waiting for transfers between devices, per_device(): lax.ppermute(base, 'row', [(i + 2, i) for i in range(row_count - 2)])  7.35 us
    ppermute x1, starting transfers between devices, per_device(): lax.ppermute(base, 'row', [(i, i + 2) for i in range(row_count - 2)])  5.62 us
    ppermute x1, waiting for transfers between devices, per_device(): lax.ppermute(left, 'col', [(i + 1, i) for i in range(col_count - 1)])  5.58 us
    pallas_call x1, Pallas kernels, per_device(): call(place_kernel, 'place_vias', (arr(2, 2, 64, 128), arr(2, 2, 2, 2, 64,...  5.34 us
    ppermute x1, starting transfers between devices, per_device(): lax.ppermute(right, 'col', [(i, i + 1) for i in range(col_count - 1)])  5.04 us
    unnamed x20, local copies, waits for them, and re-layouts  4.26 us
    ppermute x1, waiting for transfers between devices, per_device(): got = lax.ppermute(send, 'die', [(0, 1), (1, 0)])  3.83 us
  transfers between devices with their start and end apart: 7, of which 4 were waited for; matrix products, arithmetic and copies ran while one was open for 0% of the time, Pallas kernels for 0%

profile of v1, /device:TPU:120, one launch (start us, length us, event | category | flops | bytes accessed | tf_op | source)
XLA Modules:
  0.0 61.4 jit_solution(6041029856238989426)
XLA Ops:
  0.6 0.7 %copy-done.6 = s32[2,8,32]{2,1,0:T(8,128)S(1)} copy-done((s32[2,8,32]{2,1,0:T(8,128)S(1)}, s32[2,8,32]{2,1,0:T(8,128)}, u32[]{:S(2)}) %copy-start.6) | copy-done | bytes 2072
  1.3 1.2 %copy-done.3 = f32[2,2,2,32,8,32]{5,4,3,2,1,0:T(8,128)S(1)} copy-done((f32[2,2,2,32,8,32]{5,4,3,2,1,0:T(8,128)S(1)}, f32[2,2,2,32,8,32]{5,4,3,2,1,0:T(8,128)}, u32[]{:S(2)}) %copy-start.3) | copy-done | bytes 262168
  2.6 0.9 %copy-done.4 = s32[2,32,8,32]{3,2,1,0:T(8,128)S(1)} copy-done((s32[2,32,8,32]{3,2,1,0:T(8,128)S(1)}, s32[2,32,8,32]{3,2,1,0:T(8,128)}, u32[]{:S(2)}) %copy-start.4) | copy-done | bytes 65560
  3.5 0.8 %copy-done.5 = f32[2,2,2,8,32]{4,3,2,1,0:T(8,128)S(1)} copy-done((f32[2,2,2,8,32]{4,3,2,1,0:T(8,128)S(1)}, f32[2,2,2,8,32]{4,3,2,1,0:T(8,128)}, u32[]{:S(2)}) %copy-start.5) | copy-done | bytes 8216
  4.3 0.0 copy-start.8
  4.3 3.1 %pack_vias.1 = (f32[2,32,8,128]{3,2,1,0:T(8,128)S(1)}, s32[2,8,8,128]{3,2,1,0:T(8,128)S(1)}, f32[3,8,128]{2,1,0:T(8,128)S(1)}, f32[33,8,128]{2,1,0:T(8,128)S(1)}) custom-call(s32[1]{0:T(128)} %bitcast.die_ref, f32[2,2,2,32,8,32]{5,4,3,2,1,0:T(8,128)S(1)} %copy-done.3, s32[2,32,8,32]{3,2,1,0:T(8,128)S(1)} %copy-done.4, f32[2,2,2,8,32]{4,3,2,1,0:T(8,128)S(1)} %copy-done.5, ...), custom_call_target="tpu_custom_call" | custom-call | tf_op jit(solution)/shard_map/pack_vias/pallas_call | solution.py:538
  7.3 1.6 %collective-permute-start = (f32[33,8,128]{2,1,0:T(8,128)S(1)}, f32[33,8,128]{2,1,0:T(8,128)S(1)}, u32[]{:S(2)}, u32[]{:S(2)}) collective-permute-start(f32[33,8,128]{2,1,0:T(8,128)S(1)} %get-tuple-element.16.send_ref), channel_id=1, source_target_pairs={{0,128},{128,0},{1,129},{129,1},{2,130},{130,2},{3,131},{131,3},{4... | collective-permute-start | bytes 405512 | tf_op jit(solution)/shard_map/ppermute | solution.py:543
  8.9 3.8 %collective-permute-done.got_ref = f32[33,8,128]{2,1,0:T(8,128)S(1)} collective-permute-done((f32[33,8,128]{2,1,0:T(8,128)S(1)}, f32[33,8,128]{2,1,0:T(8,128)S(1)}, u32[]{:S(2)}, u32[]{:S(2)}) %collective-permute-start) | collective-permute-done | bytes 135200 | tf_op jit(solution)/shard_map/ppermute | solution.py:543
  12.8 0.6 %copy-done.9 = s32[1,4]{1,0:T(1,128)S(1)} copy-done((s32[1,4]{1,0:T(1,128)S(1)}, s32[1,4]{1,0:T(1,128)}, u32[]{:S(2)}) %copy-start.9) | copy-done | bytes 40
  13.4 5.3 %place_vias.1 = (f32[2,2,64,128]{3,2,1,0:T(8,128)S(1)}, f32[2,2,2,2,64,128]{5,4,3,2,1,0:T(8,128)S(1)}, f32[456,128]{1,0:T(8,128)S(1)}, f32[456,128]{1,0:T(8,128)S(1)}, f32[40,128]{1,0:T(8,128)S(1)}) custom-call(s32[1]{0:T(128)} %bitcast.die_ref, s32[1,4]{1,0:T(1,128)S(1)} %copy-done.9, f32[2,32,8,128]{3,2,1,0:T(8,128)S(1)} %get-tuple-element.13.packed_ref, ...), custom_call_target="tpu_custom_call" | custom-call | tf_op jit(solution)/shard_map/place_vias/pallas_call | solution.py:546
  18.8 1.9 %collective-permute-start.1 = (f32[456,128]{1,0:T(8,128)S(1)}, f32[456,128]{1,0:T(8,128)S(1)}, u32[]{:S(2)}, u32[]{:S(2)}) collective-permute-start(f32[456,128]{1,0:T(8,128)S(1)} %get-tuple-element.20), channel_id=1, source_target_pairs={{8,0},{16,8},{24,16},{32,24},{40,32},{48,40},{56,48},{64,56},{72,6... | collective-permute-start | bytes 700424 | tf_op jit(solution)/shard_map/ppermute | solution.py:552
  20.7 2.4 %collective-permute-start.2 = (f32[456,128]{1,0:T(8,128)S(1)}, f32[456,128]{1,0:T(8,128)S(1)}, u32[]{:S(2)}, u32[]{:S(2)}) collective-permute-start(f32[456,128]{1,0:T(8,128)S(1)} %get-tuple-element.21), channel_id=1, source_target_pairs={{0,8},{8,16},{16,24},{24,32},{32,40},{40,48},{48,56},{56,64},{64,7... | collective-permute-start | bytes 700424 | tf_op jit(solution)/shard_map/ppermute | solution.py:553
  23.1 5.6 %collective-permute-start.4 = (f32[40,128]{1,0:T(8,128)S(1)}, f32[40,128]{1,0:T(8,128)S(1)}, u32[]{:S(2)}, u32[]{:S(2)}) collective-permute-start(f32[40,128]{1,0:T(8,128)S(1)} %get-tuple-element.19.base_ref), channel_id=1, source_target_pairs={{0,16},{8,24},{16,32},{24,40},{32,48},{40,56},{48,64},{56,72},{64,... | collective-permute-start | bytes 61448 | tf_op jit(solution)/shard_map/ppermute | solution.py:555
  28.7 1.9 %collective-permute-start.3 = (f32[40,128]{1,0:T(8,128)S(1)}, f32[40,128]{1,0:T(8,128)S(1)}, u32[]{:S(2)}, u32[]{:S(2)}) collective-permute-start(f32[40,128]{1,0:T(8,128)S(1)} %get-tuple-element.19.base_ref), channel_id=1, source_target_pairs={{16,0},{24,8},{32,16},{40,24},{48,32},{56,40},{64,48},{72,56},{80,... | collective-permute-start | bytes 61448 | tf_op jit(solution)/shard_map/ppermute | solution.py:554
  30.7 0.0 collective-permute-done.4.above2_ref
  30.7 7.4 %collective-permute-done.3.below2_ref = f32[40,128]{1,0:T(8,128)S(1)} collective-permute-done((f32[40,128]{1,0:T(8,128)S(1)}, f32[40,128]{1,0:T(8,128)S(1)}, u32[]{:S(2)}, u32[]{:S(2)}) %collective-permute-start.3) | collective-permute-done | bytes 20512 | tf_op jit(solution)/shard_map/ppermute | solution.py:554
  38.0 0.0 collective-permute-done.1.below_ref
  38.0 0.0 collective-permute-done.2.above_ref
  38.0 0.5 column_strips.1
  38.6 5.0 %collective-permute-start.5 = (f32[272,128]{1,0:T(8,128)S(1)}, f32[272,128]{1,0:T(8,128)S(1)}, u32[]{:S(2)}, u32[]{:S(2)}) collective-permute-start(f32[272,128]{1,0:T(8,128)S(1)} %get-tuple-element.22), channel_id=1, source_target_pairs={{0,1},{1,2},{2,3},{3,4},{4,5},{5,6},{6,7},{8,9},{9,10},{10,11},{11... | collective-permute-start | bytes 417800 | tf_op jit(solution)/shard_map/ppermute | solution.py:562
  43.6 1.9 %collective-permute-start.6 = (f32[272,128]{1,0:T(8,128)S(1)}, f32[272,128]{1,0:T(8,128)S(1)}, u32[]{:S(2)}, u32[]{:S(2)}) collective-permute-start(f32[272,128]{1,0:T(8,128)S(1)} %get-tuple-element.23), channel_id=1, source_target_pairs={{1,0},{2,1},{3,2},{4,3},{5,4},{6,5},{7,6},{9,8},{10,9},{11,10},{12... | collective-permute-start | bytes 417800 | tf_op jit(solution)/shard_map/ppermute | solution.py:561
  45.5 0.6 %collective-permute-done.5.fromleft_ref = f32[272,128]{1,0:T(8,128)S(1)} collective-permute-done((f32[272,128]{1,0:T(8,128)S(1)}, f32[272,128]{1,0:T(8,128)S(1)}, u32[]{:S(2)}, u32[]{:S(2)}) %collective-permute-start.5) | collective-permute-done | bytes 139296 | tf_op jit(solution)/shard_map/ppermute | solution.py:562
  46.2 5.6 %collective-permute-done.6.fromright_ref = f32[272,128]{1,0:T(8,128)S(1)} collective-permute-done((f32[272,128]{1,0:T(8,128)S(1)}, f32[272,128]{1,0:T(8,128)S(1)}, u32[]{:S(2)}, u32[]{:S(2)}) %collective-permute-start.6) | collective-permute-done | bytes 139296 | tf_op jit(solution)/shard_map/ppermute | solution.py:561
  51.8 9.6 %solve.1 = (f32[2,2,64,256]{3,2,1,0:T(8,128)}, f32[2,8,32]{2,1,0:T(8,128)}) custom-call(f32[2,2,64,256]{3,2,1,0:T(8,128)S(1)} %copy-done, f32[2,64,256]{2,1,0:T(8,128)S(1)} %copy-done.2, f32[2,2,64,256]{3,2,1,0:T(8,128)S(1)} %copy-done.1, f32[2,2,64,128]{3,2,1,0:T(8,128)S(1)} %get-tuple-element.17.counts_ref, ...), custom_call_target="tpu_custom_call" | custom-call | tf_op jit(solution)/shard_map/solve/pallas_call | solution.py:569
  (14 shorter events, 0.0 us)
Async XLA Ops:
  0.6 0.7 %copy-start.6 = (s32[2,8,32]{2,1,0:T(8,128)S(1)}, s32[2,8,32]{2,1,0:T(8,128)}, u32[]{:S(2)}) copy-start(s32[2,8,32]{2,1,0:T(8,128)} %load_cell_ref.1) | copy-start | bytes 6148
  1.3 1.2 %copy-start.3 = (f32[2,2,2,32,8,32]{5,4,3,2,1,0:T(8,128)S(1)}, f32[2,2,2,32,8,32]{5,4,3,2,1,0:T(8,128)}, u32[]{:S(2)}) copy-start(f32[2,2,2,32,8,32]{5,4,3,2,1,0:T(8,128)} %via_ref.1) | copy-start | bytes 786436
  2.6 0.9 %copy-start.4 = (s32[2,32,8,32]{3,2,1,0:T(8,128)S(1)}, s32[2,32,8,32]{3,2,1,0:T(8,128)}, u32[]{:S(2)}) copy-start(s32[2,32,8,32]{3,2,1,0:T(8,128)} %cell_ref.1) | copy-start | bytes 196612
  3.5 0.8 %copy-start.5 = (f32[2,2,2,8,32]{4,3,2,1,0:T(8,128)S(1)}, f32[2,2,2,8,32]{4,3,2,1,0:T(8,128)}, u32[]{:S(2)}) copy-start(f32[2,2,2,8,32]{4,3,2,1,0:T(8,128)} %load_ref.1) | copy-start | bytes 24580
  4.3 8.5 %copy-start = (f32[2,2,64,256]{3,2,1,0:T(8,128)S(1)}, f32[2,2,64,256]{3,2,1,0:T(8,128)}, u32[]{:S(2)}) copy-start(f32[2,2,64,256]{3,2,1,0:T(8,128)} %sheet_ref.5) | copy-start | bytes 786436
  4.3 8.5 %copy-start.1 = (f32[2,2,64,256]{3,2,1,0:T(8,128)S(1)}, f32[2,2,64,256]{3,2,1,0:T(8,128)}, u32[]{:S(2)}) copy-start(f32[2,2,64,256]{3,2,1,0:T(8,128)} %drop_ref.5) | copy-start | bytes 786436
  4.3 8.5 %copy-start.2 = (f32[2,64,256]{2,1,0:T(8,128)S(1)}, f32[2,64,256]{2,1,0:T(8,128)}, u32[]{:S(2)}) copy-start(f32[2,64,256]{2,1,0:T(8,128)} %cap_ref.5) | copy-start | bytes 393220
  4.3 8.5 %copy-start.7 = (f32[2,8,32]{2,1,0:T(8,128)S(1)}, f32[2,8,32]{2,1,0:T(8,128)}, u32[]{:S(2)}) copy-start(f32[2,8,32]{2,1,0:T(8,128)} %base_sheet_ref.1) | copy-start | bytes 6148
  4.3 8.5 %copy-start.8 = (f32[2,8,32]{2,1,0:T(8,128)S(1)}, f32[2,8,32]{2,1,0:T(8,128)}, u32[]{:S(2)}) copy-start(f32[2,8,32]{2,1,0:T(8,128)} %base_start_ref.1) | copy-start | bytes 6148
  7.3 5.4 %collective-permute-start = (f32[33,8,128]{2,1,0:T(8,128)S(1)}, f32[33,8,128]{2,1,0:T(8,128)S(1)}, u32[]{:S(2)}, u32[]{:S(2)}) collective-permute-start(f32[33,8,128]{2,1,0:T(8,128)S(1)} %get-tuple-element.16.send_ref), channel_id=1, source_target_pairs={{0,128},{128,0},{1,129},{129,1},{2,130},{130,2},{3,131},{131,3},{4... | collective-permute-start | bytes 405512 | tf_op jit(solution)/shard_map/ppermute | solution.py:543
  12.8 0.7 %copy-start.9 = (s32[1,4]{1,0:T(1,128)S(1)}, s32[1,4]{1,0:T(1,128)}, u32[]{:S(2)}) copy-start(s32[1,4]{1,0:T(1,128)} %bump_ref.1) | copy-start | bytes 52
  18.8 19.3 %collective-permute-start.1 = (f32[456,128]{1,0:T(8,128)S(1)}, f32[456,128]{1,0:T(8,128)S(1)}, u32[]{:S(2)}, u32[]{:S(2)}) collective-permute-start(f32[456,128]{1,0:T(8,128)S(1)} %get-tuple-element.20), channel_id=1, source_target_pairs={{8,0},{16,8},{24,16},{32,24},{40,32},{48,40},{56,48},{64,56},{72,6... | collective-permute-start | bytes 700424 | tf_op jit(solution)/shard_map/ppermute | solution.py:552
  20.7 17.3 %collective-permute-start.2 = (f32[456,128]{1,0:T(8,128)S(1)}, f32[456,128]{1,0:T(8,128)S(1)}, u32[]{:S(2)}, u32[]{:S(2)}) collective-permute-start(f32[456,128]{1,0:T(8,128)S(1)} %get-tuple-element.21), channel_id=1, source_target_pairs={{0,8},{8,16},{16,24},{24,32},{32,40},{40,48},{48,56},{56,64},{64,7... | collective-permute-start | bytes 700424 | tf_op jit(solution)/shard_map/ppermute | solution.py:553
  23.1 7.6 %collective-permute-start.4 = (f32[40,128]{1,0:T(8,128)S(1)}, f32[40,128]{1,0:T(8,128)S(1)}, u32[]{:S(2)}, u32[]{:S(2)}) collective-permute-start(f32[40,128]{1,0:T(8,128)S(1)} %get-tuple-element.19.base_ref), channel_id=1, source_target_pairs={{0,16},{8,24},{16,32},{24,40},{32,48},{40,56},{48,64},{56,72},{64,... | collective-permute-start | bytes 61448 | tf_op jit(solution)/shard_map/ppermute | solution.py:555
  28.7 9.3 %collective-permute-start.3 = (f32[40,128]{1,0:T(8,128)S(1)}, f32[40,128]{1,0:T(8,128)S(1)}, u32[]{:S(2)}, u32[]{:S(2)}) collective-permute-start(f32[40,128]{1,0:T(8,128)S(1)} %get-tuple-element.19.base_ref), channel_id=1, source_target_pairs={{16,0},{24,8},{32,16},{40,24},{48,32},{56,40},{64,48},{72,56},{80,... | collective-permute-start | bytes 61448 | tf_op jit(solution)/shard_map/ppermute | solution.py:554
  38.6 7.6 %collective-permute-start.5 = (f32[272,128]{1,0:T(8,128)S(1)}, f32[272,128]{1,0:T(8,128)S(1)}, u32[]{:S(2)}, u32[]{:S(2)}) collective-permute-start(f32[272,128]{1,0:T(8,128)S(1)} %get-tuple-element.22), channel_id=1, source_target_pairs={{0,1},{1,2},{2,3},{3,4},{4,5},{5,6},{6,7},{8,9},{9,10},{10,11},{11... | collective-permute-start | bytes 417800 | tf_op jit(solution)/shard_map/ppermute | solution.py:562
  43.6 8.2 %collective-permute-start.6 = (f32[272,128]{1,0:T(8,128)S(1)}, f32[272,128]{1,0:T(8,128)S(1)}, u32[]{:S(2)}, u32[]{:S(2)}) collective-permute-start(f32[272,128]{1,0:T(8,128)S(1)} %get-tuple-element.23), channel_id=1, source_target_pairs={{1,0},{2,1},{3,2},{4,3},{5,4},{6,5},{7,6},{9,8},{10,9},{11,10},{12... | collective-permute-start | bytes 417800 | tf_op jit(solution)/shard_map/ppermute | solution.py:561

commit v2 on v1

v2 whole, which is shorter than its diff:
```python
import jax
import jax.numpy as jnp
from jax import lax
from jax.experimental import pallas as pl
from jax.experimental.pallas import tpu as pltpu
from jax.sharding import PartitionSpec as P

SWEEPS = 6
STEPS = 2
VIAS = 32

VIA_CONDUCT = 1.0
VIA_RESIST = 4.0
BUMP_CONDUCT = 50.0
BASE_CAPACITY = 0.1
LOWER_BOUND = 0.1
UPPER_BOUND = 1.9

MIDDLE = 0.5 * (UPPER_BOUND + LOWER_BOUND)
HALF = 0.5 * (UPPER_BOUND - LOWER_BOUND)

GROUPS = 12
F32 = jnp.float32


def sweep_weights():
    scaled = MIDDLE / HALF
    ratio = 1.0 / scaled
    pairs = []
    for _ in range(SWEEPS - 1):
        following = 1.0 / (2.0 * scaled - ratio)
        pairs.append((following * ratio, 2.0 * following / HALF))
        ratio = following
    return pairs


WEIGHTS = sweep_weights()


def lane_iota():
    return lax.broadcasted_iota(jnp.int32, (8, 128), 1)


def sub_iota(width=128):
    return lax.broadcasted_iota(jnp.int32, (8, width), 0)


def roll(x, shift, axis):
    shift = shift % x.shape[axis]
    return pltpu.roll(x, shift, axis) if shift else x


def rows(g):
    return pl.ds(8 * g, 8)


def spread_nets(ref):
    gap = jnp.zeros((8, 16), F32)
    return jnp.concatenate([gap, ref[0], gap, gap, ref[1], gap], axis=1)


def pack_kernel(place_ref, bump_ref, via_hbm, sheet_hbm, start_hbm, packed_ref, send_ref, far_ref, via_ref, sheet_ref, start_ref, sems):
    copies = [pltpu.make_async_copy(via_hbm.at[t, d], via_ref.at[t, d], sems.at[2 * t + d]) for t in range(2) for d in range(2)]
    copies.append(pltpu.make_async_copy(sheet_hbm, sheet_ref, sems.at[4]))
    copies.append(pltpu.make_async_copy(start_hbm, start_ref, sems.at[5]))
    for copy in copies:
        copy.start()
    later = place_ref[0].astype(F32)
    lane, sub = lane_iota(), sub_iota()
    bump = jnp.zeros((8, 128), F32)
    column = lane % 64 - 16
    for k in range(4):
        bump = jnp.where((column // 8 == k) & (sub * 8 + column % 8 == bump_ref[0, k]), 1.0, bump)
    for copy in copies:
        copy.wait()
    total = jnp.zeros((8, 128), F32)
    for v in range(VIAS):
        parts = []
        for d in range(2):
            part = jnp.concatenate([via_ref[t, d, n, v] for t in range(2) for n in range(2)], axis=1)
            packed_ref[d, v] = part
            parts.append(part)
        both = parts[0] + parts[1]
        send_ref[v] = both + later * parts[0]
        total = total + both
    send_ref[VIAS] = total
    far_ref[rows(0), :] = spread_nets(sheet_ref)
    far_ref[rows(1), :] = spread_nets(start_ref)
    far_ref[rows(2), :] = bump
    far_ref[rows(3), :] = total


def spread_matrix(height, width):
    row = lax.broadcasted_iota(jnp.int32, (height, width), 0) % 128
    column = lax.broadcasted_iota(jnp.int32, (height, width), 1)
    return jnp.where(row == column // 8, 1.0, 0.0).astype(jnp.bfloat16)


def halves(value):
    high = value.astype(jnp.bfloat16)
    low = (value - high.astype(F32)).astype(jnp.bfloat16)
    return jnp.concatenate([high, low], axis=1)


def prepare_kernel(cell_ref, load_cell_ref, load_ref, cells_ref, load_cells_ref, loads_ref, spread_ref, counts_ref):
    within = (lane_iota() % 8).astype(F32)
    spread = spread_matrix(32, 256)
    for d in range(2):
        cells = cell_ref[d].reshape(8 * VIAS, 32).astype(F32).astype(jnp.bfloat16)
        wide = jnp.dot(cells, spread, preferred_element_type=F32)
        load_cell = load_cell_ref[d].astype(F32).astype(jnp.bfloat16)
        load_cell = jnp.dot(load_cell, spread, preferred_element_type=F32)
        for half in range(2):
            lanes = slice(128 * half, 128 * half + 128)
            for v in range(VIAS):
                cells_ref[2 * d + half, v] = wide[8 * v : 8 * v + 8, lanes] - within
            load_cells_ref[2 * d + half] = load_cell[:, lanes] - within
    spread_ref[...] = spread_matrix(256, 1024)
    loads = jnp.concatenate([load_ref[t, d, n] for d in range(2) for t in range(2) for n in range(2)], axis=0)
    high = loads.astype(jnp.bfloat16)
    low = (loads - high.astype(F32)).astype(jnp.bfloat16)
    wide = jnp.dot(high, spread, preferred_element_type=F32) + jnp.dot(low, spread, preferred_element_type=F32)
    for d in range(2):
        for half in range(2):
            for m in range(4):
                loads_ref[2 * d + half, m] = wide[32 * d + 8 * m : 32 * d + 8 * m + 8, 128 * half : 128 * half + 128]

    def count(i, carry):
        state = [jnp.zeros((8, 128), F32) for _ in range(8)]
        for v in range(VIAS):
            cell = cells_ref[i, v]
            for oi in range(8):
                state[oi] = state[oi] + jnp.where(cell == 8.0 * oi, 1.0, 0.0)
        for oi in range(8):
            counts_ref[i, pl.ds(oi, 8, stride=8), :] = state[oi]
        return carry

    lax.fori_loop(0, 4, count, 0)


def shared(first, second, shift):
    return jnp.where(sub_iota() < shift, first, roll(second, shift, 0))


def shared_low(first, second, shift):
    return jnp.where(sub_iota() >= shift, first, roll(second, shift, 0))


def place_kernel(
    place_ref, packed_ref, send_ref, got_ref, cells_ref, load_cells_ref, loads_ref, spread_ref, counts_ref, far_ref,
    sheet_ref, cap_ref, drop_ref, field_ref, even_ref, odd_ref, base_ref, values_ref,
):
    lane = lane_iota()
    later = place_ref[0].astype(F32)
    even = place_ref[1] % 2 == 0
    weights = (
        (VIA_RESIST * (4.0 - 2.0 * later), VIA_RESIST * (3.0 - 2.0 * later), VIA_RESIST * (1.0 + later)),
        (VIA_RESIST * (3.0 - 2.0 * later), VIA_RESIST * (3.0 - 2.0 * later), VIA_RESIST),
    )
    size = (8 * VIAS, 128)
    first, second, got = packed_ref[0].reshape(size), packed_ref[1].reshape(size), got_ref[0:VIAS].reshape(size)
    for d in range(2):
        mixed = weights[d][0] * first + weights[d][1] * second + weights[d][2] * got
        wide = jnp.dot(halves(mixed), spread_ref[...], preferred_element_type=F32)
        for half in range(2):
            for m in range(4):
                start = 256 * m + 128 * half
                values_ref[2 * d + half, m] = wide[:, start : start + 128].reshape(VIAS, 8, 128)

    def add(i, carry):
        cell = load_cells_ref[i]
        loads = [loads_ref[i, m] for m in range(4)]
        state = []
        for oi in range(8):
            hit = cell == 8.0 * oi
            state.append([jnp.where(hit, load, 0.0) for load in loads])
        for v in range(VIAS):
            cell = cells_ref[i, v]
            values = [values_ref[i, m, v] for m in range(4)]
            for oi in range(8):
                hit = cell == 8.0 * oi
                state[oi] = [old + jnp.where(hit, value, 0.0) for old, value in zip(state[oi], values)]
        for oi in range(8):
            for m in range(4):
                field_ref[m, i, pl.ds(oi, 8, stride=8), :] = state[oi][m]
        return carry

    lax.fori_loop(0, 4, add, 0)

    place = 0

    def put(up, down):
        nonlocal place
        even_ref[rows(place), :] = jnp.where(even, down, up)
        odd_ref[rows(place), :] = jnp.where(even, up, down)
        place += 1

    def pair(first, second):
        put(first(0), first(7))
        put(second(0), second(7))
        put(shared(first(1), second(1), 4), shared_low(first(6), second(6), 4))

    for d in range(2):
        for half in range(2):
            lanes = pl.ds(half * 128, 128)
            for n in range(2):
                pair(lambda g: sheet_ref[d, n, rows(g), lanes], lambda g: drop_ref[d, n, rows(g), lanes])
                one = lambda g: field_ref[n, 2 * d + half, rows(g), :]
                two = lambda g: field_ref[2 + n, 2 * d + half, rows(g), :]
                put(one(0), one(7))
                put(shared(one(1), two(0), 3), shared_low(one(6), two(7), 5))
            pair(lambda g: cap_ref[d, rows(g), lanes], lambda g: counts_ref[2 * d + half, rows(g), :])

    parts = [far_ref[rows(0), :], far_ref[rows(1), :], far_ref[rows(2), :], send_ref[VIAS] + got_ref[VIAS]]
    for part in range(4):
        base_ref[rows(part), :] = parts[part]
        put(parts[part], parts[part])


BASE = 4
ROW_GROUPS = 52 + BASE


def row_place(d, half, n, kind):
    start = (d * 2 + half) * 13
    return start + 10 if kind == 2 else start + 5 * n + 3 * kind


def below_rows(ref, d, half, n, kind, second):
    start = row_place(d, half, n, kind)
    if kind == 1:
        if second:
            return roll(ref[rows(start + 1), :], -3, 0), None
        return ref[rows(start), :], ref[rows(start + 1), :]
    last = ref[rows(start + 2), :]
    if second:
        return ref[rows(start + 1), :], roll(last, -4, 0)
    return ref[rows(start), :], last


def above_rows(ref, d, half, n, kind, second):
    start = row_place(d, half, n, kind)
    if kind == 1:
        if second:
            return roll(ref[rows(start + 1), :], -5, 0), None
        return ref[rows(start), :], ref[rows(start + 1), :]
    last = ref[rows(start + 2), :]
    if second:
        return ref[rows(start + 1), :], roll(last, -4, 0)
    return ref[rows(start), :], last


def column_groups(own, below, above, d, half, n, kind, second):
    low = below_rows(below, d, half, n, kind, second)
    high = above_rows(above, d, half, n, kind, second)
    return [own(g) for g in range(8)] + [low[0], low[1], high[1], high[0]]


COL_GROUPS = 2 * GROUPS + 10


def strip_kernel(
    place_ref, sheet_ref, cap_ref, drop_ref, counts_ref, field_ref, base_ref, even_ref, odd_ref, near_ref, next_ref, far_ref,
    left_ref, right_ref, below_ref, above_ref, wide_ref,
):
    lane = lane_iota()
    within = lane % 16
    row, last = place_ref[1], place_ref[3]
    even, low = row % 2 == 0, row % 4 < 2

    def pick(flag, yes, no, inside):
        return jnp.where(inside, jnp.where(flag, yes, no), 0.0)

    for g in range(ROW_GROUPS):
        a, b = even_ref[rows(g), :], odd_ref[rows(g), :]
        below_ref[rows(g), :] = pick(even, a, b, row < last)
        above_ref[rows(g), :] = pick(even, b, a, row > 0)

    own = (lane % 64 >= 16) & (lane % 64 < 48)

    def spread_steps(value):
        out = []
        for t in range(2):
            moved = jnp.where(lane < 64, roll(value, 16 - 64 * t, 1), roll(value, 48 - 64 * t, 1))
            out.append(jnp.where(own, moved, 0.0))
        return out

    groups = []
    for g in range(5):
        if g == 0:
            parts = [base_ref[rows(f), :] for f in range(BASE)]
        elif g in (1, 4):
            ref = below_ref if g == 1 else above_ref
            parts = [ref[rows(ROW_GROUPS - BASE + f), :] for f in range(BASE)]
        else:
            inside = row + 2 <= last if g == 2 else row >= 2
            flag = low if g == 2 else jnp.logical_not(low)
            parts = [pick(flag, near_ref[rows(f), :], next_ref[rows(f), :], inside) for f in range(BASE)]
            parts[3] = parts[3] + pick(flag, far_ref[rows(0), :], far_ref[rows(1), :], inside)
        one, two = spread_steps(parts[3])
        groups.append([parts[0], parts[1], one, two, parts[2]])
        for f in range(5):
            wide_ref[rows(5 * f + g), :] = groups[g][f]

    def fields(half):
        lanes = pl.ds(half * 128, 128)
        first, second = [], []
        for d in range(2):
            for n in range(2):
                first.append(column_groups(
                    lambda g: sheet_ref[d, n, rows(g), lanes], below_ref, above_ref, d, half, n, 0, False))
        for d in range(2):
            for n in range(2):
                first.append(column_groups(
                    lambda g: drop_ref[d, n, rows(g), lanes], below_ref, above_ref, d, half, n, 0, True))
        for d in range(2):
            second.append(column_groups(
                lambda g: cap_ref[d, rows(g), lanes], below_ref, above_ref, d, half, 0, 2, False))
        for d in range(2):
            second.append(column_groups(
                lambda g: counts_ref[2 * d + half, rows(g), :], below_ref, above_ref, d, half, 0, 2, True))
        for d in range(2):
            for n in range(2):
                one = column_groups(
                    lambda g: field_ref[n, 2 * d + half, rows(g), :], below_ref, above_ref, d, half, n, 1, False)
                two = column_groups(
                    lambda g: field_ref[2 + n, 2 * d + half, rows(g), :], below_ref, above_ref, d, half, n, 1, True)
                merged = []
                for a, b in zip(one, two):
                    if b is None:
                        merged.append(a)
                    elif half == 0:
                        merged.append(jnp.where(within < 11, a, roll(b, 11, 1)))
                    else:
                        merged.append(jnp.where(within >= 5, a, roll(b, -11, 1)))
                second.append(merged)
        return first, second

    def join(chunks, origin):
        out = roll(chunks[0], -origin, 1)
        for k in range(1, 8):
            out = jnp.where(lane // 16 == k, roll(chunks[k], 16 * k - origin, 1), out)
        return out

    for half, ref, origin in ((0, left_ref, 0), (1, right_ref, 112)):
        for part, chunks in enumerate(fields(half)):
            for g in range(GROUPS):
                ref[rows(part * GROUPS + g), :] = join([chunk[g] for chunk in chunks], origin)

    start = 2 * GROUPS
    quarter = (lane % 64) // 16
    for g in range(5):
        sheet, drop, one, two, bump = groups[g]
        left = jnp.where(
            quarter == 1, sheet,
            jnp.where(quarter == 2, roll(drop, 16, 1), jnp.where(quarter == 3, roll(one, 32, 1), roll(two, -16, 1))),
        )
        right = jnp.where(
            quarter == 2, sheet,
            jnp.where(quarter == 3, roll(drop, 16, 1), jnp.where(quarter == 1, roll(two, -16, 1), roll(one, -32, 1))),
        )
        left_ref[rows(start + g), :] = left
        right_ref[rows(start + g), :] = right
        left_ref[rows(start + 5 + g), :] = bump
        right_ref[rows(start + 5 + g), :] = bump


def connect(center, neighbour):
    return jnp.where(neighbour > 0.0, 2.0 / (center + neighbour), 0.0)


def three_terms(k):
    if k == 0:
        return 1.0 - 1.0 / MIDDLE, 0.0, 1.0 / MIDDLE
    a, b = WEIGHTS[k - 1]
    return 1.0 + a - b, -a, b


def advance(k, value, previous, total):
    fore, back, gain = three_terms(k)
    out = total if gain == 1.0 else gain * total
    if fore != 0.0:
        out = out + fore * value
    return out + back * previous() if k else out


def base_solve(fields):
    sheet, state, arriving, bump = fields
    steps = [(1, 0), (-1, 0), (1, 1), (-1, 1)]
    inside = sheet > 0.0
    links = [jnp.where(inside, connect(sheet, roll(sheet, s, a)), 0.0) for s, a in steps]
    diagonal = BASE_CAPACITY + links[0] + links[1] + links[2] + links[3] + BUMP_CONDUCT * bump
    inverse = 1.0 / diagonal
    links = [inverse * link for link in links]
    results = []
    for t in range(STEPS):
        source = inverse * (BASE_CAPACITY * state + arriving[t])
        previous = None
        for k in range(SWEEPS):
            total = (links[0] * roll(state, 1, 0) + links[1] * roll(state, -1, 0)) + (
                links[2] * roll(state, 1, 1) + links[3] * roll(state, -1, 1)
            ) + source
            state, previous = advance(k, state, lambda: previous, total), state
        results.append(state)
    return results


def needed(halo):
    if halo > 8:
        return list(range(GROUPS))
    return list(range(8)) + ([8, 11] if halo > 0 else [])


def solve_kernel(
    place_ref, sheet_ref, cap_ref, drop_ref, counts_ref, field_ref, wide_ref, below_ref, above_ref,
    fromleft_ref, fromright_ref, out_ref, base_out_ref,
    s_ext, x_ext, c_ext, k_ext, f_ext, base_ext, link_up, link_down, link_left, link_right, inv_ext, src, alt,
):
    lane = lane_iota()
    has_left, has_right = place_ref[2] > 0, place_ref[2] < place_ref[4]

    start = 2 * GROUPS
    quarter = (lane % 64) // 16
    take_left, take_right = (quarter == 0) & has_left, (quarter == 3) & has_right
    from_left = [fromleft_ref[rows(start + g), :] for g in range(10)]
    from_right = [fromright_ref[rows(start + g), :] for g in range(10)]
    fields = []
    for field in range(5):
        out = []
        for g in range(5):
            right_shift = (32, 16, 0, 48, 32)[field]
            left_shift = (-32, -48, 0, -16, -32)[field]
            group = g + 5 * (field == 4)
            value = jnp.where(take_right, roll(from_right[group], right_shift, 1), wide_ref[rows(5 * field + g), :])
            out.append(jnp.where(take_left, roll(from_left[group], left_shift, 1), value))
        fields.append(jnp.concatenate(out, axis=0))
    solved = base_solve((fields[0], fields[1], (fields[2], fields[3]), fields[4]))
    for t in range(STEPS):
        base_ext[t] = solved[t]
    for n in range(2):
        base_out_ref[n] = roll(solved[1][0:8], -(64 * n + 16), 1)[:, 0:32]

    at_left, at_right = (lane >= 112) & has_left, (lane < 16) & has_right

    def third(part, chunk, g):
        right = fromright_ref[rows(part * GROUPS + g), :]
        left = fromleft_ref[rows(part * GROUPS + g), :]
        value = jnp.where(at_right, roll(right, -16 * chunk, 1), 0.0)
        return jnp.where(at_left, roll(left, 112 - 16 * chunk, 1), value)

    def fill(target, index, own, d, n, kind, second, part, chunk, shift=0):
        for half in range(2):
            for g, value in enumerate(
                column_groups(lambda g: own(half, g), below_ref, above_ref, d, half, n, kind, second)
            ):
                if value is not None:
                    target[index, rows(g), pl.ds(half * 128, 128)] = value
        for g in range(GROUPS):
            if shift and g in (9, 10):
                continue
            value = third(part, chunk, g)
            if shift:
                value = jnp.where(lane < 64, roll(value, -shift, 1), roll(value, shift, 1))
            target[index, rows(g), pl.ds(256, 128)] = value

    for d in range(2):
        fill(c_ext, d, lambda half, g: cap_ref[d, rows(g), pl.ds(half * 128, 128)], d, 0, 2, False, 1, d)
        fill(k_ext, d, lambda half, g: counts_ref[2 * d + half, rows(g), :], d, 0, 2, True, 1, 2 + d)
        for n in range(2):
            i = 2 * d + n
            fill(s_ext, i, lambda half, g: sheet_ref[d, n, rows(g), pl.ds(half * 128, 128)], d, n, 0, False, 0, i)
            fill(x_ext, i, lambda half, g: drop_ref[d, n, rows(g), pl.ds(half * 128, 128)], d, n, 0, True, 0, 4 + i)
            fill(f_ext, i, lambda half, g: field_ref[n, 2 * d + half, rows(g), :], d, n, 1, False, 1, 4 + i)
            fill(f_ext, 4 + i, lambda half, g: field_ref[2 + n, 2 * d + half, rows(g), :], d, n, 1, True, 1, 4 + i, 11)

    sub = sub_iota(384)
    tile = [lane // 8 + 16, lane // 8 + 32, jnp.where(lane < 64, lane // 8 + 48, lane // 8)]

    def image(i, carry):
        d = i // 2
        n = i % 2

        def get(ref, g):
            return ref[rows(g % GROUPS), :]

        def above(value, before):
            return jnp.where(sub == 0, roll(before, 1, 0), roll(value, 1, 0))

        def below(value, after):
            return jnp.where(sub == 7, roll(after, -1, 0), roll(value, -1, 0))

        for g in range(GROUPS):
            here = s_ext[i, rows(g), :]
            after = s_ext[i, rows((g + 1) % GROUPS), :]
            inside = here > 0.0
            down = jnp.where(inside, connect(here, below(here, after)), 0.0)
            right = jnp.where(inside, connect(here, roll(here, -1, 1)), 0.0)
            link_down[rows(g), :] = down
            link_right[rows(g), :] = right
            link_left[rows(g), :] = roll(right, 1, 1)
        for g in range(GROUPS):
            link_up[rows(g), :] = above(get(link_down, g), get(link_down, g - 1))
        for g in range(GROUPS):
            ups, downs = get(link_up, g), get(link_down, g)
            lefts, rights = get(link_left, g), get(link_right, g)
            diagonal = c_ext[d, rows(g), :] + ups + downs + lefts + rights + VIA_CONDUCT * k_ext[d, rows(g), :]
            inverse = jnp.where(diagonal > 0.0, 1.0 / diagonal, 0.0)
            inv_ext[rows(g), :] = inverse
            link_up[rows(g), :] = inverse * ups
            link_left[rows(g), :] = inverse * lefts
            link_right[rows(g), :] = inverse * rights
        for g in range(GROUPS):
            link_down[rows(g), :] = get(inv_ext, g) * get(link_down, g)

        for t in range(STEPS):
            for k in range(SWEEPS):
                for g in needed(11 - 6 * t - k):
                    def read(near):
                        near = near % GROUPS
                        return alt[rows(near), :] if k % 2 else x_ext[i, rows(near), :]

                    value = read(g)
                    total = get(link_up, g) * above(value, read(g - 1)) + get(link_down, g) * below(value, read(g + 1))
                    total = total + (get(link_left, g) * roll(value, 1, 1) + get(link_right, g) * roll(value, -1, 1))
                    if k == 0:
                        spread = jnp.broadcast_to(base_ext[t, pl.ds(base_row(g), 1), :], (8, 128))
                        pieces = [jnp.take_along_axis(spread, index + 64 * n, axis=1) for index in tile]
                        source = c_ext[d, rows(g), :] * value + f_ext[4 * t + i, rows(g), :]
                        source = source + k_ext[d, rows(g), :] * jnp.concatenate(pieces, axis=1)
                        source = get(inv_ext, g) * source
                        src[rows(g), :] = source
                    else:
                        source = get(src, g)
                    total = total + source
                    if k % 2:
                        x_ext[i, rows(g), :] = advance(k, value, lambda: x_ext[i, rows(g), :], total)
                    else:
                        alt[rows(g), :] = advance(k, value, lambda: alt[rows(g), :], total)
        for g in range(8):
            out_ref[d, n, rows(g), :] = x_ext[i, rows(g), pl.ds(0, 256)]
        return carry

    lax.fori_loop(0, 4, image, 0)


def base_row(g):
    return g if g < 10 else 28 + g


def spec(count):
    return [pl.BlockSpec(memory_space=pltpu.VMEM)] * count


def smem():
    return pl.BlockSpec(memory_space=pltpu.SMEM)


def hbm():
    return pl.BlockSpec(memory_space=pltpu.HBM)


def call(kernel, name, outs, ins, scratch=(), limit=24):
    return pl.pallas_call(
        kernel,
        out_shape=outs,
        in_specs=ins,
        out_specs=spec(len(outs)),
        scratch_shapes=list(scratch),
        compiler_params=pltpu.CompilerParams(vmem_limit_bytes=limit * 1024 * 1024),
        name=name,
    )


def arr(*shape, dtype=F32):
    return jax.ShapeDtypeStruct(shape, dtype)


def swaps(count, offset, distance=1):
    pairs = []
    for i in range(count):
        if ((i - offset) // distance) % 2 == 0:
            j = (i + distance) % count
            pairs += [(i, j), (j, i)]
    return pairs


def per_device(
    sheet_res, capacity, drop_start, load_cell, load_current, via_cell, via_current, base_sheet, base_start, bump_cell
):
    row_count = lax.axis_size("row")
    col_count = lax.axis_size("col")
    place = jnp.stack(
        [lax.axis_index("die"), lax.axis_index("row"), lax.axis_index("col"), row_count - 1, col_count - 1]
    ).astype(jnp.int32)
    others = [(0, 1), (1, 0)]

    packed, send, far = call(
        pack_kernel, "pack_vias", (arr(2, VIAS, 8, 128), arr(VIAS + 1, 8, 128), arr(8 * BASE, 128)),
        [smem(), smem(), hbm(), hbm(), hbm()],
        [pltpu.VMEM((2, 2, 2, VIAS, 8, 32), F32), pltpu.VMEM((2, 8, 32), F32), pltpu.VMEM((2, 8, 32), F32),
         pltpu.SemaphoreType.DMA((6,))],
    )(place, bump_cell, via_current, base_sheet, base_start)
    got = lax.ppermute(send, "die", others)
    near = lax.ppermute(far, "row", swaps(row_count, 0, 2))
    after = lax.ppermute(far, "row", swaps(row_count, 2, 2))

    cells, load_cells, loads, spread, counts = call(
        prepare_kernel, "spread_cells",
        (arr(4, VIAS, 8, 128), arr(4, 8, 128), arr(4, 4, 8, 128), arr(256, 1024, dtype=jnp.bfloat16), arr(4, 64, 128)),
        spec(3),
    )(via_cell, load_cell, load_current)

    rows_shape = arr(8 * ROW_GROUPS, 128)
    field, even, odd, base = call(
        place_kernel, "place_vias", (arr(4, 4, 64, 128), rows_shape, rows_shape, arr(8 * BASE, 128)),
        [smem()] + spec(12), [pltpu.VMEM((4, 4, VIAS, 8, 128), F32)],
    )(place, packed, send, got, cells, load_cells, loads, spread, counts, far, sheet_res, capacity, drop_start)

    even = lax.ppermute(even, "row", swaps(row_count, 0))
    odd = lax.ppermute(odd, "row", swaps(row_count, 1))
    shares = jnp.concatenate([near[24:32], after[24:32]], axis=0)
    shares = lax.ppermute(shares, "die", others)

    strip_shape = arr(8 * COL_GROUPS, 128)
    left, right, below, above, wide = call(
        strip_kernel, "column_strips", (strip_shape, strip_shape, rows_shape, rows_shape, arr(200, 128)), [smem()] + spec(11)
    )(place, sheet_res, capacity, drop_start, counts, field, base, even, odd, near, after, shares)
    from_right = lax.ppermute(left, "col", [(i, (i - 1) % col_count) for i in range(col_count)])
    from_left = lax.ppermute(right, "col", [(i, (i + 1) % col_count) for i in range(col_count)])

    ext = (96, 384)
    scratch = [
        pltpu.VMEM((4,) + ext, F32), pltpu.VMEM((4,) + ext, F32), pltpu.VMEM((2,) + ext, F32),
        pltpu.VMEM((2,) + ext, F32), pltpu.VMEM((8,) + ext, F32), pltpu.VMEM((2, 40, 128), F32),
    ] + [pltpu.VMEM(ext, F32)] * 7
    return call(
        solve_kernel, "solve", (arr(2, 2, 64, 256), arr(2, 8, 32)), [smem()] + spec(10), scratch,
    )(place, sheet_res, capacity, drop_start, counts, field, wide, below, above, from_left, from_right)


def solution(mesh):
    in_specs = (
        P("die", None, "row", "col"),
        P("die", "row", "col"),
        P("die", None, "row", "col"),
        P("die", "row", "col"),
        P(None, "die", None, "row", "col"),
        P("die", None, "row", "col"),
        P(None, "die", None, None, "row", "col"),
        P(None, "row", "col"),
        P(None, "row", "col"),
        P("row", "col"),
    )
    out_specs = (P("die", None, "row", "col"), P(None, "row", "col"))
    return jax.shard_map(
        per_device, mesh=mesh, in_specs=in_specs, out_specs=out_specs, check_vma=False
    )
```

time: 61.8 us -> 49.2 us (0.80)
  the two profiles are of different devices: /device:TPU:120 before, /device:TPU:96 now
where the time goes in v2:
time: 49.2 us; the launch traced here: 49 us
  waiting for transfers between devices  18.6 us (38%)
  Pallas kernels  15.5 us (32%)
  starting transfers between devices  12.2 us (25%)
  local copies, waits for them, and re-layouts  1.96 us (4%)
  between operations  0.73 us (1%)
    pallas_call x1, Pallas kernels, per_device(): call(solve_kernel, 'solve', (arr(2, 2, 64, 256), arr(2, 8, 32)), [smem()]...  9.99 us
    ppermute x1, starting transfers between devices, per_device(): odd = lax.ppermute(odd, 'row', swaps(row_count, 1))  5.58 us
    ppermute x1, waiting for transfers between devices, per_device(): lax.ppermute(left, 'col', [(i, (i - 1) % col_count) for i in range(col_co...  3.67 us
    ppermute x1, waiting for transfers between devices, per_device(): after = lax.ppermute(far, 'row', swaps(row_count, 2, 2))  3.61 us
    ppermute x1, starting transfers between devices, per_device(): lax.ppermute(right, 'col', [(i, (i + 1) % col_count) for i in range(col_c...  3.21 us
    ppermute x1, waiting for transfers between devices, per_device(): got = lax.ppermute(send, 'die', others)  3.09 us
    ppermute x1, waiting for transfers between devices, per_device(): shares = lax.ppermute(shares, 'die', others)  3.06 us
    pallas_call x1, Pallas kernels, per_device(): call(place_kernel, 'place_vias', (arr(4, 4, 64, 128), rows_shape, rows_sh...  2.72 us
  transfers between devices with their start and end apart: 8, of which 6 were waited for; matrix products, arithmetic and copies ran while one was open for 0% of the time, Pallas kernels for 1%

profile of v2, /device:TPU:96, one launch (start us, length us, event | category | flops | bytes accessed | tf_op | source)
XLA Modules:
  0.0 49.0 jit_solution(10428950554532993639)
XLA Ops:
  0.7 0.1 stack.15.place_ref
  0.8 0.5 %copy-done.9 = s32[1,4]{1,0:T(1,128)S(1)} copy-done((s32[1,4]{1,0:T(1,128)S(1)}, s32[1,4]{1,0:T(1,128)}, u32[]{:S(2)}) %copy-start.9) | copy-done | bytes 40
  1.3 0.1 copy-done.6
  1.3 0.0 copy-done.7
  1.4 1.2 %copy-done.3 = f32[2,2,2,32,8,32]{5,4,3,2,1,0:T(8,128)S(1)} copy-done((f32[2,2,2,32,8,32]{5,4,3,2,1,0:T(8,128)S(1)}, f32[2,2,2,32,8,32]{5,4,3,2,1,0:T(8,128)}, u32[]{:S(2)}) %copy-start.3) | copy-done | bytes 262168
  2.6 0.0 copy-start.2
  2.6 1.0 %pack_vias.1 = (f32[2,32,8,128]{3,2,1,0:T(8,128)S(1)}, f32[33,8,128]{2,1,0:T(8,128)S(1)}, f32[32,128]{1,0:T(8,128)S(1)}) custom-call(s32[5]{0:T(128)S(1)} %stack.15.place_ref, s32[1,4]{1,0:T(1,128)S(1)} %copy-done.9, f32[2,2,2,32,8,32]{5,4,3,2,1,0:T(8,128)S(1)} %copy-done.3, f32[2,8,32]{2,1,0:T(8,128)S(1)} %copy-done.6, f32[2,8,32]{2,1,0:T(8,128)S(1)} %copy-done.7), custom_call_target="tpu_custom_call" | custom-call | tf_op jit(solution)/shard_map/pack_vias/pallas_call | solution.py:597
  3.6 0.0 copy-start
  3.6 1.6 %collective-permute-start = (f32[33,8,128]{2,1,0:T(8,128)S(1)}, f32[33,8,128]{2,1,0:T(8,128)S(1)}, u32[]{:S(2)}, u32[]{:S(2)}) collective-permute-start(f32[33,8,128]{2,1,0:T(8,128)S(1)} %get-tuple-element.21.send_ref), channel_id=1, source_target_pairs={{0,128},{128,0},{1,129},{129,1},{2,130},{130,2},{3,131},{131,3},{4... | collective-permute-start | bytes 405512 | tf_op jit(solution)/shard_map/ppermute | solution.py:603
  5.2 0.7 %spread_cells.1 = (f32[4,32,8,128]{3,2,1,0:T(8,128)S(1)}, f32[4,8,128]{2,1,0:T(8,128)S(1)}, f32[4,4,8,128]{3,2,1,0:T(8,128)S(1)}, bf16[256,1024]{1,0:T(8,128)(2,1)S(1)}, f32[4,64,128]{2,1,0:T(8,128)S(1)}) custom-call(s32[2,32,8,32]{3,2,1,0:T(8,128)S(1)} %copy-done.4, s32[2,8,32]{2,1,0:T(8,128)S(1)} %copy-done.8, f32[2,2,2,8,32]{4,3,2,1,0:T(8,128)S(1)} %copy-done.5), custom_call_target="tpu_custom_call" | custom-call | tf_op jit(solution)/shard_map/spread_cells/pallas_call | solution.py:607
  5.9 3.1 %collective-permute-done.got_ref = f32[33,8,128]{2,1,0:T(8,128)S(1)} collective-permute-done((f32[33,8,128]{2,1,0:T(8,128)S(1)}, f32[33,8,128]{2,1,0:T(8,128)S(1)}, u32[]{:S(2)}, u32[]{:S(2)}) %collective-permute-start) | collective-permute-done | bytes 135200 | tf_op jit(solution)/shard_map/ppermute | solution.py:603
  9.0 2.7 %place_vias.1 = (f32[4,4,64,128]{3,2,1,0:T(8,128)S(1)}, f32[448,128]{1,0:T(8,128)S(1)}, f32[448,128]{1,0:T(8,128)S(1)}, f32[32,128]{1,0:T(8,128)S(1)}) custom-call(s32[5]{0:T(128)S(1)} %stack.15.place_ref, f32[2,32,8,128]{3,2,1,0:T(8,128)S(1)} %get-tuple-element.20.packed_ref, f32[33,8,128]{2,1,0:T(8,128)S(1)} %get-tuple-element.21.send_ref, ...), custom_call_target="tpu_custom_call" | custom-call | tf_op jit(solution)/shard_map/place_vias/pallas_call | solution.py:614
  11.8 0.1 collective-permute-start.1
  11.9 5.6 %collective-permute-start.2 = (f32[448,128]{1,0:T(8,128)S(1)}, f32[448,128]{1,0:T(8,128)S(1)}, u32[]{:S(2)}, u32[]{:S(2)}) collective-permute-start(f32[448,128]{1,0:T(8,128)S(1)} %get-tuple-element.30), channel_id=1, source_target_pairs={{8,16},{16,8},{24,32},{32,24},{40,48},{48,40},{56,64},{64,56},{72,... | collective-permute-start | bytes 688136 | tf_op jit(solution)/shard_map/ppermute | solution.py:620
  17.5 1.2 %collective-permute-start.4 = (f32[32,128]{1,0:T(8,128)S(1)}, f32[32,128]{1,0:T(8,128)S(1)}, u32[]{:S(2)}, u32[]{:S(2)}) collective-permute-start(f32[32,128]{1,0:T(8,128)S(1)} %get-tuple-element.26.far_ref), channel_id=1, source_target_pairs={{16,32},{32,16},{24,40},{40,24},{48,64},{64,48},{56,72},{72,56},{8... | collective-permute-start | bytes 49160 | tf_op jit(solution)/shard_map/ppermute | solution.py:605
  18.6 2.5 %collective-permute-done.3.near_ref = f32[32,128]{1,0:T(8,128)S(1)} collective-permute-done((f32[32,128]{1,0:T(8,128)S(1)}, f32[32,128]{1,0:T(8,128)S(1)}, u32[]{:S(2)}, u32[]{:S(2)}) %collective-permute-start.3) | collective-permute-done | bytes 16416 | tf_op jit(solution)/shard_map/ppermute | solution.py:604
  21.2 3.6 %collective-permute-done.4.next_ref = f32[32,128]{1,0:T(8,128)S(1)} collective-permute-done((f32[32,128]{1,0:T(8,128)S(1)}, f32[32,128]{1,0:T(8,128)S(1)}, u32[]{:S(2)}, u32[]{:S(2)}) %collective-permute-start.4) | collective-permute-done | bytes 16416 | tf_op jit(solution)/shard_map/ppermute | solution.py:605
  24.8 0.6 %collective-permute-start.5 = (f32[16,128]{1,0:T(8,128)S(1)}, f32[16,128]{1,0:T(8,128)S(1)}, u32[]{:S(2)}, u32[]{:S(2)}) collective-permute-start(f32[16,128]{1,0:T(8,128)S(1)} %pad_maximum_fusion), channel_id=1, source_target_pairs={{0,128},{128,0},{1,129},{129,1},{2,130},{130,2},{3,131},{131,3},{4... | collective-permute-start | bytes 24584 | tf_op jit(solution)/shard_map/ppermute | solution.py:622
  25.4 3.1 %collective-permute-done.5.far_ref = f32[16,128]{1,0:T(8,128)S(1)} collective-permute-done((f32[16,128]{1,0:T(8,128)S(1)}, f32[16,128]{1,0:T(8,128)S(1)}, u32[]{:S(2)}, u32[]{:S(2)}) %collective-permute-start.5) | collective-permute-done | bytes 8224 | tf_op jit(solution)/shard_map/ppermute | solution.py:622
  28.5 1.1 %column_strips.1 = (f32[272,128]{1,0:T(8,128)S(1)}, f32[272,128]{1,0:T(8,128)S(1)}, f32[448,128]{1,0:T(8,128)S(1)}, f32[448,128]{1,0:T(8,128)S(1)}, f32[200,128]{1,0:T(8,128)S(1)}) custom-call(s32[5]{0:T(128)S(1)} %stack.15.place_ref, f32[2,2,64,256]{3,2,1,0:T(8,128)S(1)} %copy-done, f32[2,64,256]{2,1,0:T(8,128)S(1)} %copy-done.2, ...), custom_call_target="tpu_custom_call" | custom-call | tf_op jit(solution)/shard_map/column_strips/pallas_call | solution.py:625
  29.6 3.2 %collective-permute-start.6 = (f32[272,128]{1,0:T(8,128)S(1)}, f32[272,128]{1,0:T(8,128)S(1)}, u32[]{:S(2)}, u32[]{:S(2)}) collective-permute-start(f32[272,128]{1,0:T(8,128)S(1)} %get-tuple-element.34), channel_id=1, source_target_pairs={{0,1},{1,2},{2,3},{3,4},{4,5},{5,6},{6,7},{7,0},{8,9},{9,10},{10,1... | collective-permute-start | bytes 417800 | tf_op jit(solution)/shard_map/ppermute | solution.py:629
  32.8 2.6 %collective-permute-done.6.fromleft_ref = f32[272,128]{1,0:T(8,128)S(1)} collective-permute-done((f32[272,128]{1,0:T(8,128)S(1)}, f32[272,128]{1,0:T(8,128)S(1)}, u32[]{:S(2)}, u32[]{:S(2)}) %collective-permute-start.6) | collective-permute-done | bytes 139296 | tf_op jit(solution)/shard_map/ppermute | solution.py:629
  35.4 3.7 %collective-permute-done.7.fromright_ref = f32[272,128]{1,0:T(8,128)S(1)} collective-permute-done((f32[272,128]{1,0:T(8,128)S(1)}, f32[272,128]{1,0:T(8,128)S(1)}, u32[]{:S(2)}, u32[]{:S(2)}) %collective-permute-start.7) | collective-permute-done | bytes 139296 | tf_op jit(solution)/shard_map/ppermute | solution.py:628
  39.1 10.0 %solve.1 = (f32[2,2,64,256]{3,2,1,0:T(8,128)}, f32[2,8,32]{2,1,0:T(8,128)}) custom-call(s32[5]{0:T(128)S(1)} %stack.15.place_ref, f32[2,2,64,256]{3,2,1,0:T(8,128)S(1)} %copy-done, f32[2,64,256]{2,1,0:T(8,128)S(1)} %copy-done.2, f32[2,2,64,256]{3,2,1,0:T(8,128)S(1)} %copy-done.1, f32[4,64,128]{2,1,0:T(8,128)S(1)} %get-tuple-element.19.counts_ref, ...), custom_call_target="tpu_custom_call" | custom-call | tf_op jit(solution)/shard_map/solve/pallas_call | solution.py:636
  (21 shorter events, 0.0 us)
Async XLA Ops:
  0.6 0.7 %copy-start.9 = (s32[1,4]{1,0:T(1,128)S(1)}, s32[1,4]{1,0:T(1,128)}, u32[]{:S(2)}) copy-start(s32[1,4]{1,0:T(1,128)} %bump_ref.1) | copy-start | bytes 52
  0.6 0.7 %copy-start.6 = (f32[2,8,32]{2,1,0:T(8,128)S(1)}, f32[2,8,32]{2,1,0:T(8,128)}, u32[]{:S(2)}) copy-start(f32[2,8,32]{2,1,0:T(8,128)} %sheet_hbm.1) | copy-start | bytes 6148
  0.7 0.7 %copy-start.7 = (f32[2,8,32]{2,1,0:T(8,128)S(1)}, f32[2,8,32]{2,1,0:T(8,128)}, u32[]{:S(2)}) copy-start(f32[2,8,32]{2,1,0:T(8,128)} %start_hbm.1) | copy-start | bytes 6148
  1.4 1.2 %copy-start.3 = (f32[2,2,2,32,8,32]{5,4,3,2,1,0:T(8,128)S(1)}, f32[2,2,2,32,8,32]{5,4,3,2,1,0:T(8,128)}, u32[]{:S(2)}) copy-start(f32[2,2,2,32,8,32]{5,4,3,2,1,0:T(8,128)} %via_hbm.1) | copy-start | bytes 786436
  2.6 2.6 %copy-start.4 = (s32[2,32,8,32]{3,2,1,0:T(8,128)S(1)}, s32[2,32,8,32]{3,2,1,0:T(8,128)}, u32[]{:S(2)}) copy-start(s32[2,32,8,32]{3,2,1,0:T(8,128)} %cell_ref.1) | copy-start | bytes 196612
  2.6 2.6 %copy-start.5 = (f32[2,2,2,8,32]{4,3,2,1,0:T(8,128)S(1)}, f32[2,2,2,8,32]{4,3,2,1,0:T(8,128)}, u32[]{:S(2)}) copy-start(f32[2,2,2,8,32]{4,3,2,1,0:T(8,128)} %load_ref.1) | copy-start | bytes 24580
  2.6 2.6 %copy-start.8 = (s32[2,8,32]{2,1,0:T(8,128)S(1)}, s32[2,8,32]{2,1,0:T(8,128)}, u32[]{:S(2)}) copy-start(s32[2,8,32]{2,1,0:T(8,128)} %load_cell_ref.1) | copy-start | bytes 6148
  2.6 6.4 %copy-start.1 = (f32[2,2,64,256]{3,2,1,0:T(8,128)S(1)}, f32[2,2,64,256]{3,2,1,0:T(8,128)}, u32[]{:S(2)}) copy-start(f32[2,2,64,256]{3,2,1,0:T(8,128)} %drop_ref.5) | copy-start | bytes 786436
  2.6 6.4 %copy-start.2 = (f32[2,64,256]{2,1,0:T(8,128)S(1)}, f32[2,64,256]{2,1,0:T(8,128)}, u32[]{:S(2)}) copy-start(f32[2,64,256]{2,1,0:T(8,128)} %cap_ref.5) | copy-start | bytes 393220
  3.6 5.4 %copy-start = (f32[2,2,64,256]{3,2,1,0:T(8,128)S(1)}, f32[2,2,64,256]{3,2,1,0:T(8,128)}, u32[]{:S(2)}) copy-start(f32[2,2,64,256]{3,2,1,0:T(8,128)} %sheet_ref.5) | copy-start | bytes 786436
  3.6 5.4 %collective-permute-start = (f32[33,8,128]{2,1,0:T(8,128)S(1)}, f32[33,8,128]{2,1,0:T(8,128)S(1)}, u32[]{:S(2)}, u32[]{:S(2)}) collective-permute-start(f32[33,8,128]{2,1,0:T(8,128)S(1)} %get-tuple-element.21.send_ref), channel_id=1, source_target_pairs={{0,128},{128,0},{1,129},{129,1},{2,130},{130,2},{3,131},{131,3},{4... | collective-permute-start | bytes 405512 | tf_op jit(solution)/shard_map/ppermute | solution.py:603
  11.8 16.7 %collective-permute-start.1 = (f32[448,128]{1,0:T(8,128)S(1)}, f32[448,128]{1,0:T(8,128)S(1)}, u32[]{:S(2)}, u32[]{:S(2)}) collective-permute-start(f32[448,128]{1,0:T(8,128)S(1)} %get-tuple-element.29), channel_id=1, source_target_pairs={{0,8},{8,0},{16,24},{24,16},{32,40},{40,32},{48,56},{56,48},{64,72... | collective-permute-start | bytes 688136 | tf_op jit(solution)/shard_map/ppermute | solution.py:619
  11.9 16.6 %collective-permute-start.2 = (f32[448,128]{1,0:T(8,128)S(1)}, f32[448,128]{1,0:T(8,128)S(1)}, u32[]{:S(2)}, u32[]{:S(2)}) collective-permute-start(f32[448,128]{1,0:T(8,128)S(1)} %get-tuple-element.30), channel_id=1, source_target_pairs={{8,16},{16,8},{24,32},{32,24},{40,48},{48,40},{56,64},{64,56},{72,... | collective-permute-start | bytes 688136 | tf_op jit(solution)/shard_map/ppermute | solution.py:620
  17.5 3.7 %collective-permute-start.3 = (f32[32,128]{1,0:T(8,128)S(1)}, f32[32,128]{1,0:T(8,128)S(1)}, u32[]{:S(2)}, u32[]{:S(2)}) collective-permute-start(f32[32,128]{1,0:T(8,128)S(1)} %get-tuple-element.26.far_ref), channel_id=1, source_target_pairs={{0,16},{16,0},{8,24},{24,8},{32,48},{48,32},{40,56},{56,40},{64,80... | collective-permute-start | bytes 49160 | tf_op jit(solution)/shard_map/ppermute | solution.py:604
  17.5 7.4 %collective-permute-start.4 = (f32[32,128]{1,0:T(8,128)S(1)}, f32[32,128]{1,0:T(8,128)S(1)}, u32[]{:S(2)}, u32[]{:S(2)}) collective-permute-start(f32[32,128]{1,0:T(8,128)S(1)} %get-tuple-element.26.far_ref), channel_id=1, source_target_pairs={{16,32},{32,16},{24,40},{40,24},{48,64},{64,48},{56,72},{72,56},{8... | collective-permute-start | bytes 49160 | tf_op jit(solution)/shard_map/ppermute | solution.py:605
  24.8 3.7 %collective-permute-start.5 = (f32[16,128]{1,0:T(8,128)S(1)}, f32[16,128]{1,0:T(8,128)S(1)}, u32[]{:S(2)}, u32[]{:S(2)}) collective-permute-start(f32[16,128]{1,0:T(8,128)S(1)} %pad_maximum_fusion), channel_id=1, source_target_pairs={{0,128},{128,0},{1,129},{129,1},{2,130},{130,2},{3,131},{131,3},{4... | collective-permute-start | bytes 24584 | tf_op jit(solution)/shard_map/ppermute | solution.py:622
  29.6 5.8 %collective-permute-start.6 = (f32[272,128]{1,0:T(8,128)S(1)}, f32[272,128]{1,0:T(8,128)S(1)}, u32[]{:S(2)}, u32[]{:S(2)}) collective-permute-start(f32[272,128]{1,0:T(8,128)S(1)} %get-tuple-element.34), channel_id=1, source_target_pairs={{0,1},{1,2},{2,3},{3,4},{4,5},{5,6},{6,7},{7,0},{8,9},{9,10},{10,1... | collective-permute-start | bytes 417800 | tf_op jit(solution)/shard_map/ppermute | solution.py:629
  32.8 6.3 %collective-permute-start.7 = (f32[272,128]{1,0:T(8,128)S(1)}, f32[272,128]{1,0:T(8,128)S(1)}, u32[]{:S(2)}, u32[]{:S(2)}) collective-permute-start(f32[272,128]{1,0:T(8,128)S(1)} %get-tuple-element.35), channel_id=1, source_target_pairs={{0,7},{1,0},{2,1},{3,2},{4,3},{5,4},{6,5},{7,6},{8,15},{9,8},{10,9... | collective-permute-start | bytes 417800 | tf_op jit(solution)/shard_map/ppermute | solution.py:628

commit v3 on v2

--- a/solution.py
+++ b/solution.py
@@ -54,25 +54,8 @@
     return pl.ds(8 * g, 8)
 
 
-def spread_nets(ref):
-    gap = jnp.zeros((8, 16), F32)
-    return jnp.concatenate([gap, ref[0], gap, gap, ref[1], gap], axis=1)
-
-
-def pack_kernel(place_ref, bump_ref, via_hbm, sheet_hbm, start_hbm, packed_ref, send_ref, far_ref, via_ref, sheet_ref, start_ref, sems):
-    copies = [pltpu.make_async_copy(via_hbm.at[t, d], via_ref.at[t, d], sems.at[2 * t + d]) for t in range(2) for d in range(2)]
-    copies.append(pltpu.make_async_copy(sheet_hbm, sheet_ref, sems.at[4]))
-    copies.append(pltpu.make_async_copy(start_hbm, start_ref, sems.at[5]))
-    for copy in copies:
-        copy.start()
+def pack_kernel(place_ref, via_ref, packed_ref, send_ref):
     later = place_ref[0].astype(F32)
-    lane, sub = lane_iota(), sub_iota()
-    bump = jnp.zeros((8, 128), F32)
-    column = lane % 64 - 16
-    for k in range(4):
-        bump = jnp.where((column // 8 == k) & (sub * 8 + column % 8 == bump_ref[0, k]), 1.0, bump)
-    for copy in copies:
-        copy.wait()
     total = jnp.zeros((8, 128), F32)
     for v in range(VIAS):
         parts = []
@@ -84,10 +67,23 @@
         send_ref[v] = both + later * parts[0]
         total = total + both
     send_ref[VIAS] = total
+
+
+def spread_nets(ref):
+    gap = jnp.zeros((8, 16), F32)
+    return jnp.concatenate([gap, ref[0], gap, gap, ref[1], gap], axis=1)
+
+
+def base_kernel(bump_ref, sheet_ref, start_ref, send_ref, far_ref):
+    lane, sub = lane_iota(), sub_iota()
+    bump = jnp.zeros((8, 128), F32)
+    column = lane % 64 - 16
+    for k in range(4):
+        bump = jnp.where((column // 8 == k) & (sub * 8 + column % 8 == bump_ref[0, k]), 1.0, bump)
     far_ref[rows(0), :] = spread_nets(sheet_ref)
     far_ref[rows(1), :] = spread_nets(start_ref)
     far_ref[rows(2), :] = bump
-    far_ref[rows(3), :] = total
+    far_ref[rows(3), :] = send_ref[VIAS]
 
 
 def spread_matrix(height, width):
@@ -148,7 +144,7 @@
 
 def place_kernel(
     place_ref, packed_ref, send_ref, got_ref, cells_ref, load_cells_ref, loads_ref, spread_ref, counts_ref, far_ref,
-    sheet_ref, cap_ref, drop_ref, field_ref, even_ref, odd_ref, base_ref, values_ref,
+    near_ref, next_ref, sheet_ref, cap_ref, drop_ref, field_ref, even_ref, odd_ref, base_ref, shares_ref, values_ref,
 ):
     lane = lane_iota()
     later = place_ref[0].astype(F32)
@@ -187,6 +183,9 @@
 
     lax.fori_loop(0, 4, add, 0)
 
+    shares_ref[rows(0), :] = near_ref[rows(3), :]
+    shares_ref[rows(1), :] = next_ref[rows(3), :]
+
     place = 0
 
     def put(up, down):
@@ -226,33 +225,21 @@
     return start + 10 if kind == 2 else start + 5 * n + 3 * kind
 
 
-def below_rows(ref, d, half, n, kind, second):
+def near_rows(read, d, half, n, kind, second, upper):
     start = row_place(d, half, n, kind)
     if kind == 1:
         if second:
-            return roll(ref[rows(start + 1), :], -3, 0), None
-        return ref[rows(start), :], ref[rows(start + 1), :]
-    last = ref[rows(start + 2), :]
+            return roll(read(start + 1), -5 if upper else -3, 0), None
+        return read(start), read(start + 1)
+    last = read(start + 2)
     if second:
-        return ref[rows(start + 1), :], roll(last, -4, 0)
-    return ref[rows(start), :], last
-
-
-def above_rows(ref, d, half, n, kind, second):
-    start = row_place(d, half, n, kind)
-    if kind == 1:
-        if second:
-            return roll(ref[rows(start + 1), :], -5, 0), None
-        return ref[rows(start), :], ref[rows(start + 1), :]
-    last = ref[rows(start + 2), :]
-    if second:
-        return ref[rows(start + 1), :], roll(last, -4, 0)
-    return ref[rows(start), :], last
+        return read(start + 1), roll(last, -4, 0)
+    return read(start), last
 
 
 def column_groups(own, below, above, d, half, n, kind, second):
-    low = below_rows(below, d, half, n, kind, second)
-    high = above_rows(above, d, half, n, kind, second)
+    low = near_rows(below, d, half, n, kind, second, False)
+    high = near_rows(above, d, half, n, kind, second, True)
     return [own(g) for g in range(8)] + [low[0], low[1], high[1], high[0]]
 
 
@@ -261,20 +248,18 @@
 
 def strip_kernel(
     place_ref, sheet_ref, cap_ref, drop_ref, counts_ref, field_ref, base_ref, even_ref, odd_ref, near_ref, next_ref, far_ref,
-    left_ref, right_ref, below_ref, above_ref, wide_ref,
+    left_ref, right_ref, wide_ref,
 ):
     lane = lane_iota()
     within = lane % 16
     row, last = place_ref[1], place_ref[3]
     even, low = row % 2 == 0, row % 4 < 2
 
-    def pick(flag, yes, no, inside):
-        return jnp.where(inside, jnp.where(flag, yes, no), 0.0)
-
-    for g in range(ROW_GROUPS):
-        a, b = even_ref[rows(g), :], odd_ref[rows(g), :]
-        below_ref[rows(g), :] = pick(even, a, b, row < last)
-        above_ref[rows(g), :] = pick(even, b, a, row > 0)
+    def below(g):
+        return jnp.where(even, even_ref[rows(g), :], odd_ref[rows(g), :])
+
+    def above(g):
+        return jnp.where(even, odd_ref[rows(g), :], even_ref[rows(g), :])
 
     own = (lane % 64 >= 16) & (lane % 64 < 48)
 
@@ -290,13 +275,14 @@
         if g == 0:
             parts = [base_ref[rows(f), :] for f in range(BASE)]
         elif g in (1, 4):
-            ref = below_ref if g == 1 else above_ref
-            parts = [ref[rows(ROW_GROUPS - BASE + f), :] for f in range(BASE)]
+            read, inside = (below, row < last) if g == 1 else (above, row > 0)
+            parts = [jnp.where(inside, read(ROW_GROUPS - BASE + f), 0.0) for f in range(BASE)]
         else:
             inside = row + 2 <= last if g == 2 else row >= 2
             flag = low if g == 2 else jnp.logical_not(low)
-            parts = [pick(flag, near_ref[rows(f), :], next_ref[rows(f), :], inside) for f in range(BASE)]
-            parts[3] = parts[3] + pick(flag, far_ref[rows(0), :], far_ref[rows(1), :], inside)
+            parts = [jnp.where(flag, near_ref[rows(f), :], next_ref[rows(f), :]) for f in range(BASE)]
+            parts[3] = parts[3] + jnp.where(flag, far_ref[rows(0), :], far_ref[rows(1), :])
+            parts = [jnp.where(inside, part, 0.0) for part in parts]
         one, two = spread_steps(parts[3])
         groups.append([parts[0], parts[1], one, two, parts[2]])
         for f in range(5):
@@ -307,24 +293,21 @@
         first, second = [], []
         for d in range(2):
             for n in range(2):
-                first.append(column_groups(
-                    lambda g: sheet_ref[d, n, rows(g), lanes], below_ref, above_ref, d, half, n, 0, False))
+                first.append(column_groups(lambda g: sheet_ref[d, n, rows(g), lanes], below, above, d, half, n, 0, False))
         for d in range(2):
             for n in range(2):
-                first.append(column_groups(
-                    lambda g: drop_ref[d, n, rows(g), lanes], below_ref, above_ref, d, half, n, 0, True))
+                first.append(column_groups(lambda g: drop_ref[d, n, rows(g), lanes], below, above, d, half, n, 0, True))
         for d in range(2):
-            second.append(column_groups(
-                lambda g: cap_ref[d, rows(g), lanes], below_ref, above_ref, d, half, 0, 2, False))
+            second.append(column_groups(lambda g: cap_ref[d, rows(g), lanes], below, above, d, half, 0, 2, False))
         for d in range(2):
-            second.append(column_groups(
-                lambda g: counts_ref[2 * d + half, rows(g), :], below_ref, above_ref, d, half, 0, 2, True))
+            second.append(
+                column_groups(lambda g: counts_ref[2 * d + half, rows(g), :], below, above, d, half, 0, 2, True))
         for d in range(2):
             for n in range(2):
                 one = column_groups(
-                    lambda g: field_ref[n, 2 * d + half, rows(g), :], below_ref, above_ref, d, half, n, 1, False)
+                    lambda g: field_ref[n, 2 * d + half, rows(g), :], below, above, d, half, n, 1, False)
                 two = column_groups(
-                    lambda g: field_ref[2 + n, 2 * d + half, rows(g), :], below_ref, above_ref, d, half, n, 1, True)
+                    lambda g: field_ref[2 + n, 2 * d + half, rows(g), :], below, above, d, half, n, 1, True)
                 merged = []
                 for a, b in zip(one, two):
                     if b is None:
@@ -336,16 +319,13 @@
                 second.append(merged)
         return first, second
 
-    def join(chunks, origin):
-        out = roll(chunks[0], -origin, 1)
-        for k in range(1, 8):
-            out = jnp.where(lane // 16 == k, roll(chunks[k], 16 * k - origin, 1), out)
-        return out
-
-    for half, ref, origin in ((0, left_ref, 0), (1, right_ref, 112)):
+    for half, ref in ((0, left_ref), (1, right_ref)):
         for part, chunks in enumerate(fields(half)):
             for g in range(GROUPS):
-                ref[rows(part * GROUPS + g), :] = join([chunk[g] for chunk in chunks], origin)
+                out = chunks[0][g]
+                for k in range(1, 8):
+                    out = jnp.where((lane // 16 + half) % 8 == k, roll(chunks[k][g], 16 * k, 1), out)
+                ref[rows(part * GROUPS + g), :] = out
 
     start = 2 * GROUPS
     quarter = (lane % 64) // 16
@@ -363,6 +343,63 @@
         right_ref[rows(start + g), :] = right
         left_ref[rows(start + 5 + g), :] = bump
         right_ref[rows(start + 5 + g), :] = bump
+
+
+def assemble_kernel(
+    place_ref, sheet_ref, cap_ref, drop_ref, counts_ref, field_ref, even_ref, odd_ref,
+    s_ref, x_ref, c_ref, k_ref, one_ref, two_ref, up_ref, down_ref, left_ref, right_ref, diag_ref, spread_ref,
+):
+    row, last = place_ref[1], place_ref[3]
+    even = row % 2 == 0
+    sub, lane = sub_iota(256), lax.broadcasted_iota(jnp.int32, (8, 256), 1)
+
+    def below(g):
+        return jnp.where(row < last, jnp.where(even, even_ref[rows(g), :], odd_ref[rows(g), :]), 0.0)
+
+    def above(g):
+        return jnp.where(row > 0, jnp.where(even, odd_ref[rows(g), :], even_ref[rows(g), :]), 0.0)
+
+    def both(own, d, n, kind, second):
+        sides = [column_groups(lambda g: own(half, g), below, above, d, half, n, kind, second) for half in range(2)]
+        return [None if a is None else jnp.concatenate([a, b], axis=1) for a, b in zip(*sides)]
+
+    for d in range(2):
+        caps = both(lambda half, g: cap_ref[d, rows(g), pl.ds(half * 128, 128)], d, 0, 2, False)
+        counts = both(lambda half, g: counts_ref[2 * d + half, rows(g), :], d, 0, 2, True)
+        for g in range(GROUPS):
+            c_ref[d, rows(g), :] = caps[g]
+            k_ref[d, rows(g), :] = counts[g]
+        for n in range(2):
+            i = 2 * d + n
+            sheets = both(lambda half, g: sheet_ref[d, n, rows(g), pl.ds(half * 128, 128)], d, n, 0, False)
+            drops = both(lambda half, g: drop_ref[d, n, rows(g), pl.ds(half * 128, 128)], d, n, 0, True)
+            ones = both(lambda half, g: field_ref[n, 2 * d + half, rows(g), :], d, n, 1, False)
+            twos = both(lambda half, g: field_ref[2 + n, 2 * d + half, rows(g), :], d, n, 1, True)
+            for g in range(GROUPS):
+                s_ref[i, rows(g), :] = sheets[g]
+                x_ref[i, rows(g), :] = drops[g]
+                one_ref[i, rows(g), :] = c_ref[d, rows(g), :] * drops[g] + ones[g]
+                if twos[g] is not None:
+                    two_ref[i, rows(g), :] = twos[g]
+            for g in range(GROUPS):
+                here, after = s_ref[i, rows(g), :], s_ref[i, rows((g + 1) % GROUPS), :]
+                under = jnp.where(sub == 7, roll(after, -1, 0), roll(here, -1, 0))
+                inside = here > 0.0
+                down_ref[i, rows(g), :] = jnp.where(inside, connect(here, under), 0.0)
+                right = jnp.where(inside & (lane < 255), connect(here, roll(here, -1, 1)), 0.0)
+                right_ref[i, rows(g), :] = right
+                left_ref[i, rows(g), :] = roll(right, 1, 1)
+            for g in range(GROUPS):
+                here, before = down_ref[i, rows(g), :], down_ref[i, rows((g - 1) % GROUPS), :]
+                up = jnp.where(sub == 0, roll(before, 1, 0), roll(here, 1, 0))
+                up_ref[i, rows(g), :] = up
+                diag = c_ref[d, rows(g), :] + up + here + left_ref[i, rows(g), :] + right_ref[i, rows(g), :]
+                diag_ref[i, rows(g), :] = diag + VIA_CONDUCT * k_ref[d, rows(g), :]
+    source = lax.broadcasted_iota(jnp.int32, (256, 384), 0) % 128
+    column = lax.broadcasted_iota(jnp.int32, (256, 384), 1)
+    column = jnp.where(column < 256, 16 + column // 8, jnp.where(column < 320, 48, 0) + (column - 256) // 8)
+    for n in range(2):
+        spread_ref[n] = jnp.where(source == column + 64 * n, 1.0, 0.0).astype(jnp.bfloat16)
 
 
 def connect(center, neighbour):
@@ -412,12 +449,13 @@
 
 
 def solve_kernel(
-    place_ref, sheet_ref, cap_ref, drop_ref, counts_ref, field_ref, wide_ref, below_ref, above_ref,
-    fromleft_ref, fromright_ref, out_ref, base_out_ref,
-    s_ext, x_ext, c_ext, k_ext, f_ext, base_ext, link_up, link_down, link_left, link_right, inv_ext, src, alt,
+    place_ref, s_ref, x_ref, c_ref, k_ref, one_ref, two_ref, up_ref, down_ref, left_ref, right_ref, diag_ref, spread_ref,
+    wide_ref, fromleft_ref, fromright_ref, out_ref, base_out_ref,
+    c_ext, k_ext, f_ext, bound, link_up, link_down, link_left, link_right, inv_ext, src, state, alt,
 ):
     lane = lane_iota()
-    has_left, has_right = place_ref[2] > 0, place_ref[2] < place_ref[4]
+    row, col = place_ref[1], place_ref[2]
+    has_left, has_right = col > 0, col < place_ref[4]
 
     start = 2 * GROUPS
     quarter = (lane % 64) // 16
@@ -436,111 +474,92 @@
         fields.append(jnp.concatenate(out, axis=0))
     solved = base_solve((fields[0], fields[1], (fields[2], fields[3]), fields[4]))
     for t in range(STEPS):
-        base_ext[t] = solved[t]
+        pieces = halves(solved[t])
+        for n in range(2):
+            bound[2 * t + n] = jnp.dot(pieces, spread_ref[n], preferred_element_type=F32)
     for n in range(2):
         base_out_ref[n] = roll(solved[1][0:8], -(64 * n + 16), 1)[:, 0:32]
 
-    at_left, at_right = (lane >= 112) & has_left, (lane < 16) & has_right
-
     def third(part, chunk, g):
-        right = fromright_ref[rows(part * GROUPS + g), :]
-        left = fromleft_ref[rows(part * GROUPS + g), :]
-        value = jnp.where(at_right, roll(right, -16 * chunk, 1), 0.0)
-        return jnp.where(at_left, roll(left, 112 - 16 * chunk, 1), value)
-
-    def fill(target, index, own, d, n, kind, second, part, chunk, shift=0):
-        for half in range(2):
-            for g, value in enumerate(
-                column_groups(lambda g: own(half, g), below_ref, above_ref, d, half, n, kind, second)
-            ):
-                if value is not None:
-                    target[index, rows(g), pl.ds(half * 128, 128)] = value
+        right_ok, left_ok = has_right, has_left
+        if g in (8, 9):
+            right_ok, left_ok = right_ok & (row < place_ref[3]), left_ok & (row < place_ref[3])
+        if g in (10, 11):
+            right_ok, left_ok = right_ok & (row > 0), left_ok & (row > 0)
+        right = jnp.where((lane // 16 == chunk) & right_ok, fromright_ref[rows(part * GROUPS + g), :], 0.0)
+        value = jnp.where((lane // 16 == (chunk + 7) % 8) & left_ok, fromleft_ref[rows(part * GROUPS + g), :], right)
+        return roll(value, -16 * chunk, 1)
+
+    sub, sub3 = sub_iota(), sub_iota(384)
+
+    def above(value, before, index):
+        return jnp.where(index == 0, roll(before, 1, 0), roll(value, 1, 0))
+
+    def below(value, after, index):
+        return jnp.where(index == 7, roll(after, -1, 0), roll(value, -1, 0))
+
+    for i in range(4):
+        d, n = i // 2, i % 2
+
+        def wide(ref, g, extra, index=i):
+            return jnp.concatenate([ref[index, rows(g), :], extra], axis=1)
+
+        if n == 0:
+            for g in range(GROUPS):
+                c_ext[rows(g), :] = wide(c_ref, g, third(1, d, g), d)
+                k_ext[rows(g), :] = wide(k_ref, g, third(1, 2 + d, g), d)
+        sheets = [third(0, i, g) for g in range(GROUPS)]
         for g in range(GROUPS):
-            if shift and g in (9, 10):
-                continue
-            value = third(part, chunk, g)
-            if shift:
-                value = jnp.where(lane < 64, roll(value, -shift, 1), roll(value, shift, 1))
-            target[index, rows(g), pl.ds(256, 128)] = value
-
-    for d in range(2):
-        fill(c_ext, d, lambda half, g: cap_ref[d, rows(g), pl.ds(half * 128, 128)], d, 0, 2, False, 1, d)
-        fill(k_ext, d, lambda half, g: counts_ref[2 * d + half, rows(g), :], d, 0, 2, True, 1, 2 + d)
-        for n in range(2):
-            i = 2 * d + n
-            fill(s_ext, i, lambda half, g: sheet_ref[d, n, rows(g), pl.ds(half * 128, 128)], d, n, 0, False, 0, i)
-            fill(x_ext, i, lambda half, g: drop_ref[d, n, rows(g), pl.ds(half * 128, 128)], d, n, 0, True, 0, 4 + i)
-            fill(f_ext, i, lambda half, g: field_ref[n, 2 * d + half, rows(g), :], d, n, 1, False, 1, 4 + i)
-            fill(f_ext, 4 + i, lambda half, g: field_ref[2 + n, 2 * d + half, rows(g), :], d, n, 1, True, 1, 4 + i, 11)
-
-    sub = sub_iota(384)
-    tile = [lane // 8 + 16, lane // 8 + 32, jnp.where(lane < 64, lane // 8 + 48, lane // 8)]
-
-    def image(i, carry):
-        d = i // 2
-        n = i % 2
-
-        def get(ref, g):
-            return ref[rows(g % GROUPS), :]
-
-        def above(value, before):
-            return jnp.where(sub == 0, roll(before, 1, 0), roll(value, 1, 0))
-
-        def below(value, after):
-            return jnp.where(sub == 7, roll(after, -1, 0), roll(value, -1, 0))
-
-        for g in range(GROUPS):
-            here = s_ext[i, rows(g), :]
-            after = s_ext[i, rows((g + 1) % GROUPS), :]
+            here = sheets[g]
             inside = here > 0.0
-            down = jnp.where(inside, connect(here, below(here, after)), 0.0)
-            right = jnp.where(inside, connect(here, roll(here, -1, 1)), 0.0)
-            link_down[rows(g), :] = down
-            link_right[rows(g), :] = right
-            link_left[rows(g), :] = roll(right, 1, 1)
-        for g in range(GROUPS):
-            link_up[rows(g), :] = above(get(link_down, g), get(link_down, g - 1))
-        for g in range(GROUPS):
-            ups, downs = get(link_up, g), get(link_down, g)
-            lefts, rights = get(link_left, g), get(link_right, g)
-            diagonal = c_ext[d, rows(g), :] + ups + downs + lefts + rights + VIA_CONDUCT * k_ext[d, rows(g), :]
-            inverse = jnp.where(diagonal > 0.0, 1.0 / diagonal, 0.0)
+            low, high = s_ref[i, rows(g), pl.ds(0, 128)], s_ref[i, rows(g), pl.ds(128, 128)]
+            after = jnp.where(lane == 127, roll(low, -1, 1), roll(here, -1, 1))
+            before = jnp.where(lane == 0, roll(high, 1, 1), roll(here, 1, 1))
+            right = jnp.where(inside, connect(here, after), 0.0)
+            left = jnp.where(inside, connect(here, before), 0.0)
+            down = jnp.where(inside, connect(here, below(here, sheets[(g + 1) % GROUPS], sub)), 0.0)
+            up = jnp.where(inside, connect(here, above(here, sheets[(g - 1) % GROUPS], sub)), 0.0)
+            first = jnp.where(lane == 0, roll(right, 1, 1), 0.0)
+            final = jnp.where(lane == 127, roll(left, -1, 1), 0.0)
+            diag = wide(diag_ref, g, 0.0 * here) + jnp.concatenate(
+                [first, final, c_ext[rows(g), pl.ds(256, 128)] + up + down + left + right
+                 + VIA_CONDUCT * k_ext[rows(g), pl.ds(256, 128)]], axis=1)
+            inverse = jnp.where(diag > 0.0, 1.0 / diag, 0.0)
             inv_ext[rows(g), :] = inverse
-            link_up[rows(g), :] = inverse * ups
-            link_left[rows(g), :] = inverse * lefts
-            link_right[rows(g), :] = inverse * rights
-        for g in range(GROUPS):
-            link_down[rows(g), :] = get(inv_ext, g) * get(link_down, g)
+            zero = jnp.zeros_like(first)
+            link_up[rows(g), :] = inverse * wide(up_ref, g, up)
+            link_down[rows(g), :] = inverse * wide(down_ref, g, down)
+            link_left[rows(g), :] = inverse * (wide(left_ref, g, left) + jnp.concatenate([first, zero, zero], axis=1))
+            link_right[rows(g), :] = inverse * (wide(right_ref, g, right) + jnp.concatenate([zero, final, zero], axis=1))
+            drop = third(0, 4 + i, g)
+            state[rows(g), :] = wide(x_ref, g, drop)
+            one = third(1, 4 + i, g)
+            f_ext[0, rows(g), :] = wide(one_ref, g, c_ext[rows(g), pl.ds(256, 128)] * drop + one)
+            if g not in (9, 10):
+                two = jnp.where(lane < 64, roll(one, -11, 1), roll(one, 11, 1))
+                f_ext[1, rows(g), :] = wide(two_ref, g, two)
 
         for t in range(STEPS):
             for k in range(SWEEPS):
+                now, then = (alt, state) if k % 2 else (state, alt)
                 for g in needed(11 - 6 * t - k):
-                    def read(near):
-                        near = near % GROUPS
-                        return alt[rows(near), :] if k % 2 else x_ext[i, rows(near), :]
-
-                    value = read(g)
-                    total = get(link_up, g) * above(value, read(g - 1)) + get(link_down, g) * below(value, read(g + 1))
-                    total = total + (get(link_left, g) * roll(value, 1, 1) + get(link_right, g) * roll(value, -1, 1))
+                    value = now[rows(g), :]
+                    total = link_up[rows(g), :] * above(value, now[rows((g - 1) % GROUPS), :], sub3)
+                    total = total + link_down[rows(g), :] * below(value, now[rows((g + 1) % GROUPS), :], sub3)
+                    total = total + (
+                        link_left[rows(g), :] * roll(value, 1, 1) + link_right[rows(g), :] * roll(value, -1, 1))
                     if k == 0:
-                        spread = jnp.broadcast_to(base_ext[t, pl.ds(base_row(g), 1), :], (8, 128))
-                        pieces = [jnp.take_along_axis(spread, index + 64 * n, axis=1) for index in tile]
-                        source = c_ext[d, rows(g), :] * value + f_ext[4 * t + i, rows(g), :]
-                        source = source + k_ext[d, rows(g), :] * jnp.concatenate(pieces, axis=1)
-                        source = get(inv_ext, g) * source
+                        spread = jnp.broadcast_to(bound[2 * t + n, pl.ds(base_row(g), 1), :], (8, 384))
+                        source = f_ext[t, rows(g), :] + k_ext[rows(g), :] * spread
+                        if t:
+                            source = source + c_ext[rows(g), :] * value
+                        source = inv_ext[rows(g), :] * source
                         src[rows(g), :] = source
                     else:
-                        source = get(src, g)
-                    total = total + source
-                    if k % 2:
-                        x_ext[i, rows(g), :] = advance(k, value, lambda: x_ext[i, rows(g), :], total)
-                    else:
-                        alt[rows(g), :] = advance(k, value, lambda: alt[rows(g), :], total)
+                        source = src[rows(g), :]
+                    then[rows(g), :] = advance(k, value, lambda: then[rows(g), :], total + source)
         for g in range(8):
-            out_ref[d, n, rows(g), :] = x_ext[i, rows(g), pl.ds(0, 256)]
-        return carry
-
-    lax.fori_loop(0, 4, image, 0)
+            out_ref[d, n, rows(g), :] = state[rows(g), pl.ds(0, 256)]
 
 
 def base_row(g):
@@ -553,10 +572,6 @@
 
 def smem():
     return pl.BlockSpec(memory_space=pltpu.SMEM)
-
-
-def hbm():
-    return pl.BlockSpec(memory_space=pltpu.HBM)
 
 
 def call(kernel, name, outs, ins, scratch=(), limit=24):
@@ -594,13 +609,13 @@
     ).astype(jnp.int32)
     others = [(0, 1), (1, 0)]
 
-    packed, send, far = call(
-        pack_kernel, "pack_vias", (arr(2, VIAS, 8, 128), arr(VIAS + 1, 8, 128), arr(8 * BASE, 128)),
-        [smem(), smem(), hbm(), hbm(), hbm()],
-        [pltpu.VMEM((2, 2, 2, VIAS, 8, 32), F32), pltpu.VMEM((2, 8, 32), F32), pltpu.VMEM((2, 8, 32), F32),
-         pltpu.SemaphoreType.DMA((6,))],
-    )(place, bump_cell, via_current, base_sheet, base_start)
+    packed, send = call(pack_kernel, "pack_vias", (arr(2, VIAS, 8, 128), arr(VIAS + 1, 8, 128)), [smem()] + spec(1))(
+        place, via_current
+    )
     got = lax.ppermute(send, "die", others)
+    far = call(base_kernel, "pack_base", (arr(8 * BASE, 128),), [smem()] + spec(3))(
+        bump_cell, base_sheet, base_start, send
+    )[0]
     near = lax.ppermute(far, "row", swaps(row_count, 0, 2))
     after = lax.ppermute(far, "row", swaps(row_count, 2, 2))
 
@@ -611,31 +626,33 @@
     )(via_cell, load_cell, load_current)
 
     rows_shape = arr(8 * ROW_GROUPS, 128)
-    field, even, odd, base = call(
-        place_kernel, "place_vias", (arr(4, 4, 64, 128), rows_shape, rows_shape, arr(8 * BASE, 128)),
-        [smem()] + spec(12), [pltpu.VMEM((4, 4, VIAS, 8, 128), F32)],
-    )(place, packed, send, got, cells, load_cells, loads, spread, counts, far, sheet_res, capacity, drop_start)
+    field, even, odd, base, shares = call(
+        place_kernel, "place_vias", (arr(4, 4, 64, 128), rows_shape, rows_shape, arr(8 * BASE, 128), arr(16, 128)),
+        [smem()] + spec(14), [pltpu.VMEM((4, 4, VIAS, 8, 128), F32)],
+    )(place, packed, send, got, cells, load_cells, loads, spread, counts, far, near, after, sheet_res, capacity, drop_start)
 
     even = lax.ppermute(even, "row", swaps(row_count, 0))
     odd = lax.ppermute(odd, "row", swaps(row_count, 1))
-    shares = jnp.concatenate([near[24:32], after[24:32]], axis=0)
     shares = lax.ppermute(shares, "die", others)
 
     strip_shape = arr(8 * COL_GROUPS, 128)
-    left, right, below, above, wide = call(
-        strip_kernel, "column_strips", (strip_shape, strip_shape, rows_shape, rows_shape, arr(200, 128)), [smem()] + spec(11)
+    left, right, wide = call(
+        strip_kernel, "column_strips", (strip_shape, strip_shape, arr(200, 128)), [smem()] + spec(11)
     )(place, sheet_res, capacity, drop_start, counts, field, base, even, odd, near, after, shares)
     from_right = lax.ppermute(left, "col", [(i, (i - 1) % col_count) for i in range(col_count)])
     from_left = lax.ppermute(right, "col", [(i, (i + 1) % col_count) for i in range(col_count)])
 
-    ext = (96, 384)
-    scratch = [
-        pltpu.VMEM((4,) + ext, F32), pltpu.VMEM((4,) + ext, F32), pltpu.VMEM((2,) + ext, F32),
-        pltpu.VMEM((2,) + ext, F32), pltpu.VMEM((8,) + ext, F32), pltpu.VMEM((2, 40, 128), F32),
-    ] + [pltpu.VMEM(ext, F32)] * 7
-    return call(
-        solve_kernel, "solve", (arr(2, 2, 64, 256), arr(2, 8, 32)), [smem()] + spec(10), scratch,
-    )(place, sheet_res, capacity, drop_start, counts, field, wide, below, above, from_left, from_right)
+    image, pair = arr(4, 96, 256), arr(2, 96, 256)
+    parts = call(
+        assemble_kernel, "assemble",
+        (image, image, pair, pair) + (image,) * 7 + (arr(2, 256, 384, dtype=jnp.bfloat16),), [smem()] + spec(7),
+    )(place, sheet_res, capacity, drop_start, counts, field, even, odd)
+
+    ext = pltpu.VMEM((96, 384), F32)
+    scratch = [ext, ext, pltpu.VMEM((2, 96, 384), F32), pltpu.VMEM((4, 40, 384), F32)] + [ext] * 8
+    return call(solve_kernel, "solve", (arr(2, 2, 64, 256), arr(2, 8, 32)), [smem()] + spec(15), scratch)(
+        place, *parts, wide, from_left, from_right
+    )
 
 
 def solution(mesh):

time: 49.2 us -> 49.2 us (level)
  waiting for transfers between devices: 18.6 us -> 13 us
  Pallas kernels: 15.5 us -> 19.8 us
  starting transfers between devices: 12.2 us -> 14.1 us
  local copies, waits for them, and re-layouts: 1.96 us -> 1.35 us
    ppermute x1, starting transfers between devices: 1.19 us -> 5.24 us  [per_device(): after = lax.ppermute(far, 'row', swaps(row_count, 2, 2))]
    ppermute x1, waiting for transfers between devices: 3.09 us -> 0.01 us  [per_device(): got = lax.ppermute(send, 'die', others)]
    pallas_call x1, Pallas kernels: 9.99 us -> 12.6 us  [per_device(): call(solve_kernel, 'solve', (arr(2, 2, 64, 256), arr(2, 8, 32)), [smem()]...]
    pallas_call x1 -> x3, Pallas kernels: 1.1 us -> 3.1 us  [the longest x1 1.39 us: per_device(): call(assemble_kernel, 'assemble', (image, image, pair, pair) + (image,) *...]
    ppermute x1, starting transfers between devices: 5.58 us -> 3.73 us  [per_device(): odd = lax.ppermute(odd, 'row', swaps(row_count, 1))]
    ppermute x1, waiting for transfers between devices: 2.55 us -> 0.78 us  [per_device(): near = lax.ppermute(far, 'row', swaps(row_count, 0, 2))]
    ppermute x1, waiting for transfers between devices: 3.61 us -> 2.21 us  [per_device(): after = lax.ppermute(far, 'row', swaps(row_count, 2, 2))]
    ppermute x1, waiting for transfers between devices: 2.6 us -> 1.19 us  [per_device(): lax.ppermute(right, 'col', [(i, (i + 1) % col_count) for i in range(col_c...]
  transfers between devices with their start and end apart: 8 -> 8, of which waited for: 6 -> 6; matrix products, arithmetic and copies ran while one was open for 0% -> 0% of each run, Pallas kernels for 1% -> 6%
where the time goes in v3:
time: 49.2 us; the launch traced here: 49.1 us
  Pallas kernels  19.8 us (40%)
  starting transfers between devices  14.1 us (29%)
  waiting for transfers between devices  13 us (26%)
  local copies, waits for them, and re-layouts  1.35 us (3%)
  between operations  0.75 us (2%)
    pallas_call x1, Pallas kernels, per_device(): call(solve_kernel, 'solve', (arr(2, 2, 64, 256), arr(2, 8, 32)), [smem()]...  12.6 us
    ppermute x1, starting transfers between devices, per_device(): after = lax.ppermute(far, 'row', swaps(row_count, 2, 2))  5.24 us
    ppermute x1, waiting for transfers between devices, per_device(): shares = lax.ppermute(shares, 'die', others)  4.08 us
    ppermute x1, starting transfers between devices, per_device(): odd = lax.ppermute(odd, 'row', swaps(row_count, 1))  3.73 us
    ppermute x1, waiting for transfers between devices, per_device(): lax.ppermute(left, 'col', [(i, (i - 1) % col_count) for i in range(col_co...  3.67 us
    ppermute x1, starting transfers between devices, per_device(): lax.ppermute(right, 'col', [(i, (i + 1) % col_count) for i in range(col_c...  3.21 us
    pallas_call x1, Pallas kernels, per_device(): call(place_kernel, 'place_vias', (arr(4, 4, 64, 128), rows_shape, rows_sh...  2.61 us
    ppermute x1, waiting for transfers between devices, per_device(): after = lax.ppermute(far, 'row', swaps(row_count, 2, 2))  2.21 us
  transfers between devices with their start and end apart: 8, of which 6 were waited for; matrix products, arithmetic and copies ran while one was open for 0% of the time, Pallas kernels for 6%

profile of v3, /device:TPU:96, one launch (start us, length us, event | category | flops | bytes accessed | tf_op | source)
XLA Modules:
  0.0 49.1 jit_solution(2066881318408545758)
XLA Ops:
  0.6 0.1 stack.15.place_ref
  0.7 1.2 %copy-done.3 = f32[2,2,2,32,8,32]{5,4,3,2,1,0:T(8,128)S(1)} copy-done((f32[2,2,2,32,8,32]{5,4,3,2,1,0:T(8,128)S(1)}, f32[2,2,2,32,8,32]{5,4,3,2,1,0:T(8,128)}, u32[]{:S(2)}) %copy-start.3) | copy-done | bytes 262168
  2.0 0.0 copy-start.5
  2.0 0.0 copy-start.1
  2.0 0.8 %pack_vias.1 = (f32[2,32,8,128]{3,2,1,0:T(8,128)S(1)}, f32[33,8,128]{2,1,0:T(8,128)S(1)}) custom-call(s32[5]{0:T(128)S(1)} %stack.15.place_ref, f32[2,2,2,32,8,32]{5,4,3,2,1,0:T(8,128)S(1)} %copy-done.3), custom_call_target="tpu_custom_call" | custom-call | tf_op jit(solution)/shard_map/pack_vias/pallas_call | solution.py:612
  2.8 0.0 copy-start
  2.8 1.6 %collective-permute-start = (f32[33,8,128]{2,1,0:T(8,128)S(1)}, f32[33,8,128]{2,1,0:T(8,128)S(1)}, u32[]{:S(2)}, u32[]{:S(2)}) collective-permute-start(f32[33,8,128]{2,1,0:T(8,128)S(1)} %get-tuple-element.31.send_ref), channel_id=1, source_target_pairs={{0,128},{128,0},{1,129},{129,1},{2,130},{130,2},{3,131},{131,3},{4... | collective-permute-start | bytes 405512 | tf_op jit(solution)/shard_map/ppermute | solution.py:615
  4.4 0.6 %pack_base.1.far_ref = f32[32,128]{1,0:T(8,128)S(1)} custom-call(s32[1,4]{1,0:T(1,128)S(1)} %copy-done.9, f32[2,8,32]{2,1,0:T(8,128)S(1)} %copy-done.7, f32[2,8,32]{2,1,0:T(8,128)S(1)} %copy-done.8, f32[33,8,128]{2,1,0:T(8,128)S(1)} %get-tuple-element.31.send_ref), custom_call_target="tpu_custom_call" | custom-call | tf_op jit(solution)/shard_map/pack_base/pallas_call | solution.py:616
  5.0 5.2 %collective-permute-start.2 = (f32[32,128]{1,0:T(8,128)S(1)}, f32[32,128]{1,0:T(8,128)S(1)}, u32[]{:S(2)}, u32[]{:S(2)}) collective-permute-start(f32[32,128]{1,0:T(8,128)S(1)} %pack_base.1.far_ref), channel_id=1, source_target_pairs={{16,32},{32,16},{24,40},{40,24},{48,64},{64,48},{56,72},{72,56},{8... | collective-permute-start | bytes 49160 | tf_op jit(solution)/shard_map/ppermute | solution.py:620
  10.3 0.7 %spread_cells.1 = (f32[4,32,8,128]{3,2,1,0:T(8,128)S(1)}, f32[4,8,128]{2,1,0:T(8,128)S(1)}, f32[4,4,8,128]{3,2,1,0:T(8,128)S(1)}, bf16[256,1024]{1,0:T(8,128)(2,1)S(1)}, f32[4,64,128]{2,1,0:T(8,128)S(1)}) custom-call(s32[2,32,8,32]{3,2,1,0:T(8,128)S(1)} %copy-done.4, s32[2,8,32]{2,1,0:T(8,128)S(1)} %copy-done.6, f32[2,2,2,8,32]{4,3,2,1,0:T(8,128)S(1)} %copy-done.5), custom_call_target="tpu_custom_call" | custom-call | tf_op jit(solution)/shard_map/spread_cells/pallas_call | solution.py:622
  11.0 2.2 %collective-permute-done.2.next_ref = f32[32,128]{1,0:T(8,128)S(1)} collective-permute-done((f32[32,128]{1,0:T(8,128)S(1)}, f32[32,128]{1,0:T(8,128)S(1)}, u32[]{:S(2)}, u32[]{:S(2)}) %collective-permute-start.2) | collective-permute-done | bytes 16416 | tf_op jit(solution)/shard_map/ppermute | solution.py:620
  13.2 0.8 %collective-permute-done.1.near_ref = f32[32,128]{1,0:T(8,128)S(1)} collective-permute-done((f32[32,128]{1,0:T(8,128)S(1)}, f32[32,128]{1,0:T(8,128)S(1)}, u32[]{:S(2)}, u32[]{:S(2)}) %collective-permute-start.1) | collective-permute-done | bytes 16416 | tf_op jit(solution)/shard_map/ppermute | solution.py:619
  14.0 2.6 %place_vias.1 = (f32[4,4,64,128]{3,2,1,0:T(8,128)S(1)}, f32[448,128]{1,0:T(8,128)S(1)}, f32[448,128]{1,0:T(8,128)S(1)}, f32[32,128]{1,0:T(8,128)S(1)}, f32[16,128]{1,0:T(8,128)S(1)}) custom-call(s32[5]{0:T(128)S(1)} %stack.15.place_ref, f32[2,32,8,128]{3,2,1,0:T(8,128)S(1)} %get-tuple-element.30.packed_ref, f32[33,8,128]{2,1,0:T(8,128)S(1)} %get-tuple-element.31.send_ref, ...), custom_call_target="tpu_custom_call" | custom-call | tf_op jit(solution)/shard_map/place_vias/pallas_call | solution.py:629
  16.6 0.1 collective-permute-start.3
  16.7 3.7 %collective-permute-start.4 = (f32[448,128]{1,0:T(8,128)S(1)}, f32[448,128]{1,0:T(8,128)S(1)}, u32[]{:S(2)}, u32[]{:S(2)}) collective-permute-start(f32[448,128]{1,0:T(8,128)S(1)} %get-tuple-element.38), channel_id=1, source_target_pairs={{8,16},{16,8},{24,32},{32,24},{40,48},{48,40},{56,64},{64,56},{72,... | collective-permute-start | bytes 688136 | tf_op jit(solution)/shard_map/ppermute | solution.py:635
  20.5 0.2 collective-permute-start.5
  20.7 4.1 %collective-permute-done.5.far_ref = f32[16,128]{1,0:T(8,128)S(1)} collective-permute-done((f32[16,128]{1,0:T(8,128)S(1)}, f32[16,128]{1,0:T(8,128)S(1)}, u32[]{:S(2)}, u32[]{:S(2)}) %collective-permute-start.5) | collective-permute-done | bytes 8224 | tf_op jit(solution)/shard_map/ppermute | solution.py:636
  24.8 1.1 %collective-permute-done.4.odd_ref = f32[448,128]{1,0:T(8,128)S(1)} collective-permute-done((f32[448,128]{1,0:T(8,128)S(1)}, f32[448,128]{1,0:T(8,128)S(1)}, u32[]{:S(2)}, u32[]{:S(2)}) %collective-permute-start.4) | collective-permute-done | bytes 229408 | tf_op jit(solution)/shard_map/ppermute | solution.py:635
  25.9 1.1 %column_strips.1 = (f32[272,128]{1,0:T(8,128)S(1)}, f32[272,128]{1,0:T(8,128)S(1)}, f32[200,128]{1,0:T(8,128)S(1)}) custom-call(s32[5]{0:T(128)S(1)} %stack.15.place_ref, f32[2,2,64,256]{3,2,1,0:T(8,128)S(1)} %copy-done, f32[2,64,256]{2,1,0:T(8,128)S(1)} %copy-done.2, f32[2,2,64,256]{3,2,1,0:T(8,128)S(1)} %copy-done.1, ...), custom_call_target="tpu_custom_call" | custom-call | tf_op jit(solution)/shard_map/column_strips/pallas_call | solution.py:639
  27.0 3.2 %collective-permute-start.6 = (f32[272,128]{1,0:T(8,128)S(1)}, f32[272,128]{1,0:T(8,128)S(1)}, u32[]{:S(2)}, u32[]{:S(2)}) collective-permute-start(f32[272,128]{1,0:T(8,128)S(1)} %get-tuple-element.54), channel_id=1, source_target_pairs={{0,1},{1,2},{2,3},{3,4},{4,5},{5,6},{6,7},{7,0},{8,9},{9,10},{10,1... | collective-permute-start | bytes 417800 | tf_op jit(solution)/shard_map/ppermute | solution.py:643
  30.2 1.4 %assemble.1 = (f32[4,96,256]{2,1,0:T(8,128)S(1)}, f32[4,96,256]{2,1,0:T(8,128)S(1)}, f32[2,96,256]{2,1,0:T(8,128)S(1)}, f32[2,96,256]{2,1,0:T(8,128)S(1)}, f32[4...) custom-call(s32[5]{0:T(128)S(1)} %stack.15.place_ref, ...), custom_call_target="tpu_custom_call" | custom-call | tf_op jit(solution)/shard_map/assemble/pallas_call | solution.py:646
  31.6 1.2 %collective-permute-done.6.fromleft_ref = f32[272,128]{1,0:T(8,128)S(1)} collective-permute-done((f32[272,128]{1,0:T(8,128)S(1)}, f32[272,128]{1,0:T(8,128)S(1)}, u32[]{:S(2)}, u32[]{:S(2)}) %collective-permute-start.6) | collective-permute-done | bytes 139296 | tf_op jit(solution)/shard_map/ppermute | solution.py:643
  32.8 3.7 %collective-permute-done.7.fromright_ref = f32[272,128]{1,0:T(8,128)S(1)} collective-permute-done((f32[272,128]{1,0:T(8,128)S(1)}, f32[272,128]{1,0:T(8,128)S(1)}, u32[]{:S(2)}, u32[]{:S(2)}) %collective-permute-start.7) | collective-permute-done | bytes 139296 | tf_op jit(solution)/shard_map/ppermute | solution.py:642
  36.5 12.6 %solve.1 = (f32[2,2,64,256]{3,2,1,0:T(8,128)}, f32[2,8,32]{2,1,0:T(8,128)}) custom-call(s32[5]{0:T(128)S(1)} %stack.15.place_ref, f32[4,96,256]{2,1,0:T(8,128)S(1)} %get-tuple-element.39.s_ref, f32[4,96,256]{2,1,0:T(8,128)S(1)} %get-tuple-element.40.x_ref, f32[2,96,256]{2,1,0:T(8,128)S(1)} %get-tuple-element.41.c_ref, ...), custom_call_target="tpu_custom_call" | custom-call | tf_op jit(solution)/shard_map/solve/pallas_call | solution.py:653
  (20 shorter events, 0.0 us)
Async XLA Ops:
  0.7 1.2 %copy-start.3 = (f32[2,2,2,32,8,32]{5,4,3,2,1,0:T(8,128)S(1)}, f32[2,2,2,32,8,32]{5,4,3,2,1,0:T(8,128)}, u32[]{:S(2)}) copy-start(f32[2,2,2,32,8,32]{5,4,3,2,1,0:T(8,128)} %via_ref.1) | copy-start | bytes 786436
  1.9 2.5 %copy-start.7 = (f32[2,8,32]{2,1,0:T(8,128)S(1)}, f32[2,8,32]{2,1,0:T(8,128)}, u32[]{:S(2)}) copy-start(f32[2,8,32]{2,1,0:T(8,128)} %sheet_ref.4) | copy-start | bytes 6148
  1.9 2.5 %copy-start.8 = (f32[2,8,32]{2,1,0:T(8,128)S(1)}, f32[2,8,32]{2,1,0:T(8,128)}, u32[]{:S(2)}) copy-start(f32[2,8,32]{2,1,0:T(8,128)} %start_ref.1) | copy-start | bytes 6148
  2.0 2.5 %copy-start.9 = (s32[1,4]{1,0:T(1,128)S(1)}, s32[1,4]{1,0:T(1,128)}, u32[]{:S(2)}) copy-start(s32[1,4]{1,0:T(1,128)} %bump_ref.1) | copy-start | bytes 52
  2.0 8.3 %copy-start.4 = (s32[2,32,8,32]{3,2,1,0:T(8,128)S(1)}, s32[2,32,8,32]{3,2,1,0:T(8,128)}, u32[]{:S(2)}) copy-start(s32[2,32,8,32]{3,2,1,0:T(8,128)} %cell_ref.1) | copy-start | bytes 196612
  2.0 8.3 %copy-start.5 = (f32[2,2,2,8,32]{4,3,2,1,0:T(8,128)S(1)}, f32[2,2,2,8,32]{4,3,2,1,0:T(8,128)}, u32[]{:S(2)}) copy-start(f32[2,2,2,8,32]{4,3,2,1,0:T(8,128)} %load_ref.1) | copy-start | bytes 24580
  2.0 8.3 %copy-start.6 = (s32[2,8,32]{2,1,0:T(8,128)S(1)}, s32[2,8,32]{2,1,0:T(8,128)}, u32[]{:S(2)}) copy-start(s32[2,8,32]{2,1,0:T(8,128)} %load_cell_ref.1) | copy-start | bytes 6148
  2.0 12.0 %copy-start.1 = (f32[2,2,64,256]{3,2,1,0:T(8,128)S(1)}, f32[2,2,64,256]{3,2,1,0:T(8,128)}, u32[]{:S(2)}) copy-start(f32[2,2,64,256]{3,2,1,0:T(8,128)} %drop_ref.5) | copy-start | bytes 786436
  2.8 11.2 %copy-start = (f32[2,2,64,256]{3,2,1,0:T(8,128)S(1)}, f32[2,2,64,256]{3,2,1,0:T(8,128)}, u32[]{:S(2)}) copy-start(f32[2,2,64,256]{3,2,1,0:T(8,128)} %sheet_ref.7) | copy-start | bytes 786436
  2.8 11.2 %collective-permute-start = (f32[33,8,128]{2,1,0:T(8,128)S(1)}, f32[33,8,128]{2,1,0:T(8,128)S(1)}, u32[]{:S(2)}, u32[]{:S(2)}) collective-permute-start(f32[33,8,128]{2,1,0:T(8,128)S(1)} %get-tuple-element.31.send_ref), channel_id=1, source_target_pairs={{0,128},{128,0},{1,129},{129,1},{2,130},{130,2},{3,131},{131,3},{4... | collective-permute-start | bytes 405512 | tf_op jit(solution)/shard_map/ppermute | solution.py:615
  5.0 9.0 %copy-start.2 = (f32[2,64,256]{2,1,0:T(8,128)S(1)}, f32[2,64,256]{2,1,0:T(8,128)}, u32[]{:S(2)}) copy-start(f32[2,64,256]{2,1,0:T(8,128)} %cap_ref.5) | copy-start | bytes 393220
  5.0 8.2 %collective-permute-start.2 = (f32[32,128]{1,0:T(8,128)S(1)}, f32[32,128]{1,0:T(8,128)S(1)}, u32[]{:S(2)}, u32[]{:S(2)}) collective-permute-start(f32[32,128]{1,0:T(8,128)S(1)} %pack_base.1.far_ref), channel_id=1, source_target_pairs={{16,32},{32,16},{24,40},{40,24},{48,64},{64,48},{56,72},{72,56},{8... | collective-permute-start | bytes 49160 | tf_op jit(solution)/shard_map/ppermute | solution.py:620
  10.3 3.7 %collective-permute-start.1 = (f32[32,128]{1,0:T(8,128)S(1)}, f32[32,128]{1,0:T(8,128)S(1)}, u32[]{:S(2)}, u32[]{:S(2)}) collective-permute-start(f32[32,128]{1,0:T(8,128)S(1)} %pack_base.1.far_ref), channel_id=1, source_target_pairs={{0,16},{16,0},{8,24},{24,8},{32,48},{48,32},{40,56},{56,40},{64,80... | collective-permute-start | bytes 49160 | tf_op jit(solution)/shard_map/ppermute | solution.py:619
  16.6 8.1 %collective-permute-start.3 = (f32[448,128]{1,0:T(8,128)S(1)}, f32[448,128]{1,0:T(8,128)S(1)}, u32[]{:S(2)}, u32[]{:S(2)}) collective-permute-start(f32[448,128]{1,0:T(8,128)S(1)} %get-tuple-element.37), channel_id=1, source_target_pairs={{0,8},{8,0},{16,24},{24,16},{32,40},{40,32},{48,56},{56,48},{64,72... | collective-permute-start | bytes 688136 | tf_op jit(solution)/shard_map/ppermute | solution.py:634
  16.7 9.1 %collective-permute-start.4 = (f32[448,128]{1,0:T(8,128)S(1)}, f32[448,128]{1,0:T(8,128)S(1)}, u32[]{:S(2)}, u32[]{:S(2)}) collective-permute-start(f32[448,128]{1,0:T(8,128)S(1)} %get-tuple-element.38), channel_id=1, source_target_pairs={{8,16},{16,8},{24,32},{32,24},{40,48},{48,40},{56,64},{64,56},{72,... | collective-permute-start | bytes 688136 | tf_op jit(solution)/shard_map/ppermute | solution.py:635
  20.5 4.3 %collective-permute-start.5 = (f32[16,128]{1,0:T(8,128)S(1)}, f32[16,128]{1,0:T(8,128)S(1)}, u32[]{:S(2)}, u32[]{:S(2)}) collective-permute-start(f32[16,128]{1,0:T(8,128)S(1)} %get-tuple-element.52), channel_id=1, source_target_pairs={{0,128},{128,0},{1,129},{129,1},{2,130},{130,2},{3,131},{131,3},{4... | collective-permute-start | bytes 24584 | tf_op jit(solution)/shard_map/ppermute | solution.py:636
  27.0 5.8 %collective-permute-start.6 = (f32[272,128]{1,0:T(8,128)S(1)}, f32[272,128]{1,0:T(8,128)S(1)}, u32[]{:S(2)}, u32[]{:S(2)}) collective-permute-start(f32[272,128]{1,0:T(8,128)S(1)} %get-tuple-element.54), channel_id=1, source_target_pairs={{0,1},{1,2},{2,3},{3,4},{4,5},{5,6},{6,7},{7,0},{8,9},{9,10},{10,1... | collective-permute-start | bytes 417800 | tf_op jit(solution)/shard_map/ppermute | solution.py:643
  30.2 6.3 %collective-permute-start.7 = (f32[272,128]{1,0:T(8,128)S(1)}, f32[272,128]{1,0:T(8,128)S(1)}, u32[]{:S(2)}, u32[]{:S(2)}) collective-permute-start(f32[272,128]{1,0:T(8,128)S(1)} %get-tuple-element.55), channel_id=1, source_target_pairs={{0,7},{1,0},{2,1},{3,2},{4,3},{5,4},{6,5},{7,6},{8,15},{9,8},{10,9... | collective-permute-start | bytes 417800 | tf_op jit(solution)/shard_map/ppermute | solution.py:642

commit v4 on v3

--- a/solution.py
+++ b/solution.py
@@ -508,56 +508,61 @@
             for g in range(GROUPS):
                 c_ext[rows(g), :] = wide(c_ref, g, third(1, d, g), d)
                 k_ext[rows(g), :] = wide(k_ref, g, third(1, 2 + d, g), d)
-        sheets = [third(0, i, g) for g in range(GROUPS)]
-        for g in range(GROUPS):
-            here = sheets[g]
-            inside = here > 0.0
-            low, high = s_ref[i, rows(g), pl.ds(0, 128)], s_ref[i, rows(g), pl.ds(128, 128)]
-            after = jnp.where(lane == 127, roll(low, -1, 1), roll(here, -1, 1))
-            before = jnp.where(lane == 0, roll(high, 1, 1), roll(here, 1, 1))
-            right = jnp.where(inside, connect(here, after), 0.0)
-            left = jnp.where(inside, connect(here, before), 0.0)
-            down = jnp.where(inside, connect(here, below(here, sheets[(g + 1) % GROUPS], sub)), 0.0)
-            up = jnp.where(inside, connect(here, above(here, sheets[(g - 1) % GROUPS], sub)), 0.0)
-            first = jnp.where(lane == 0, roll(right, 1, 1), 0.0)
-            final = jnp.where(lane == 127, roll(left, -1, 1), 0.0)
-            diag = wide(diag_ref, g, 0.0 * here) + jnp.concatenate(
-                [first, final, c_ext[rows(g), pl.ds(256, 128)] + up + down + left + right
-                 + VIA_CONDUCT * k_ext[rows(g), pl.ds(256, 128)]], axis=1)
-            inverse = jnp.where(diag > 0.0, 1.0 / diag, 0.0)
-            inv_ext[rows(g), :] = inverse
-            zero = jnp.zeros_like(first)
-            link_up[rows(g), :] = inverse * wide(up_ref, g, up)
-            link_down[rows(g), :] = inverse * wide(down_ref, g, down)
-            link_left[rows(g), :] = inverse * (wide(left_ref, g, left) + jnp.concatenate([first, zero, zero], axis=1))
-            link_right[rows(g), :] = inverse * (wide(right_ref, g, right) + jnp.concatenate([zero, final, zero], axis=1))
-            drop = third(0, 4 + i, g)
-            state[rows(g), :] = wide(x_ref, g, drop)
-            one = third(1, 4 + i, g)
-            f_ext[0, rows(g), :] = wide(one_ref, g, c_ext[rows(g), pl.ds(256, 128)] * drop + one)
-            if g not in (9, 10):
-                two = jnp.where(lane < 64, roll(one, -11, 1), roll(one, 11, 1))
-                f_ext[1, rows(g), :] = wide(two_ref, g, two)
-
-        for t in range(STEPS):
-            for k in range(SWEEPS):
-                now, then = (alt, state) if k % 2 else (state, alt)
-                for g in needed(11 - 6 * t - k):
-                    value = now[rows(g), :]
-                    total = link_up[rows(g), :] * above(value, now[rows((g - 1) % GROUPS), :], sub3)
-                    total = total + link_down[rows(g), :] * below(value, now[rows((g + 1) % GROUPS), :], sub3)
-                    total = total + (
-                        link_left[rows(g), :] * roll(value, 1, 1) + link_right[rows(g), :] * roll(value, -1, 1))
-                    if k == 0:
-                        spread = jnp.broadcast_to(bound[2 * t + n, pl.ds(base_row(g), 1), :], (8, 384))
-                        source = f_ext[t, rows(g), :] + k_ext[rows(g), :] * spread
-                        if t:
-                            source = source + c_ext[rows(g), :] * value
-                        source = inv_ext[rows(g), :] * source
-                        src[rows(g), :] = source
-                    else:
-                        source = src[rows(g), :]
-                    then[rows(g), :] = advance(k, value, lambda: then[rows(g), :], total + source)
+        @pl.when(place_ref[3] >= 0)
+        def _():
+            sheets = [third(0, i, g) for g in range(GROUPS)]
+            for g in range(GROUPS):
+                here = sheets[g]
+                inside = here > 0.0
+                low, high = s_ref[i, rows(g), pl.ds(0, 128)], s_ref[i, rows(g), pl.ds(128, 128)]
+                after = roll(jnp.where(lane == 0, low, here), -1, 1)
+                before = roll(jnp.where(lane == 127, high, here), 1, 1)
+                right = jnp.where(inside, connect(here, after), 0.0)
+                left = jnp.where(inside, connect(here, before), 0.0)
+                down = jnp.where(inside, connect(here, below(here, sheets[(g + 1) % GROUPS], sub)), 0.0)
+                up = jnp.where(inside, connect(here, above(here, sheets[(g - 1) % GROUPS], sub)), 0.0)
+                first = jnp.where(lane == 0, roll(right, 1, 1), 0.0)
+                final = jnp.where(lane == 127, roll(left, -1, 1), 0.0)
+                diag = wide(diag_ref, g, 0.0 * here) + jnp.concatenate(
+                    [first, final, c_ext[rows(g), pl.ds(256, 128)] + up + down + left + right
+                     + VIA_CONDUCT * k_ext[rows(g), pl.ds(256, 128)]], axis=1)
+                inverse = jnp.where(diag > 0.0, 1.0 / diag, 0.0)
+                inv_ext[rows(g), :] = inverse
+                zero = jnp.zeros_like(first)
+                link_up[rows(g), :] = inverse * wide(up_ref, g, up)
+                link_down[rows(g), :] = inverse * wide(down_ref, g, down)
+                link_left[rows(g), :] = inverse * (wide(left_ref, g, left) + jnp.concatenate([first, zero, zero], axis=1))
+                link_right[rows(g), :] = inverse * (wide(right_ref, g, right) + jnp.concatenate([zero, final, zero], axis=1))
+                drop = third(0, 4 + i, g)
+                state[rows(g), :] = wide(x_ref, g, drop)
+                one = third(1, 4 + i, g)
+                f_ext[0, rows(g), :] = wide(one_ref, g, c_ext[rows(g), pl.ds(256, 128)] * drop + one)
+                if g not in (9, 10):
+                    two = jnp.where(lane < 64, roll(one, -11, 1), roll(one, 11, 1))
+                    f_ext[1, rows(g), :] = wide(two_ref, g, two)
+
+        @pl.when(place_ref[3] >= 0)
+        def _():
+            for t in range(STEPS):
+                for k in range(SWEEPS):
+                    now, then = (alt, state) if k % 2 else (state, alt)
+                    for g in needed(11 - 6 * t - k):
+                        value = now[rows(g), :]
+                        total = link_up[rows(g), :] * above(value, now[rows((g - 1) % GROUPS), :], sub3)
+                        total = total + link_down[rows(g), :] * below(value, now[rows((g + 1) % GROUPS), :], sub3)
+                        total = total + (
+                            link_left[rows(g), :] * roll(value, 1, 1) + link_right[rows(g), :] * roll(value, -1, 1))
+                        if k == 0:
+                            spread = jnp.broadcast_to(bound[2 * t + n, pl.ds(base_row(g), 1), :], (8, 384))
+                            source = f_ext[t, rows(g), :] + k_ext[rows(g), :] * spread
+                            if t:
+                                source = source + c_ext[rows(g), :] * value
+                            source = inv_ext[rows(g), :] * source
+                            src[rows(g), :] = source
+                        else:
+                            source = src[rows(g), :]
+                        then[rows(g), :] = advance(k, value, lambda: then[rows(g), :], total + source)
+
         for g in range(8):
             out_ref[d, n, rows(g), :] = state[rows(g), pl.ds(0, 256)]
 

time: 49.2 us -> 44.4 us (0.902)
  Pallas kernels: 19.8 us -> 15 us
    pallas_call x1, Pallas kernels: 12.6 us -> 7.79 us  [per_device(): call(solve_kernel, 'solve', (arr(2, 2, 64, 256), arr(2, 8, 32)), [smem()]...]
where the time goes in v4:
time: 44.4 us; the launch traced here: 44.3 us
  Pallas kernels  15 us (34%)
  starting transfers between devices  14.1 us (32%)
  waiting for transfers between devices  13 us (29%)
  local copies, waits for them, and re-layouts  1.35 us (3%)
  between operations  0.75 us (2%)
    pallas_call x1, Pallas kernels, per_device(): call(solve_kernel, 'solve', (arr(2, 2, 64, 256), arr(2, 8, 32)), [smem()]...  7.79 us
    ppermute x1, starting transfers between devices, per_device(): after = lax.ppermute(far, 'row', swaps(row_count, 2, 2))  5.24 us
    ppermute x1, waiting for transfers between devices, per_device(): shares = lax.ppermute(shares, 'die', others)  4.08 us
    ppermute x1, starting transfers between devices, per_device(): odd = lax.ppermute(odd, 'row', swaps(row_count, 1))  3.73 us
    ppermute x1, waiting for transfers between devices, per_device(): lax.ppermute(left, 'col', [(i, (i - 1) % col_count) for i in range(col_co...  3.67 us
    ppermute x1, starting transfers between devices, per_device(): lax.ppermute(right, 'col', [(i, (i + 1) % col_count) for i in range(col_c...  3.21 us
    pallas_call x1, Pallas kernels, per_device(): call(place_kernel, 'place_vias', (arr(4, 4, 64, 128), rows_shape, rows_sh...  2.61 us
    ppermute x1, waiting for transfers between devices, per_device(): after = lax.ppermute(far, 'row', swaps(row_count, 2, 2))  2.2 us
  transfers between devices with their start and end apart: 8, of which 6 were waited for; matrix products, arithmetic and copies ran while one was open for 0% of the time, Pallas kernels for 6%

profile of v4, /device:TPU:96, one launch (start us, length us, event | category | flops | bytes accessed | tf_op | source)
XLA Modules:
  0.0 44.3 jit_solution(14725571314614402791)
XLA Ops:
  0.6 0.1 stack.15.place_ref
  0.7 1.2 %copy-done.3 = f32[2,2,2,32,8,32]{5,4,3,2,1,0:T(8,128)S(1)} copy-done((f32[2,2,2,32,8,32]{5,4,3,2,1,0:T(8,128)S(1)}, f32[2,2,2,32,8,32]{5,4,3,2,1,0:T(8,128)}, u32[]{:S(2)}) %copy-start.3) | copy-done | bytes 262168
  2.0 0.0 copy-start.6
  2.0 0.0 copy-start.1
  2.0 0.8 %pack_vias.1 = (f32[2,32,8,128]{3,2,1,0:T(8,128)S(1)}, f32[33,8,128]{2,1,0:T(8,128)S(1)}) custom-call(s32[5]{0:T(128)S(1)} %stack.15.place_ref, f32[2,2,2,32,8,32]{5,4,3,2,1,0:T(8,128)S(1)} %copy-done.3), custom_call_target="tpu_custom_call" | custom-call | tf_op jit(solution)/shard_map/pack_vias/pallas_call | solution.py:617
  2.8 0.0 copy-start
  2.8 1.6 %collective-permute-start = (f32[33,8,128]{2,1,0:T(8,128)S(1)}, f32[33,8,128]{2,1,0:T(8,128)S(1)}, u32[]{:S(2)}, u32[]{:S(2)}) collective-permute-start(f32[33,8,128]{2,1,0:T(8,128)S(1)} %get-tuple-element.31.send_ref), channel_id=1, source_target_pairs={{0,128},{128,0},{1,129},{129,1},{2,130},{130,2},{3,131},{131,3},{4... | collective-permute-start | bytes 405512 | tf_op jit(solution)/shard_map/ppermute | solution.py:620
  4.4 0.6 %pack_base.1.far_ref = f32[32,128]{1,0:T(8,128)S(1)} custom-call(s32[1,4]{1,0:T(1,128)S(1)} %copy-done.9, f32[2,8,32]{2,1,0:T(8,128)S(1)} %copy-done.7, f32[2,8,32]{2,1,0:T(8,128)S(1)} %copy-done.8, f32[33,8,128]{2,1,0:T(8,128)S(1)} %get-tuple-element.31.send_ref), custom_call_target="tpu_custom_call" | custom-call | tf_op jit(solution)/shard_map/pack_base/pallas_call | solution.py:621
  5.0 5.2 %collective-permute-start.2 = (f32[32,128]{1,0:T(8,128)S(1)}, f32[32,128]{1,0:T(8,128)S(1)}, u32[]{:S(2)}, u32[]{:S(2)}) collective-permute-start(f32[32,128]{1,0:T(8,128)S(1)} %pack_base.1.far_ref), channel_id=1, source_target_pairs={{16,32},{32,16},{24,40},{40,24},{48,64},{64,48},{56,72},{72,56},{8... | collective-permute-start | bytes 49160 | tf_op jit(solution)/shard_map/ppermute | solution.py:625
  10.3 0.7 %spread_cells.1 = (f32[4,32,8,128]{3,2,1,0:T(8,128)S(1)}, f32[4,8,128]{2,1,0:T(8,128)S(1)}, f32[4,4,8,128]{3,2,1,0:T(8,128)S(1)}, bf16[256,1024]{1,0:T(8,128)(2,1)S(1)}, f32[4,64,128]{2,1,0:T(8,128)S(1)}) custom-call(s32[2,32,8,32]{3,2,1,0:T(8,128)S(1)} %copy-done.4, s32[2,8,32]{2,1,0:T(8,128)S(1)} %copy-done.6, f32[2,2,2,8,32]{4,3,2,1,0:T(8,128)S(1)} %copy-done.5), custom_call_target="tpu_custom_call" | custom-call | tf_op jit(solution)/shard_map/spread_cells/pallas_call | solution.py:627
  11.0 2.2 %collective-permute-done.2.next_ref = f32[32,128]{1,0:T(8,128)S(1)} collective-permute-done((f32[32,128]{1,0:T(8,128)S(1)}, f32[32,128]{1,0:T(8,128)S(1)}, u32[]{:S(2)}, u32[]{:S(2)}) %collective-permute-start.2) | collective-permute-done | bytes 16416 | tf_op jit(solution)/shard_map/ppermute | solution.py:625
  13.2 0.8 %collective-permute-done.1.near_ref = f32[32,128]{1,0:T(8,128)S(1)} collective-permute-done((f32[32,128]{1,0:T(8,128)S(1)}, f32[32,128]{1,0:T(8,128)S(1)}, u32[]{:S(2)}, u32[]{:S(2)}) %collective-permute-start.1) | collective-permute-done | bytes 16416 | tf_op jit(solution)/shard_map/ppermute | solution.py:624
  14.0 2.6 %place_vias.1 = (f32[4,4,64,128]{3,2,1,0:T(8,128)S(1)}, f32[448,128]{1,0:T(8,128)S(1)}, f32[448,128]{1,0:T(8,128)S(1)}, f32[32,128]{1,0:T(8,128)S(1)}, f32[16,128]{1,0:T(8,128)S(1)}) custom-call(s32[5]{0:T(128)S(1)} %stack.15.place_ref, f32[2,32,8,128]{3,2,1,0:T(8,128)S(1)} %get-tuple-element.30.packed_ref, f32[33,8,128]{2,1,0:T(8,128)S(1)} %get-tuple-element.31.send_ref, ...), custom_call_target="tpu_custom_call" | custom-call | tf_op jit(solution)/shard_map/place_vias/pallas_call | solution.py:634
  16.6 0.1 collective-permute-start.3
  16.7 3.7 %collective-permute-start.4 = (f32[448,128]{1,0:T(8,128)S(1)}, f32[448,128]{1,0:T(8,128)S(1)}, u32[]{:S(2)}, u32[]{:S(2)}) collective-permute-start(f32[448,128]{1,0:T(8,128)S(1)} %get-tuple-element.38), channel_id=1, source_target_pairs={{8,16},{16,8},{24,32},{32,24},{40,48},{48,40},{56,64},{64,56},{72,... | collective-permute-start | bytes 688136 | tf_op jit(solution)/shard_map/ppermute | solution.py:640
  20.5 0.2 collective-permute-start.5
  20.7 4.1 %collective-permute-done.5.far_ref = f32[16,128]{1,0:T(8,128)S(1)} collective-permute-done((f32[16,128]{1,0:T(8,128)S(1)}, f32[16,128]{1,0:T(8,128)S(1)}, u32[]{:S(2)}, u32[]{:S(2)}) %collective-permute-start.5) | collective-permute-done | bytes 8224 | tf_op jit(solution)/shard_map/ppermute | solution.py:641
  24.8 1.1 %collective-permute-done.4.odd_ref = f32[448,128]{1,0:T(8,128)S(1)} collective-permute-done((f32[448,128]{1,0:T(8,128)S(1)}, f32[448,128]{1,0:T(8,128)S(1)}, u32[]{:S(2)}, u32[]{:S(2)}) %collective-permute-start.4) | collective-permute-done | bytes 229408 | tf_op jit(solution)/shard_map/ppermute | solution.py:640
  25.9 1.1 %column_strips.1 = (f32[272,128]{1,0:T(8,128)S(1)}, f32[272,128]{1,0:T(8,128)S(1)}, f32[200,128]{1,0:T(8,128)S(1)}) custom-call(s32[5]{0:T(128)S(1)} %stack.15.place_ref, f32[2,2,64,256]{3,2,1,0:T(8,128)S(1)} %copy-done, f32[2,64,256]{2,1,0:T(8,128)S(1)} %copy-done.2, f32[2,2,64,256]{3,2,1,0:T(8,128)S(1)} %copy-done.1, ...), custom_call_target="tpu_custom_call" | custom-call | tf_op jit(solution)/shard_map/column_strips/pallas_call | solution.py:644
  27.0 3.2 %collective-permute-start.6 = (f32[272,128]{1,0:T(8,128)S(1)}, f32[272,128]{1,0:T(8,128)S(1)}, u32[]{:S(2)}, u32[]{:S(2)}) collective-permute-start(f32[272,128]{1,0:T(8,128)S(1)} %get-tuple-element.54), channel_id=1, source_target_pairs={{0,1},{1,2},{2,3},{3,4},{4,5},{5,6},{6,7},{7,0},{8,9},{9,10},{10,1... | collective-permute-start | bytes 417800 | tf_op jit(solution)/shard_map/ppermute | solution.py:648
  30.2 1.4 %assemble.1 = (f32[4,96,256]{2,1,0:T(8,128)S(1)}, f32[4,96,256]{2,1,0:T(8,128)S(1)}, f32[2,96,256]{2,1,0:T(8,128)S(1)}, f32[2,96,256]{2,1,0:T(8,128)S(1)}, f32[4...) custom-call(s32[5]{0:T(128)S(1)} %stack.15.place_ref, ...), custom_call_target="tpu_custom_call" | custom-call | tf_op jit(solution)/shard_map/assemble/pallas_call | solution.py:651
  31.6 1.2 %collective-permute-done.6.fromleft_ref = f32[272,128]{1,0:T(8,128)S(1)} collective-permute-done((f32[272,128]{1,0:T(8,128)S(1)}, f32[272,128]{1,0:T(8,128)S(1)}, u32[]{:S(2)}, u32[]{:S(2)}) %collective-permute-start.6) | collective-permute-done | bytes 139296 | tf_op jit(solution)/shard_map/ppermute | solution.py:648
  32.8 3.7 %collective-permute-done.7.fromright_ref = f32[272,128]{1,0:T(8,128)S(1)} collective-permute-done((f32[272,128]{1,0:T(8,128)S(1)}, f32[272,128]{1,0:T(8,128)S(1)}, u32[]{:S(2)}, u32[]{:S(2)}) %collective-permute-start.7) | collective-permute-done | bytes 139296 | tf_op jit(solution)/shard_map/ppermute | solution.py:647
  36.5 7.8 %solve.1 = (f32[2,2,64,256]{3,2,1,0:T(8,128)}, f32[2,8,32]{2,1,0:T(8,128)}) custom-call(s32[5]{0:T(128)S(1)} %stack.15.place_ref, f32[4,96,256]{2,1,0:T(8,128)S(1)} %get-tuple-element.39.s_ref, f32[4,96,256]{2,1,0:T(8,128)S(1)} %get-tuple-element.40.x_ref, f32[2,96,256]{2,1,0:T(8,128)S(1)} %get-tuple-element.41.c_ref, ...), custom_call_target="tpu_custom_call" | custom-call | tf_op jit(solution)/shard_map/solve/pallas_call | solution.py:658
  (20 shorter events, 0.0 us)
Async XLA Ops:
  0.7 1.2 %copy-start.3 = (f32[2,2,2,32,8,32]{5,4,3,2,1,0:T(8,128)S(1)}, f32[2,2,2,32,8,32]{5,4,3,2,1,0:T(8,128)}, u32[]{:S(2)}) copy-start(f32[2,2,2,32,8,32]{5,4,3,2,1,0:T(8,128)} %via_ref.1) | copy-start | bytes 786436
  1.9 2.5 %copy-start.7 = (f32[2,8,32]{2,1,0:T(8,128)S(1)}, f32[2,8,32]{2,1,0:T(8,128)}, u32[]{:S(2)}) copy-start(f32[2,8,32]{2,1,0:T(8,128)} %sheet_ref.4) | copy-start | bytes 6148
  1.9 2.5 %copy-start.8 = (f32[2,8,32]{2,1,0:T(8,128)S(1)}, f32[2,8,32]{2,1,0:T(8,128)}, u32[]{:S(2)}) copy-start(f32[2,8,32]{2,1,0:T(8,128)} %start_ref.1) | copy-start | bytes 6148
  2.0 2.5 %copy-start.9 = (s32[1,4]{1,0:T(1,128)S(1)}, s32[1,4]{1,0:T(1,128)}, u32[]{:S(2)}) copy-start(s32[1,4]{1,0:T(1,128)} %bump_ref.1) | copy-start | bytes 52
  2.0 8.3 %copy-start.4 = (s32[2,32,8,32]{3,2,1,0:T(8,128)S(1)}, s32[2,32,8,32]{3,2,1,0:T(8,128)}, u32[]{:S(2)}) copy-start(s32[2,32,8,32]{3,2,1,0:T(8,128)} %cell_ref.1) | copy-start | bytes 196612
  2.0 8.3 %copy-start.5 = (f32[2,2,2,8,32]{4,3,2,1,0:T(8,128)S(1)}, f32[2,2,2,8,32]{4,3,2,1,0:T(8,128)}, u32[]{:S(2)}) copy-start(f32[2,2,2,8,32]{4,3,2,1,0:T(8,128)} %load_ref.1) | copy-start | bytes 24580
  2.0 8.3 %copy-start.6 = (s32[2,8,32]{2,1,0:T(8,128)S(1)}, s32[2,8,32]{2,1,0:T(8,128)}, u32[]{:S(2)}) copy-start(s32[2,8,32]{2,1,0:T(8,128)} %load_cell_ref.1) | copy-start | bytes 6148
  2.0 12.0 %copy-start.1 = (f32[2,2,64,256]{3,2,1,0:T(8,128)S(1)}, f32[2,2,64,256]{3,2,1,0:T(8,128)}, u32[]{:S(2)}) copy-start(f32[2,2,64,256]{3,2,1,0:T(8,128)} %drop_ref.5) | copy-start | bytes 786436
  2.8 11.2 %copy-start = (f32[2,2,64,256]{3,2,1,0:T(8,128)S(1)}, f32[2,2,64,256]{3,2,1,0:T(8,128)}, u32[]{:S(2)}) copy-start(f32[2,2,64,256]{3,2,1,0:T(8,128)} %sheet_ref.7) | copy-start | bytes 786436
  2.8 11.2 %collective-permute-start = (f32[33,8,128]{2,1,0:T(8,128)S(1)}, f32[33,8,128]{2,1,0:T(8,128)S(1)}, u32[]{:S(2)}, u32[]{:S(2)}) collective-permute-start(f32[33,8,128]{2,1,0:T(8,128)S(1)} %get-tuple-element.31.send_ref), channel_id=1, source_target_pairs={{0,128},{128,0},{1,129},{129,1},{2,130},{130,2},{3,131},{131,3},{4... | collective-permute-start | bytes 405512 | tf_op jit(solution)/shard_map/ppermute | solution.py:620
  5.0 9.0 %copy-start.2 = (f32[2,64,256]{2,1,0:T(8,128)S(1)}, f32[2,64,256]{2,1,0:T(8,128)}, u32[]{:S(2)}) copy-start(f32[2,64,256]{2,1,0:T(8,128)} %cap_ref.5) | copy-start | bytes 393220
  5.0 8.2 %collective-permute-start.2 = (f32[32,128]{1,0:T(8,128)S(1)}, f32[32,128]{1,0:T(8,128)S(1)}, u32[]{:S(2)}, u32[]{:S(2)}) collective-permute-start(f32[32,128]{1,0:T(8,128)S(1)} %pack_base.1.far_ref), channel_id=1, source_target_pairs={{16,32},{32,16},{24,40},{40,24},{48,64},{64,48},{56,72},{72,56},{8... | collective-permute-start | bytes 49160 | tf_op jit(solution)/shard_map/ppermute | solution.py:625
  10.3 3.7 %collective-permute-start.1 = (f32[32,128]{1,0:T(8,128)S(1)}, f32[32,128]{1,0:T(8,128)S(1)}, u32[]{:S(2)}, u32[]{:S(2)}) collective-permute-start(f32[32,128]{1,0:T(8,128)S(1)} %pack_base.1.far_ref), channel_id=1, source_target_pairs={{0,16},{16,0},{8,24},{24,8},{32,48},{48,32},{40,56},{56,40},{64,80... | collective-permute-start | bytes 49160 | tf_op jit(solution)/shard_map/ppermute | solution.py:624
  16.6 8.1 %collective-permute-start.3 = (f32[448,128]{1,0:T(8,128)S(1)}, f32[448,128]{1,0:T(8,128)S(1)}, u32[]{:S(2)}, u32[]{:S(2)}) collective-permute-start(f32[448,128]{1,0:T(8,128)S(1)} %get-tuple-element.37), channel_id=1, source_target_pairs={{0,8},{8,0},{16,24},{24,16},{32,40},{40,32},{48,56},{56,48},{64,72... | collective-permute-start | bytes 688136 | tf_op jit(solution)/shard_map/ppermute | solution.py:639
  16.7 9.1 %collective-permute-start.4 = (f32[448,128]{1,0:T(8,128)S(1)}, f32[448,128]{1,0:T(8,128)S(1)}, u32[]{:S(2)}, u32[]{:S(2)}) collective-permute-start(f32[448,128]{1,0:T(8,128)S(1)} %get-tuple-element.38), channel_id=1, source_target_pairs={{8,16},{16,8},{24,32},{32,24},{40,48},{48,40},{56,64},{64,56},{72,... | collective-permute-start | bytes 688136 | tf_op jit(solution)/shard_map/ppermute | solution.py:640
  20.5 4.3 %collective-permute-start.5 = (f32[16,128]{1,0:T(8,128)S(1)}, f32[16,128]{1,0:T(8,128)S(1)}, u32[]{:S(2)}, u32[]{:S(2)}) collective-permute-start(f32[16,128]{1,0:T(8,128)S(1)} %get-tuple-element.52), channel_id=1, source_target_pairs={{0,128},{128,0},{1,129},{129,1},{2,130},{130,2},{3,131},{131,3},{4... | collective-permute-start | bytes 24584 | tf_op jit(solution)/shard_map/ppermute | solution.py:641
  27.0 5.8 %collective-permute-start.6 = (f32[272,128]{1,0:T(8,128)S(1)}, f32[272,128]{1,0:T(8,128)S(1)}, u32[]{:S(2)}, u32[]{:S(2)}) collective-permute-start(f32[272,128]{1,0:T(8,128)S(1)} %get-tuple-element.54), channel_id=1, source_target_pairs={{0,1},{1,2},{2,3},{3,4},{4,5},{5,6},{6,7},{7,0},{8,9},{9,10},{10,1... | collective-permute-start | bytes 417800 | tf_op jit(solution)/shard_map/ppermute | solution.py:648
  30.2 6.3 %collective-permute-start.7 = (f32[272,128]{1,0:T(8,128)S(1)}, f32[272,128]{1,0:T(8,128)S(1)}, u32[]{:S(2)}, u32[]{:S(2)}) collective-permute-start(f32[272,128]{1,0:T(8,128)S(1)} %get-tuple-element.55), channel_id=1, source_target_pairs={{0,7},{1,0},{2,1},{3,2},{4,3},{5,4},{6,5},{7,6},{8,15},{9,8},{10,9... | collective-permute-start | bytes 417800 | tf_op jit(solution)/shard_map/ppermute | solution.py:647

commit v5 on v4

--- a/solution.py
+++ b/solution.py
@@ -74,16 +74,70 @@
     return jnp.concatenate([gap, ref[0], gap, gap, ref[1], gap], axis=1)
 
 
-def base_kernel(bump_ref, sheet_ref, start_ref, send_ref, far_ref):
+def shared(first, second, shift):
+    return jnp.where(sub_iota() < shift, first, roll(second, shift, 0))
+
+
+def shared_low(first, second, shift):
+    return jnp.where(sub_iota() >= shift, first, roll(second, shift, 0))
+
+
+class RowSender:
+    def __init__(self, even, even_ref, odd_ref):
+        self.even, self.even_ref, self.odd_ref, self.place = even, even_ref, odd_ref, 0
+
+    def put(self, up, down):
+        self.even_ref[rows(self.place), :] = jnp.where(self.even, down, up)
+        self.odd_ref[rows(self.place), :] = jnp.where(self.even, up, down)
+        self.place += 1
+
+    def pair(self, first, second):
+        self.put(first(0), first(7))
+        self.put(second(0), second(7))
+        self.put(shared(first(1), second(1), 4), shared_low(first(6), second(6), 4))
+
+
+BASE = 4
+EARLY = 30
+LATE = 22
+
+
+def early_kernel(
+    place_ref, bump_ref, base_sheet_ref, base_start_ref, send_ref, sheet_ref, cap_ref, drop_ref, even_ref, odd_ref, base_ref
+):
     lane, sub = lane_iota(), sub_iota()
     bump = jnp.zeros((8, 128), F32)
     column = lane % 64 - 16
     for k in range(4):
         bump = jnp.where((column // 8 == k) & (sub * 8 + column % 8 == bump_ref[0, k]), 1.0, bump)
-    far_ref[rows(0), :] = spread_nets(sheet_ref)
-    far_ref[rows(1), :] = spread_nets(start_ref)
-    far_ref[rows(2), :] = bump
-    far_ref[rows(3), :] = send_ref[VIAS]
+    for part, value in enumerate([spread_nets(base_sheet_ref), spread_nets(base_start_ref), bump, send_ref[VIAS]]):
+        base_ref[rows(part), :] = value
+        even_ref[rows(EARLY + part), :] = value
+    sender = RowSender(place_ref[1] % 2 == 0, even_ref, odd_ref)
+    for d in range(2):
+        for half in range(2):
+            lanes = pl.ds(half * 128, 128)
+            for n in range(2):
+                sender.pair(lambda g: sheet_ref[d, n, rows(g), lanes], lambda g: drop_ref[d, n, rows(g), lanes])
+        sender.pair(lambda g: cap_ref[d, rows(g), pl.ds(0, 128)], lambda g: cap_ref[d, rows(g), pl.ds(128, 128)])
+
+
+def chip_kernel(place_ref, odd_ref, base_ref, got_ref, between_ref, far_ref):
+    even = place_ref[1] % 2 == 0
+    for g in range(EARLY):
+        between_ref[rows(g), :] = odd_ref[rows(g), :]
+    for part in range(BASE):
+        own, got = base_ref[rows(part), :], got_ref[rows(EARLY + part), :]
+        for slot, value in enumerate([jnp.where(even, own, got), jnp.where(even, got, own)]):
+            between_ref[rows(EARLY + BASE * slot + part), :] = value
+            far_ref[rows(BASE * slot + part), :] = value
+
+
+def shares_kernel(after_ref, first_ref, between_ref, far_ref, shares_ref):
+    shares_ref[rows(0), :] = first_ref[rows(EARLY + 3), :]
+    for slot in range(2):
+        shares_ref[rows(1 + slot), :] = between_ref[rows(EARLY + BASE * slot + 3), :]
+        shares_ref[rows(3 + slot), :] = far_ref[rows(BASE * slot + 3), :]
 
 
 def spread_matrix(height, width):
@@ -134,17 +188,9 @@
     lax.fori_loop(0, 4, count, 0)
 
 
-def shared(first, second, shift):
-    return jnp.where(sub_iota() < shift, first, roll(second, shift, 0))
-
-
-def shared_low(first, second, shift):
-    return jnp.where(sub_iota() >= shift, first, roll(second, shift, 0))
-
-
 def place_kernel(
-    place_ref, packed_ref, send_ref, got_ref, cells_ref, load_cells_ref, loads_ref, spread_ref, counts_ref, far_ref,
-    near_ref, next_ref, sheet_ref, cap_ref, drop_ref, field_ref, even_ref, odd_ref, base_ref, shares_ref, values_ref,
+    place_ref, packed_ref, send_ref, got_ref, cells_ref, load_cells_ref, loads_ref, spread_ref, counts_ref, _,
+    field_ref, even_ref, odd_ref, arriving_ref, values_ref,
 ):
     lane = lane_iota()
     later = place_ref[0].astype(F32)
@@ -183,83 +229,70 @@
 
     lax.fori_loop(0, 4, add, 0)
 
-    shares_ref[rows(0), :] = near_ref[rows(3), :]
-    shares_ref[rows(1), :] = next_ref[rows(3), :]
-
-    place = 0
-
-    def put(up, down):
-        nonlocal place
-        even_ref[rows(place), :] = jnp.where(even, down, up)
-        odd_ref[rows(place), :] = jnp.where(even, up, down)
-        place += 1
-
-    def pair(first, second):
-        put(first(0), first(7))
-        put(second(0), second(7))
-        put(shared(first(1), second(1), 4), shared_low(first(6), second(6), 4))
-
+    arriving_ref[...] = send_ref[VIAS] + got_ref[VIAS]
+    sender = RowSender(even, even_ref, odd_ref)
     for d in range(2):
         for half in range(2):
-            lanes = pl.ds(half * 128, 128)
             for n in range(2):
-                pair(lambda g: sheet_ref[d, n, rows(g), lanes], lambda g: drop_ref[d, n, rows(g), lanes])
                 one = lambda g: field_ref[n, 2 * d + half, rows(g), :]
                 two = lambda g: field_ref[2 + n, 2 * d + half, rows(g), :]
-                put(one(0), one(7))
-                put(shared(one(1), two(0), 3), shared_low(one(6), two(7), 5))
-            pair(lambda g: cap_ref[d, rows(g), lanes], lambda g: counts_ref[2 * d + half, rows(g), :])
-
-    parts = [far_ref[rows(0), :], far_ref[rows(1), :], far_ref[rows(2), :], send_ref[VIAS] + got_ref[VIAS]]
-    for part in range(4):
-        base_ref[rows(part), :] = parts[part]
-        put(parts[part], parts[part])
-
-
-BASE = 4
-ROW_GROUPS = 52 + BASE
-
-
-def row_place(d, half, n, kind):
-    start = (d * 2 + half) * 13
-    return start + 10 if kind == 2 else start + 5 * n + 3 * kind
-
-
-def near_rows(read, d, half, n, kind, second, upper):
-    start = row_place(d, half, n, kind)
-    if kind == 1:
-        if second:
-            return roll(read(start + 1), -5 if upper else -3, 0), None
-        return read(start), read(start + 1)
-    last = read(start + 2)
-    if second:
-        return read(start + 1), roll(last, -4, 0)
-    return read(start), last
-
-
-def column_groups(own, below, above, d, half, n, kind, second):
-    low = near_rows(below, d, half, n, kind, second, False)
-    high = near_rows(above, d, half, n, kind, second, True)
+                sender.put(one(0), one(7))
+                sender.put(shared(one(1), two(0), 3), shared_low(one(6), two(7), 5))
+        sender.pair(lambda g: counts_ref[2 * d, rows(g), :], lambda g: counts_ref[2 * d + 1, rows(g), :])
+
+
+SHEET, DROP, CAPACITY, COUNTS, FIRST, SECOND = range(6)
+
+
+def near_rows(read, kind, d, half, n, upper):
+    early, late = read
+    if kind in (FIRST, SECOND):
+        start = 11 * d + 4 * half + 2 * n
+        if kind == SECOND:
+            return roll(late(start + 1), -5 if upper else -3, 0), None
+        return late(start), late(start + 1)
+    if kind in (SHEET, DROP):
+        take, start, second = early, 15 * d + 6 * half + 3 * n, kind == DROP
+    elif kind == CAPACITY:
+        take, start, second = early, 15 * d + 12, half == 1
+    else:
+        take, start, second = late, 11 * d + 8, half == 1
+    last = take(start + 2)
+    return (take(start + 1), roll(last, -4, 0)) if second else (take(start), last)
+
+
+def column_groups(own, below, above, kind, d, half, n):
+    low = near_rows(below, kind, d, half, n, False)
+    high = near_rows(above, kind, d, half, n, True)
     return [own(g) for g in range(8)] + [low[0], low[1], high[1], high[0]]
 
 
+def readers(even, below, above, first_ref, between_ref, even_ref, odd_ref):
+    def make(inside, flag, a_ref, b_ref):
+        def read(g):
+            value = jnp.where(flag, a_ref[rows(g), :], b_ref[rows(g), :])
+            return value if inside is None else jnp.where(inside, value, 0.0)
+        return read
+
+    odd = jnp.logical_not(even)
+    return (
+        (make(below, even, first_ref, between_ref), make(below, even, even_ref, odd_ref)),
+        (make(above, odd, first_ref, between_ref), make(above, odd, even_ref, odd_ref)),
+    )
+
+
 COL_GROUPS = 2 * GROUPS + 10
 
 
 def strip_kernel(
-    place_ref, sheet_ref, cap_ref, drop_ref, counts_ref, field_ref, base_ref, even_ref, odd_ref, near_ref, next_ref, far_ref,
-    left_ref, right_ref, wide_ref,
+    place_ref, sheet_ref, cap_ref, drop_ref, counts_ref, field_ref, base_ref, arriving_ref, first_ref, between_ref, far_ref,
+    even_ref, odd_ref, shares_ref, left_ref, right_ref, wide_ref,
 ):
     lane = lane_iota()
     within = lane % 16
     row, last = place_ref[1], place_ref[3]
-    even, low = row % 2 == 0, row % 4 < 2
-
-    def below(g):
-        return jnp.where(even, even_ref[rows(g), :], odd_ref[rows(g), :])
-
-    def above(g):
-        return jnp.where(even, odd_ref[rows(g), :], even_ref[rows(g), :])
+    even = row % 2 == 0
+    below, above = readers(even, None, None, first_ref, between_ref, even_ref, odd_ref)
 
     own = (lane % 64 >= 16) & (lane % 64 < 48)
 
@@ -270,62 +303,67 @@
             out.append(jnp.where(own, moved, 0.0))
         return out
 
+    def block(ref, start, share):
+        parts = [ref[rows(start + f), :] for f in range(BASE)]
+        parts[3] = parts[3] + shares_ref[rows(share), :]
+        return parts
+
+    def choose(a, b, inside):
+        return [jnp.where(inside, jnp.where(even, x, y), 0.0) for x, y in zip(a, b)]
+
+    partner = block(first_ref, EARLY, 0)
+    between = [block(between_ref, EARLY + BASE * slot, 1 + slot) for slot in range(2)]
+    far = [block(far_ref, BASE * slot, 3 + slot) for slot in range(2)]
     groups = []
-    for g in range(5):
-        if g == 0:
-            parts = [base_ref[rows(f), :] for f in range(BASE)]
-        elif g in (1, 4):
-            read, inside = (below, row < last) if g == 1 else (above, row > 0)
-            parts = [jnp.where(inside, read(ROW_GROUPS - BASE + f), 0.0) for f in range(BASE)]
-        else:
-            inside = row + 2 <= last if g == 2 else row >= 2
-            flag = low if g == 2 else jnp.logical_not(low)
-            parts = [jnp.where(flag, near_ref[rows(f), :], next_ref[rows(f), :]) for f in range(BASE)]
-            parts[3] = parts[3] + jnp.where(flag, far_ref[rows(0), :], far_ref[rows(1), :])
-            parts = [jnp.where(inside, part, 0.0) for part in parts]
+    for g, parts in enumerate([
+        [base_ref[rows(f), :] for f in range(3)] + [arriving_ref[...]],
+        choose(partner, between[0], row < last),
+        choose(far[0], between[1], row + 2 <= last),
+        choose(between[0], far[1], row >= 2),
+        choose(between[1], partner, row > 0),
+    ]):
         one, two = spread_steps(parts[3])
         groups.append([parts[0], parts[1], one, two, parts[2]])
         for f in range(5):
             wide_ref[rows(5 * f + g), :] = groups[g][f]
 
-    def fields(half):
+    def fields(part, half):
         lanes = pl.ds(half * 128, 128)
-        first, second = [], []
-        for d in range(2):
-            for n in range(2):
-                first.append(column_groups(lambda g: sheet_ref[d, n, rows(g), lanes], below, above, d, half, n, 0, False))
-        for d in range(2):
-            for n in range(2):
-                first.append(column_groups(lambda g: drop_ref[d, n, rows(g), lanes], below, above, d, half, n, 0, True))
-        for d in range(2):
-            second.append(column_groups(lambda g: cap_ref[d, rows(g), lanes], below, above, d, half, 0, 2, False))
-        for d in range(2):
-            second.append(
-                column_groups(lambda g: counts_ref[2 * d + half, rows(g), :], below, above, d, half, 0, 2, True))
-        for d in range(2):
-            for n in range(2):
-                one = column_groups(
-                    lambda g: field_ref[n, 2 * d + half, rows(g), :], below, above, d, half, n, 1, False)
-                two = column_groups(
-                    lambda g: field_ref[2 + n, 2 * d + half, rows(g), :], below, above, d, half, n, 1, True)
-                merged = []
-                for a, b in zip(one, two):
-                    if b is None:
-                        merged.append(a)
-                    elif half == 0:
-                        merged.append(jnp.where(within < 11, a, roll(b, 11, 1)))
-                    else:
-                        merged.append(jnp.where(within >= 5, a, roll(b, -11, 1)))
-                second.append(merged)
-        return first, second
+        images = [(d, n) for d in range(2) for n in range(2)]
+        if part == 0:
+            return [
+                column_groups(lambda g: ref[d, n, rows(g), lanes], below, above, kind, d, half, n)
+                for kind, ref in ((SHEET, sheet_ref), (DROP, drop_ref)) for d, n in images
+            ]
+        out = [column_groups(lambda g: cap_ref[d, rows(g), lanes], below, above, CAPACITY, d, half, 0) for d in range(2)]
+        out += [
+            column_groups(lambda g: counts_ref[2 * d + half, rows(g), :], below, above, COUNTS, d, half, 0)
+            for d in range(2)
+        ]
+        for d, n in images:
+            one = column_groups(lambda g: field_ref[n, 2 * d + half, rows(g), :], below, above, FIRST, d, half, n)
+            two = column_groups(lambda g: field_ref[2 + n, 2 * d + half, rows(g), :], below, above, SECOND, d, half, n)
+            merged = []
+            for a, b in zip(one, two):
+                if b is None:
+                    merged.append(a)
+                elif half == 0:
+                    merged.append(jnp.where(within < 11, a, roll(b, 11, 1)))
+                else:
+                    merged.append(jnp.where(within >= 5, a, roll(b, -11, 1)))
+            out.append(merged)
+        return out
 
     for half, ref in ((0, left_ref), (1, right_ref)):
-        for part, chunks in enumerate(fields(half)):
-            for g in range(GROUPS):
-                out = chunks[0][g]
-                for k in range(1, 8):
-                    out = jnp.where((lane // 16 + half) % 8 == k, roll(chunks[k][g], 16 * k, 1), out)
-                ref[rows(part * GROUPS + g), :] = out
+        for part in range(2):
+            @pl.when(place_ref[3] >= 0)
+            def _():
+                chunks = fields(part, half)
+                for g in range(GROUPS):
+                    out = chunks[0][g]
+                    for k in range(1, 8):
+                        out = jnp.where((lane // 16 + half) % 8 == k, roll(chunks[k][g], 16 * k, 1), out)
+                    ref[rows(part * GROUPS + g), :] = out
 
     start = 2 * GROUPS
     quarter = (lane % 64) // 16
@@ -346,35 +384,29 @@
 
 
 def assemble_kernel(
-    place_ref, sheet_ref, cap_ref, drop_ref, counts_ref, field_ref, even_ref, odd_ref,
+    place_ref, sheet_ref, cap_ref, drop_ref, counts_ref, field_ref, first_ref, between_ref, even_ref, odd_ref,
     s_ref, x_ref, c_ref, k_ref, one_ref, two_ref, up_ref, down_ref, left_ref, right_ref, diag_ref, spread_ref,
 ):
     row, last = place_ref[1], place_ref[3]
-    even = row % 2 == 0
     sub, lane = sub_iota(256), lax.broadcasted_iota(jnp.int32, (8, 256), 1)
-
-    def below(g):
-        return jnp.where(row < last, jnp.where(even, even_ref[rows(g), :], odd_ref[rows(g), :]), 0.0)
-
-    def above(g):
-        return jnp.where(row > 0, jnp.where(even, odd_ref[rows(g), :], even_ref[rows(g), :]), 0.0)
-
-    def both(own, d, n, kind, second):
-        sides = [column_groups(lambda g: own(half, g), below, above, d, half, n, kind, second) for half in range(2)]
+    below, above = readers(row % 2 == 0, row < last, row > 0, first_ref, between_ref, even_ref, odd_ref)
+
+    def both(own, kind, d, n):
+        sides = [column_groups(lambda g: own(half, g), below, above, kind, d, half, n) for half in range(2)]
         return [None if a is None else jnp.concatenate([a, b], axis=1) for a, b in zip(*sides)]
 
     for d in range(2):
-        caps = both(lambda half, g: cap_ref[d, rows(g), pl.ds(half * 128, 128)], d, 0, 2, False)
-        counts = both(lambda half, g: counts_ref[2 * d + half, rows(g), :], d, 0, 2, True)
+        caps = both(lambda half, g: cap_ref[d, rows(g), pl.ds(half * 128, 128)], CAPACITY, d, 0)
+        counts = both(lambda half, g: counts_ref[2 * d + half, rows(g), :], COUNTS, d, 0)
         for g in range(GROUPS):
             c_ref[d, rows(g), :] = caps[g]
             k_ref[d, rows(g), :] = counts[g]
         for n in range(2):
             i = 2 * d + n
-            sheets = both(lambda half, g: sheet_ref[d, n, rows(g), pl.ds(half * 128, 128)], d, n, 0, False)
-            drops = both(lambda half, g: drop_ref[d, n, rows(g), pl.ds(half * 128, 128)], d, n, 0, True)
-            ones = both(lambda half, g: field_ref[n, 2 * d + half, rows(g), :], d, n, 1, False)
-            twos = both(lambda half, g: field_ref[2 + n, 2 * d + half, rows(g), :], d, n, 1, True)
+            sheets = both(lambda half, g: sheet_ref[d, n, rows(g), pl.ds(half * 128, 128)], SHEET, d, n)
+            drops = both(lambda half, g: drop_ref[d, n, rows(g), pl.ds(half * 128, 128)], DROP, d, n)
+            ones = both(lambda half, g: field_ref[n, 2 * d + half, rows(g), :], FIRST, d, n)
+            twos = both(lambda half, g: field_ref[2 + n, 2 * d + half, rows(g), :], SECOND, d, n)
             for g in range(GROUPS):
                 s_ref[i, rows(g), :] = sheets[g]
                 x_ref[i, rows(g), :] = drops[g]
@@ -618,40 +650,48 @@
         place, via_current
     )
     got = lax.ppermute(send, "die", others)
-    far = call(base_kernel, "pack_base", (arr(8 * BASE, 128),), [smem()] + spec(3))(
-        bump_cell, base_sheet, base_start, send
-    )[0]
-    near = lax.ppermute(far, "row", swaps(row_count, 0, 2))
-    after = lax.ppermute(far, "row", swaps(row_count, 2, 2))
-
+    def buffer(count):
+        return arr(8 * count, 128)
+
+    even, odd, base = call(
+        early_kernel, "pack_early", (buffer(EARLY + BASE), buffer(EARLY), buffer(BASE)), [smem(), smem()] + spec(6)
+    )(place, bump_cell, base_sheet, base_start, send, sheet_res, capacity, drop_start)
+    first = lax.ppermute(even, "row", swaps(row_count, 0))
     cells, load_cells, loads, spread, counts = call(
         prepare_kernel, "spread_cells",
         (arr(4, VIAS, 8, 128), arr(4, 8, 128), arr(4, 4, 8, 128), arr(256, 1024, dtype=jnp.bfloat16), arr(4, 64, 128)),
         spec(3),
     )(via_cell, load_cell, load_current)
-
-    rows_shape = arr(8 * ROW_GROUPS, 128)
-    field, even, odd, base, shares = call(
-        place_kernel, "place_vias", (arr(4, 4, 64, 128), rows_shape, rows_shape, arr(8 * BASE, 128), arr(16, 128)),
-        [smem()] + spec(14), [pltpu.VMEM((4, 4, VIAS, 8, 128), F32)],
-    )(place, packed, send, got, cells, load_cells, loads, spread, counts, far, near, after, sheet_res, capacity, drop_start)
+    between, far = call(chip_kernel, "pack_chip", (buffer(EARLY + 2 * BASE), buffer(2 * BASE)), [smem()] + spec(3))(
+        place, odd, base, first
+    )
+    far = lax.ppermute(
+        far, "row", [(i, (i + 3 if i % 2 == 0 else i - 3) % row_count) for i in range(row_count)]
+    )
+    between = lax.ppermute(between, "row", swaps(row_count, 1))
+
+    field, even, odd, arriving = call(
+        place_kernel, "place_vias", (arr(4, 4, 64, 128), buffer(LATE), buffer(LATE), buffer(1)),
+        [smem()] + spec(9), [pltpu.VMEM((4, 4, VIAS, 8, 128), F32)],
+    )(place, packed, send, got, cells, load_cells, loads, spread, counts, far)
 
     even = lax.ppermute(even, "row", swaps(row_count, 0))
     odd = lax.ppermute(odd, "row", swaps(row_count, 1))
+    shares = call(shares_kernel, "pack_shares", (buffer(5),), spec(4))(arriving, first, between, far)[0]
     shares = lax.ppermute(shares, "die", others)
 
     strip_shape = arr(8 * COL_GROUPS, 128)
     left, right, wide = call(
-        strip_kernel, "column_strips", (strip_shape, strip_shape, arr(200, 128)), [smem()] + spec(11)
-    )(place, sheet_res, capacity, drop_start, counts, field, base, even, odd, near, after, shares)
+        strip_kernel, "column_strips", (strip_shape, strip_shape, arr(200, 128)), [smem()] + spec(13)
+    )(place, sheet_res, capacity, drop_start, counts, field, base, arriving, first, between, far, even, odd, shares)
     from_right = lax.ppermute(left, "col", [(i, (i - 1) % col_count) for i in range(col_count)])
     from_left = lax.ppermute(right, "col", [(i, (i + 1) % col_count) for i in range(col_count)])
 
     image, pair = arr(4, 96, 256), arr(2, 96, 256)
     parts = call(
         assemble_kernel, "assemble",
-        (image, image, pair, pair) + (image,) * 7 + (arr(2, 256, 384, dtype=jnp.bfloat16),), [smem()] + spec(7),
-    )(place, sheet_res, capacity, drop_start, counts, field, even, odd)
+        (image, image, pair, pair) + (image,) * 7 + (arr(2, 256, 384, dtype=jnp.bfloat16),), [smem()] + spec(9),
+    )(place, sheet_res, capacity, drop_start, counts, field, first, between, even, odd)
 
     ext = pltpu.VMEM((96, 384), F32)
     scratch = [ext, ext, pltpu.VMEM((2, 96, 384), F32), pltpu.VMEM((4, 40, 384), F32)] + [ext] * 8

time: 44.4 us -> 45.3 us (1.020)
  waiting for transfers between devices: 13 us -> 11 us
  starting transfers between devices: 14.1 us -> 15.4 us
  Pallas kernels: 15 us -> 16 us
  local copies, waits for them, and re-layouts: 1.35 us -> 2.03 us
    ppermute x1, waiting for transfers between devices: 4.08 us -> 0.01 us  [per_device(): shares = lax.ppermute(shares, 'die', others)]
    ppermute x1, waiting for transfers between devices: 1.11 us -> 3.53 us  [per_device(): odd = lax.ppermute(odd, 'row', swaps(row_count, 1))]
    ppermute x1, starting transfers between devices: 0.09 us -> 1.47 us  [per_device(): even = lax.ppermute(even, 'row', swaps(row_count, 0))]
    unnamed x20, local copies, waits for them, and re-layouts: 1.27 us -> 1.94 us
    pallas_call x2 -> x4, Pallas kernels: 3.23 us -> 3.78 us  [the longest x1 2.61 us: per_device(): call(place_kernel, 'place_vias', (arr(4, 4, 64, 128), buffer(LATE), buffe...]
    ppermute x2 -> x3, waiting for transfers between devices: 2.98 us -> 2.57 us  [the longest x1 2.56 us: per_device(): lax.ppermute(far, 'row', [(i, (i + 3 if i % 2 == 0 else i - 3) % row_coun...]
    ppermute x2 -> x3, starting transfers between devices: 5.25 us -> 5.16 us  [the longest x1 5.08 us: per_device(): between = lax.ppermute(between, 'row', swaps(row_count, 1))]
  transfers between devices with their start and end apart: 8 -> 9, of which waited for: 6 -> 4; matrix products, arithmetic and copies ran while one was open for 0% -> 0% of each run, Pallas kernels for 6% -> 12%
where the time goes in v5:
time: 45.3 us; the launch traced here: 45.2 us
  Pallas kernels  16 us (35%)
  starting transfers between devices  15.4 us (34%)
  waiting for transfers between devices  11 us (24%)
  local copies, waits for them, and re-layouts  2.03 us (4%)
  between operations  0.74 us (2%)
    pallas_call x1, Pallas kernels, per_device(): call(solve_kernel, 'solve', (arr(2, 2, 64, 256), arr(2, 8, 32)), [smem()]...  7.79 us
    ppermute x1, starting transfers between devices, per_device(): between = lax.ppermute(between, 'row', swaps(row_count, 1))  5.08 us
    ppermute x1, waiting for transfers between devices, per_device(): lax.ppermute(left, 'col', [(i, (i - 1) % col_count) for i in range(col_co...  3.67 us
    ppermute x1, waiting for transfers between devices, per_device(): odd = lax.ppermute(odd, 'row', swaps(row_count, 1))  3.53 us
    ppermute x1, starting transfers between devices, per_device(): odd = lax.ppermute(odd, 'row', swaps(row_count, 1))  3.43 us
    ppermute x1, starting transfers between devices, per_device(): lax.ppermute(right, 'col', [(i, (i + 1) % col_count) for i in range(col_c...  3.2 us
    pallas_call x1, Pallas kernels, per_device(): call(place_kernel, 'place_vias', (arr(4, 4, 64, 128), buffer(LATE), buffe...  2.61 us
    ppermute x1, waiting for transfers between devices, per_device(): lax.ppermute(far, 'row', [(i, (i + 3 if i % 2 == 0 else i - 3) % row_coun...  2.56 us
  transfers between devices with their start and end apart: 9, of which 4 were waited for; matrix products, arithmetic and copies ran while one was open for 0% of the time, Pallas kernels for 12%

profile of v5, /device:TPU:96, one launch (start us, length us, event | category | flops | bytes accessed | tf_op | source)
XLA Modules:
  0.0 45.2 jit_solution(389200739918615019)
XLA Ops:
  0.6 0.1 stack.15.place_ref
  0.7 1.2 %copy-done.3 = f32[2,2,2,32,8,32]{5,4,3,2,1,0:T(8,128)S(1)} copy-done((f32[2,2,2,32,8,32]{5,4,3,2,1,0:T(8,128)S(1)}, f32[2,2,2,32,8,32]{5,4,3,2,1,0:T(8,128)}, u32[]{:S(2)}) %copy-start.3) | copy-done | bytes 262168
  2.0 0.8 %pack_vias.1 = (f32[2,32,8,128]{3,2,1,0:T(8,128)S(1)}, f32[33,8,128]{2,1,0:T(8,128)S(1)}) custom-call(s32[5]{0:T(128)S(1)} %stack.15.place_ref, f32[2,2,2,32,8,32]{5,4,3,2,1,0:T(8,128)S(1)} %copy-done.3), custom_call_target="tpu_custom_call" | custom-call | tf_op jit(solution)/shard_map/pack_vias/pallas_call | solution.py:649
  2.8 0.1 copy-done
  2.9 0.1 copy-done.1
  3.0 0.5 %copy-done.9 = s32[1,4]{1,0:T(1,128)S(1)} copy-done((s32[1,4]{1,0:T(1,128)S(1)}, s32[1,4]{1,0:T(1,128)}, u32[]{:S(2)}) %copy-start.9) | copy-done | bytes 40
  3.5 0.6 %pack_early.1 = (f32[272,128]{1,0:T(8,128)S(1)}, f32[240,128]{1,0:T(8,128)S(1)}, f32[32,128]{1,0:T(8,128)S(1)}) custom-call(s32[5]{0:T(128)S(1)} %stack.15.place_ref, s32[1,4]{1,0:T(1,128)S(1)} %copy-done.9, f32[2,8,32]{2,1,0:T(8,128)S(1)} %copy-done.6, f32[2,8,32]{2,1,0:T(8,128)S(1)} %copy-done.7, f32[33,8,128]{2,1,0:T(8,128)S(1)} %get-tuple-element.35.send_ref, ...), custom_call_target="tpu_custom_call" | custom-call | tf_op jit(solution)/shard_map/pack_early/pallas_call | solution.py:656
  4.1 0.1 collective-permute-start.1
  4.2 1.6 %collective-permute-start = (f32[33,8,128]{2,1,0:T(8,128)S(1)}, f32[33,8,128]{2,1,0:T(8,128)S(1)}, u32[]{:S(2)}, u32[]{:S(2)}) collective-permute-start(f32[33,8,128]{2,1,0:T(8,128)S(1)} %get-tuple-element.35.send_ref), channel_id=1, source_target_pairs={{0,128},{128,0},{1,129},{129,1},{2,130},{130,2},{3,131},{131,3},{4... | collective-permute-start | bytes 405512 | tf_op jit(solution)/shard_map/ppermute | solution.py:652
  5.8 0.6 %pack_chip.1 = (f32[304,128]{1,0:T(8,128)S(1)}, f32[64,128]{1,0:T(8,128)S(1)}) custom-call(s32[5]{0:T(128)S(1)} %stack.15.place_ref, f32[240,128]{1,0:T(8,128)S(1)} %get-tuple-element.40.odd_ref, f32[32,128]{1,0:T(8,128)S(1)} %get-tuple-element.41.base_ref, f32[272,128]{1,0:T(8,128)S(1)} %collective-permute-done.1.got_ref.first_ref), custom_call_target="tpu_custom_call" | custom-call | tf_op jit(solution)/shard_map/pack_chip/pallas_call | solution.py:665
  6.3 5.1 %collective-permute-start.3 = (f32[304,128]{1,0:T(8,128)S(1)}, f32[304,128]{1,0:T(8,128)S(1)}, u32[]{:S(2)}, u32[]{:S(2)}) collective-permute-start(f32[304,128]{1,0:T(8,128)S(1)} %get-tuple-element.45), channel_id=1, source_target_pairs={{8,16},{16,8},{24,32},{32,24},{40,48},{48,40},{56,64},{64,56},{72,... | collective-permute-start | bytes 466952 | tf_op jit(solution)/shard_map/ppermute | solution.py:671
  11.4 0.7 %spread_cells.1 = (f32[4,32,8,128]{3,2,1,0:T(8,128)S(1)}, f32[4,8,128]{2,1,0:T(8,128)S(1)}, f32[4,4,8,128]{3,2,1,0:T(8,128)S(1)}, bf16[256,1024]{1,0:T(8,128)(2,1)S(1)}, f32[4,64,128]{2,1,0:T(8,128)S(1)}) custom-call(s32[2,32,8,32]{3,2,1,0:T(8,128)S(1)} %copy-done.4, s32[2,8,32]{2,1,0:T(8,128)S(1)} %copy-done.8, f32[2,2,2,8,32]{4,3,2,1,0:T(8,128)S(1)} %copy-done.5), custom_call_target="tpu_custom_call" | custom-call | tf_op jit(solution)/shard_map/spread_cells/pallas_call | solution.py:660
  12.2 2.6 %collective-permute-done.2._.far_ref = f32[64,128]{1,0:T(8,128)S(1)} collective-permute-done((f32[64,128]{1,0:T(8,128)S(1)}, f32[64,128]{1,0:T(8,128)S(1)}, u32[]{:S(2)}, u32[]{:S(2)}) %collective-permute-start.2) | collective-permute-done | bytes 32800 | tf_op jit(solution)/shard_map/ppermute | solution.py:668
  14.8 2.6 %place_vias.1 = (f32[4,4,64,128]{3,2,1,0:T(8,128)S(1)}, f32[176,128]{1,0:T(8,128)S(1)}, f32[176,128]{1,0:T(8,128)S(1)}, f32[8,128]{1,0:T(8,128)S(1)}) custom-call(s32[5]{0:T(128)S(1)} %stack.15.place_ref, f32[2,32,8,128]{3,2,1,0:T(8,128)S(1)} %get-tuple-element.34.packed_ref, f32[33,8,128]{2,1,0:T(8,128)S(1)} %get-tuple-element.35.send_ref, ...), custom_call_target="tpu_custom_call" | custom-call | tf_op jit(solution)/shard_map/place_vias/pallas_call | solution.py:673
  17.4 1.5 %collective-permute-start.4 = (f32[176,128]{1,0:T(8,128)S(1)}, f32[176,128]{1,0:T(8,128)S(1)}, u32[]{:S(2)}, u32[]{:S(2)}) collective-permute-start(f32[176,128]{1,0:T(8,128)S(1)} %get-tuple-element.46), channel_id=1, source_target_pairs={{0,8},{8,0},{16,24},{24,16},{32,40},{40,32},{48,56},{56,48},{64,72... | collective-permute-start | bytes 270344 | tf_op jit(solution)/shard_map/ppermute | solution.py:678
  18.8 3.4 %collective-permute-start.5 = (f32[176,128]{1,0:T(8,128)S(1)}, f32[176,128]{1,0:T(8,128)S(1)}, u32[]{:S(2)}, u32[]{:S(2)}) collective-permute-start(f32[176,128]{1,0:T(8,128)S(1)} %get-tuple-element.47), channel_id=1, source_target_pairs={{8,16},{16,8},{24,32},{32,24},{40,48},{48,40},{56,64},{64,56},{72,... | collective-permute-start | bytes 270344 | tf_op jit(solution)/shard_map/ppermute | solution.py:679
  22.3 0.6 %collective-permute-start.6 = (f32[40,128]{1,0:T(8,128)S(1)}, f32[40,128]{1,0:T(8,128)S(1)}, u32[]{:S(2)}, u32[]{:S(2)}) collective-permute-start(f32[40,128]{1,0:T(8,128)S(1)} %pack_shares.1), channel_id=1, source_target_pairs={{0,128},{128,0},{1,129},{129,1},{2,130},{130,2},{3,131},{131,3},{4... | collective-permute-start | bytes 61448 | tf_op jit(solution)/shard_map/ppermute | solution.py:681
  22.9 3.5 %collective-permute-done.5.odd_ref = f32[176,128]{1,0:T(8,128)S(1)} collective-permute-done((f32[176,128]{1,0:T(8,128)S(1)}, f32[176,128]{1,0:T(8,128)S(1)}, u32[]{:S(2)}, u32[]{:S(2)}) %collective-permute-start.5) | collective-permute-done | bytes 90144 | tf_op jit(solution)/shard_map/ppermute | solution.py:679
  26.4 1.5 %column_strips.1 = (f32[272,128]{1,0:T(8,128)S(1)}, f32[272,128]{1,0:T(8,128)S(1)}, f32[200,128]{1,0:T(8,128)S(1)}) custom-call(s32[5]{0:T(128)S(1)} %stack.15.place_ref, f32[2,2,64,256]{3,2,1,0:T(8,128)S(1)} %copy-done, f32[2,64,256]{2,1,0:T(8,128)S(1)} %copy-done.2, f32[2,2,64,256]{3,2,1,0:T(8,128)S(1)} %copy-done.1, ...), custom_call_target="tpu_custom_call" | custom-call | tf_op jit(solution)/shard_map/column_strips/pallas_call | solution.py:684
  27.9 3.2 %collective-permute-start.7 = (f32[272,128]{1,0:T(8,128)S(1)}, f32[272,128]{1,0:T(8,128)S(1)}, u32[]{:S(2)}, u32[]{:S(2)}) collective-permute-start(f32[272,128]{1,0:T(8,128)S(1)} %get-tuple-element.62), channel_id=1, source_target_pairs={{0,1},{1,2},{2,3},{3,4},{4,5},{5,6},{6,7},{7,0},{8,9},{9,10},{10,1... | collective-permute-start | bytes 417800 | tf_op jit(solution)/shard_map/ppermute | solution.py:688
  31.1 1.4 %assemble.1 = (f32[4,96,256]{2,1,0:T(8,128)S(1)}, f32[4,96,256]{2,1,0:T(8,128)S(1)}, f32[2,96,256]{2,1,0:T(8,128)S(1)}, f32[2,96,256]{2,1,0:T(8,128)S(1)}, f32[4...) custom-call(s32[5]{0:T(128)S(1)} %stack.15.place_ref, ...), custom_call_target="tpu_custom_call" | custom-call | tf_op jit(solution)/shard_map/assemble/pallas_call | solution.py:691
  32.5 1.2 %collective-permute-done.7.fromleft_ref = f32[272,128]{1,0:T(8,128)S(1)} collective-permute-done((f32[272,128]{1,0:T(8,128)S(1)}, f32[272,128]{1,0:T(8,128)S(1)}, u32[]{:S(2)}, u32[]{:S(2)}) %collective-permute-start.7) | collective-permute-done | bytes 139296 | tf_op jit(solution)/shard_map/ppermute | solution.py:688
  33.7 3.7 %collective-permute-done.8.fromright_ref = f32[272,128]{1,0:T(8,128)S(1)} collective-permute-done((f32[272,128]{1,0:T(8,128)S(1)}, f32[272,128]{1,0:T(8,128)S(1)}, u32[]{:S(2)}, u32[]{:S(2)}) %collective-permute-start.8) | collective-permute-done | bytes 139296 | tf_op jit(solution)/shard_map/ppermute | solution.py:687
  37.4 7.8 %solve.1 = (f32[2,2,64,256]{3,2,1,0:T(8,128)}, f32[2,8,32]{2,1,0:T(8,128)}) custom-call(s32[5]{0:T(128)S(1)} %stack.15.place_ref, f32[4,96,256]{2,1,0:T(8,128)S(1)} %get-tuple-element.48.s_ref, f32[4,96,256]{2,1,0:T(8,128)S(1)} %get-tuple-element.49.x_ref, f32[2,96,256]{2,1,0:T(8,128)S(1)} %get-tuple-element.50.c_ref, ...), custom_call_target="tpu_custom_call" | custom-call | tf_op jit(solution)/shard_map/solve/pallas_call | solution.py:698
  (24 shorter events, 0.1 us)
Async XLA Ops:
  0.7 1.2 %copy-start.3 = (f32[2,2,2,32,8,32]{5,4,3,2,1,0:T(8,128)S(1)}, f32[2,2,2,32,8,32]{5,4,3,2,1,0:T(8,128)}, u32[]{:S(2)}) copy-start(f32[2,2,2,32,8,32]{5,4,3,2,1,0:T(8,128)} %via_ref.1) | copy-start | bytes 786436
  1.9 0.9 %copy-start = (f32[2,2,64,256]{3,2,1,0:T(8,128)S(1)}, f32[2,2,64,256]{3,2,1,0:T(8,128)}, u32[]{:S(2)}) copy-start(f32[2,2,64,256]{3,2,1,0:T(8,128)} %sheet_ref.5) | copy-start | bytes 786436
  1.9 1.0 %copy-start.1 = (f32[2,2,64,256]{3,2,1,0:T(8,128)S(1)}, f32[2,2,64,256]{3,2,1,0:T(8,128)}, u32[]{:S(2)}) copy-start(f32[2,2,64,256]{3,2,1,0:T(8,128)} %drop_ref.5) | copy-start | bytes 786436
  2.0 1.1 %copy-start.2 = (f32[2,64,256]{2,1,0:T(8,128)S(1)}, f32[2,64,256]{2,1,0:T(8,128)}, u32[]{:S(2)}) copy-start(f32[2,64,256]{2,1,0:T(8,128)} %cap_ref.5) | copy-start | bytes 393220
  2.0 1.1 %copy-start.6 = (f32[2,8,32]{2,1,0:T(8,128)S(1)}, f32[2,8,32]{2,1,0:T(8,128)}, u32[]{:S(2)}) copy-start(f32[2,8,32]{2,1,0:T(8,128)} %base_sheet_ref.1) | copy-start | bytes 6148
  2.0 1.1 %copy-start.7 = (f32[2,8,32]{2,1,0:T(8,128)S(1)}, f32[2,8,32]{2,1,0:T(8,128)}, u32[]{:S(2)}) copy-start(f32[2,8,32]{2,1,0:T(8,128)} %base_start_ref.1) | copy-start | bytes 6148
  2.8 0.7 %copy-start.9 = (s32[1,4]{1,0:T(1,128)S(1)}, s32[1,4]{1,0:T(1,128)}, u32[]{:S(2)}) copy-start(s32[1,4]{1,0:T(1,128)} %bump_ref.1) | copy-start | bytes 52
  3.5 7.9 %copy-start.5 = (f32[2,2,2,8,32]{4,3,2,1,0:T(8,128)S(1)}, f32[2,2,2,8,32]{4,3,2,1,0:T(8,128)}, u32[]{:S(2)}) copy-start(f32[2,2,2,8,32]{4,3,2,1,0:T(8,128)} %load_ref.1) | copy-start | bytes 24580
  4.1 7.3 %copy-start.4 = (s32[2,32,8,32]{3,2,1,0:T(8,128)S(1)}, s32[2,32,8,32]{3,2,1,0:T(8,128)}, u32[]{:S(2)}) copy-start(s32[2,32,8,32]{3,2,1,0:T(8,128)} %cell_ref.1) | copy-start | bytes 196612
  4.1 1.7 %collective-permute-start.1 = (f32[272,128]{1,0:T(8,128)S(1)}, f32[272,128]{1,0:T(8,128)S(1)}, u32[]{:S(2)}, u32[]{:S(2)}) collective-permute-start(f32[272,128]{1,0:T(8,128)S(1)} %get-tuple-element.42), channel_id=1, source_target_pairs={{0,8},{8,0},{16,24},{24,16},{32,40},{40,32},{48,56},{56,48},{64,72... | collective-permute-start | bytes 417800 | tf_op jit(solution)/shard_map/ppermute | solution.py:659
  4.2 8.0 %collective-permute-start = (f32[33,8,128]{2,1,0:T(8,128)S(1)}, f32[33,8,128]{2,1,0:T(8,128)S(1)}, u32[]{:S(2)}, u32[]{:S(2)}) collective-permute-start(f32[33,8,128]{2,1,0:T(8,128)S(1)} %get-tuple-element.35.send_ref), channel_id=1, source_target_pairs={{0,128},{128,0},{1,129},{129,1},{2,130},{130,2},{3,131},{131,3},{4... | collective-permute-start | bytes 405512 | tf_op jit(solution)/shard_map/ppermute | solution.py:652
  5.8 5.7 %copy-start.8 = (s32[2,8,32]{2,1,0:T(8,128)S(1)}, s32[2,8,32]{2,1,0:T(8,128)}, u32[]{:S(2)}) copy-start(s32[2,8,32]{2,1,0:T(8,128)} %load_cell_ref.1) | copy-start | bytes 6148
  6.3 15.9 %collective-permute-start.3 = (f32[304,128]{1,0:T(8,128)S(1)}, f32[304,128]{1,0:T(8,128)S(1)}, u32[]{:S(2)}, u32[]{:S(2)}) collective-permute-start(f32[304,128]{1,0:T(8,128)S(1)} %get-tuple-element.45), channel_id=1, source_target_pairs={{8,16},{16,8},{24,32},{32,24},{40,48},{48,40},{56,64},{64,56},{72,... | collective-permute-start | bytes 466952 | tf_op jit(solution)/shard_map/ppermute | solution.py:671
  11.4 3.3 %collective-permute-start.2 = (f32[64,128]{1,0:T(8,128)S(1)}, f32[64,128]{1,0:T(8,128)S(1)}, u32[]{:S(2)}, u32[]{:S(2)}) collective-permute-start(f32[64,128]{1,0:T(8,128)S(1)} %get-tuple-element.43), channel_id=1, source_target_pairs={{0,24},{8,112},{16,40},{24,0},{32,56},{40,16},{48,72},{56,32},{64,... | collective-permute-start | bytes 98312 | tf_op jit(solution)/shard_map/ppermute | solution.py:668
  17.4 5.5 %collective-permute-start.4 = (f32[176,128]{1,0:T(8,128)S(1)}, f32[176,128]{1,0:T(8,128)S(1)}, u32[]{:S(2)}, u32[]{:S(2)}) collective-permute-start(f32[176,128]{1,0:T(8,128)S(1)} %get-tuple-element.46), channel_id=1, source_target_pairs={{0,8},{8,0},{16,24},{24,16},{32,40},{40,32},{48,56},{56,48},{64,72... | collective-permute-start | bytes 270344 | tf_op jit(solution)/shard_map/ppermute | solution.py:678
  18.8 7.6 %collective-permute-start.5 = (f32[176,128]{1,0:T(8,128)S(1)}, f32[176,128]{1,0:T(8,128)S(1)}, u32[]{:S(2)}, u32[]{:S(2)}) collective-permute-start(f32[176,128]{1,0:T(8,128)S(1)} %get-tuple-element.47), channel_id=1, source_target_pairs={{8,16},{16,8},{24,32},{32,24},{40,48},{48,40},{56,64},{64,56},{72,... | collective-permute-start | bytes 270344 | tf_op jit(solution)/shard_map/ppermute | solution.py:679
  22.3 4.1 %collective-permute-start.6 = (f32[40,128]{1,0:T(8,128)S(1)}, f32[40,128]{1,0:T(8,128)S(1)}, u32[]{:S(2)}, u32[]{:S(2)}) collective-permute-start(f32[40,128]{1,0:T(8,128)S(1)} %pack_shares.1), channel_id=1, source_target_pairs={{0,128},{128,0},{1,129},{129,1},{2,130},{130,2},{3,131},{131,3},{4... | collective-permute-start | bytes 61448 | tf_op jit(solution)/shard_map/ppermute | solution.py:681
  27.9 5.8 %collective-permute-start.7 = (f32[272,128]{1,0:T(8,128)S(1)}, f32[272,128]{1,0:T(8,128)S(1)}, u32[]{:S(2)}, u32[]{:S(2)}) collective-permute-start(f32[272,128]{1,0:T(8,128)S(1)} %get-tuple-element.62), channel_id=1, source_target_pairs={{0,1},{1,2},{2,3},{3,4},{4,5},{5,6},{6,7},{7,0},{8,9},{9,10},{10,1... | collective-permute-start | bytes 417800 | tf_op jit(solution)/shard_map/ppermute | solution.py:688
  31.1 6.3 %collective-permute-start.8 = (f32[272,128]{1,0:T(8,128)S(1)}, f32[272,128]{1,0:T(8,128)S(1)}, u32[]{:S(2)}, u32[]{:S(2)}) collective-permute-start(f32[272,128]{1,0:T(8,128)S(1)} %get-tuple-element.63), channel_id=1, source_target_pairs={{0,7},{1,0},{2,1},{3,2},{4,3},{5,4},{6,5},{7,6},{8,15},{9,8},{10,9... | collective-permute-start | bytes 417800 | tf_op jit(solution)/shard_map/ppermute | solution.py:687

commit v6 on v5

--- a/solution.py
+++ b/solution.py
@@ -102,42 +102,43 @@
 LATE = 22
 
 
-def early_kernel(
-    place_ref, bump_ref, base_sheet_ref, base_start_ref, send_ref, sheet_ref, cap_ref, drop_ref, even_ref, odd_ref, base_ref
-):
+def base_kernel(bump_ref, sheet_ref, start_ref, send_ref, base_ref):
     lane, sub = lane_iota(), sub_iota()
     bump = jnp.zeros((8, 128), F32)
     column = lane % 64 - 16
     for k in range(4):
         bump = jnp.where((column // 8 == k) & (sub * 8 + column % 8 == bump_ref[0, k]), 1.0, bump)
-    for part, value in enumerate([spread_nets(base_sheet_ref), spread_nets(base_start_ref), bump, send_ref[VIAS]]):
+    for part, value in enumerate([spread_nets(sheet_ref), spread_nets(start_ref), bump, send_ref[VIAS]]):
         base_ref[rows(part), :] = value
-        even_ref[rows(EARLY + part), :] = value
-    sender = RowSender(place_ref[1] % 2 == 0, even_ref, odd_ref)
+
+
+def chip_kernel(place_ref, base_ref, got_ref, sheet_ref, cap_ref, drop_ref, within_ref, between_ref):
+    even = place_ref[1] % 2 == 0
+    sender = RowSender(even, within_ref, between_ref)
     for d in range(2):
         for half in range(2):
             lanes = pl.ds(half * 128, 128)
             for n in range(2):
                 sender.pair(lambda g: sheet_ref[d, n, rows(g), lanes], lambda g: drop_ref[d, n, rows(g), lanes])
         sender.pair(lambda g: cap_ref[d, rows(g), pl.ds(0, 128)], lambda g: cap_ref[d, rows(g), pl.ds(128, 128)])
-
-
-def chip_kernel(place_ref, odd_ref, base_ref, got_ref, between_ref, far_ref):
-    even = place_ref[1] % 2 == 0
-    for g in range(EARLY):
-        between_ref[rows(g), :] = odd_ref[rows(g), :]
     for part in range(BASE):
-        own, got = base_ref[rows(part), :], got_ref[rows(EARLY + part), :]
+        own, got = base_ref[rows(part), :], got_ref[rows(part), :]
         for slot, value in enumerate([jnp.where(even, own, got), jnp.where(even, got, own)]):
             between_ref[rows(EARLY + BASE * slot + part), :] = value
-            far_ref[rows(BASE * slot + part), :] = value
-
-
-def shares_kernel(after_ref, first_ref, between_ref, far_ref, shares_ref):
-    shares_ref[rows(0), :] = first_ref[rows(EARLY + 3), :]
+
+
+def relay_kernel(place_ref, between_ref, relay_ref):
+    even = place_ref[1] % 2 == 0
+    for part in range(BASE):
+        a, b = between_ref[rows(EARLY + part), :], between_ref[rows(EARLY + BASE + part), :]
+        relay_ref[rows(part), :] = jnp.where(even, b, a)
+
+
+def shares_kernel(first_ref, between_ref, relayed_ref, shares_ref):
+    shares_ref[rows(0), :] = first_ref[rows(3), :]
     for slot in range(2):
         shares_ref[rows(1 + slot), :] = between_ref[rows(EARLY + BASE * slot + 3), :]
-        shares_ref[rows(3 + slot), :] = far_ref[rows(BASE * slot + 3), :]
+    shares_ref[rows(3), :] = relayed_ref[rows(3), :]
 
 
 def spread_matrix(height, width):
@@ -189,7 +190,7 @@
 
 
 def place_kernel(
-    place_ref, packed_ref, send_ref, got_ref, cells_ref, load_cells_ref, loads_ref, spread_ref, counts_ref, _,
+    place_ref, packed_ref, send_ref, got_ref, cells_ref, load_cells_ref, loads_ref, spread_ref, counts_ref, early_ref,
     field_ref, even_ref, odd_ref, arriving_ref, values_ref,
 ):
     lane = lane_iota()
@@ -230,6 +231,8 @@
     lax.fori_loop(0, 4, add, 0)
 
     arriving_ref[...] = send_ref[VIAS] + got_ref[VIAS]
+    for g in range(EARLY):
+        even_ref[rows(LATE + g), :] = early_ref[rows(g), :]
     sender = RowSender(even, even_ref, odd_ref)
     for d in range(2):
         for half in range(2):
@@ -267,17 +270,16 @@
     return [own(g) for g in range(8)] + [low[0], low[1], high[1], high[0]]
 
 
-def readers(even, below, above, first_ref, between_ref, even_ref, odd_ref):
-    def make(inside, flag, a_ref, b_ref):
+def readers(even, below, above, within_ref, between_ref, late_ref):
+    def make(inside, near, skip, far_ref):
         def read(g):
-            value = jnp.where(flag, a_ref[rows(g), :], b_ref[rows(g), :])
+            value = jnp.where(near, within_ref[rows(skip + g), :], far_ref[rows(g), :])
             return value if inside is None else jnp.where(inside, value, 0.0)
         return read
 
     odd = jnp.logical_not(even)
-    return (
-        (make(below, even, first_ref, between_ref), make(below, even, even_ref, odd_ref)),
-        (make(above, odd, first_ref, between_ref), make(above, odd, even_ref, odd_ref)),
+    return tuple(
+        (make(inside, near, LATE, between_ref), make(inside, near, 0, late_ref)) for inside, near in ((below, even), (above, odd))
     )
 
 
@@ -285,14 +287,15 @@
 
 
 def strip_kernel(
-    place_ref, sheet_ref, cap_ref, drop_ref, counts_ref, field_ref, base_ref, arriving_ref, first_ref, between_ref, far_ref,
-    even_ref, odd_ref, shares_ref, left_ref, right_ref, wide_ref,
+    place_ref, sheet_ref, cap_ref, drop_ref, counts_ref, field_ref, base_ref, arriving_ref, first_ref, between_ref,
+    within_ref, late_ref, relayed_ref, shares_ref, even_ref, odd_ref, wide_ref,
 ):
     lane = lane_iota()
     within = lane % 16
     row, last = place_ref[1], place_ref[3]
     even = row % 2 == 0
-    below, above = readers(even, None, None, first_ref, between_ref, even_ref, odd_ref)
+    below, above = readers(even, None, None, within_ref, between_ref, late_ref)
+    even_col = place_ref[2] % 2 == 0
 
     own = (lane % 64 >= 16) & (lane % 64 < 48)
 
@@ -311,15 +314,15 @@
     def choose(a, b, inside):
         return [jnp.where(inside, jnp.where(even, x, y), 0.0) for x, y in zip(a, b)]
 
-    partner = block(first_ref, EARLY, 0)
+    partner = block(first_ref, 0, 0)
     between = [block(between_ref, EARLY + BASE * slot, 1 + slot) for slot in range(2)]
-    far = [block(far_ref, BASE * slot, 3 + slot) for slot in range(2)]
+    relayed = block(relayed_ref, 0, 3)
     groups = []
     for g, parts in enumerate([
         [base_ref[rows(f), :] for f in range(3)] + [arriving_ref[...]],
         choose(partner, between[0], row < last),
-        choose(far[0], between[1], row + 2 <= last),
-        choose(between[0], far[1], row >= 2),
+        choose(relayed, between[1], row + 2 <= last),
+        choose(between[0], relayed, row >= 2),
         choose(between[1], partner, row > 0),
     ]):
         one, two = spread_steps(parts[3])
@@ -354,16 +357,20 @@
             out.append(merged)
         return out
 
-    for half, ref in ((0, left_ref), (1, right_ref)):
-        for part in range(2):
-            @pl.when(place_ref[3] >= 0)
-            def _():
-                chunks = fields(part, half)
-                for g in range(GROUPS):
-                    out = chunks[0][g]
-                    for k in range(1, 8):
-                        out = jnp.where((lane // 16 + half) % 8 == k, roll(chunks[k][g], 16 * k, 1), out)
-                    ref[rows(part * GROUPS + g), :] = out
+    def put(place, left, right):
+        even_ref[rows(place), :] = jnp.where(even_col, right, left)
+        odd_ref[rows(place), :] = jnp.where(even_col, left, right)
+
+    for part in range(2):
+        sides = [fields(part, half) for half in range(2)]
+        for g in range(GROUPS):
+            out = []
+            for half, chunks in enumerate(sides):
+                value = chunks[0][g]
+                for k in range(1, 8):
+                    value = jnp.where((lane // 16 + half) % 8 == k, roll(chunks[k][g], 16 * k, 1), value)
+                out.append(value)
+            put(part * GROUPS + g, *out)
 
     start = 2 * GROUPS
     quarter = (lane % 64) // 16
@@ -377,19 +384,17 @@
             quarter == 2, sheet,
             jnp.where(quarter == 3, roll(drop, 16, 1), jnp.where(quarter == 1, roll(two, -16, 1), roll(one, -32, 1))),
         )
-        left_ref[rows(start + g), :] = left
-        right_ref[rows(start + g), :] = right
-        left_ref[rows(start + 5 + g), :] = bump
-        right_ref[rows(start + 5 + g), :] = bump
+        put(start + g, left, right)
+        put(start + 5 + g, bump, bump)
 
 
 def assemble_kernel(
-    place_ref, sheet_ref, cap_ref, drop_ref, counts_ref, field_ref, first_ref, between_ref, even_ref, odd_ref,
+    place_ref, sheet_ref, cap_ref, drop_ref, counts_ref, field_ref, within_ref, between_ref, late_ref,
     s_ref, x_ref, c_ref, k_ref, one_ref, two_ref, up_ref, down_ref, left_ref, right_ref, diag_ref, spread_ref,
 ):
     row, last = place_ref[1], place_ref[3]
     sub, lane = sub_iota(256), lax.broadcasted_iota(jnp.int32, (8, 256), 1)
-    below, above = readers(row % 2 == 0, row < last, row > 0, first_ref, between_ref, even_ref, odd_ref)
+    below, above = readers(row % 2 == 0, row < last, row > 0, within_ref, between_ref, late_ref)
 
     def both(own, kind, d, n):
         sides = [column_groups(lambda g: own(half, g), below, above, kind, d, half, n) for half in range(2)]
@@ -482,18 +487,23 @@
 
 def solve_kernel(
     place_ref, s_ref, x_ref, c_ref, k_ref, one_ref, two_ref, up_ref, down_ref, left_ref, right_ref, diag_ref, spread_ref,
-    wide_ref, fromleft_ref, fromright_ref, out_ref, base_out_ref,
+    wide_ref, even_ref, odd_ref, out_ref, base_out_ref,
     c_ext, k_ext, f_ext, bound, link_up, link_down, link_left, link_right, inv_ext, src, state, alt,
 ):
     lane = lane_iota()
     row, col = place_ref[1], place_ref[2]
     has_left, has_right = col > 0, col < place_ref[4]
+    even_col = col % 2 == 0
+
+    def from_left(g):
+        return jnp.where(even_col, odd_ref[rows(g), :], even_ref[rows(g), :])
+
+    def from_right(g):
+        return jnp.where(even_col, even_ref[rows(g), :], odd_ref[rows(g), :])
 
     start = 2 * GROUPS
     quarter = (lane % 64) // 16
     take_left, take_right = (quarter == 0) & has_left, (quarter == 3) & has_right
-    from_left = [fromleft_ref[rows(start + g), :] for g in range(10)]
-    from_right = [fromright_ref[rows(start + g), :] for g in range(10)]
     fields = []
     for field in range(5):
         out = []
@@ -501,8 +511,8 @@
             right_shift = (32, 16, 0, 48, 32)[field]
             left_shift = (-32, -48, 0, -16, -32)[field]
             group = g + 5 * (field == 4)
-            value = jnp.where(take_right, roll(from_right[group], right_shift, 1), wide_ref[rows(5 * field + g), :])
-            out.append(jnp.where(take_left, roll(from_left[group], left_shift, 1), value))
+            value = jnp.where(take_right, roll(from_right(start + group), right_shift, 1), wide_ref[rows(5 * field + g), :])
+            out.append(jnp.where(take_left, roll(from_left(start + group), left_shift, 1), value))
         fields.append(jnp.concatenate(out, axis=0))
     solved = base_solve((fields[0], fields[1], (fields[2], fields[3]), fields[4]))
     for t in range(STEPS):
@@ -518,8 +528,8 @@
             right_ok, left_ok = right_ok & (row < place_ref[3]), left_ok & (row < place_ref[3])
         if g in (10, 11):
             right_ok, left_ok = right_ok & (row > 0), left_ok & (row > 0)
-        right = jnp.where((lane // 16 == chunk) & right_ok, fromright_ref[rows(part * GROUPS + g), :], 0.0)
-        value = jnp.where((lane // 16 == (chunk + 7) % 8) & left_ok, fromleft_ref[rows(part * GROUPS + g), :], right)
+        right = jnp.where((lane // 16 == chunk) & right_ok, from_right(part * GROUPS + g), 0.0)
+        value = jnp.where((lane // 16 == (chunk + 7) % 8) & left_ok, from_left(part * GROUPS + g), right)
         return roll(value, -16 * chunk, 1)
 
     sub, sub3 = sub_iota(), sub_iota(384)
@@ -620,20 +630,24 @@
         scratch_shapes=list(scratch),
         compiler_params=pltpu.CompilerParams(vmem_limit_bytes=limit * 1024 * 1024),
         name=name,
+        cost_estimate=HINTS.get(name),
     )
+
+
+LONG = pl.CostEstimate(flops=10**9, bytes_accessed=10**7, transcendentals=0)
+NONE = pl.CostEstimate(flops=0, bytes_accessed=0, transcendentals=0)
+HINTS = {"spread_cells": NONE, "pack_early": NONE, "place_vias": LONG, "pack_relay": LONG}
 
 
 def arr(*shape, dtype=F32):
     return jax.ShapeDtypeStruct(shape, dtype)
 
 
-def swaps(count, offset, distance=1):
-    pairs = []
-    for i in range(count):
-        if ((i - offset) // distance) % 2 == 0:
-            j = (i + distance) % count
-            pairs += [(i, j), (j, i)]
-    return pairs
+def swaps(count, offset):
+    partner = list(range(count))
+    for i in range(offset, count - 1, 2):
+        partner[i], partner[i + 1] = i + 1, i
+    return list(enumerate(partner))
 
 
 def per_device(
@@ -653,50 +667,46 @@
     def buffer(count):
         return arr(8 * count, 128)
 
-    even, odd, base = call(
-        early_kernel, "pack_early", (buffer(EARLY + BASE), buffer(EARLY), buffer(BASE)), [smem(), smem()] + spec(6)
-    )(place, bump_cell, base_sheet, base_start, send, sheet_res, capacity, drop_start)
-    first = lax.ppermute(even, "row", swaps(row_count, 0))
+    base = call(base_kernel, "pack_base", (buffer(BASE),), [smem()] + spec(3))(bump_cell, base_sheet, base_start, send)[0]
+    first = lax.ppermute(base, "row", swaps(row_count, 0))
+    early, between = call(chip_kernel, "pack_early", (buffer(EARLY), buffer(EARLY + 2 * BASE)), [smem()] + spec(5))(
+        place, base, first, sheet_res, capacity, drop_start
+    )
+    between = lax.ppermute(between, "row", swaps(row_count, 1))
     cells, load_cells, loads, spread, counts = call(
         prepare_kernel, "spread_cells",
         (arr(4, VIAS, 8, 128), arr(4, 8, 128), arr(4, 4, 8, 128), arr(256, 1024, dtype=jnp.bfloat16), arr(4, 64, 128)),
         spec(3),
     )(via_cell, load_cell, load_current)
-    between, far = call(chip_kernel, "pack_chip", (buffer(EARLY + 2 * BASE), buffer(2 * BASE)), [smem()] + spec(3))(
-        place, odd, base, first
-    )
-    far = lax.ppermute(
-        far, "row", [(i, (i + 3 if i % 2 == 0 else i - 3) % row_count) for i in range(row_count)]
-    )
-    between = lax.ppermute(between, "row", swaps(row_count, 1))
 
     field, even, odd, arriving = call(
-        place_kernel, "place_vias", (arr(4, 4, 64, 128), buffer(LATE), buffer(LATE), buffer(1)),
+        place_kernel, "place_vias", (arr(4, 4, 64, 128), buffer(LATE + EARLY), buffer(LATE), buffer(1)),
         [smem()] + spec(9), [pltpu.VMEM((4, 4, VIAS, 8, 128), F32)],
-    )(place, packed, send, got, cells, load_cells, loads, spread, counts, far)
-
-    even = lax.ppermute(even, "row", swaps(row_count, 0))
-    odd = lax.ppermute(odd, "row", swaps(row_count, 1))
-    shares = call(shares_kernel, "pack_shares", (buffer(5),), spec(4))(arriving, first, between, far)[0]
+    )(place, packed, send, got, cells, load_cells, loads, spread, counts, early)
+
+    late = lax.ppermute(odd, "row", swaps(row_count, 1))
+    within = lax.ppermute(even, "row", swaps(row_count, 0))
+    relay = call(relay_kernel, "pack_relay", (buffer(BASE),), [smem()] + spec(1))(place, between)[0]
+    relayed = lax.ppermute(relay, "row", swaps(row_count, 0))
+    shares = call(shares_kernel, "pack_shares", (buffer(4),), spec(3))(first, between, relayed)[0]
     shares = lax.ppermute(shares, "die", others)
 
-    strip_shape = arr(8 * COL_GROUPS, 128)
-    left, right, wide = call(
-        strip_kernel, "column_strips", (strip_shape, strip_shape, arr(200, 128)), [smem()] + spec(13)
-    )(place, sheet_res, capacity, drop_start, counts, field, base, arriving, first, between, far, even, odd, shares)
-    from_right = lax.ppermute(left, "col", [(i, (i - 1) % col_count) for i in range(col_count)])
-    from_left = lax.ppermute(right, "col", [(i, (i + 1) % col_count) for i in range(col_count)])
+    even, odd, wide = call(
+        strip_kernel, "column_strips", (buffer(COL_GROUPS), buffer(COL_GROUPS), arr(200, 128)), [smem()] + spec(13)
+    )(place, sheet_res, capacity, drop_start, counts, field, base, arriving, first, between, within, late, relayed, shares)
+    even = lax.ppermute(even, "col", swaps(col_count, 0))
+    odd = lax.ppermute(odd, "col", swaps(col_count, 1))
 
     image, pair = arr(4, 96, 256), arr(2, 96, 256)
     parts = call(
         assemble_kernel, "assemble",
-        (image, image, pair, pair) + (image,) * 7 + (arr(2, 256, 384, dtype=jnp.bfloat16),), [smem()] + spec(9),
-    )(place, sheet_res, capacity, drop_start, counts, field, first, between, even, odd)
+        (image, image, pair, pair) + (image,) * 7 + (arr(2, 256, 384, dtype=jnp.bfloat16),), [smem()] + spec(8),
+    )(place, sheet_res, capacity, drop_start, counts, field, within, between, late)
 
     ext = pltpu.VMEM((96, 384), F32)
     scratch = [ext, ext, pltpu.VMEM((2, 96, 384), F32), pltpu.VMEM((4, 40, 384), F32)] + [ext] * 8
     return call(solve_kernel, "solve", (arr(2, 2, 64, 256), arr(2, 8, 32)), [smem()] + spec(15), scratch)(
-        place, *parts, wide, from_left, from_right
+        place, *parts, wide, even, odd
     )
 
 

time: 45.3 us -> 42.6 us (0.940)
  the two profiles are of different devices: /device:TPU:96 before, /device:TPU:102 now
where the time goes in v6:
time: 42.6 us; the launch traced here: 41.8 us
  starting transfers between devices  17.7 us (42%)
  Pallas kernels  16.3 us (38%)
  waiting for transfers between devices  5.72 us (13%)
  local copies, waits for them, and re-layouts  1.35 us (3%)
  between operations  0.83 us (2%)
    pallas_call x1, Pallas kernels, per_device(): call(solve_kernel, 'solve', (arr(2, 2, 64, 256), arr(2, 8, 32)), [smem()]...  7.83 us
    ppermute x1, starting transfers between devices, per_device(): odd = lax.ppermute(odd, 'col', swaps(col_count, 1))  5.93 us
    ppermute x1, starting transfers between devices, per_device(): between = lax.ppermute(between, 'row', swaps(row_count, 1))  5.24 us
    ppermute x1, starting transfers between devices, per_device(): late = lax.ppermute(odd, 'row', swaps(row_count, 1))  3.94 us
    pallas_call x1, Pallas kernels, per_device(): call(place_kernel, 'place_vias', (arr(4, 4, 64, 128), buffer(LATE + EARLY...  2.6 us
    ppermute x1, waiting for transfers between devices, per_device(): shares = lax.ppermute(shares, 'die', others)  2.54 us
    ppermute x1, waiting for transfers between devices, per_device(): odd = lax.ppermute(odd, 'col', swaps(col_count, 1))  1.6 us
    pallas_call x1, Pallas kernels, per_device(): call(assemble_kernel, 'assemble', (image, image, pair, pair) + (image,) *...  1.41 us
  transfers between devices with their start and end apart: 9, of which 4 were waited for; matrix products, arithmetic and copies ran while one was open for 0% of the time, Pallas kernels for 16%

profile of v6, /device:TPU:102, one launch (start us, length us, event | category | flops | bytes accessed | tf_op | source)
XLA Modules:
  0.0 41.8 jit_solution(14668732419345448884)
XLA Ops:
  0.6 0.1 stack.15.place_ref
  0.7 1.2 %copy-done.3 = f32[2,2,2,32,8,32]{5,4,3,2,1,0:T(8,128)S(1)} copy-done((f32[2,2,2,32,8,32]{5,4,3,2,1,0:T(8,128)S(1)}, f32[2,2,2,32,8,32]{5,4,3,2,1,0:T(8,128)}, u32[]{:S(2)}) %copy-start.3) | copy-done | bytes 262168
  2.0 0.8 %pack_vias.1 = (f32[2,32,8,128]{3,2,1,0:T(8,128)S(1)}, f32[33,8,128]{2,1,0:T(8,128)S(1)}) custom-call(s32[5]{0:T(128)S(1)} %stack.15.place_ref, f32[2,2,2,32,8,32]{5,4,3,2,1,0:T(8,128)S(1)} %copy-done.3), custom_call_target="tpu_custom_call" | custom-call | tf_op jit(solution)/shard_map/pack_vias/pallas_call | solution.py:663
  2.8 0.9 %collective-permute-start = (f32[33,8,128]{2,1,0:T(8,128)S(1)}, f32[33,8,128]{2,1,0:T(8,128)S(1)}, u32[]{:S(2)}, u32[]{:S(2)}) collective-permute-start(f32[33,8,128]{2,1,0:T(8,128)S(1)} %get-tuple-element.32.send_ref), channel_id=1, source_target_pairs={{0,128},{128,0},{1,129},{129,1},{2,130},{130,2},{3,131},{131,3},{4... | collective-permute-start | bytes 405512 | tf_op jit(solution)/shard_map/ppermute | solution.py:666
  3.7 0.6 %pack_base.1.base_ref = f32[32,128]{1,0:T(8,128)S(1)} custom-call(s32[1,4]{1,0:T(1,128)S(1)} %copy-done.9, f32[2,8,32]{2,1,0:T(8,128)S(1)} %copy-done.7, f32[2,8,32]{2,1,0:T(8,128)S(1)} %copy-done.8, f32[33,8,128]{2,1,0:T(8,128)S(1)} %get-tuple-element.32.send_ref), custom_call_target="tpu_custom_call" | custom-call | tf_op jit(solution)/shard_map/pack_base/pallas_call | solution.py:670
  4.4 0.1 collective-permute-start.1
  4.5 0.7 %spread_cells.1 = (f32[4,32,8,128]{3,2,1,0:T(8,128)S(1)}, f32[4,8,128]{2,1,0:T(8,128)S(1)}, f32[4,4,8,128]{3,2,1,0:T(8,128)S(1)}, bf16[256,1024]{1,0:T(8,128)(2,1)S(1)}, f32[4,64,128]{2,1,0:T(8,128)S(1)}) custom-call(s32[2,32,8,32]{3,2,1,0:T(8,128)S(1)} %copy-done.4, s32[2,8,32]{2,1,0:T(8,128)S(1)} %copy-done.6, f32[2,2,2,8,32]{4,3,2,1,0:T(8,128)S(1)} %copy-done.5), custom_call_target="tpu_custom_call" | custom-call | tf_op jit(solution)/shard_map/spread_cells/pallas_call | solution.py:676
  5.2 0.4 collective-permute-done.1.got_ref.first_ref
  5.6 0.6 %pack_early.1 = (f32[240,128]{1,0:T(8,128)S(1)}, f32[304,128]{1,0:T(8,128)S(1)}) custom-call(s32[5]{0:T(128)S(1)} %stack.15.place_ref, f32[32,128]{1,0:T(8,128)S(1)} %pack_base.1.base_ref, f32[32,128]{1,0:T(8,128)S(1)} %collective-permute-done.1.got_ref.first_ref, f32[2,2,64,256]{3,2,1,0:T(8,128)S(1)} %copy-done, f32[2,64,256]{2,1,0:T(8,128)S(1)} %copy-done.2, ...), custom_call_target="tpu_custom_call" | custom-call | tf_op jit(solution)/shard_map/pack_early/pallas_call | solution.py:672
  6.2 5.2 %collective-permute-start.3 = (f32[304,128]{1,0:T(8,128)S(1)}, f32[304,128]{1,0:T(8,128)S(1)}, u32[]{:S(2)}, u32[]{:S(2)}) collective-permute-start(f32[304,128]{1,0:T(8,128)S(1)} %get-tuple-element.40), channel_id=1, source_target_pairs={{0,0},{8,16},{16,8},{24,32},{32,24},{40,48},{48,40},{56,64},{64,56... | collective-permute-start | bytes 466952 | tf_op jit(solution)/shard_map/ppermute | solution.py:675
  11.5 2.6 %place_vias.1 = (f32[4,4,64,128]{3,2,1,0:T(8,128)S(1)}, f32[416,128]{1,0:T(8,128)S(1)}, f32[176,128]{1,0:T(8,128)S(1)}, f32[8,128]{1,0:T(8,128)S(1)}) custom-call(s32[5]{0:T(128)S(1)} %stack.15.place_ref, f32[2,32,8,128]{3,2,1,0:T(8,128)S(1)} %get-tuple-element.31.packed_ref, f32[33,8,128]{2,1,0:T(8,128)S(1)} %get-tuple-element.32.send_ref, ...), custom_call_target="tpu_custom_call" | custom-call | flops 1000000000 | bytes 10000000 | tf_op jit(solution)/shard_map/place_vias/pallas_call | solution.py:682
  14.1 0.1 collective-permute-start.2
  14.2 3.9 %collective-permute-start.4 = (f32[176,128]{1,0:T(8,128)S(1)}, f32[176,128]{1,0:T(8,128)S(1)}, u32[]{:S(2)}, u32[]{:S(2)}) collective-permute-start(f32[176,128]{1,0:T(8,128)S(1)} %get-tuple-element.41), channel_id=1, source_target_pairs={{0,0},{8,16},{16,8},{24,32},{32,24},{40,48},{48,40},{56,64},{64,56... | collective-permute-start | bytes 270344 | tf_op jit(solution)/shard_map/ppermute | solution.py:687
  18.1 0.6 %pack_relay.1 = f32[32,128]{1,0:T(8,128)S(1)} custom-call(s32[5]{0:T(128)S(1)} %stack.15.place_ref, f32[304,128]{1,0:T(8,128)S(1)} %collective-permute-done.3.between_ref), custom_call_target="tpu_custom_call" | custom-call | flops 1000000000 | bytes 10000000 | tf_op jit(solution)/shard_map/pack_relay/pallas_call | solution.py:689
  18.7 0.1 collective-permute-start.5
  18.8 1.2 %collective-permute-done.5.relayed_ref = f32[32,128]{1,0:T(8,128)S(1)} collective-permute-done((f32[32,128]{1,0:T(8,128)S(1)}, f32[32,128]{1,0:T(8,128)S(1)}, u32[]{:S(2)}, u32[]{:S(2)}) %collective-permute-start.5) | collective-permute-done | bytes 16416 | tf_op jit(solution)/shard_map/ppermute | solution.py:690
  20.0 1.2 %collective-permute-start.6 = (f32[32,128]{1,0:T(8,128)S(1)}, f32[32,128]{1,0:T(8,128)S(1)}, u32[]{:S(2)}, u32[]{:S(2)}) collective-permute-start(f32[32,128]{1,0:T(8,128)S(1)} %pack_shares.1), channel_id=1, source_target_pairs={{0,128},{128,0},{1,129},{129,1},{2,130},{130,2},{3,131},{131,3},{4... | collective-permute-start | bytes 49160 | tf_op jit(solution)/shard_map/ppermute | solution.py:692
  21.1 2.5 %collective-permute-done.6.shares_ref = f32[32,128]{1,0:T(8,128)S(1)} collective-permute-done((f32[32,128]{1,0:T(8,128)S(1)}, f32[32,128]{1,0:T(8,128)S(1)}, u32[]{:S(2)}, u32[]{:S(2)}) %collective-permute-start.6) | collective-permute-done | bytes 16416 | tf_op jit(solution)/shard_map/ppermute | solution.py:692
  23.7 1.1 %column_strips.1 = (f32[272,128]{1,0:T(8,128)S(1)}, f32[272,128]{1,0:T(8,128)S(1)}, f32[200,128]{1,0:T(8,128)S(1)}) custom-call(s32[5]{0:T(128)S(1)} %stack.15.place_ref, f32[2,2,64,256]{3,2,1,0:T(8,128)S(1)} %copy-done, f32[2,64,256]{2,1,0:T(8,128)S(1)} %copy-done.2, f32[2,2,64,256]{3,2,1,0:T(8,128)S(1)} %copy-done.1, ...), custom_call_target="tpu_custom_call" | custom-call | tf_op jit(solution)/shard_map/column_strips/pallas_call | solution.py:694
  24.8 0.2 collective-permute-start.7
  25.1 5.9 %collective-permute-start.8 = (f32[272,128]{1,0:T(8,128)S(1)}, f32[272,128]{1,0:T(8,128)S(1)}, u32[]{:S(2)}, u32[]{:S(2)}) collective-permute-start(f32[272,128]{1,0:T(8,128)S(1)} %get-tuple-element.57), channel_id=1, source_target_pairs={{0,0},{1,2},{2,1},{3,4},{4,3},{5,6},{6,5},{7,7},{8,8},{9,10},{10,9... | collective-permute-start | bytes 417800 | tf_op jit(solution)/shard_map/ppermute | solution.py:698
  31.0 1.4 %assemble.1 = (f32[4,96,256]{2,1,0:T(8,128)S(1)}, f32[4,96,256]{2,1,0:T(8,128)S(1)}, f32[2,96,256]{2,1,0:T(8,128)S(1)}, f32[2,96,256]{2,1,0:T(8,128)S(1)}, f32[4...) custom-call(s32[5]{0:T(128)S(1)} %stack.15.place_ref, ...), custom_call_target="tpu_custom_call" | custom-call | tf_op jit(solution)/shard_map/assemble/pallas_call | solution.py:701
  32.4 1.6 %collective-permute-done.8.odd_ref = f32[272,128]{1,0:T(8,128)S(1)} collective-permute-done((f32[272,128]{1,0:T(8,128)S(1)}, f32[272,128]{1,0:T(8,128)S(1)}, u32[]{:S(2)}, u32[]{:S(2)}) %collective-permute-start.8) | collective-permute-done | bytes 139296 | tf_op jit(solution)/shard_map/ppermute | solution.py:698
  34.0 7.8 %solve.1 = (f32[2,2,64,256]{3,2,1,0:T(8,128)}, f32[2,8,32]{2,1,0:T(8,128)}) custom-call(s32[5]{0:T(128)S(1)} %stack.15.place_ref, f32[4,96,256]{2,1,0:T(8,128)S(1)} %get-tuple-element.42.s_ref, f32[4,96,256]{2,1,0:T(8,128)S(1)} %get-tuple-element.43.x_ref, f32[2,96,256]{2,1,0:T(8,128)S(1)} %get-tuple-element.44.c_ref, ...), custom_call_target="tpu_custom_call" | custom-call | tf_op jit(solution)/shard_map/solve/pallas_call | solution.py:708
  (25 shorter events, 0.1 us)
Async XLA Ops:
  0.7 1.2 %copy-start.3 = (f32[2,2,2,32,8,32]{5,4,3,2,1,0:T(8,128)S(1)}, f32[2,2,2,32,8,32]{5,4,3,2,1,0:T(8,128)}, u32[]{:S(2)}) copy-start(f32[2,2,2,32,8,32]{5,4,3,2,1,0:T(8,128)} %via_ref.1) | copy-start | bytes 786436
  1.9 1.8 %copy-start.7 = (f32[2,8,32]{2,1,0:T(8,128)S(1)}, f32[2,8,32]{2,1,0:T(8,128)}, u32[]{:S(2)}) copy-start(f32[2,8,32]{2,1,0:T(8,128)} %sheet_ref.4) | copy-start | bytes 6148
  1.9 1.8 %copy-start.8 = (f32[2,8,32]{2,1,0:T(8,128)S(1)}, f32[2,8,32]{2,1,0:T(8,128)}, u32[]{:S(2)}) copy-start(f32[2,8,32]{2,1,0:T(8,128)} %start_ref.1) | copy-start | bytes 6148
  2.0 1.8 %copy-start.9 = (s32[1,4]{1,0:T(1,128)S(1)}, s32[1,4]{1,0:T(1,128)}, u32[]{:S(2)}) copy-start(s32[1,4]{1,0:T(1,128)} %bump_ref.1) | copy-start | bytes 52
  2.0 2.5 %copy-start.4 = (s32[2,32,8,32]{3,2,1,0:T(8,128)S(1)}, s32[2,32,8,32]{3,2,1,0:T(8,128)}, u32[]{:S(2)}) copy-start(s32[2,32,8,32]{3,2,1,0:T(8,128)} %cell_ref.1) | copy-start | bytes 196612
  2.0 2.5 %copy-start.5 = (f32[2,2,2,8,32]{4,3,2,1,0:T(8,128)S(1)}, f32[2,2,2,8,32]{4,3,2,1,0:T(8,128)}, u32[]{:S(2)}) copy-start(f32[2,2,2,8,32]{4,3,2,1,0:T(8,128)} %load_ref.1) | copy-start | bytes 24580
  2.0 2.5 %copy-start.6 = (s32[2,8,32]{2,1,0:T(8,128)S(1)}, s32[2,8,32]{2,1,0:T(8,128)}, u32[]{:S(2)}) copy-start(s32[2,8,32]{2,1,0:T(8,128)} %load_cell_ref.1) | copy-start | bytes 6148
  2.0 3.6 %copy-start.1 = (f32[2,2,64,256]{3,2,1,0:T(8,128)S(1)}, f32[2,2,64,256]{3,2,1,0:T(8,128)}, u32[]{:S(2)}) copy-start(f32[2,2,64,256]{3,2,1,0:T(8,128)} %drop_ref.5) | copy-start | bytes 786436
  2.8 2.8 %copy-start = (f32[2,2,64,256]{3,2,1,0:T(8,128)S(1)}, f32[2,2,64,256]{3,2,1,0:T(8,128)}, u32[]{:S(2)}) copy-start(f32[2,2,64,256]{3,2,1,0:T(8,128)} %sheet_ref.7) | copy-start | bytes 786436
  2.8 8.6 %collective-permute-start = (f32[33,8,128]{2,1,0:T(8,128)S(1)}, f32[33,8,128]{2,1,0:T(8,128)S(1)}, u32[]{:S(2)}, u32[]{:S(2)}) collective-permute-start(f32[33,8,128]{2,1,0:T(8,128)S(1)} %get-tuple-element.32.send_ref), channel_id=1, source_target_pairs={{0,128},{128,0},{1,129},{129,1},{2,130},{130,2},{3,131},{131,3},{4... | collective-permute-start | bytes 405512 | tf_op jit(solution)/shard_map/ppermute | solution.py:666
  4.4 1.3 %copy-start.2 = (f32[2,64,256]{2,1,0:T(8,128)S(1)}, f32[2,64,256]{2,1,0:T(8,128)}, u32[]{:S(2)}) copy-start(f32[2,64,256]{2,1,0:T(8,128)} %cap_ref.5) | copy-start | bytes 393220
  4.4 1.2 %collective-permute-start.1 = (f32[32,128]{1,0:T(8,128)S(1)}, f32[32,128]{1,0:T(8,128)S(1)}, u32[]{:S(2)}, u32[]{:S(2)}) collective-permute-start(f32[32,128]{1,0:T(8,128)S(1)} %pack_base.1.base_ref), channel_id=1, source_target_pairs={{0,8},{8,0},{16,24},{24,16},{32,40},{40,32},{48,56},{56,48},{64,72... | collective-permute-start | bytes 49160 | tf_op jit(solution)/shard_map/ppermute | solution.py:671
  6.2 11.9 %collective-permute-start.3 = (f32[304,128]{1,0:T(8,128)S(1)}, f32[304,128]{1,0:T(8,128)S(1)}, u32[]{:S(2)}, u32[]{:S(2)}) collective-permute-start(f32[304,128]{1,0:T(8,128)S(1)} %get-tuple-element.40), channel_id=1, source_target_pairs={{0,0},{8,16},{16,8},{24,32},{32,24},{40,48},{48,40},{56,64},{64,56... | collective-permute-start | bytes 466952 | tf_op jit(solution)/shard_map/ppermute | solution.py:675
  14.1 9.6 %collective-permute-start.2 = (f32[416,128]{1,0:T(8,128)S(1)}, f32[416,128]{1,0:T(8,128)S(1)}, u32[]{:S(2)}, u32[]{:S(2)}) collective-permute-start(f32[416,128]{1,0:T(8,128)S(1)} %get-tuple-element.39), channel_id=1, source_target_pairs={{0,8},{8,0},{16,24},{24,16},{32,40},{40,32},{48,56},{56,48},{64,72... | collective-permute-start | bytes 638984 | tf_op jit(solution)/shard_map/ppermute | solution.py:688
  14.2 9.5 %collective-permute-start.4 = (f32[176,128]{1,0:T(8,128)S(1)}, f32[176,128]{1,0:T(8,128)S(1)}, u32[]{:S(2)}, u32[]{:S(2)}) collective-permute-start(f32[176,128]{1,0:T(8,128)S(1)} %get-tuple-element.41), channel_id=1, source_target_pairs={{0,0},{8,16},{16,8},{24,32},{32,24},{40,48},{48,40},{56,64},{64,56... | collective-permute-start | bytes 270344 | tf_op jit(solution)/shard_map/ppermute | solution.py:687
  18.7 1.3 %collective-permute-start.5 = (f32[32,128]{1,0:T(8,128)S(1)}, f32[32,128]{1,0:T(8,128)S(1)}, u32[]{:S(2)}, u32[]{:S(2)}) collective-permute-start(f32[32,128]{1,0:T(8,128)S(1)} %pack_relay.1), channel_id=1, source_target_pairs={{0,8},{8,0},{16,24},{24,16},{32,40},{40,32},{48,56},{56,48},{64,72... | collective-permute-start | bytes 49160 | tf_op jit(solution)/shard_map/ppermute | solution.py:690
  20.0 3.7 %collective-permute-start.6 = (f32[32,128]{1,0:T(8,128)S(1)}, f32[32,128]{1,0:T(8,128)S(1)}, u32[]{:S(2)}, u32[]{:S(2)}) collective-permute-start(f32[32,128]{1,0:T(8,128)S(1)} %pack_shares.1), channel_id=1, source_target_pairs={{0,128},{128,0},{1,129},{129,1},{2,130},{130,2},{3,131},{131,3},{4... | collective-permute-start | bytes 49160 | tf_op jit(solution)/shard_map/ppermute | solution.py:692
  24.8 7.6 %collective-permute-start.7 = (f32[272,128]{1,0:T(8,128)S(1)}, f32[272,128]{1,0:T(8,128)S(1)}, u32[]{:S(2)}, u32[]{:S(2)}) collective-permute-start(f32[272,128]{1,0:T(8,128)S(1)} %get-tuple-element.56), channel_id=1, source_target_pairs={{0,1},{1,0},{2,3},{3,2},{4,5},{5,4},{6,7},{7,6},{8,9},{9,8},{10,11... | collective-permute-start | bytes 417800 | tf_op jit(solution)/shard_map/ppermute | solution.py:697
  25.1 9.0 %collective-permute-start.8 = (f32[272,128]{1,0:T(8,128)S(1)}, f32[272,128]{1,0:T(8,128)S(1)}, u32[]{:S(2)}, u32[]{:S(2)}) collective-permute-start(f32[272,128]{1,0:T(8,128)S(1)} %get-tuple-element.57), channel_id=1, source_target_pairs={{0,0},{1,2},{2,1},{3,4},{4,3},{5,6},{6,5},{7,7},{8,8},{9,10},{10,9... | collective-permute-start | bytes 417800 | tf_op jit(solution)/shard_map/ppermute | solution.py:698

commit v7 on v6

--- a/solution.py
+++ b/solution.py
@@ -54,8 +54,8 @@
     return pl.ds(8 * g, 8)
 
 
-def pack_kernel(place_ref, via_ref, packed_ref, send_ref):
-    later = place_ref[0].astype(F32)
+def pack_kernel(via_ref, packed_ref, send_ref):
+    later = lax.axis_index("die").astype(F32)
     total = jnp.zeros((8, 128), F32)
     for v in range(VIAS):
         parts = []
@@ -107,13 +107,13 @@
     bump = jnp.zeros((8, 128), F32)
     column = lane % 64 - 16
     for k in range(4):
-        bump = jnp.where((column // 8 == k) & (sub * 8 + column % 8 == bump_ref[0, k]), 1.0, bump)
+        bump = jnp.where((column // 8 == k) & (sub * 8 + column % 8 == bump_ref[0:1, k : k + 1]), 1.0, bump)
     for part, value in enumerate([spread_nets(sheet_ref), spread_nets(start_ref), bump, send_ref[VIAS]]):
         base_ref[rows(part), :] = value
 
 
-def chip_kernel(place_ref, base_ref, got_ref, sheet_ref, cap_ref, drop_ref, within_ref, between_ref):
-    even = place_ref[1] % 2 == 0
+def chip_kernel(base_ref, got_ref, sheet_ref, cap_ref, drop_ref, within_ref, between_ref):
+    even = lax.axis_index("row") % 2 == 0
     sender = RowSender(even, within_ref, between_ref)
     for d in range(2):
         for half in range(2):
@@ -127,8 +127,8 @@
             between_ref[rows(EARLY + BASE * slot + part), :] = value
 
 
-def relay_kernel(place_ref, between_ref, relay_ref):
-    even = place_ref[1] % 2 == 0
+def relay_kernel(between_ref, relay_ref):
+    even = lax.axis_index("row") % 2 == 0
     for part in range(BASE):
         a, b = between_ref[rows(EARLY + part), :], between_ref[rows(EARLY + BASE + part), :]
         relay_ref[rows(part), :] = jnp.where(even, b, a)
@@ -190,12 +190,12 @@
 
 
 def place_kernel(
-    place_ref, packed_ref, send_ref, got_ref, cells_ref, load_cells_ref, loads_ref, spread_ref, counts_ref, early_ref,
+    packed_ref, send_ref, got_ref, cells_ref, load_cells_ref, loads_ref, spread_ref, counts_ref, early_ref,
     field_ref, even_ref, odd_ref, arriving_ref, values_ref,
 ):
     lane = lane_iota()
-    later = place_ref[0].astype(F32)
-    even = place_ref[1] % 2 == 0
+    later = lax.axis_index("die").astype(F32)
+    even = lax.axis_index("row") % 2 == 0
     weights = (
         (VIA_RESIST * (4.0 - 2.0 * later), VIA_RESIST * (3.0 - 2.0 * later), VIA_RESIST * (1.0 + later)),
         (VIA_RESIST * (3.0 - 2.0 * later), VIA_RESIST * (3.0 - 2.0 * later), VIA_RESIST),
@@ -287,15 +287,15 @@
 
 
 def strip_kernel(
-    place_ref, sheet_ref, cap_ref, drop_ref, counts_ref, field_ref, base_ref, arriving_ref, first_ref, between_ref,
+    sheet_ref, cap_ref, drop_ref, counts_ref, field_ref, base_ref, arriving_ref, first_ref, between_ref,
     within_ref, late_ref, relayed_ref, shares_ref, even_ref, odd_ref, wide_ref,
 ):
     lane = lane_iota()
     within = lane % 16
-    row, last = place_ref[1], place_ref[3]
+    row, last = lax.axis_index("row"), (lax.axis_size("row") - 1)
     even = row % 2 == 0
     below, above = readers(even, None, None, within_ref, between_ref, late_ref)
-    even_col = place_ref[2] % 2 == 0
+    even_col = lax.axis_index("col") % 2 == 0
 
     own = (lane % 64 >= 16) & (lane % 64 < 48)
 
@@ -357,9 +357,9 @@
             out.append(merged)
         return out
 
-    def put(place, left, right):
-        even_ref[rows(place), :] = jnp.where(even_col, right, left)
-        odd_ref[rows(place), :] = jnp.where(even_col, left, right)
+    def put(index, left, right):
+        even_ref[rows(index), :] = jnp.where(even_col, right, left)
+        odd_ref[rows(index), :] = jnp.where(even_col, left, right)
 
     for part in range(2):
         sides = [fields(part, half) for half in range(2)]
@@ -389,10 +389,10 @@
 
 
 def assemble_kernel(
-    place_ref, sheet_ref, cap_ref, drop_ref, counts_ref, field_ref, within_ref, between_ref, late_ref,
+    sheet_ref, cap_ref, drop_ref, counts_ref, field_ref, within_ref, between_ref, late_ref,
     s_ref, x_ref, c_ref, k_ref, one_ref, two_ref, up_ref, down_ref, left_ref, right_ref, diag_ref, spread_ref,
 ):
-    row, last = place_ref[1], place_ref[3]
+    row, last = lax.axis_index("row"), (lax.axis_size("row") - 1)
     sub, lane = sub_iota(256), lax.broadcasted_iota(jnp.int32, (8, 256), 1)
     below, above = readers(row % 2 == 0, row < last, row > 0, within_ref, between_ref, late_ref)
 
@@ -486,13 +486,13 @@
 
 
 def solve_kernel(
-    place_ref, s_ref, x_ref, c_ref, k_ref, one_ref, two_ref, up_ref, down_ref, left_ref, right_ref, diag_ref, spread_ref,
+    s_ref, x_ref, c_ref, k_ref, one_ref, two_ref, up_ref, down_ref, left_ref, right_ref, diag_ref, spread_ref,
     wide_ref, even_ref, odd_ref, out_ref, base_out_ref,
     c_ext, k_ext, f_ext, bound, link_up, link_down, link_left, link_right, inv_ext, src, state, alt,
 ):
     lane = lane_iota()
-    row, col = place_ref[1], place_ref[2]
-    has_left, has_right = col > 0, col < place_ref[4]
+    row, col = lax.axis_index("row"), lax.axis_index("col")
+    has_left, has_right = col > 0, col < (lax.axis_size("col") - 1)
     even_col = col % 2 == 0
 
     def from_left(g):
@@ -525,7 +525,7 @@
     def third(part, chunk, g):
         right_ok, left_ok = has_right, has_left
         if g in (8, 9):
-            right_ok, left_ok = right_ok & (row < place_ref[3]), left_ok & (row < place_ref[3])
+            right_ok, left_ok = right_ok & (row < (lax.axis_size("row") - 1)), left_ok & (row < (lax.axis_size("row") - 1))
         if g in (10, 11):
             right_ok, left_ok = right_ok & (row > 0), left_ok & (row > 0)
         right = jnp.where((lane // 16 == chunk) & right_ok, from_right(part * GROUPS + g), 0.0)
@@ -550,7 +550,7 @@
             for g in range(GROUPS):
                 c_ext[rows(g), :] = wide(c_ref, g, third(1, d, g), d)
                 k_ext[rows(g), :] = wide(k_ref, g, third(1, 2 + d, g), d)
-        @pl.when(place_ref[3] >= 0)
+        @pl.when(row >= 0)
         def _():
             sheets = [third(0, i, g) for g in range(GROUPS)]
             for g in range(GROUPS):
@@ -583,7 +583,7 @@
                     two = jnp.where(lane < 64, roll(one, -11, 1), roll(one, 11, 1))
                     f_ext[1, rows(g), :] = wide(two_ref, g, two)
 
-        @pl.when(place_ref[3] >= 0)
+        @pl.when(row >= 0)
         def _():
             for t in range(STEPS):
                 for k in range(SWEEPS):
@@ -617,10 +617,6 @@
     return [pl.BlockSpec(memory_space=pltpu.VMEM)] * count
 
 
-def smem():
-    return pl.BlockSpec(memory_space=pltpu.SMEM)
-
-
 def call(kernel, name, outs, ins, scratch=(), limit=24):
     return pl.pallas_call(
         kernel,
@@ -655,22 +651,17 @@
 ):
     row_count = lax.axis_size("row")
     col_count = lax.axis_size("col")
-    place = jnp.stack(
-        [lax.axis_index("die"), lax.axis_index("row"), lax.axis_index("col"), row_count - 1, col_count - 1]
-    ).astype(jnp.int32)
     others = [(0, 1), (1, 0)]
 
-    packed, send = call(pack_kernel, "pack_vias", (arr(2, VIAS, 8, 128), arr(VIAS + 1, 8, 128)), [smem()] + spec(1))(
-        place, via_current
-    )
+    packed, send = call(pack_kernel, "pack_vias", (arr(2, VIAS, 8, 128), arr(VIAS + 1, 8, 128)), spec(1))(via_current)
     got = lax.ppermute(send, "die", others)
     def buffer(count):
         return arr(8 * count, 128)
 
-    base = call(base_kernel, "pack_base", (buffer(BASE),), [smem()] + spec(3))(bump_cell, base_sheet, base_start, send)[0]
+    base = call(base_kernel, "pack_base", (buffer(BASE),), spec(4))(bump_cell, base_sheet, base_start, send)[0]
     first = lax.ppermute(base, "row", swaps(row_count, 0))
-    early, between = call(chip_kernel, "pack_early", (buffer(EARLY), buffer(EARLY + 2 * BASE)), [smem()] + spec(5))(
-        place, base, first, sheet_res, capacity, drop_start
+    early, between = call(chip_kernel, "pack_early", (buffer(EARLY), buffer(EARLY + 2 * BASE)), spec(5))(
+        base, first, sheet_res, capacity, drop_start
     )
     between = lax.ppermute(between, "row", swaps(row_count, 1))
     cells, load_cells, loads, spread, counts = call(
@@ -681,32 +672,32 @@
 
     field, even, odd, arriving = call(
         place_kernel, "place_vias", (arr(4, 4, 64, 128), buffer(LATE + EARLY), buffer(LATE), buffer(1)),
-        [smem()] + spec(9), [pltpu.VMEM((4, 4, VIAS, 8, 128), F32)],
-    )(place, packed, send, got, cells, load_cells, loads, spread, counts, early)
+        spec(9), [pltpu.VMEM((4, 4, VIAS, 8, 128), F32)],
+    )(packed, send, got, cells, load_cells, loads, spread, counts, early)
 
     late = lax.ppermute(odd, "row", swaps(row_count, 1))
     within = lax.ppermute(even, "row", swaps(row_count, 0))
-    relay = call(relay_kernel, "pack_relay", (buffer(BASE),), [smem()] + spec(1))(place, between)[0]
+    relay = call(relay_kernel, "pack_relay", (buffer(BASE),), spec(1))(between)[0]
     relayed = lax.ppermute(relay, "row", swaps(row_count, 0))
     shares = call(shares_kernel, "pack_shares", (buffer(4),), spec(3))(first, between, relayed)[0]
     shares = lax.ppermute(shares, "die", others)
 
     even, odd, wide = call(
-        strip_kernel, "column_strips", (buffer(COL_GROUPS), buffer(COL_GROUPS), arr(200, 128)), [smem()] + spec(13)
-    )(place, sheet_res, capacity, drop_start, counts, field, base, arriving, first, between, within, late, relayed, shares)
+        strip_kernel, "column_strips", (buffer(COL_GROUPS), buffer(COL_GROUPS), arr(200, 128)), spec(13)
+    )(sheet_res, capacity, drop_start, counts, field, base, arriving, first, between, within, late, relayed, shares)
     even = lax.ppermute(even, "col", swaps(col_count, 0))
     odd = lax.ppermute(odd, "col", swaps(col_count, 1))
 
     image, pair = arr(4, 96, 256), arr(2, 96, 256)
     parts = call(
         assemble_kernel, "assemble",
-        (image, image, pair, pair) + (image,) * 7 + (arr(2, 256, 384, dtype=jnp.bfloat16),), [smem()] + spec(8),
-    )(place, sheet_res, capacity, drop_start, counts, field, within, between, late)
+        (image, image, pair, pair) + (image,) * 7 + (arr(2, 256, 384, dtype=jnp.bfloat16),), spec(8),
+    )(sheet_res, capacity, drop_start, counts, field, within, between, late)
 
     ext = pltpu.VMEM((96, 384), F32)
     scratch = [ext, ext, pltpu.VMEM((2, 96, 384), F32), pltpu.VMEM((4, 40, 384), F32)] + [ext] * 8
-    return call(solve_kernel, "solve", (arr(2, 2, 64, 256), arr(2, 8, 32)), [smem()] + spec(15), scratch)(
-        place, *parts, wide, even, odd
+    return call(solve_kernel, "solve", (arr(2, 2, 64, 256), arr(2, 8, 32)), spec(15), scratch)(
+        *parts, wide, even, odd
     )
 
 

time: 42.6 us -> 39.3 us (0.923)
  Pallas kernels: 16.3 us -> 12.1 us
  waiting for transfers between devices: 5.72 us -> 6.86 us
    pallas_call x3, Pallas kernels: 9 us -> 7.67 us  [the longest x1 7.58 us: per_device(): call(solve_kernel, 'solve', (arr(2, 2, 64, 256), arr(2, 8, 32)), spec(15)...]
    pallas_call x1, Pallas kernels: 1.41 us -> 0.73 us  [per_device(): call(assemble_kernel, 'assemble', (image, image, pair, pair) + (image,) *...]
    ppermute x1, waiting for transfers between devices: 1.6 us -> 2.27 us  [per_device(): odd = lax.ppermute(odd, 'col', swaps(col_count, 1))]
    pallas_call x1, Pallas kernels: 2.6 us -> 2.05 us  [per_device(): call(place_kernel, 'place_vias', (arr(4, 4, 64, 128), buffer(LATE + EARLY...]
    pallas_call x1, Pallas kernels: 0.81 us -> 0.27 us  [per_device(): call(pack_kernel, 'pack_vias', (arr(2, VIAS, 8, 128), arr(VIAS + 1, 8, 12...]
    pallas_call x1, Pallas kernels: 0.57 us -> 0.04 us  [per_device(): call(chip_kernel, 'pack_early', (buffer(EARLY), buffer(EARLY + 2 * BASE))...]
    pallas_call x1, Pallas kernels: 1.14 us -> 0.61 us  [per_device(): call(strip_kernel, 'column_strips', (buffer(COL_GROUPS), buffer(COL_GROUP...]
    ppermute x1, waiting for transfers between devices: 0.01 us -> 0.46 us  [per_device(): late = lax.ppermute(odd, 'row', swaps(row_count, 1))]
  transfers between devices with their start and end apart: 9 -> 9, of which waited for: 4 -> 5; matrix products, arithmetic and copies ran while one was open for 0% -> 0% of each run, Pallas kernels for 16% -> 9%
where the time goes in v7:
time: 39.3 us; the launch traced here: 38.8 us
  starting transfers between devices  17.7 us (45%)
  Pallas kernels  12.1 us (31%)
  waiting for transfers between devices  6.86 us (17%)
  local copies, waits for them, and re-layouts  1.26 us (3%)
  between operations  0.84 us (2%)
    pallas_call x1, Pallas kernels, per_device(): call(solve_kernel, 'solve', (arr(2, 2, 64, 256), arr(2, 8, 32)), spec(15)...  7.58 us
    ppermute x1, starting transfers between devices, per_device(): odd = lax.ppermute(odd, 'col', swaps(col_count, 1))  5.93 us
    ppermute x1, starting transfers between devices, per_device(): between = lax.ppermute(between, 'row', swaps(row_count, 1))  5.23 us
    ppermute x1, starting transfers between devices, per_device(): late = lax.ppermute(odd, 'row', swaps(row_count, 1))  3.94 us
    ppermute x1, waiting for transfers between devices, per_device(): shares = lax.ppermute(shares, 'die', others)  2.54 us
    ppermute x1, waiting for transfers between devices, per_device(): odd = lax.ppermute(odd, 'col', swaps(col_count, 1))  2.27 us
    pallas_call x1, Pallas kernels, per_device(): call(place_kernel, 'place_vias', (arr(4, 4, 64, 128), buffer(LATE + EARLY...  2.05 us
    unnamed x20, local copies, waits for them, and re-layouts  1.26 us
  transfers between devices with their start and end apart: 9, of which 5 were waited for; matrix products, arithmetic and copies ran while one was open for 0% of the time, Pallas kernels for 9%

profile of v7, /device:TPU:102, one launch (start us, length us, event | category | flops | bytes accessed | tf_op | source)
XLA Modules:
  0.0 38.8 jit_solution(11736913355997853612)
XLA Ops:
  0.6 1.2 %copy-done.3 = f32[2,2,2,32,8,32]{5,4,3,2,1,0:T(8,128)S(1)} copy-done((f32[2,2,2,32,8,32]{5,4,3,2,1,0:T(8,128)S(1)}, f32[2,2,2,32,8,32]{5,4,3,2,1,0:T(8,128)}, u32[]{:S(2)}) %copy-start.3) | copy-done | bytes 262168
  1.9 0.3 pack_vias.1
  2.2 0.0 copy-start
  2.2 0.9 %collective-permute-start = (f32[33,8,128]{2,1,0:T(8,128)S(1)}, f32[33,8,128]{2,1,0:T(8,128)S(1)}, u32[]{:S(2)}, u32[]{:S(2)}) collective-permute-start(f32[33,8,128]{2,1,0:T(8,128)S(1)} %get-tuple-element.32.send_ref), channel_id=1, source_target_pairs={{0,128},{128,0},{1,129},{129,1},{2,130},{130,2},{3,131},{131,3},{4... | collective-permute-start | bytes 405512 | tf_op jit(solution)/shard_map/ppermute | solution.py:657
  3.1 0.1 pack_base.1.base_ref
  3.2 0.0 copy-start.2
  3.2 0.1 collective-permute-start.1
  3.3 0.7 %spread_cells.1 = (f32[4,32,8,128]{3,2,1,0:T(8,128)S(1)}, f32[4,8,128]{2,1,0:T(8,128)S(1)}, f32[4,4,8,128]{3,2,1,0:T(8,128)S(1)}, bf16[256,1024]{1,0:T(8,128)(2,1)S(1)}, f32[4,64,128]{2,1,0:T(8,128)S(1)}) custom-call(s32[2,32,8,32]{3,2,1,0:T(8,128)S(1)} %copy-done.4, s32[2,8,32]{2,1,0:T(8,128)S(1)} %copy-done.6, f32[2,2,2,8,32]{4,3,2,1,0:T(8,128)S(1)} %copy-done.5), custom_call_target="tpu_custom_call" | custom-call | tf_op jit(solution)/shard_map/spread_cells/pallas_call | solution.py:667
  4.1 0.4 %collective-permute-done.1.got_ref.first_ref = f32[32,128]{1,0:T(8,128)S(1)} collective-permute-done((f32[32,128]{1,0:T(8,128)S(1)}, f32[32,128]{1,0:T(8,128)S(1)}, u32[]{:S(2)}, u32[]{:S(2)}) %collective-permute-start.1) | collective-permute-done | bytes 16416 | tf_op jit(solution)/shard_map/ppermute | solution.py:662
  4.5 5.2 %collective-permute-start.3 = (f32[304,128]{1,0:T(8,128)S(1)}, f32[304,128]{1,0:T(8,128)S(1)}, u32[]{:S(2)}, u32[]{:S(2)}) collective-permute-start(f32[304,128]{1,0:T(8,128)S(1)} %get-tuple-element.40), channel_id=1, source_target_pairs={{0,0},{8,16},{16,8},{24,32},{32,24},{40,48},{48,40},{56,64},{64,56... | collective-permute-start | bytes 466952 | tf_op jit(solution)/shard_map/ppermute | solution.py:666
  9.8 2.1 %place_vias.1 = (f32[4,4,64,128]{3,2,1,0:T(8,128)S(1)}, f32[416,128]{1,0:T(8,128)S(1)}, f32[176,128]{1,0:T(8,128)S(1)}, f32[8,128]{1,0:T(8,128)S(1)}) custom-call(f32[2,32,8,128]{3,2,1,0:T(8,128)S(1)} %get-tuple-element.31.packed_ref, f32[33,8,128]{2,1,0:T(8,128)S(1)} %get-tuple-element.32.send_ref, f32[33,8,128]{2,1,0:T(8,128)S(1)} %collective-permute-done.got_ref, ...), custom_call_target="tpu_custom_call" | custom-call | flops 1000000000 | bytes 10000000 | tf_op jit(solution)/shard_map/place_vias/pallas_call | solution.py:673
  11.8 0.1 collective-permute-start.2
  11.9 3.9 %collective-permute-start.4 = (f32[176,128]{1,0:T(8,128)S(1)}, f32[176,128]{1,0:T(8,128)S(1)}, u32[]{:S(2)}, u32[]{:S(2)}) collective-permute-start(f32[176,128]{1,0:T(8,128)S(1)} %get-tuple-element.41), channel_id=1, source_target_pairs={{0,0},{8,16},{16,8},{24,32},{32,24},{40,48},{48,40},{56,64},{64,56... | collective-permute-start | bytes 270344 | tf_op jit(solution)/shard_map/ppermute | solution.py:678
  15.9 0.1 collective-permute-start.5
  16.0 1.2 %collective-permute-done.5.relayed_ref = f32[32,128]{1,0:T(8,128)S(1)} collective-permute-done((f32[32,128]{1,0:T(8,128)S(1)}, f32[32,128]{1,0:T(8,128)S(1)}, u32[]{:S(2)}, u32[]{:S(2)}) %collective-permute-start.5) | collective-permute-done | bytes 16416 | tf_op jit(solution)/shard_map/ppermute | solution.py:681
  17.2 1.2 %collective-permute-start.6 = (f32[32,128]{1,0:T(8,128)S(1)}, f32[32,128]{1,0:T(8,128)S(1)}, u32[]{:S(2)}, u32[]{:S(2)}) collective-permute-start(f32[32,128]{1,0:T(8,128)S(1)} %pack_shares.1), channel_id=1, source_target_pairs={{0,128},{128,0},{1,129},{129,1},{2,130},{130,2},{3,131},{131,3},{4... | collective-permute-start | bytes 49160 | tf_op jit(solution)/shard_map/ppermute | solution.py:683
  18.4 2.5 %collective-permute-done.6.shares_ref = f32[32,128]{1,0:T(8,128)S(1)} collective-permute-done((f32[32,128]{1,0:T(8,128)S(1)}, f32[32,128]{1,0:T(8,128)S(1)}, u32[]{:S(2)}, u32[]{:S(2)}) %collective-permute-start.6) | collective-permute-done | bytes 16416 | tf_op jit(solution)/shard_map/ppermute | solution.py:683
  20.9 0.5 %collective-permute-done.4.late_ref = f32[176,128]{1,0:T(8,128)S(1)} collective-permute-done((f32[176,128]{1,0:T(8,128)S(1)}, f32[176,128]{1,0:T(8,128)S(1)}, u32[]{:S(2)}, u32[]{:S(2)}) %collective-permute-start.4) | collective-permute-done | bytes 90144 | tf_op jit(solution)/shard_map/ppermute | solution.py:678
  21.4 0.6 %column_strips.1 = (f32[272,128]{1,0:T(8,128)S(1)}, f32[272,128]{1,0:T(8,128)S(1)}, f32[200,128]{1,0:T(8,128)S(1)}) custom-call(f32[2,2,64,256]{3,2,1,0:T(8,128)S(1)} %copy-done, f32[2,64,256]{2,1,0:T(8,128)S(1)} %copy-done.2, f32[2,2,64,256]{3,2,1,0:T(8,128)S(1)} %copy-done.1, f32[4,64,128]{2,1,0:T(8,128)S(1)} %get-tuple-element.30.counts_ref, ...), custom_call_target="tpu_custom_call" | custom-call | tf_op jit(solution)/shard_map/column_strips/pallas_call | solution.py:685
  22.0 0.2 collective-permute-start.7
  22.2 5.9 %collective-permute-start.8 = (f32[272,128]{1,0:T(8,128)S(1)}, f32[272,128]{1,0:T(8,128)S(1)}, u32[]{:S(2)}, u32[]{:S(2)}) collective-permute-start(f32[272,128]{1,0:T(8,128)S(1)} %get-tuple-element.57), channel_id=1, source_target_pairs={{0,0},{1,2},{2,1},{3,4},{4,3},{5,6},{6,5},{7,7},{8,8},{9,10},{10,9... | collective-permute-start | bytes 417800 | tf_op jit(solution)/shard_map/ppermute | solution.py:689
  28.2 0.7 %assemble.1 = (f32[4,96,256]{2,1,0:T(8,128)S(1)}, f32[4,96,256]{2,1,0:T(8,128)S(1)}, f32[2,96,256]{2,1,0:T(8,128)S(1)}, f32[2,96,256]{2,1,0:T(8,128)S(1)}, f32[4...) custom-call(f32[2,2,64,256]{3,2,1,0:T(8,128)S(1)} %copy-done, ...), custom_call_target="tpu_custom_call" | custom-call | tf_op jit(solution)/shard_map/assemble/pallas_call | solution.py:692
  28.9 2.3 %collective-permute-done.8.odd_ref = f32[272,128]{1,0:T(8,128)S(1)} collective-permute-done((f32[272,128]{1,0:T(8,128)S(1)}, f32[272,128]{1,0:T(8,128)S(1)}, u32[]{:S(2)}, u32[]{:S(2)}) %collective-permute-start.8) | collective-permute-done | bytes 139296 | tf_op jit(solution)/shard_map/ppermute | solution.py:689
  31.2 7.6 %solve.1 = (f32[2,2,64,256]{3,2,1,0:T(8,128)}, f32[2,8,32]{2,1,0:T(8,128)}) custom-call(f32[4,96,256]{2,1,0:T(8,128)S(1)} %get-tuple-element.42.s_ref, f32[4,96,256]{2,1,0:T(8,128)S(1)} %get-tuple-element.43.x_ref, f32[2,96,256]{2,1,0:T(8,128)S(1)} %get-tuple-element.44.c_ref, f32[2,96,256]{2,1,0:T(8,128)S(1)} %get-tuple-element.45.k_ref, ...), custom_call_target="tpu_custom_call" | custom-call | tf_op jit(solution)/shard_map/solve/pallas_call | solution.py:699
  (24 shorter events, 0.1 us)
Async XLA Ops:
  0.6 1.2 %copy-start.3 = (f32[2,2,2,32,8,32]{5,4,3,2,1,0:T(8,128)S(1)}, f32[2,2,2,32,8,32]{5,4,3,2,1,0:T(8,128)}, u32[]{:S(2)}) copy-start(f32[2,2,2,32,8,32]{5,4,3,2,1,0:T(8,128)} %via_ref.1) | copy-start | bytes 786436
  1.9 1.2 %copy-start.7 = (f32[2,8,32]{2,1,0:T(8,128)S(1)}, f32[2,8,32]{2,1,0:T(8,128)}, u32[]{:S(2)}) copy-start(f32[2,8,32]{2,1,0:T(8,128)} %sheet_ref.4) | copy-start | bytes 6148
  1.9 1.2 %copy-start.8 = (f32[2,8,32]{2,1,0:T(8,128)S(1)}, f32[2,8,32]{2,1,0:T(8,128)}, u32[]{:S(2)}) copy-start(f32[2,8,32]{2,1,0:T(8,128)} %start_ref.1) | copy-start | bytes 6148
  1.9 1.2 %copy-start.9 = (s32[1,4]{1,0:T(1,128)S(1)}, s32[1,4]{1,0:T(1,128)}, u32[]{:S(2)}) copy-start(s32[1,4]{1,0:T(1,128)} %bump_ref.1) | copy-start | bytes 52
  1.9 1.4 %copy-start.4 = (s32[2,32,8,32]{3,2,1,0:T(8,128)S(1)}, s32[2,32,8,32]{3,2,1,0:T(8,128)}, u32[]{:S(2)}) copy-start(s32[2,32,8,32]{3,2,1,0:T(8,128)} %cell_ref.1) | copy-start | bytes 196612
  1.9 1.4 %copy-start.5 = (f32[2,2,2,8,32]{4,3,2,1,0:T(8,128)S(1)}, f32[2,2,2,8,32]{4,3,2,1,0:T(8,128)}, u32[]{:S(2)}) copy-start(f32[2,2,2,8,32]{4,3,2,1,0:T(8,128)} %load_ref.1) | copy-start | bytes 24580
  1.9 1.4 %copy-start.6 = (s32[2,8,32]{2,1,0:T(8,128)S(1)}, s32[2,8,32]{2,1,0:T(8,128)}, u32[]{:S(2)}) copy-start(s32[2,8,32]{2,1,0:T(8,128)} %load_cell_ref.1) | copy-start | bytes 6148
  1.9 2.6 %copy-start.1 = (f32[2,2,64,256]{3,2,1,0:T(8,128)S(1)}, f32[2,2,64,256]{3,2,1,0:T(8,128)}, u32[]{:S(2)}) copy-start(f32[2,2,64,256]{3,2,1,0:T(8,128)} %drop_ref.5) | copy-start | bytes 786436
  2.2 2.3 %copy-start = (f32[2,2,64,256]{3,2,1,0:T(8,128)S(1)}, f32[2,2,64,256]{3,2,1,0:T(8,128)}, u32[]{:S(2)}) copy-start(f32[2,2,64,256]{3,2,1,0:T(8,128)} %sheet_ref.7) | copy-start | bytes 786436
  2.2 7.6 %collective-permute-start = (f32[33,8,128]{2,1,0:T(8,128)S(1)}, f32[33,8,128]{2,1,0:T(8,128)S(1)}, u32[]{:S(2)}, u32[]{:S(2)}) collective-permute-start(f32[33,8,128]{2,1,0:T(8,128)S(1)} %get-tuple-element.32.send_ref), channel_id=1, source_target_pairs={{0,128},{128,0},{1,129},{129,1},{2,130},{130,2},{3,131},{131,3},{4... | collective-permute-start | bytes 405512 | tf_op jit(solution)/shard_map/ppermute | solution.py:657
  3.2 1.3 %copy-start.2 = (f32[2,64,256]{2,1,0:T(8,128)S(1)}, f32[2,64,256]{2,1,0:T(8,128)}, u32[]{:S(2)}) copy-start(f32[2,64,256]{2,1,0:T(8,128)} %cap_ref.5) | copy-start | bytes 393220
  3.2 1.3 %collective-permute-start.1 = (f32[32,128]{1,0:T(8,128)S(1)}, f32[32,128]{1,0:T(8,128)S(1)}, u32[]{:S(2)}, u32[]{:S(2)}) collective-permute-start(f32[32,128]{1,0:T(8,128)S(1)} %pack_base.1.base_ref), channel_id=1, source_target_pairs={{0,8},{8,0},{16,24},{24,16},{32,40},{40,32},{48,56},{56,48},{64,72... | collective-permute-start | bytes 49160 | tf_op jit(solution)/shard_map/ppermute | solution.py:662
  4.5 11.4 %collective-permute-start.3 = (f32[304,128]{1,0:T(8,128)S(1)}, f32[304,128]{1,0:T(8,128)S(1)}, u32[]{:S(2)}, u32[]{:S(2)}) collective-permute-start(f32[304,128]{1,0:T(8,128)S(1)} %get-tuple-element.40), channel_id=1, source_target_pairs={{0,0},{8,16},{16,8},{24,32},{32,24},{40,48},{48,40},{56,64},{64,56... | collective-permute-start | bytes 466952 | tf_op jit(solution)/shard_map/ppermute | solution.py:666
  11.8 9.6 %collective-permute-start.2 = (f32[416,128]{1,0:T(8,128)S(1)}, f32[416,128]{1,0:T(8,128)S(1)}, u32[]{:S(2)}, u32[]{:S(2)}) collective-permute-start(f32[416,128]{1,0:T(8,128)S(1)} %get-tuple-element.39), channel_id=1, source_target_pairs={{0,8},{8,0},{16,24},{24,16},{32,40},{40,32},{48,56},{56,48},{64,72... | collective-permute-start | bytes 638984 | tf_op jit(solution)/shard_map/ppermute | solution.py:679
  11.9 9.5 %collective-permute-start.4 = (f32[176,128]{1,0:T(8,128)S(1)}, f32[176,128]{1,0:T(8,128)S(1)}, u32[]{:S(2)}, u32[]{:S(2)}) collective-permute-start(f32[176,128]{1,0:T(8,128)S(1)} %get-tuple-element.41), channel_id=1, source_target_pairs={{0,0},{8,16},{16,8},{24,32},{32,24},{40,48},{48,40},{56,64},{64,56... | collective-permute-start | bytes 270344 | tf_op jit(solution)/shard_map/ppermute | solution.py:678
  15.9 1.3 %collective-permute-start.5 = (f32[32,128]{1,0:T(8,128)S(1)}, f32[32,128]{1,0:T(8,128)S(1)}, u32[]{:S(2)}, u32[]{:S(2)}) collective-permute-start(f32[32,128]{1,0:T(8,128)S(1)} %pack_relay.1), channel_id=1, source_target_pairs={{0,8},{8,0},{16,24},{24,16},{32,40},{40,32},{48,56},{56,48},{64,72... | collective-permute-start | bytes 49160 | tf_op jit(solution)/shard_map/ppermute | solution.py:681
  17.2 3.7 %collective-permute-start.6 = (f32[32,128]{1,0:T(8,128)S(1)}, f32[32,128]{1,0:T(8,128)S(1)}, u32[]{:S(2)}, u32[]{:S(2)}) collective-permute-start(f32[32,128]{1,0:T(8,128)S(1)} %pack_shares.1), channel_id=1, source_target_pairs={{0,128},{128,0},{1,129},{129,1},{2,130},{130,2},{3,131},{131,3},{4... | collective-permute-start | bytes 49160 | tf_op jit(solution)/shard_map/ppermute | solution.py:683
  22.0 6.9 %collective-permute-start.7 = (f32[272,128]{1,0:T(8,128)S(1)}, f32[272,128]{1,0:T(8,128)S(1)}, u32[]{:S(2)}, u32[]{:S(2)}) collective-permute-start(f32[272,128]{1,0:T(8,128)S(1)} %get-tuple-element.56), channel_id=1, source_target_pairs={{0,1},{1,0},{2,3},{3,2},{4,5},{5,4},{6,7},{7,6},{8,9},{9,8},{10,11... | collective-permute-start | bytes 417800 | tf_op jit(solution)/shard_map/ppermute | solution.py:688
  22.2 9.0 %collective-permute-start.8 = (f32[272,128]{1,0:T(8,128)S(1)}, f32[272,128]{1,0:T(8,128)S(1)}, u32[]{:S(2)}, u32[]{:S(2)}) collective-permute-start(f32[272,128]{1,0:T(8,128)S(1)} %get-tuple-element.57), channel_id=1, source_target_pairs={{0,0},{1,2},{2,1},{3,4},{4,3},{5,6},{6,5},{7,7},{8,8},{9,10},{10,9... | collective-permute-start | bytes 417800 | tf_op jit(solution)/shard_map/ppermute | solution.py:689

commit v8 on v7

--- a/solution.py
+++ b/solution.py
@@ -54,7 +54,7 @@
     return pl.ds(8 * g, 8)
 
 
-def pack_kernel(via_ref, packed_ref, send_ref):
+def pack_kernel(via_ref, packed_ref, send_ref, total_ref):
     later = lax.axis_index("die").astype(F32)
     total = jnp.zeros((8, 128), F32)
     for v in range(VIAS):
@@ -66,7 +66,7 @@
         both = parts[0] + parts[1]
         send_ref[v] = both + later * parts[0]
         total = total + both
-    send_ref[VIAS] = total
+    total_ref[...] = total
 
 
 def spread_nets(ref):
@@ -102,13 +102,13 @@
 LATE = 22
 
 
-def base_kernel(bump_ref, sheet_ref, start_ref, send_ref, base_ref):
+def base_kernel(bump_ref, sheet_ref, start_ref, total_ref, got_ref, base_ref):
     lane, sub = lane_iota(), sub_iota()
     bump = jnp.zeros((8, 128), F32)
     column = lane % 64 - 16
     for k in range(4):
         bump = jnp.where((column // 8 == k) & (sub * 8 + column % 8 == bump_ref[0:1, k : k + 1]), 1.0, bump)
-    for part, value in enumerate([spread_nets(sheet_ref), spread_nets(start_ref), bump, send_ref[VIAS]]):
+    for part, value in enumerate([spread_nets(sheet_ref), spread_nets(start_ref), bump, total_ref[...] + got_ref[...]]):
         base_ref[rows(part), :] = value
 
 
@@ -132,13 +132,6 @@
     for part in range(BASE):
         a, b = between_ref[rows(EARLY + part), :], between_ref[rows(EARLY + BASE + part), :]
         relay_ref[rows(part), :] = jnp.where(even, b, a)
-
-
-def shares_kernel(first_ref, between_ref, relayed_ref, shares_ref):
-    shares_ref[rows(0), :] = first_ref[rows(3), :]
-    for slot in range(2):
-        shares_ref[rows(1 + slot), :] = between_ref[rows(EARLY + BASE * slot + 3), :]
-    shares_ref[rows(3), :] = relayed_ref[rows(3), :]
 
 
 def spread_matrix(height, width):
@@ -190,8 +183,8 @@
 
 
 def place_kernel(
-    packed_ref, send_ref, got_ref, cells_ref, load_cells_ref, loads_ref, spread_ref, counts_ref, early_ref,
-    field_ref, even_ref, odd_ref, arriving_ref, values_ref,
+    packed_ref, got_ref, cells_ref, load_cells_ref, loads_ref, spread_ref, counts_ref,
+    field_ref, even_ref, odd_ref, values_ref,
 ):
     lane = lane_iota()
     later = lax.axis_index("die").astype(F32)
@@ -201,7 +194,7 @@
         (VIA_RESIST * (3.0 - 2.0 * later), VIA_RESIST * (3.0 - 2.0 * later), VIA_RESIST),
     )
     size = (8 * VIAS, 128)
-    first, second, got = packed_ref[0].reshape(size), packed_ref[1].reshape(size), got_ref[0:VIAS].reshape(size)
+    first, second, got = packed_ref[0].reshape(size), packed_ref[1].reshape(size), got_ref[...].reshape(size)
     for d in range(2):
         mixed = weights[d][0] * first + weights[d][1] * second + weights[d][2] * got
         wide = jnp.dot(halves(mixed), spread_ref[...], preferred_element_type=F32)
@@ -230,9 +223,6 @@
 
     lax.fori_loop(0, 4, add, 0)
 
-    arriving_ref[...] = send_ref[VIAS] + got_ref[VIAS]
-    for g in range(EARLY):
-        even_ref[rows(LATE + g), :] = early_ref[rows(g), :]
     sender = RowSender(even, even_ref, odd_ref)
     for d in range(2):
         for half in range(2):
@@ -270,16 +260,17 @@
     return [own(g) for g in range(8)] + [low[0], low[1], high[1], high[0]]
 
 
-def readers(even, below, above, within_ref, between_ref, late_ref):
-    def make(inside, near, skip, far_ref):
+def readers(even, below, above, early_ref, between_ref, within_ref, late_ref):
+    def make(inside, near, near_ref, far_ref):
         def read(g):
-            value = jnp.where(near, within_ref[rows(skip + g), :], far_ref[rows(g), :])
+            value = jnp.where(near, near_ref[rows(g), :], far_ref[rows(g), :])
             return value if inside is None else jnp.where(inside, value, 0.0)
         return read
 
     odd = jnp.logical_not(even)
     return tuple(
-        (make(inside, near, LATE, between_ref), make(inside, near, 0, late_ref)) for inside, near in ((below, even), (above, odd))
+        (make(inside, near, early_ref, between_ref), make(inside, near, within_ref, late_ref))
+        for inside, near in ((below, even), (above, odd))
     )
 
 
@@ -287,14 +278,14 @@
 
 
 def strip_kernel(
-    sheet_ref, cap_ref, drop_ref, counts_ref, field_ref, base_ref, arriving_ref, first_ref, between_ref,
-    within_ref, late_ref, relayed_ref, shares_ref, even_ref, odd_ref, wide_ref,
+    sheet_ref, cap_ref, drop_ref, counts_ref, field_ref, base_ref, first_ref, early_ref, between_ref,
+    within_ref, late_ref, relayed_ref, even_ref, odd_ref, wide_ref,
 ):
     lane = lane_iota()
     within = lane % 16
     row, last = lax.axis_index("row"), (lax.axis_size("row") - 1)
     even = row % 2 == 0
-    below, above = readers(even, None, None, within_ref, between_ref, late_ref)
+    below, above = readers(even, None, None, early_ref, between_ref, within_ref, late_ref)
     even_col = lax.axis_index("col") % 2 == 0
 
     own = (lane % 64 >= 16) & (lane % 64 < 48)
@@ -306,20 +297,18 @@
             out.append(jnp.where(own, moved, 0.0))
         return out
 
-    def block(ref, start, share):
-        parts = [ref[rows(start + f), :] for f in range(BASE)]
-        parts[3] = parts[3] + shares_ref[rows(share), :]
-        return parts
+    def block(ref, start):
+        return [ref[rows(start + f), :] for f in range(BASE)]
 
     def choose(a, b, inside):
         return [jnp.where(inside, jnp.where(even, x, y), 0.0) for x, y in zip(a, b)]
 
-    partner = block(first_ref, 0, 0)
-    between = [block(between_ref, EARLY + BASE * slot, 1 + slot) for slot in range(2)]
-    relayed = block(relayed_ref, 0, 3)
+    partner = block(first_ref, 0)
+    between = [block(between_ref, EARLY + BASE * slot) for slot in range(2)]
+    relayed = block(relayed_ref, 0)
     groups = []
     for g, parts in enumerate([
-        [base_ref[rows(f), :] for f in range(3)] + [arriving_ref[...]],
+        block(base_ref, 0),
         choose(partner, between[0], row < last),
         choose(relayed, between[1], row + 2 <= last),
         choose(between[0], relayed, row >= 2),
@@ -389,12 +378,12 @@
 
 
 def assemble_kernel(
-    sheet_ref, cap_ref, drop_ref, counts_ref, field_ref, within_ref, between_ref, late_ref,
+    sheet_ref, cap_ref, drop_ref, counts_ref, field_ref, early_ref, between_ref, within_ref, late_ref,
     s_ref, x_ref, c_ref, k_ref, one_ref, two_ref, up_ref, down_ref, left_ref, right_ref, diag_ref, spread_ref,
 ):
     row, last = lax.axis_index("row"), (lax.axis_size("row") - 1)
     sub, lane = sub_iota(256), lax.broadcasted_iota(jnp.int32, (8, 256), 1)
-    below, above = readers(row % 2 == 0, row < last, row > 0, within_ref, between_ref, late_ref)
+    below, above = readers(row % 2 == 0, row < last, row > 0, early_ref, between_ref, within_ref, late_ref)
 
     def both(own, kind, d, n):
         sides = [column_groups(lambda g: own(half, g), below, above, kind, d, half, n) for half in range(2)]
@@ -632,7 +621,7 @@
 
 LONG = pl.CostEstimate(flops=10**9, bytes_accessed=10**7, transcendentals=0)
 NONE = pl.CostEstimate(flops=0, bytes_accessed=0, transcendentals=0)
-HINTS = {"spread_cells": NONE, "pack_early": NONE, "place_vias": LONG, "pack_relay": LONG}
+HINTS = {"spread_cells": NONE, "pack_early": NONE, "place_vias": LONG, "pack_relay": LONG, "pack_base": LONG}
 
 
 def arr(*shape, dtype=F32):
@@ -653,46 +642,46 @@
     col_count = lax.axis_size("col")
     others = [(0, 1), (1, 0)]
 
-    packed, send = call(pack_kernel, "pack_vias", (arr(2, VIAS, 8, 128), arr(VIAS + 1, 8, 128)), spec(1))(via_current)
-    got = lax.ppermute(send, "die", others)
     def buffer(count):
         return arr(8 * count, 128)
 
-    base = call(base_kernel, "pack_base", (buffer(BASE),), spec(4))(bump_cell, base_sheet, base_start, send)[0]
+    packed, send, total = call(pack_kernel, "pack_vias", (arr(2, VIAS, 8, 128), arr(VIAS, 8, 128), buffer(1)), spec(1))(via_current)
+    other = lax.ppermute(total, "die", others)
+    got = lax.ppermute(send, "die", others)
+    base = call(base_kernel, "pack_base", (buffer(BASE),), spec(5))(bump_cell, base_sheet, base_start, total, other)[0]
     first = lax.ppermute(base, "row", swaps(row_count, 0))
     early, between = call(chip_kernel, "pack_early", (buffer(EARLY), buffer(EARLY + 2 * BASE)), spec(5))(
         base, first, sheet_res, capacity, drop_start
     )
     between = lax.ppermute(between, "row", swaps(row_count, 1))
+    early = lax.ppermute(early, "row", swaps(row_count, 0))
     cells, load_cells, loads, spread, counts = call(
         prepare_kernel, "spread_cells",
         (arr(4, VIAS, 8, 128), arr(4, 8, 128), arr(4, 4, 8, 128), arr(256, 1024, dtype=jnp.bfloat16), arr(4, 64, 128)),
         spec(3),
     )(via_cell, load_cell, load_current)
 
-    field, even, odd, arriving = call(
-        place_kernel, "place_vias", (arr(4, 4, 64, 128), buffer(LATE + EARLY), buffer(LATE), buffer(1)),
-        spec(9), [pltpu.VMEM((4, 4, VIAS, 8, 128), F32)],
-    )(packed, send, got, cells, load_cells, loads, spread, counts, early)
+    field, even, odd = call(
+        place_kernel, "place_vias", (arr(4, 4, 64, 128), buffer(LATE), buffer(LATE)),
+        spec(7), [pltpu.VMEM((4, 4, VIAS, 8, 128), F32)],
+    )(packed, got, cells, load_cells, loads, spread, counts)
 
     late = lax.ppermute(odd, "row", swaps(row_count, 1))
     within = lax.ppermute(even, "row", swaps(row_count, 0))
     relay = call(relay_kernel, "pack_relay", (buffer(BASE),), spec(1))(between)[0]
     relayed = lax.ppermute(relay, "row", swaps(row_count, 0))
-    shares = call(shares_kernel, "pack_shares", (buffer(4),), spec(3))(first, between, relayed)[0]
-    shares = lax.ppermute(shares, "die", others)
 
     even, odd, wide = call(
-        strip_kernel, "column_strips", (buffer(COL_GROUPS), buffer(COL_GROUPS), arr(200, 128)), spec(13)
-    )(sheet_res, capacity, drop_start, counts, field, base, arriving, first, between, within, late, relayed, shares)
+        strip_kernel, "column_strips", (buffer(COL_GROUPS), buffer(COL_GROUPS), arr(200, 128)), spec(12)
+    )(sheet_res, capacity, drop_start, counts, field, base, first, early, between, within, late, relayed)
     even = lax.ppermute(even, "col", swaps(col_count, 0))
     odd = lax.ppermute(odd, "col", swaps(col_count, 1))
 
     image, pair = arr(4, 96, 256), arr(2, 96, 256)
     parts = call(
         assemble_kernel, "assemble",
-        (image, image, pair, pair) + (image,) * 7 + (arr(2, 256, 384, dtype=jnp.bfloat16),), spec(8),
-    )(sheet_res, capacity, drop_start, counts, field, within, between, late)
+        (image, image, pair, pair) + (image,) * 7 + (arr(2, 256, 384, dtype=jnp.bfloat16),), spec(9),
+    )(sheet_res, capacity, drop_start, counts, field, early, between, within, late)
 
     ext = pltpu.VMEM((96, 384), F32)
     scratch = [ext, ext, pltpu.VMEM((2, 96, 384), F32), pltpu.VMEM((4, 40, 384), F32)] + [ext] * 8

time: 39.3 us -> 43.5 us (1.11)
  waiting for transfers between devices: 6.86 us -> 10.7 us
  starting transfers between devices: 17.7 us -> 18.3 us
    ppermute x1, waiting for transfers between devices: 0.46 us -> 4.47 us  [per_device(): late = lax.ppermute(odd, 'row', swaps(row_count, 1))]
    ppermute x1 -> x2, waiting for transfers between devices: 2.54 us -> 1.58 us  [the longest x1 1.57 us: per_device(): other = lax.ppermute(total, 'die', others)]
    ppermute x1, waiting for transfers between devices: 0.41 us -> 1.17 us  [per_device(): first = lax.ppermute(base, 'row', swaps(row_count, 0))]
    ppermute x1, starting transfers between devices: 0.09 us -> 0.56 us  [per_device(): within = lax.ppermute(even, 'row', swaps(row_count, 0))]
    ppermute x1 -> x2, starting transfers between devices: 1.2 us -> 1.01 us  [the longest x1 0.91 us: per_device(): other = lax.ppermute(total, 'die', others)]
    pallas_call x4 -> x3, Pallas kernels: 2.4 us -> 2.4 us  [the longest x1 2.06 us: per_device(): call(place_kernel, 'place_vias', (arr(4, 4, 64, 128), buffer(LATE), buffe...]
  transfers between devices with their start and end apart: 9 -> 10, of which waited for: 5 -> 5; matrix products, arithmetic and copies ran while one was open for 0% -> 0% of each run, Pallas kernels for 9% -> 8%
where the time goes in v8:
time: 43.5 us; the launch traced here: 43.2 us
  starting transfers between devices  18.3 us (42%)
  Pallas kernels  12.1 us (28%)
  waiting for transfers between devices  10.7 us (25%)
  local copies, waits for them, and re-layouts  1.26 us (3%)
  between operations  0.84 us (2%)
    pallas_call x1, Pallas kernels, per_device(): call(solve_kernel, 'solve', (arr(2, 2, 64, 256), arr(2, 8, 32)), spec(15)...  7.58 us
    ppermute x1, starting transfers between devices, per_device(): odd = lax.ppermute(odd, 'col', swaps(col_count, 1))  5.92 us
    ppermute x1, starting transfers between devices, per_device(): between = lax.ppermute(between, 'row', swaps(row_count, 1))  5.52 us
    ppermute x1, waiting for transfers between devices, per_device(): late = lax.ppermute(odd, 'row', swaps(row_count, 1))  4.47 us
    ppermute x1, starting transfers between devices, per_device(): late = lax.ppermute(odd, 'row', swaps(row_count, 1))  3.66 us
    ppermute x1, waiting for transfers between devices, per_device(): odd = lax.ppermute(odd, 'col', swaps(col_count, 1))  2.28 us
    pallas_call x1, Pallas kernels, per_device(): call(place_kernel, 'place_vias', (arr(4, 4, 64, 128), buffer(LATE), buffe...  2.06 us
    ppermute x1, waiting for transfers between devices, per_device(): other = lax.ppermute(total, 'die', others)  1.57 us
  transfers between devices with their start and end apart: 10, of which 5 were waited for; matrix products, arithmetic and copies ran while one was open for 0% of the time, Pallas kernels for 8%

profile of v8, /device:TPU:102, one launch (start us, length us, event | category | flops | bytes accessed | tf_op | source)
XLA Modules:
  0.0 43.2 jit_solution(18059476793856218564)
XLA Ops:
  0.6 1.2 %copy-done.3 = f32[2,2,2,32,8,32]{5,4,3,2,1,0:T(8,128)S(1)} copy-done((f32[2,2,2,32,8,32]{5,4,3,2,1,0:T(8,128)S(1)}, f32[2,2,2,32,8,32]{5,4,3,2,1,0:T(8,128)}, u32[]{:S(2)}) %copy-start.3) | copy-done | bytes 262168
  1.9 0.3 pack_vias.1
  2.1 0.9 %collective-permute-start.1 = (f32[8,128]{1,0:T(8,128)S(1)}, f32[8,128]{1,0:T(8,128)S(1)}, u32[]{:S(2)}, u32[]{:S(2)}) collective-permute-start(f32[8,128]{1,0:T(8,128)S(1)} %get-tuple-element.38.total_ref), channel_id=1, source_target_pairs={{0,128},{128,0},{1,129},{129,1},{2,130},{130,2},{3,131},{131,3},{4... | collective-permute-start | bytes 12296 | tf_op jit(solution)/shard_map/ppermute | solution.py:649
  3.1 1.2 %collective-permute-start = (f32[32,8,128]{2,1,0:T(8,128)S(1)}, f32[32,8,128]{2,1,0:T(8,128)S(1)}, u32[]{:S(2)}, u32[]{:S(2)}) collective-permute-start(f32[32,8,128]{2,1,0:T(8,128)S(1)} %get-tuple-element.32), channel_id=1, source_target_pairs={{0,128},{128,0},{1,129},{129,1},{2,130},{130,2},{3,131},{131,3},{4... | collective-permute-start | bytes 393224 | tf_op jit(solution)/shard_map/ppermute | solution.py:650
  4.3 1.6 %collective-permute-done.1.got_ref = f32[8,128]{1,0:T(8,128)S(1)} collective-permute-done((f32[8,128]{1,0:T(8,128)S(1)}, f32[8,128]{1,0:T(8,128)S(1)}, u32[]{:S(2)}, u32[]{:S(2)}) %collective-permute-start.1) | collective-permute-done | bytes 4128 | tf_op jit(solution)/shard_map/ppermute | solution.py:649
  5.9 0.1 pack_base.1.base_ref
  6.0 0.0 copy-start.5
  6.0 0.1 collective-permute-start.2
  6.1 1.2 %collective-permute-done.2.got_ref.first_ref = f32[32,128]{1,0:T(8,128)S(1)} collective-permute-done((f32[32,128]{1,0:T(8,128)S(1)}, f32[32,128]{1,0:T(8,128)S(1)}, u32[]{:S(2)}, u32[]{:S(2)}) %collective-permute-start.2) | collective-permute-done | bytes 16416 | tf_op jit(solution)/shard_map/ppermute | solution.py:652
  7.3 5.5 %collective-permute-start.4 = (f32[304,128]{1,0:T(8,128)S(1)}, f32[304,128]{1,0:T(8,128)S(1)}, u32[]{:S(2)}, u32[]{:S(2)}) collective-permute-start(f32[304,128]{1,0:T(8,128)S(1)} %get-tuple-element.40), channel_id=1, source_target_pairs={{0,0},{8,16},{16,8},{24,32},{32,24},{40,48},{48,40},{56,64},{64,56... | collective-permute-start | bytes 466952 | tf_op jit(solution)/shard_map/ppermute | solution.py:656
  12.9 0.7 %spread_cells.1 = (f32[4,32,8,128]{3,2,1,0:T(8,128)S(1)}, f32[4,8,128]{2,1,0:T(8,128)S(1)}, f32[4,4,8,128]{3,2,1,0:T(8,128)S(1)}, bf16[256,1024]{1,0:T(8,128)(2,1)S(1)}, f32[4,64,128]{2,1,0:T(8,128)S(1)}) custom-call(s32[2,32,8,32]{3,2,1,0:T(8,128)S(1)} %copy-done.4, s32[2,8,32]{2,1,0:T(8,128)S(1)} %copy-done.6, f32[2,2,2,8,32]{4,3,2,1,0:T(8,128)S(1)} %copy-done.5), custom_call_target="tpu_custom_call" | custom-call | tf_op jit(solution)/shard_map/spread_cells/pallas_call | solution.py:658
  13.6 0.1 collective-permute-start.3
  13.7 2.1 %place_vias.1 = (f32[4,4,64,128]{3,2,1,0:T(8,128)S(1)}, f32[176,128]{1,0:T(8,128)S(1)}, f32[176,128]{1,0:T(8,128)S(1)}) custom-call(f32[2,32,8,128]{3,2,1,0:T(8,128)S(1)} %get-tuple-element.31.packed_ref, f32[32,8,128]{2,1,0:T(8,128)S(1)} %collective-permute-done.got_ref, f32[4,32,8,128]{3,2,1,0:T(8,128)S(1)} %get-tuple-element.33.cells_ref, ...), custom_call_target="tpu_custom_call" | custom-call | flops 1000000000 | bytes 10000000 | tf_op jit(solution)/shard_map/place_vias/pallas_call | solution.py:664
  15.8 0.6 %collective-permute-start.5 = (f32[176,128]{1,0:T(8,128)S(1)}, f32[176,128]{1,0:T(8,128)S(1)}, u32[]{:S(2)}, u32[]{:S(2)}) collective-permute-start(f32[176,128]{1,0:T(8,128)S(1)} %get-tuple-element.41), channel_id=1, source_target_pairs={{0,8},{8,0},{16,24},{24,16},{32,40},{40,32},{48,56},{56,48},{64,72... | collective-permute-start | bytes 270344 | tf_op jit(solution)/shard_map/ppermute | solution.py:670
  16.4 3.7 %collective-permute-start.6 = (f32[176,128]{1,0:T(8,128)S(1)}, f32[176,128]{1,0:T(8,128)S(1)}, u32[]{:S(2)}, u32[]{:S(2)}) collective-permute-start(f32[176,128]{1,0:T(8,128)S(1)} %get-tuple-element.42), channel_id=1, source_target_pairs={{0,0},{8,16},{16,8},{24,32},{32,24},{40,48},{48,40},{56,64},{64,56... | collective-permute-start | bytes 270344 | tf_op jit(solution)/shard_map/ppermute | solution.py:669
  20.1 0.1 collective-permute-start.7
  20.2 1.2 %collective-permute-done.7.relayed_ref = f32[32,128]{1,0:T(8,128)S(1)} collective-permute-done((f32[32,128]{1,0:T(8,128)S(1)}, f32[32,128]{1,0:T(8,128)S(1)}, u32[]{:S(2)}, u32[]{:S(2)}) %collective-permute-start.7) | collective-permute-done | bytes 16416 | tf_op jit(solution)/shard_map/ppermute | solution.py:672
  21.3 4.5 %collective-permute-done.6.late_ref = f32[176,128]{1,0:T(8,128)S(1)} collective-permute-done((f32[176,128]{1,0:T(8,128)S(1)}, f32[176,128]{1,0:T(8,128)S(1)}, u32[]{:S(2)}, u32[]{:S(2)}) %collective-permute-start.6) | collective-permute-done | bytes 90144 | tf_op jit(solution)/shard_map/ppermute | solution.py:669
  25.8 0.6 %column_strips.1 = (f32[272,128]{1,0:T(8,128)S(1)}, f32[272,128]{1,0:T(8,128)S(1)}, f32[200,128]{1,0:T(8,128)S(1)}) custom-call(f32[2,2,64,256]{3,2,1,0:T(8,128)S(1)} %copy-done, f32[2,64,256]{2,1,0:T(8,128)S(1)} %copy-done.2, f32[2,2,64,256]{3,2,1,0:T(8,128)S(1)} %copy-done.1, f32[4,64,128]{2,1,0:T(8,128)S(1)} %get-tuple-element.30.counts_ref, ...), custom_call_target="tpu_custom_call" | custom-call | tf_op jit(solution)/shard_map/column_strips/pallas_call | solution.py:674
  26.4 0.2 collective-permute-start.8
  26.6 5.9 %collective-permute-start.9 = (f32[272,128]{1,0:T(8,128)S(1)}, f32[272,128]{1,0:T(8,128)S(1)}, u32[]{:S(2)}, u32[]{:S(2)}) collective-permute-start(f32[272,128]{1,0:T(8,128)S(1)} %get-tuple-element.57), channel_id=1, source_target_pairs={{0,0},{1,2},{2,1},{3,4},{4,3},{5,6},{6,5},{7,7},{8,8},{9,10},{10,9... | collective-permute-start | bytes 417800 | tf_op jit(solution)/shard_map/ppermute | solution.py:678
  32.6 0.7 %assemble.1 = (f32[4,96,256]{2,1,0:T(8,128)S(1)}, f32[4,96,256]{2,1,0:T(8,128)S(1)}, f32[2,96,256]{2,1,0:T(8,128)S(1)}, f32[2,96,256]{2,1,0:T(8,128)S(1)}, f32[4...) custom-call(f32[2,2,64,256]{3,2,1,0:T(8,128)S(1)} %copy-done, ...), custom_call_target="tpu_custom_call" | custom-call | tf_op jit(solution)/shard_map/assemble/pallas_call | solution.py:681
  33.3 2.3 %collective-permute-done.9.odd_ref = f32[272,128]{1,0:T(8,128)S(1)} collective-permute-done((f32[272,128]{1,0:T(8,128)S(1)}, f32[272,128]{1,0:T(8,128)S(1)}, u32[]{:S(2)}, u32[]{:S(2)}) %collective-permute-start.9) | collective-permute-done | bytes 139296 | tf_op jit(solution)/shard_map/ppermute | solution.py:678
  35.6 7.6 %solve.1 = (f32[2,2,64,256]{3,2,1,0:T(8,128)}, f32[2,8,32]{2,1,0:T(8,128)}) custom-call(f32[4,96,256]{2,1,0:T(8,128)S(1)} %get-tuple-element.43.s_ref, f32[4,96,256]{2,1,0:T(8,128)S(1)} %get-tuple-element.44.x_ref, f32[2,96,256]{2,1,0:T(8,128)S(1)} %get-tuple-element.45.c_ref, f32[2,96,256]{2,1,0:T(8,128)S(1)} %get-tuple-element.46.k_ref, ...), custom_call_target="tpu_custom_call" | custom-call | tf_op jit(solution)/shard_map/solve/pallas_call | solution.py:688
  (25 shorter events, 0.1 us)
Async XLA Ops:
  0.6 1.2 %copy-start.3 = (f32[2,2,2,32,8,32]{5,4,3,2,1,0:T(8,128)S(1)}, f32[2,2,2,32,8,32]{5,4,3,2,1,0:T(8,128)}, u32[]{:S(2)}) copy-start(f32[2,2,2,32,8,32]{5,4,3,2,1,0:T(8,128)} %via_ref.1) | copy-start | bytes 786436
  1.9 4.0 %copy-start.7 = (f32[2,8,32]{2,1,0:T(8,128)S(1)}, f32[2,8,32]{2,1,0:T(8,128)}, u32[]{:S(2)}) copy-start(f32[2,8,32]{2,1,0:T(8,128)} %sheet_ref.4) | copy-start | bytes 6148
  1.9 4.0 %copy-start.8 = (f32[2,8,32]{2,1,0:T(8,128)S(1)}, f32[2,8,32]{2,1,0:T(8,128)}, u32[]{:S(2)}) copy-start(f32[2,8,32]{2,1,0:T(8,128)} %start_ref.1) | copy-start | bytes 6148
  2.1 3.7 %copy-start.9 = (s32[1,4]{1,0:T(1,128)S(1)}, s32[1,4]{1,0:T(1,128)}, u32[]{:S(2)}) copy-start(s32[1,4]{1,0:T(1,128)} %bump_ref.1) | copy-start | bytes 52
  2.1 3.7 %collective-permute-start.1 = (f32[8,128]{1,0:T(8,128)S(1)}, f32[8,128]{1,0:T(8,128)S(1)}, u32[]{:S(2)}, u32[]{:S(2)}) collective-permute-start(f32[8,128]{1,0:T(8,128)S(1)} %get-tuple-element.38.total_ref), channel_id=1, source_target_pairs={{0,128},{128,0},{1,129},{129,1},{2,130},{130,2},{3,131},{131,3},{4... | collective-permute-start | bytes 12296 | tf_op jit(solution)/shard_map/ppermute | solution.py:649
  3.1 4.2 %copy-start = (f32[2,2,64,256]{3,2,1,0:T(8,128)S(1)}, f32[2,2,64,256]{3,2,1,0:T(8,128)}, u32[]{:S(2)}) copy-start(f32[2,2,64,256]{3,2,1,0:T(8,128)} %sheet_ref.7) | copy-start | bytes 786436
  3.1 4.2 %copy-start.1 = (f32[2,2,64,256]{3,2,1,0:T(8,128)S(1)}, f32[2,2,64,256]{3,2,1,0:T(8,128)}, u32[]{:S(2)}) copy-start(f32[2,2,64,256]{3,2,1,0:T(8,128)} %drop_ref.5) | copy-start | bytes 786436
  3.1 4.2 %copy-start.2 = (f32[2,64,256]{2,1,0:T(8,128)S(1)}, f32[2,64,256]{2,1,0:T(8,128)}, u32[]{:S(2)}) copy-start(f32[2,64,256]{2,1,0:T(8,128)} %cap_ref.5) | copy-start | bytes 393220
  3.1 10.7 %collective-permute-start = (f32[32,8,128]{2,1,0:T(8,128)S(1)}, f32[32,8,128]{2,1,0:T(8,128)S(1)}, u32[]{:S(2)}, u32[]{:S(2)}) collective-permute-start(f32[32,8,128]{2,1,0:T(8,128)S(1)} %get-tuple-element.32), channel_id=1, source_target_pairs={{0,128},{128,0},{1,129},{129,1},{2,130},{130,2},{3,131},{131,3},{4... | collective-permute-start | bytes 393224 | tf_op jit(solution)/shard_map/ppermute | solution.py:650
  6.0 6.9 %copy-start.4 = (s32[2,32,8,32]{3,2,1,0:T(8,128)S(1)}, s32[2,32,8,32]{3,2,1,0:T(8,128)}, u32[]{:S(2)}) copy-start(s32[2,32,8,32]{3,2,1,0:T(8,128)} %cell_ref.1) | copy-start | bytes 196612
  6.0 6.9 %copy-start.5 = (f32[2,2,2,8,32]{4,3,2,1,0:T(8,128)S(1)}, f32[2,2,2,8,32]{4,3,2,1,0:T(8,128)}, u32[]{:S(2)}) copy-start(f32[2,2,2,8,32]{4,3,2,1,0:T(8,128)} %load_ref.1) | copy-start | bytes 24580
  6.0 6.9 %copy-start.6 = (s32[2,8,32]{2,1,0:T(8,128)S(1)}, s32[2,8,32]{2,1,0:T(8,128)}, u32[]{:S(2)}) copy-start(s32[2,8,32]{2,1,0:T(8,128)} %load_cell_ref.1) | copy-start | bytes 6148
  6.0 1.3 %collective-permute-start.2 = (f32[32,128]{1,0:T(8,128)S(1)}, f32[32,128]{1,0:T(8,128)S(1)}, u32[]{:S(2)}, u32[]{:S(2)}) collective-permute-start(f32[32,128]{1,0:T(8,128)S(1)} %pack_base.1.base_ref), channel_id=1, source_target_pairs={{0,8},{8,0},{16,24},{24,16},{32,40},{40,32},{48,56},{56,48},{64,72... | collective-permute-start | bytes 49160 | tf_op jit(solution)/shard_map/ppermute | solution.py:652
  7.3 12.7 %collective-permute-start.4 = (f32[304,128]{1,0:T(8,128)S(1)}, f32[304,128]{1,0:T(8,128)S(1)}, u32[]{:S(2)}, u32[]{:S(2)}) collective-permute-start(f32[304,128]{1,0:T(8,128)S(1)} %get-tuple-element.40), channel_id=1, source_target_pairs={{0,0},{8,16},{16,8},{24,32},{32,24},{40,48},{48,40},{56,64},{64,56... | collective-permute-start | bytes 466952 | tf_op jit(solution)/shard_map/ppermute | solution.py:656
  13.6 6.5 %collective-permute-start.3 = (f32[240,128]{1,0:T(8,128)S(1)}, f32[240,128]{1,0:T(8,128)S(1)}, u32[]{:S(2)}, u32[]{:S(2)}) collective-permute-start(f32[240,128]{1,0:T(8,128)S(1)} %get-tuple-element.39), channel_id=1, source_target_pairs={{0,8},{8,0},{16,24},{24,16},{32,40},{40,32},{48,56},{56,48},{64,72... | collective-permute-start | bytes 368648 | tf_op jit(solution)/shard_map/ppermute | solution.py:657
  15.8 5.5 %collective-permute-start.5 = (f32[176,128]{1,0:T(8,128)S(1)}, f32[176,128]{1,0:T(8,128)S(1)}, u32[]{:S(2)}, u32[]{:S(2)}) collective-permute-start(f32[176,128]{1,0:T(8,128)S(1)} %get-tuple-element.41), channel_id=1, source_target_pairs={{0,8},{8,0},{16,24},{24,16},{32,40},{40,32},{48,56},{56,48},{64,72... | collective-permute-start | bytes 270344 | tf_op jit(solution)/shard_map/ppermute | solution.py:670
  16.4 9.4 %collective-permute-start.6 = (f32[176,128]{1,0:T(8,128)S(1)}, f32[176,128]{1,0:T(8,128)S(1)}, u32[]{:S(2)}, u32[]{:S(2)}) collective-permute-start(f32[176,128]{1,0:T(8,128)S(1)} %get-tuple-element.42), channel_id=1, source_target_pairs={{0,0},{8,16},{16,8},{24,32},{32,24},{40,48},{48,40},{56,64},{64,56... | collective-permute-start | bytes 270344 | tf_op jit(solution)/shard_map/ppermute | solution.py:669
  20.1 1.3 %collective-permute-start.7 = (f32[32,128]{1,0:T(8,128)S(1)}, f32[32,128]{1,0:T(8,128)S(1)}, u32[]{:S(2)}, u32[]{:S(2)}) collective-permute-start(f32[32,128]{1,0:T(8,128)S(1)} %pack_relay.1), channel_id=1, source_target_pairs={{0,8},{8,0},{16,24},{24,16},{32,40},{40,32},{48,56},{56,48},{64,72... | collective-permute-start | bytes 49160 | tf_op jit(solution)/shard_map/ppermute | solution.py:672
  26.4 6.9 %collective-permute-start.8 = (f32[272,128]{1,0:T(8,128)S(1)}, f32[272,128]{1,0:T(8,128)S(1)}, u32[]{:S(2)}, u32[]{:S(2)}) collective-permute-start(f32[272,128]{1,0:T(8,128)S(1)} %get-tuple-element.56), channel_id=1, source_target_pairs={{0,1},{1,0},{2,3},{3,2},{4,5},{5,4},{6,7},{7,6},{8,9},{9,8},{10,11... | collective-permute-start | bytes 417800 | tf_op jit(solution)/shard_map/ppermute | solution.py:677
  26.6 9.0 %collective-permute-start.9 = (f32[272,128]{1,0:T(8,128)S(1)}, f32[272,128]{1,0:T(8,128)S(1)}, u32[]{:S(2)}, u32[]{:S(2)}) collective-permute-start(f32[272,128]{1,0:T(8,128)S(1)} %get-tuple-element.57), channel_id=1, source_target_pairs={{0,0},{1,2},{2,1},{3,4},{4,3},{5,6},{6,5},{7,7},{8,8},{9,10},{10,9... | collective-permute-start | bytes 417800 | tf_op jit(solution)/shard_map/ppermute | solution.py:678

commit v9 on v7

--- a/solution.py
+++ b/solution.py
@@ -640,10 +640,11 @@
 
 
 def swaps(count, offset):
-    partner = list(range(count))
-    for i in range(offset, count - 1, 2):
-        partner[i], partner[i + 1] = i + 1, i
-    return list(enumerate(partner))
+    pairs = []
+    for i in range(offset, count, 2):
+        j = (i + 1) % count
+        pairs += [(i, j), (j, i)]
+    return pairs
 
 
 def per_device(

time: 39.3 us -> 38.3 us (0.975)
  the two profiles are of different devices: /device:TPU:102 before, /device:TPU:2 now
where the time goes in v9:
time: 38.3 us; the launch traced here: 38.1 us
  starting transfers between devices  17.6 us (46%)
  Pallas kernels  12.3 us (32%)
  waiting for transfers between devices  6.19 us (16%)
  local copies, waits for them, and re-layouts  1.26 us (3%)
  between operations  0.8 us (2%)
    pallas_call x1, Pallas kernels, per_device(): call(solve_kernel, 'solve', (arr(2, 2, 64, 256), arr(2, 8, 32)), spec(15)...  7.75 us
    ppermute x1, starting transfers between devices, per_device(): odd = lax.ppermute(odd, 'col', swaps(col_count, 1))  4.95 us
    ppermute x1, starting transfers between devices, per_device(): late = lax.ppermute(odd, 'row', swaps(row_count, 1))  3.31 us
    ppermute x1, starting transfers between devices, per_device(): between = lax.ppermute(between, 'row', swaps(row_count, 1))  2.98 us
    ppermute x1, starting transfers between devices, per_device(): got = lax.ppermute(send, 'die', others)  2.36 us
    ppermute x1, starting transfers between devices, per_device(): even = lax.ppermute(even, 'col', swaps(col_count, 0))  2.31 us
    ppermute x1, waiting for transfers between devices, per_device(): shares = lax.ppermute(shares, 'die', others)  2.3 us
    ppermute x1, waiting for transfers between devices, per_device(): odd = lax.ppermute(odd, 'col', swaps(col_count, 1))  2.29 us
  transfers between devices with their start and end apart: 9, of which 4 were waited for; matrix products, arithmetic and copies ran while one was open for 0% of the time, Pallas kernels for 10%

profile of v9, /device:TPU:2, one launch (start us, length us, event | category | flops | bytes accessed | tf_op | source)
XLA Modules:
  0.0 38.1 jit_solution(18296775336717053868)
XLA Ops:
  0.6 1.2 %copy-done.3 = f32[2,2,2,32,8,32]{5,4,3,2,1,0:T(8,128)S(1)} copy-done((f32[2,2,2,32,8,32]{5,4,3,2,1,0:T(8,128)S(1)}, f32[2,2,2,32,8,32]{5,4,3,2,1,0:T(8,128)}, u32[]{:S(2)}) %copy-start.3) | copy-done | bytes 262168
  1.9 0.3 pack_vias.1
  2.2 0.0 copy-start
  2.2 2.4 %collective-permute-start = (f32[33,8,128]{2,1,0:T(8,128)S(1)}, f32[33,8,128]{2,1,0:T(8,128)S(1)}, u32[]{:S(2)}, u32[]{:S(2)}) collective-permute-start(f32[33,8,128]{2,1,0:T(8,128)S(1)} %get-tuple-element.32.send_ref), channel_id=1, source_target_pairs={{0,128},{128,0},{1,129},{129,1},{2,130},{130,2},{3,131},{131,3},{4... | collective-permute-start | bytes 405512 | tf_op jit(solution)/shard_map/ppermute | solution.py:658
  4.6 0.1 pack_base.1.base_ref
  4.6 0.0 copy-start.2
  4.6 0.1 collective-permute-start.1
  4.8 0.7 %spread_cells.1 = (f32[4,32,8,128]{3,2,1,0:T(8,128)S(1)}, f32[4,8,128]{2,1,0:T(8,128)S(1)}, f32[4,4,8,128]{3,2,1,0:T(8,128)S(1)}, bf16[256,1024]{1,0:T(8,128)(2,1)S(1)}, f32[4,64,128]{2,1,0:T(8,128)S(1)}) custom-call(s32[2,32,8,32]{3,2,1,0:T(8,128)S(1)} %copy-done.4, s32[2,8,32]{2,1,0:T(8,128)S(1)} %copy-done.6, f32[2,2,2,8,32]{4,3,2,1,0:T(8,128)S(1)} %copy-done.5), custom_call_target="tpu_custom_call" | custom-call | tf_op jit(solution)/shard_map/spread_cells/pallas_call | solution.py:668
  5.5 0.4 %collective-permute-done.1.got_ref.first_ref = f32[32,128]{1,0:T(8,128)S(1)} collective-permute-done((f32[32,128]{1,0:T(8,128)S(1)}, f32[32,128]{1,0:T(8,128)S(1)}, u32[]{:S(2)}, u32[]{:S(2)}) %collective-permute-start.1) | collective-permute-done | bytes 16416 | tf_op jit(solution)/shard_map/ppermute | solution.py:663
  6.0 3.0 %collective-permute-start.3 = (f32[304,128]{1,0:T(8,128)S(1)}, f32[304,128]{1,0:T(8,128)S(1)}, u32[]{:S(2)}, u32[]{:S(2)}) collective-permute-start(f32[304,128]{1,0:T(8,128)S(1)} %get-tuple-element.40), channel_id=1, source_target_pairs={{8,16},{16,8},{24,32},{32,24},{40,48},{48,40},{56,64},{64,56},{72,... | collective-permute-start | bytes 466952 | tf_op jit(solution)/shard_map/ppermute | solution.py:667
  9.0 2.0 %place_vias.1 = (f32[4,4,64,128]{3,2,1,0:T(8,128)S(1)}, f32[416,128]{1,0:T(8,128)S(1)}, f32[176,128]{1,0:T(8,128)S(1)}, f32[8,128]{1,0:T(8,128)S(1)}) custom-call(f32[2,32,8,128]{3,2,1,0:T(8,128)S(1)} %get-tuple-element.31.packed_ref, f32[33,8,128]{2,1,0:T(8,128)S(1)} %get-tuple-element.32.send_ref, f32[33,8,128]{2,1,0:T(8,128)S(1)} %collective-permute-done.got_ref, ...), custom_call_target="tpu_custom_call" | custom-call | flops 1000000000 | bytes 10000000 | tf_op jit(solution)/shard_map/place_vias/pallas_call | solution.py:674
  11.0 0.1 collective-permute-start.2
  11.1 3.3 %collective-permute-start.4 = (f32[176,128]{1,0:T(8,128)S(1)}, f32[176,128]{1,0:T(8,128)S(1)}, u32[]{:S(2)}, u32[]{:S(2)}) collective-permute-start(f32[176,128]{1,0:T(8,128)S(1)} %get-tuple-element.41), channel_id=1, source_target_pairs={{8,16},{16,8},{24,32},{32,24},{40,48},{48,40},{56,64},{64,56},{72,... | collective-permute-start | bytes 270344 | tf_op jit(solution)/shard_map/ppermute | solution.py:679
  14.4 0.1 collective-permute-start.5
  14.5 1.2 %collective-permute-done.5.relayed_ref = f32[32,128]{1,0:T(8,128)S(1)} collective-permute-done((f32[32,128]{1,0:T(8,128)S(1)}, f32[32,128]{1,0:T(8,128)S(1)}, u32[]{:S(2)}, u32[]{:S(2)}) %collective-permute-start.5) | collective-permute-done | bytes 16416 | tf_op jit(solution)/shard_map/ppermute | solution.py:682
  15.7 1.4 %collective-permute-start.6 = (f32[32,128]{1,0:T(8,128)S(1)}, f32[32,128]{1,0:T(8,128)S(1)}, u32[]{:S(2)}, u32[]{:S(2)}) collective-permute-start(f32[32,128]{1,0:T(8,128)S(1)} %pack_shares.1), channel_id=1, source_target_pairs={{0,128},{128,0},{1,129},{129,1},{2,130},{130,2},{3,131},{131,3},{4... | collective-permute-start | bytes 49160 | tf_op jit(solution)/shard_map/ppermute | solution.py:684
  17.2 2.3 %collective-permute-done.6.shares_ref = f32[32,128]{1,0:T(8,128)S(1)} collective-permute-done((f32[32,128]{1,0:T(8,128)S(1)}, f32[32,128]{1,0:T(8,128)S(1)}, u32[]{:S(2)}, u32[]{:S(2)}) %collective-permute-start.6) | collective-permute-done | bytes 16416 | tf_op jit(solution)/shard_map/ppermute | solution.py:684
  19.5 0.0 collective-permute-done.4.late_ref
  19.5 0.6 %column_strips.1 = (f32[272,128]{1,0:T(8,128)S(1)}, f32[272,128]{1,0:T(8,128)S(1)}, f32[200,128]{1,0:T(8,128)S(1)}) custom-call(f32[2,2,64,256]{3,2,1,0:T(8,128)S(1)} %copy-done, f32[2,64,256]{2,1,0:T(8,128)S(1)} %copy-done.2, f32[2,2,64,256]{3,2,1,0:T(8,128)S(1)} %copy-done.1, f32[4,64,128]{2,1,0:T(8,128)S(1)} %get-tuple-element.30.counts_ref, ...), custom_call_target="tpu_custom_call" | custom-call | tf_op jit(solution)/shard_map/column_strips/pallas_call | solution.py:686
  20.1 2.3 %collective-permute-start.7 = (f32[272,128]{1,0:T(8,128)S(1)}, f32[272,128]{1,0:T(8,128)S(1)}, u32[]{:S(2)}, u32[]{:S(2)}) collective-permute-start(f32[272,128]{1,0:T(8,128)S(1)} %get-tuple-element.56), channel_id=1, source_target_pairs={{0,1},{1,0},{2,3},{3,2},{4,5},{5,4},{6,7},{7,6},{8,9},{9,8},{10,11... | collective-permute-start | bytes 417800 | tf_op jit(solution)/shard_map/ppermute | solution.py:689
  22.4 4.9 %collective-permute-start.8 = (f32[272,128]{1,0:T(8,128)S(1)}, f32[272,128]{1,0:T(8,128)S(1)}, u32[]{:S(2)}, u32[]{:S(2)}) collective-permute-start(f32[272,128]{1,0:T(8,128)S(1)} %get-tuple-element.57), channel_id=1, source_target_pairs={{1,2},{2,1},{3,4},{4,3},{5,6},{6,5},{7,0},{0,7},{9,10},{10,9},{11,... | collective-permute-start | bytes 417800 | tf_op jit(solution)/shard_map/ppermute | solution.py:690
  27.3 0.7 %assemble.1 = (f32[4,96,256]{2,1,0:T(8,128)S(1)}, f32[4,96,256]{2,1,0:T(8,128)S(1)}, f32[2,96,256]{2,1,0:T(8,128)S(1)}, f32[2,96,256]{2,1,0:T(8,128)S(1)}, f32[4...) custom-call(f32[2,2,64,256]{3,2,1,0:T(8,128)S(1)} %copy-done, ...), custom_call_target="tpu_custom_call" | custom-call | tf_op jit(solution)/shard_map/assemble/pallas_call | solution.py:693
  28.1 2.3 %collective-permute-done.8.odd_ref = f32[272,128]{1,0:T(8,128)S(1)} collective-permute-done((f32[272,128]{1,0:T(8,128)S(1)}, f32[272,128]{1,0:T(8,128)S(1)}, u32[]{:S(2)}, u32[]{:S(2)}) %collective-permute-start.8) | collective-permute-done | bytes 139296 | tf_op jit(solution)/shard_map/ppermute | solution.py:690
  30.4 7.7 %solve.1 = (f32[2,2,64,256]{3,2,1,0:T(8,128)}, f32[2,8,32]{2,1,0:T(8,128)}) custom-call(f32[4,96,256]{2,1,0:T(8,128)S(1)} %get-tuple-element.42.s_ref, f32[4,96,256]{2,1,0:T(8,128)S(1)} %get-tuple-element.43.x_ref, f32[2,96,256]{2,1,0:T(8,128)S(1)} %get-tuple-element.44.c_ref, f32[2,96,256]{2,1,0:T(8,128)S(1)} %get-tuple-element.45.k_ref, ...), custom_call_target="tpu_custom_call" | custom-call | tf_op jit(solution)/shard_map/solve/pallas_call | solution.py:700
  (24 shorter events, 0.1 us)
Async XLA Ops:
  0.6 1.2 %copy-start.3 = (f32[2,2,2,32,8,32]{5,4,3,2,1,0:T(8,128)S(1)}, f32[2,2,2,32,8,32]{5,4,3,2,1,0:T(8,128)}, u32[]{:S(2)}) copy-start(f32[2,2,2,32,8,32]{5,4,3,2,1,0:T(8,128)} %via_ref.1) | copy-start | bytes 786436
  1.9 2.7 %copy-start.7 = (f32[2,8,32]{2,1,0:T(8,128)S(1)}, f32[2,8,32]{2,1,0:T(8,128)}, u32[]{:S(2)}) copy-start(f32[2,8,32]{2,1,0:T(8,128)} %sheet_ref.4) | copy-start | bytes 6148
  1.9 2.7 %copy-start.8 = (f32[2,8,32]{2,1,0:T(8,128)S(1)}, f32[2,8,32]{2,1,0:T(8,128)}, u32[]{:S(2)}) copy-start(f32[2,8,32]{2,1,0:T(8,128)} %start_ref.1) | copy-start | bytes 6148
  1.9 2.7 %copy-start.9 = (s32[1,4]{1,0:T(1,128)S(1)}, s32[1,4]{1,0:T(1,128)}, u32[]{:S(2)}) copy-start(s32[1,4]{1,0:T(1,128)} %bump_ref.1) | copy-start | bytes 52
  1.9 2.9 %copy-start.4 = (s32[2,32,8,32]{3,2,1,0:T(8,128)S(1)}, s32[2,32,8,32]{3,2,1,0:T(8,128)}, u32[]{:S(2)}) copy-start(s32[2,32,8,32]{3,2,1,0:T(8,128)} %cell_ref.1) | copy-start | bytes 196612
  1.9 2.9 %copy-start.5 = (f32[2,2,2,8,32]{4,3,2,1,0:T(8,128)S(1)}, f32[2,2,2,8,32]{4,3,2,1,0:T(8,128)}, u32[]{:S(2)}) copy-start(f32[2,2,2,8,32]{4,3,2,1,0:T(8,128)} %load_ref.1) | copy-start | bytes 24580
  1.9 2.9 %copy-start.6 = (s32[2,8,32]{2,1,0:T(8,128)S(1)}, s32[2,8,32]{2,1,0:T(8,128)}, u32[]{:S(2)}) copy-start(s32[2,8,32]{2,1,0:T(8,128)} %load_cell_ref.1) | copy-start | bytes 6148
  1.9 4.0 %copy-start.1 = (f32[2,2,64,256]{3,2,1,0:T(8,128)S(1)}, f32[2,2,64,256]{3,2,1,0:T(8,128)}, u32[]{:S(2)}) copy-start(f32[2,2,64,256]{3,2,1,0:T(8,128)} %drop_ref.5) | copy-start | bytes 786436
  2.2 3.8 %copy-start = (f32[2,2,64,256]{3,2,1,0:T(8,128)S(1)}, f32[2,2,64,256]{3,2,1,0:T(8,128)}, u32[]{:S(2)}) copy-start(f32[2,2,64,256]{3,2,1,0:T(8,128)} %sheet_ref.7) | copy-start | bytes 786436
  2.2 6.8 %collective-permute-start = (f32[33,8,128]{2,1,0:T(8,128)S(1)}, f32[33,8,128]{2,1,0:T(8,128)S(1)}, u32[]{:S(2)}, u32[]{:S(2)}) collective-permute-start(f32[33,8,128]{2,1,0:T(8,128)S(1)} %get-tuple-element.32.send_ref), channel_id=1, source_target_pairs={{0,128},{128,0},{1,129},{129,1},{2,130},{130,2},{3,131},{131,3},{4... | collective-permute-start | bytes 405512 | tf_op jit(solution)/shard_map/ppermute | solution.py:658
  4.6 1.3 %copy-start.2 = (f32[2,64,256]{2,1,0:T(8,128)S(1)}, f32[2,64,256]{2,1,0:T(8,128)}, u32[]{:S(2)}) copy-start(f32[2,64,256]{2,1,0:T(8,128)} %cap_ref.5) | copy-start | bytes 393220
  4.6 1.3 %collective-permute-start.1 = (f32[32,128]{1,0:T(8,128)S(1)}, f32[32,128]{1,0:T(8,128)S(1)}, u32[]{:S(2)}, u32[]{:S(2)}) collective-permute-start(f32[32,128]{1,0:T(8,128)S(1)} %pack_base.1.base_ref), channel_id=1, source_target_pairs={{0,8},{8,0},{16,24},{24,16},{32,40},{40,32},{48,56},{56,48},{64,72... | collective-permute-start | bytes 49160 | tf_op jit(solution)/shard_map/ppermute | solution.py:663
  6.0 8.5 %collective-permute-start.3 = (f32[304,128]{1,0:T(8,128)S(1)}, f32[304,128]{1,0:T(8,128)S(1)}, u32[]{:S(2)}, u32[]{:S(2)}) collective-permute-start(f32[304,128]{1,0:T(8,128)S(1)} %get-tuple-element.40), channel_id=1, source_target_pairs={{8,16},{16,8},{24,32},{32,24},{40,48},{48,40},{56,64},{64,56},{72,... | collective-permute-start | bytes 466952 | tf_op jit(solution)/shard_map/ppermute | solution.py:667
  11.0 8.4 %collective-permute-start.2 = (f32[416,128]{1,0:T(8,128)S(1)}, f32[416,128]{1,0:T(8,128)S(1)}, u32[]{:S(2)}, u32[]{:S(2)}) collective-permute-start(f32[416,128]{1,0:T(8,128)S(1)} %get-tuple-element.39), channel_id=1, source_target_pairs={{0,8},{8,0},{16,24},{24,16},{32,40},{40,32},{48,56},{56,48},{64,72... | collective-permute-start | bytes 638984 | tf_op jit(solution)/shard_map/ppermute | solution.py:680
  11.1 8.3 %collective-permute-start.4 = (f32[176,128]{1,0:T(8,128)S(1)}, f32[176,128]{1,0:T(8,128)S(1)}, u32[]{:S(2)}, u32[]{:S(2)}) collective-permute-start(f32[176,128]{1,0:T(8,128)S(1)} %get-tuple-element.41), channel_id=1, source_target_pairs={{8,16},{16,8},{24,32},{32,24},{40,48},{48,40},{56,64},{64,56},{72,... | collective-permute-start | bytes 270344 | tf_op jit(solution)/shard_map/ppermute | solution.py:679
  14.4 1.3 %collective-permute-start.5 = (f32[32,128]{1,0:T(8,128)S(1)}, f32[32,128]{1,0:T(8,128)S(1)}, u32[]{:S(2)}, u32[]{:S(2)}) collective-permute-start(f32[32,128]{1,0:T(8,128)S(1)} %pack_relay.1), channel_id=1, source_target_pairs={{0,8},{8,0},{16,24},{24,16},{32,40},{40,32},{48,56},{56,48},{64,72... | collective-permute-start | bytes 49160 | tf_op jit(solution)/shard_map/ppermute | solution.py:682
  15.7 3.7 %collective-permute-start.6 = (f32[32,128]{1,0:T(8,128)S(1)}, f32[32,128]{1,0:T(8,128)S(1)}, u32[]{:S(2)}, u32[]{:S(2)}) collective-permute-start(f32[32,128]{1,0:T(8,128)S(1)} %pack_shares.1), channel_id=1, source_target_pairs={{0,128},{128,0},{1,129},{129,1},{2,130},{130,2},{3,131},{131,3},{4... | collective-permute-start | bytes 49160 | tf_op jit(solution)/shard_map/ppermute | solution.py:684
  20.1 8.0 %collective-permute-start.7 = (f32[272,128]{1,0:T(8,128)S(1)}, f32[272,128]{1,0:T(8,128)S(1)}, u32[]{:S(2)}, u32[]{:S(2)}) collective-permute-start(f32[272,128]{1,0:T(8,128)S(1)} %get-tuple-element.56), channel_id=1, source_target_pairs={{0,1},{1,0},{2,3},{3,2},{4,5},{5,4},{6,7},{7,6},{8,9},{9,8},{10,11... | collective-permute-start | bytes 417800 | tf_op jit(solution)/shard_map/ppermute | solution.py:689
  22.4 8.0 %collective-permute-start.8 = (f32[272,128]{1,0:T(8,128)S(1)}, f32[272,128]{1,0:T(8,128)S(1)}, u32[]{:S(2)}, u32[]{:S(2)}) collective-permute-start(f32[272,128]{1,0:T(8,128)S(1)} %get-tuple-element.57), channel_id=1, source_target_pairs={{1,2},{2,1},{3,4},{4,3},{5,6},{6,5},{7,0},{0,7},{9,10},{10,9},{11,... | collective-permute-start | bytes 417800 | tf_op jit(solution)/shard_map/ppermute | solution.py:690

commit v10 on v9

--- a/solution.py
+++ b/solution.py
@@ -19,7 +19,7 @@
 MIDDLE = 0.5 * (UPPER_BOUND + LOWER_BOUND)
 HALF = 0.5 * (UPPER_BOUND - LOWER_BOUND)
 
-GROUPS = 12
+GROUPS = 11
 F32 = jnp.float32
 
 
@@ -267,7 +267,8 @@
 def column_groups(own, below, above, kind, d, half, n):
     low = near_rows(below, kind, d, half, n, False)
     high = near_rows(above, kind, d, half, n, True)
-    return [own(g) for g in range(8)] + [low[0], low[1], high[1], high[0]]
+    both = None if low[1] is None else jnp.where(sub_iota() < 4, low[1], high[1])
+    return [own(g) for g in range(8)] + [low[0], both, high[0]]
 
 
 def readers(even, below, above, within_ref, between_ref, late_ref):
@@ -283,7 +284,7 @@
     )
 
 
-COL_GROUPS = 2 * GROUPS + 10
+COL_GROUPS = 2 * GROUPS + 6
 
 
 def strip_kernel(
@@ -375,7 +376,7 @@
     start = 2 * GROUPS
     quarter = (lane % 64) // 16
     for g in range(5):
-        sheet, drop, one, two, bump = groups[g]
+        sheet, drop, one, two, _ = groups[g]
         left = jnp.where(
             quarter == 1, sheet,
             jnp.where(quarter == 2, roll(drop, 16, 1), jnp.where(quarter == 3, roll(one, 32, 1), roll(two, -16, 1))),
@@ -385,7 +386,13 @@
             jnp.where(quarter == 3, roll(drop, 16, 1), jnp.where(quarter == 1, roll(two, -16, 1), roll(one, -32, 1))),
         )
         put(start + g, left, right)
-        put(start + 5 + g, bump, bump)
+    bumps = []
+    for origin in (16, 32):
+        value = roll(groups[0][4], -origin, 1)
+        for g in range(1, 5):
+            value = jnp.where(lane // 16 == g, roll(groups[g][4], 16 * g - origin, 1), value)
+        bumps.append(value)
+    put(start + 5, *bumps)
 
 
 def assemble_kernel(
@@ -482,7 +489,7 @@
 def needed(halo):
     if halo > 8:
         return list(range(GROUPS))
-    return list(range(8)) + ([8, 11] if halo > 0 else [])
+    return list(range(8)) + ([8, 10] if halo > 0 else [])
 
 
 def solve_kernel(
@@ -508,11 +515,15 @@
     for field in range(5):
         out = []
         for g in range(5):
-            right_shift = (32, 16, 0, 48, 32)[field]
-            left_shift = (-32, -48, 0, -16, -32)[field]
-            group = g + 5 * (field == 4)
-            value = jnp.where(take_right, roll(from_right(start + group), right_shift, 1), wide_ref[rows(5 * field + g), :])
-            out.append(jnp.where(take_left, roll(from_left(start + group), left_shift, 1), value))
+            if field == 4:
+                right, left = roll(from_right(start + 5), 48 - 16 * g, 1), roll(from_left(start + 5), -16 * g, 1)
+                right = jnp.where(lane < 64, right, roll(right, 64, 1))
+                left = jnp.where(lane < 64, left, roll(left, 64, 1))
+            else:
+                right = roll(from_right(start + g), (32, 16, 0, 48)[field], 1)
+                left = roll(from_left(start + g), (-32, -48, 0, -16)[field], 1)
+            value = jnp.where(take_right, right, wide_ref[rows(5 * field + g), :])
+            out.append(jnp.where(take_left, left, value))
         fields.append(jnp.concatenate(out, axis=0))
     solved = base_solve((fields[0], fields[1], (fields[2], fields[3]), fields[4]))
     for t in range(STEPS):
@@ -522,17 +533,17 @@
     for n in range(2):
         base_out_ref[n] = roll(solved[1][0:8], -(64 * n + 16), 1)[:, 0:32]
 
+    sub, sub3 = sub_iota(), sub_iota(384)
+    last = lax.axis_size("row") - 1
+
     def third(part, chunk, g):
         right_ok, left_ok = has_right, has_left
-        if g in (8, 9):
-            right_ok, left_ok = right_ok & (row < (lax.axis_size("row") - 1)), left_ok & (row < (lax.axis_size("row") - 1))
-        if g in (10, 11):
-            right_ok, left_ok = right_ok & (row > 0), left_ok & (row > 0)
+        if g >= 8:
+            inside = {8: row < last, 9: ((sub < 4) & (row < last)) | ((sub >= 4) & (row > 0)), 10: row > 0}[g]
+            right_ok, left_ok = right_ok & inside, left_ok & inside
         right = jnp.where((lane // 16 == chunk) & right_ok, from_right(part * GROUPS + g), 0.0)
         value = jnp.where((lane // 16 == (chunk + 7) % 8) & left_ok, from_left(part * GROUPS + g), right)
         return roll(value, -16 * chunk, 1)
-
-    sub, sub3 = sub_iota(), sub_iota(384)
 
     def above(value, before, index):
         return jnp.where(index == 0, roll(before, 1, 0), roll(value, 1, 0))
@@ -579,7 +590,7 @@
                 state[rows(g), :] = wide(x_ref, g, drop)
                 one = third(1, 4 + i, g)
                 f_ext[0, rows(g), :] = wide(one_ref, g, c_ext[rows(g), pl.ds(256, 128)] * drop + one)
-                if g not in (9, 10):
+                if g != 9:
                     two = jnp.where(lane < 64, roll(one, -11, 1), roll(one, 11, 1))
                     f_ext[1, rows(g), :] = wide(two_ref, g, two)
 
@@ -595,7 +606,9 @@
                         total = total + (
                             link_left[rows(g), :] * roll(value, 1, 1) + link_right[rows(g), :] * roll(value, -1, 1))
                         if k == 0:
-                            spread = jnp.broadcast_to(bound[2 * t + n, pl.ds(base_row(g), 1), :], (8, 384))
+                            spread = jnp.broadcast_to(bound[2 * t + n, pl.ds(39 if g == 10 else g, 1), :], (8, 384))
+                            if g == 9:
+                                spread = jnp.where(sub3 < 4, spread, bound[2 * t + n, pl.ds(38, 1), :])
                             source = f_ext[t, rows(g), :] + k_ext[rows(g), :] * spread
                             if t:
                                 source = source + c_ext[rows(g), :] * value
@@ -607,10 +620,6 @@
 
         for g in range(8):
             out_ref[d, n, rows(g), :] = state[rows(g), pl.ds(0, 256)]
-
-
-def base_row(g):
-    return g if g < 10 else 28 + g
 
 
 def spec(count):
@@ -641,17 +650,23 @@
 
 def swaps(count, offset):
     pairs = []
-    for i in range(offset, count, 2):
-        j = (i + 1) % count
-        pairs += [(i, j), (j, i)]
+    for die in range(2):
+        partner = {}
+        for i in range(offset, count - 1, 2):
+            partner[i], partner[i + 1] = i + 1, i
+        for i in range(count):
+            target = die * count + partner[i] if i in partner else (1 - die) * count + i
+            pairs.append((die * count + i, target))
     return pairs
+
+
+def swap(value, axis, offset):
+    return lax.ppermute(value, ("die", axis), swaps(lax.axis_size(axis), offset))
 
 
 def per_device(
     sheet_res, capacity, drop_start, load_cell, load_current, via_cell, via_current, base_sheet, base_start, bump_cell
 ):
-    row_count = lax.axis_size("row")
-    col_count = lax.axis_size("col")
     others = [(0, 1), (1, 0)]
 
     packed, send = call(pack_kernel, "pack_vias", (arr(2, VIAS, 8, 128), arr(VIAS + 1, 8, 128)), spec(1))(via_current)
@@ -660,11 +675,11 @@
         return arr(8 * count, 128)
 
     base = call(base_kernel, "pack_base", (buffer(BASE),), spec(4))(bump_cell, base_sheet, base_start, send)[0]
-    first = lax.ppermute(base, "row", swaps(row_count, 0))
+    first = swap(base, "row", 0)
     early, between = call(chip_kernel, "pack_early", (buffer(EARLY), buffer(EARLY + 2 * BASE)), spec(5))(
         base, first, sheet_res, capacity, drop_start
     )
-    between = lax.ppermute(between, "row", swaps(row_count, 1))
+    between = swap(between, "row", 1)
     cells, load_cells, loads, spread, counts = call(
         prepare_kernel, "spread_cells",
         (arr(4, VIAS, 8, 128), arr(4, 8, 128), arr(4, 4, 8, 128), arr(256, 1024, dtype=jnp.bfloat16), arr(4, 64, 128)),
@@ -676,27 +691,27 @@
         spec(9), [pltpu.VMEM((4, 4, VIAS, 8, 128), F32)],
     )(packed, send, got, cells, load_cells, loads, spread, counts, early)
 
-    late = lax.ppermute(odd, "row", swaps(row_count, 1))
-    within = lax.ppermute(even, "row", swaps(row_count, 0))
+    late = swap(odd, "row", 1)
+    within = swap(even, "row", 0)
     relay = call(relay_kernel, "pack_relay", (buffer(BASE),), spec(1))(between)[0]
-    relayed = lax.ppermute(relay, "row", swaps(row_count, 0))
+    relayed = swap(relay, "row", 0)
     shares = call(shares_kernel, "pack_shares", (buffer(4),), spec(3))(first, between, relayed)[0]
     shares = lax.ppermute(shares, "die", others)
 
     even, odd, wide = call(
         strip_kernel, "column_strips", (buffer(COL_GROUPS), buffer(COL_GROUPS), arr(200, 128)), spec(13)
     )(sheet_res, capacity, drop_start, counts, field, base, arriving, first, between, within, late, relayed, shares)
-    even = lax.ppermute(even, "col", swaps(col_count, 0))
-    odd = lax.ppermute(odd, "col", swaps(col_count, 1))
-
-    image, pair = arr(4, 96, 256), arr(2, 96, 256)
+    even = swap(even, "col", 0)
+    odd = swap(odd, "col", 1)
+
+    image, pair = arr(4, 8 * GROUPS, 256), arr(2, 8 * GROUPS, 256)
     parts = call(
         assemble_kernel, "assemble",
         (image, image, pair, pair) + (image,) * 7 + (arr(2, 256, 384, dtype=jnp.bfloat16),), spec(8),
     )(sheet_res, capacity, drop_start, counts, field, within, between, late)
 
-    ext = pltpu.VMEM((96, 384), F32)
-    scratch = [ext, ext, pltpu.VMEM((2, 96, 384), F32), pltpu.VMEM((4, 40, 384), F32)] + [ext] * 8
+    ext = pltpu.VMEM((8 * GROUPS, 384), F32)
+    scratch = [ext, ext, pltpu.VMEM((2, 8 * GROUPS, 384), F32), pltpu.VMEM((4, 40, 384), F32)] + [ext] * 8
     return call(solve_kernel, "solve", (arr(2, 2, 64, 256), arr(2, 8, 32)), spec(15), scratch)(
         *parts, wide, even, odd
     )

time: 38.3 us -> 34.2 us (0.89)
  the two profiles are of different devices: /device:TPU:2 before, /device:TPU:102 now
where the time goes in v10:
time: 34.2 us; the launch traced here: 33.9 us
  starting transfers between devices  12.7 us (37%)
  Pallas kernels  11.9 us (35%)
  waiting for transfers between devices  7.24 us (21%)
  local copies, waits for them, and re-layouts  1.26 us (4%)
  between operations  0.79 us (2%)
    ppermute x7, starting transfers between devices, swap(): lax.ppermute(value, ('die', axis), swaps(lax.axis_size(axis), offset))  11.5 us
    pallas_call x1, Pallas kernels, per_device(): call(solve_kernel, 'solve', (arr(2, 2, 64, 256), arr(2, 8, 32)), spec(15)...  7.57 us
    ppermute x7, waiting for transfers between devices, swap(): lax.ppermute(value, ('die', axis), swaps(lax.axis_size(axis), offset))  3.79 us
    ppermute x1, waiting for transfers between devices, per_device(): shares = lax.ppermute(shares, 'die', others)  3.46 us
    pallas_call x1, Pallas kernels, per_device(): call(place_kernel, 'place_vias', (arr(4, 4, 64, 128), buffer(LATE + EARLY...  2.05 us
    unnamed x20, local copies, waits for them, and re-layouts  1.26 us
    ppermute x1, starting transfers between devices, per_device(): got = lax.ppermute(send, 'die', others)  0.91 us
    pallas_call x1, Pallas kernels, per_device(): call(prepare_kernel, 'spread_cells', (arr(4, VIAS, 8, 128), arr(4, 8, 128...  0.73 us
  transfers between devices with their start and end apart: 9, of which 5 were waited for; matrix products, arithmetic and copies ran while one was open for 0% of the time, Pallas kernels for 10%

profile of v10, /device:TPU:102, one launch (start us, length us, event | category | flops | bytes accessed | tf_op | source)
XLA Modules:
  0.0 33.9 jit_solution(16058205607687141367)
XLA Ops:
  0.6 1.2 %copy-done.3 = f32[2,2,2,32,8,32]{5,4,3,2,1,0:T(8,128)S(1)} copy-done((f32[2,2,2,32,8,32]{5,4,3,2,1,0:T(8,128)S(1)}, f32[2,2,2,32,8,32]{5,4,3,2,1,0:T(8,128)}, u32[]{:S(2)}) %copy-start.3) | copy-done | bytes 262168
  1.9 0.3 pack_vias.1
  2.2 0.0 copy-start
  2.2 0.9 %collective-permute-start = (f32[33,8,128]{2,1,0:T(8,128)S(1)}, f32[33,8,128]{2,1,0:T(8,128)S(1)}, u32[]{:S(2)}, u32[]{:S(2)}) collective-permute-start(f32[33,8,128]{2,1,0:T(8,128)S(1)} %get-tuple-element.32.send_ref), channel_id=1, source_target_pairs={{0,128},{128,0},{1,129},{129,1},{2,130},{130,2},{3,131},{131,3},{4... | collective-permute-start | bytes 405512 | tf_op jit(solution)/shard_map/ppermute | solution.py:673
  3.1 0.1 pack_base.1.base_ref
  3.2 0.0 copy-start.2
  3.2 0.1 collective-permute-start.1
  3.3 0.7 %spread_cells.1 = (f32[4,32,8,128]{3,2,1,0:T(8,128)S(1)}, f32[4,8,128]{2,1,0:T(8,128)S(1)}, f32[4,4,8,128]{3,2,1,0:T(8,128)S(1)}, bf16[256,1024]{1,0:T(8,128)(2,1)S(1)}, f32[4,64,128]{2,1,0:T(8,128)S(1)}) custom-call(s32[2,32,8,32]{3,2,1,0:T(8,128)S(1)} %copy-done.4, s32[2,8,32]{2,1,0:T(8,128)S(1)} %copy-done.6, f32[2,2,2,8,32]{4,3,2,1,0:T(8,128)S(1)} %copy-done.5), custom_call_target="tpu_custom_call" | custom-call | tf_op jit(solution)/shard_map/spread_cells/pallas_call | solution.py:683
  4.1 0.4 %collective-permute-done.1.got_ref.first_ref = f32[32,128]{1,0:T(8,128)S(1)} collective-permute-done((f32[32,128]{1,0:T(8,128)S(1)}, f32[32,128]{1,0:T(8,128)S(1)}, u32[]{:S(2)}, u32[]{:S(2)}) %collective-permute-start.1) | collective-permute-done | bytes 16416 | tf_op jit(solution)/shard_map/ppermute | solution.py:664
  4.5 3.4 %collective-permute-start.3 = (f32[304,128]{1,0:T(8,128)S(1)}, f32[304,128]{1,0:T(8,128)S(1)}, u32[]{:S(2)}, u32[]{:S(2)}) collective-permute-start(f32[304,128]{1,0:T(8,128)S(1)} %get-tuple-element.40), channel_id=1, source_target_pairs={{0,128},{8,16},{16,8},{24,32},{32,24},{40,48},{48,40},{56,64},{64,... | collective-permute-start | bytes 466952 | tf_op jit(solution)/shard_map/ppermute | solution.py:664
  7.9 2.0 %place_vias.1 = (f32[4,4,64,128]{3,2,1,0:T(8,128)S(1)}, f32[416,128]{1,0:T(8,128)S(1)}, f32[176,128]{1,0:T(8,128)S(1)}, f32[8,128]{1,0:T(8,128)S(1)}) custom-call(f32[2,32,8,128]{3,2,1,0:T(8,128)S(1)} %get-tuple-element.31.packed_ref, f32[33,8,128]{2,1,0:T(8,128)S(1)} %get-tuple-element.32.send_ref, f32[33,8,128]{2,1,0:T(8,128)S(1)} %collective-permute-done.got_ref, ...), custom_call_target="tpu_custom_call" | custom-call | flops 1000000000 | bytes 10000000 | tf_op jit(solution)/shard_map/place_vias/pallas_call | solution.py:689
  10.0 0.1 collective-permute-start.2
  10.1 3.6 %collective-permute-start.4 = (f32[176,128]{1,0:T(8,128)S(1)}, f32[176,128]{1,0:T(8,128)S(1)}, u32[]{:S(2)}, u32[]{:S(2)}) collective-permute-start(f32[176,128]{1,0:T(8,128)S(1)} %get-tuple-element.41), channel_id=1, source_target_pairs={{0,128},{8,16},{16,8},{24,32},{32,24},{40,48},{48,40},{56,64},{64,... | collective-permute-start | bytes 270344 | tf_op jit(solution)/shard_map/ppermute | solution.py:664
  13.7 0.1 collective-permute-start.5
  13.8 1.2 %collective-permute-done.5.relayed_ref = f32[32,128]{1,0:T(8,128)S(1)} collective-permute-done((f32[32,128]{1,0:T(8,128)S(1)}, f32[32,128]{1,0:T(8,128)S(1)}, u32[]{:S(2)}, u32[]{:S(2)}) %collective-permute-start.5) | collective-permute-done | bytes 16416 | tf_op jit(solution)/shard_map/ppermute | solution.py:664
  15.0 0.3 collective-permute-start.6
  15.3 3.5 %collective-permute-done.6.shares_ref = f32[32,128]{1,0:T(8,128)S(1)} collective-permute-done((f32[32,128]{1,0:T(8,128)S(1)}, f32[32,128]{1,0:T(8,128)S(1)}, u32[]{:S(2)}, u32[]{:S(2)}) %collective-permute-start.6) | collective-permute-done | bytes 16416 | tf_op jit(solution)/shard_map/ppermute | solution.py:699
  18.7 0.6 %column_strips.1 = (f32[224,128]{1,0:T(8,128)S(1)}, f32[224,128]{1,0:T(8,128)S(1)}, f32[200,128]{1,0:T(8,128)S(1)}) custom-call(f32[2,2,64,256]{3,2,1,0:T(8,128)S(1)} %copy-done, f32[2,64,256]{2,1,0:T(8,128)S(1)} %copy-done.2, f32[2,2,64,256]{3,2,1,0:T(8,128)S(1)} %copy-done.1, f32[4,64,128]{2,1,0:T(8,128)S(1)} %get-tuple-element.30.counts_ref, ...), custom_call_target="tpu_custom_call" | custom-call | tf_op jit(solution)/shard_map/column_strips/pallas_call | solution.py:701
  19.3 0.2 collective-permute-start.7
  19.5 4.0 %collective-permute-start.8 = (f32[224,128]{1,0:T(8,128)S(1)}, f32[224,128]{1,0:T(8,128)S(1)}, u32[]{:S(2)}, u32[]{:S(2)}) collective-permute-start(f32[224,128]{1,0:T(8,128)S(1)} %get-tuple-element.57), channel_id=1, source_target_pairs={{0,128},{1,2},{2,1},{3,4},{4,3},{5,6},{6,5},{7,135},{128,0},{129,1... | collective-permute-start | bytes 344072 | tf_op jit(solution)/shard_map/ppermute | solution.py:664
  23.6 0.6 %assemble.1 = (f32[4,88,256]{2,1,0:T(8,128)S(1)}, f32[4,88,256]{2,1,0:T(8,128)S(1)}, f32[2,88,256]{2,1,0:T(8,128)S(1)}, f32[2,88,256]{2,1,0:T(8,128)S(1)}, f32[4...) custom-call(f32[2,2,64,256]{3,2,1,0:T(8,128)S(1)} %copy-done, ...), custom_call_target="tpu_custom_call" | custom-call | tf_op jit(solution)/shard_map/assemble/pallas_call | solution.py:708
  24.1 0.1 collective-permute-done.7.even_ref
  24.2 2.1 %collective-permute-done.8.odd_ref = f32[224,128]{1,0:T(8,128)S(1)} collective-permute-done((f32[224,128]{1,0:T(8,128)S(1)}, f32[224,128]{1,0:T(8,128)S(1)}, u32[]{:S(2)}, u32[]{:S(2)}) %collective-permute-start.8) | collective-permute-done | bytes 114720 | tf_op jit(solution)/shard_map/ppermute | solution.py:664
  26.4 7.6 %solve.1 = (f32[2,2,64,256]{3,2,1,0:T(8,128)}, f32[2,8,32]{2,1,0:T(8,128)}) custom-call(f32[4,88,256]{2,1,0:T(8,128)S(1)} %get-tuple-element.42.s_ref, f32[4,88,256]{2,1,0:T(8,128)S(1)} %get-tuple-element.43.x_ref, f32[2,88,256]{2,1,0:T(8,128)S(1)} %get-tuple-element.44.c_ref, f32[2,88,256]{2,1,0:T(8,128)S(1)} %get-tuple-element.45.k_ref, ...), custom_call_target="tpu_custom_call" | custom-call | tf_op jit(solution)/shard_map/solve/pallas_call | solution.py:715
  (24 shorter events, 0.1 us)
Async XLA Ops:
  0.6 1.2 %copy-start.3 = (f32[2,2,2,32,8,32]{5,4,3,2,1,0:T(8,128)S(1)}, f32[2,2,2,32,8,32]{5,4,3,2,1,0:T(8,128)}, u32[]{:S(2)}) copy-start(f32[2,2,2,32,8,32]{5,4,3,2,1,0:T(8,128)} %via_ref.1) | copy-start | bytes 786436
  1.9 1.2 %copy-start.7 = (f32[2,8,32]{2,1,0:T(8,128)S(1)}, f32[2,8,32]{2,1,0:T(8,128)}, u32[]{:S(2)}) copy-start(f32[2,8,32]{2,1,0:T(8,128)} %sheet_ref.4) | copy-start | bytes 6148
  1.9 1.2 %copy-start.8 = (f32[2,8,32]{2,1,0:T(8,128)S(1)}, f32[2,8,32]{2,1,0:T(8,128)}, u32[]{:S(2)}) copy-start(f32[2,8,32]{2,1,0:T(8,128)} %start_ref.1) | copy-start | bytes 6148
  1.9 1.2 %copy-start.9 = (s32[1,4]{1,0:T(1,128)S(1)}, s32[1,4]{1,0:T(1,128)}, u32[]{:S(2)}) copy-start(s32[1,4]{1,0:T(1,128)} %bump_ref.1) | copy-start | bytes 52
  1.9 1.4 %copy-start.4 = (s32[2,32,8,32]{3,2,1,0:T(8,128)S(1)}, s32[2,32,8,32]{3,2,1,0:T(8,128)}, u32[]{:S(2)}) copy-start(s32[2,32,8,32]{3,2,1,0:T(8,128)} %cell_ref.1) | copy-start | bytes 196612
  1.9 1.4 %copy-start.5 = (f32[2,2,2,8,32]{4,3,2,1,0:T(8,128)S(1)}, f32[2,2,2,8,32]{4,3,2,1,0:T(8,128)}, u32[]{:S(2)}) copy-start(f32[2,2,2,8,32]{4,3,2,1,0:T(8,128)} %load_ref.1) | copy-start | bytes 24580
  1.9 1.4 %copy-start.6 = (s32[2,8,32]{2,1,0:T(8,128)S(1)}, s32[2,8,32]{2,1,0:T(8,128)}, u32[]{:S(2)}) copy-start(s32[2,8,32]{2,1,0:T(8,128)} %load_cell_ref.1) | copy-start | bytes 6148
  1.9 2.6 %copy-start.1 = (f32[2,2,64,256]{3,2,1,0:T(8,128)S(1)}, f32[2,2,64,256]{3,2,1,0:T(8,128)}, u32[]{:S(2)}) copy-start(f32[2,2,64,256]{3,2,1,0:T(8,128)} %drop_ref.5) | copy-start | bytes 786436
  2.2 2.3 %copy-start = (f32[2,2,64,256]{3,2,1,0:T(8,128)S(1)}, f32[2,2,64,256]{3,2,1,0:T(8,128)}, u32[]{:S(2)}) copy-start(f32[2,2,64,256]{3,2,1,0:T(8,128)} %sheet_ref.7) | copy-start | bytes 786436
  2.2 5.8 %collective-permute-start = (f32[33,8,128]{2,1,0:T(8,128)S(1)}, f32[33,8,128]{2,1,0:T(8,128)S(1)}, u32[]{:S(2)}, u32[]{:S(2)}) collective-permute-start(f32[33,8,128]{2,1,0:T(8,128)S(1)} %get-tuple-element.32.send_ref), channel_id=1, source_target_pairs={{0,128},{128,0},{1,129},{129,1},{2,130},{130,2},{3,131},{131,3},{4... | collective-permute-start | bytes 405512 | tf_op jit(solution)/shard_map/ppermute | solution.py:673
  3.2 1.3 %copy-start.2 = (f32[2,64,256]{2,1,0:T(8,128)S(1)}, f32[2,64,256]{2,1,0:T(8,128)}, u32[]{:S(2)}) copy-start(f32[2,64,256]{2,1,0:T(8,128)} %cap_ref.5) | copy-start | bytes 393220
  3.2 1.3 %collective-permute-start.1 = (f32[32,128]{1,0:T(8,128)S(1)}, f32[32,128]{1,0:T(8,128)S(1)}, u32[]{:S(2)}, u32[]{:S(2)}) collective-permute-start(f32[32,128]{1,0:T(8,128)S(1)} %pack_base.1.base_ref), channel_id=1, source_target_pairs={{0,8},{8,0},{16,24},{24,16},{32,40},{40,32},{48,56},{56,48},{64,72... | collective-permute-start | bytes 49160 | tf_op jit(solution)/shard_map/ppermute | solution.py:664
  4.5 9.2 %collective-permute-start.3 = (f32[304,128]{1,0:T(8,128)S(1)}, f32[304,128]{1,0:T(8,128)S(1)}, u32[]{:S(2)}, u32[]{:S(2)}) collective-permute-start(f32[304,128]{1,0:T(8,128)S(1)} %get-tuple-element.40), channel_id=1, source_target_pairs={{0,128},{8,16},{16,8},{24,32},{32,24},{40,48},{48,40},{56,64},{64,... | collective-permute-start | bytes 466952 | tf_op jit(solution)/shard_map/ppermute | solution.py:664
  10.0 8.7 %collective-permute-start.2 = (f32[416,128]{1,0:T(8,128)S(1)}, f32[416,128]{1,0:T(8,128)S(1)}, u32[]{:S(2)}, u32[]{:S(2)}) collective-permute-start(f32[416,128]{1,0:T(8,128)S(1)} %get-tuple-element.39), channel_id=1, source_target_pairs={{0,8},{8,0},{16,24},{24,16},{32,40},{40,32},{48,56},{56,48},{64,72... | collective-permute-start | bytes 638984 | tf_op jit(solution)/shard_map/ppermute | solution.py:664
  10.1 8.6 %collective-permute-start.4 = (f32[176,128]{1,0:T(8,128)S(1)}, f32[176,128]{1,0:T(8,128)S(1)}, u32[]{:S(2)}, u32[]{:S(2)}) collective-permute-start(f32[176,128]{1,0:T(8,128)S(1)} %get-tuple-element.41), channel_id=1, source_target_pairs={{0,128},{8,16},{16,8},{24,32},{32,24},{40,48},{48,40},{56,64},{64,... | collective-permute-start | bytes 270344 | tf_op jit(solution)/shard_map/ppermute | solution.py:664
  13.7 1.3 %collective-permute-start.5 = (f32[32,128]{1,0:T(8,128)S(1)}, f32[32,128]{1,0:T(8,128)S(1)}, u32[]{:S(2)}, u32[]{:S(2)}) collective-permute-start(f32[32,128]{1,0:T(8,128)S(1)} %pack_relay.1), channel_id=1, source_target_pairs={{0,8},{8,0},{16,24},{24,16},{32,40},{40,32},{48,56},{56,48},{64,72... | collective-permute-start | bytes 49160 | tf_op jit(solution)/shard_map/ppermute | solution.py:664
  15.0 3.7 %collective-permute-start.6 = (f32[32,128]{1,0:T(8,128)S(1)}, f32[32,128]{1,0:T(8,128)S(1)}, u32[]{:S(2)}, u32[]{:S(2)}) collective-permute-start(f32[32,128]{1,0:T(8,128)S(1)} %pack_shares.1), channel_id=1, source_target_pairs={{0,128},{128,0},{1,129},{129,1},{2,130},{130,2},{3,131},{131,3},{4... | collective-permute-start | bytes 49160 | tf_op jit(solution)/shard_map/ppermute | solution.py:699
  19.3 4.9 %collective-permute-start.7 = (f32[224,128]{1,0:T(8,128)S(1)}, f32[224,128]{1,0:T(8,128)S(1)}, u32[]{:S(2)}, u32[]{:S(2)}) collective-permute-start(f32[224,128]{1,0:T(8,128)S(1)} %get-tuple-element.56), channel_id=1, source_target_pairs={{0,1},{1,0},{2,3},{3,2},{4,5},{5,4},{6,7},{7,6},{128,129},{129,128... | collective-permute-start | bytes 344072 | tf_op jit(solution)/shard_map/ppermute | solution.py:664
  19.5 6.8 %collective-permute-start.8 = (f32[224,128]{1,0:T(8,128)S(1)}, f32[224,128]{1,0:T(8,128)S(1)}, u32[]{:S(2)}, u32[]{:S(2)}) collective-permute-start(f32[224,128]{1,0:T(8,128)S(1)} %get-tuple-element.57), channel_id=1, source_target_pairs={{0,128},{1,2},{2,1},{3,4},{4,3},{5,6},{6,5},{7,135},{128,0},{129,1... | collective-permute-start | bytes 344072 | tf_op jit(solution)/shard_map/ppermute | solution.py:664

commit v11 on v10

--- a/solution.py
+++ b/solution.py
@@ -98,8 +98,8 @@
 
 
 BASE = 4
-EARLY = 30
-LATE = 22
+EARLY = 36
+LATE = 16
 
 
 def base_kernel(bump_ref, sheet_ref, start_ref, send_ref, base_ref):
@@ -112,7 +112,7 @@
         base_ref[rows(part), :] = value
 
 
-def chip_kernel(base_ref, got_ref, sheet_ref, cap_ref, drop_ref, within_ref, between_ref):
+def chip_kernel(base_ref, got_ref, sheet_ref, cap_ref, drop_ref, counts_ref, within_ref, between_ref):
     even = lax.axis_index("row") % 2 == 0
     sender = RowSender(even, within_ref, between_ref)
     for d in range(2):
@@ -121,6 +121,7 @@
             for n in range(2):
                 sender.pair(lambda g: sheet_ref[d, n, rows(g), lanes], lambda g: drop_ref[d, n, rows(g), lanes])
         sender.pair(lambda g: cap_ref[d, rows(g), pl.ds(0, 128)], lambda g: cap_ref[d, rows(g), pl.ds(128, 128)])
+        sender.pair(lambda g: counts_ref[2 * d, rows(g), :], lambda g: counts_ref[2 * d + 1, rows(g), :])
     for part in range(BASE):
         own, got = base_ref[rows(part), :], got_ref[rows(part), :]
         for slot, value in enumerate([jnp.where(even, own, got), jnp.where(even, got, own)]):
@@ -190,7 +191,7 @@
 
 
 def place_kernel(
-    packed_ref, send_ref, got_ref, cells_ref, load_cells_ref, loads_ref, spread_ref, counts_ref, early_ref,
+    packed_ref, send_ref, got_ref, cells_ref, load_cells_ref, loads_ref, spread_ref, early_ref,
     field_ref, even_ref, odd_ref, arriving_ref, values_ref,
 ):
     lane = lane_iota()
@@ -241,7 +242,6 @@
                 two = lambda g: field_ref[2 + n, 2 * d + half, rows(g), :]
                 sender.put(one(0), one(7))
                 sender.put(shared(one(1), two(0), 3), shared_low(one(6), two(7), 5))
-        sender.pair(lambda g: counts_ref[2 * d, rows(g), :], lambda g: counts_ref[2 * d + 1, rows(g), :])
 
 
 SHEET, DROP, CAPACITY, COUNTS, FIRST, SECOND = range(6)
@@ -250,18 +250,16 @@
 def near_rows(read, kind, d, half, n, upper):
     early, late = read
     if kind in (FIRST, SECOND):
-        start = 11 * d + 4 * half + 2 * n
+        start = 8 * d + 4 * half + 2 * n
         if kind == SECOND:
             return roll(late(start + 1), -5 if upper else -3, 0), None
         return late(start), late(start + 1)
     if kind in (SHEET, DROP):
-        take, start, second = early, 15 * d + 6 * half + 3 * n, kind == DROP
-    elif kind == CAPACITY:
-        take, start, second = early, 15 * d + 12, half == 1
+        start, second = 18 * d + 6 * half + 3 * n, kind == DROP
     else:
-        take, start, second = late, 11 * d + 8, half == 1
-    last = take(start + 2)
-    return (take(start + 1), roll(last, -4, 0)) if second else (take(start), last)
+        start, second = 18 * d + (12 if kind == CAPACITY else 15), half == 1
+    last = early(start + 2)
+    return (early(start + 1), roll(last, -4, 0)) if second else (early(start), last)
 
 
 def column_groups(own, below, above, kind, d, half, n):
@@ -676,20 +674,19 @@
 
     base = call(base_kernel, "pack_base", (buffer(BASE),), spec(4))(bump_cell, base_sheet, base_start, send)[0]
     first = swap(base, "row", 0)
-    early, between = call(chip_kernel, "pack_early", (buffer(EARLY), buffer(EARLY + 2 * BASE)), spec(5))(
-        base, first, sheet_res, capacity, drop_start
-    )
-    between = swap(between, "row", 1)
     cells, load_cells, loads, spread, counts = call(
         prepare_kernel, "spread_cells",
         (arr(4, VIAS, 8, 128), arr(4, 8, 128), arr(4, 4, 8, 128), arr(256, 1024, dtype=jnp.bfloat16), arr(4, 64, 128)),
         spec(3),
     )(via_cell, load_cell, load_current)
-
+    early, between = call(chip_kernel, "pack_early", (buffer(EARLY), buffer(EARLY + 2 * BASE)), spec(6))(
+        base, first, sheet_res, capacity, drop_start, counts
+    )
+    between = swap(between, "row", 1)
     field, even, odd, arriving = call(
         place_kernel, "place_vias", (arr(4, 4, 64, 128), buffer(LATE + EARLY), buffer(LATE), buffer(1)),
-        spec(9), [pltpu.VMEM((4, 4, VIAS, 8, 128), F32)],
-    )(packed, send, got, cells, load_cells, loads, spread, counts, early)
+        spec(8), [pltpu.VMEM((4, 4, VIAS, 8, 128), F32)],
+    )(packed, send, got, cells, load_cells, loads, spread, early)
 
     late = swap(odd, "row", 1)
     within = swap(even, "row", 0)

time: 34.2 us -> 34.1 us (level)
    ppermute x1, waiting for transfers between devices: 3.46 us -> 1.24 us  [per_device(): shares = lax.ppermute(shares, 'die', others)]
    ppermute x7, waiting for transfers between devices: 3.79 us -> 5.76 us  [swap(): lax.ppermute(value, ('die', axis), swaps(lax.axis_size(axis), offset))]
  transfers between devices with their start and end apart: 9 -> 9, of which waited for: 5 -> 6; matrix products, arithmetic and copies ran while one was open for 0% -> 0% of each run, Pallas kernels for 10% -> 10%
where the time goes in v11:
time: 34.1 us; the launch traced here: 33.9 us
  starting transfers between devices  13 us (38%)
  Pallas kernels  11.8 us (35%)
  waiting for transfers between devices  7 us (21%)
  local copies, waits for them, and re-layouts  1.26 us (4%)
  between operations  0.79 us (2%)
    ppermute x7, starting transfers between devices, swap(): lax.ppermute(value, ('die', axis), swaps(lax.axis_size(axis), offset))  11.5 us
    pallas_call x1, Pallas kernels, per_device(): call(solve_kernel, 'solve', (arr(2, 2, 64, 256), arr(2, 8, 32)), spec(15)...  7.56 us
    ppermute x7, waiting for transfers between devices, swap(): lax.ppermute(value, ('die', axis), swaps(lax.axis_size(axis), offset))  5.76 us
    pallas_call x1, Pallas kernels, per_device(): call(place_kernel, 'place_vias', (arr(4, 4, 64, 128), buffer(LATE + EARLY...  2.04 us
    unnamed x20, local copies, waits for them, and re-layouts  1.26 us
    ppermute x1, waiting for transfers between devices, per_device(): shares = lax.ppermute(shares, 'die', others)  1.24 us
    ppermute x1, starting transfers between devices, per_device(): got = lax.ppermute(send, 'die', others)  0.91 us
    pallas_call x1, Pallas kernels, per_device(): call(prepare_kernel, 'spread_cells', (arr(4, VIAS, 8, 128), arr(4, 8, 128...  0.74 us
  transfers between devices with their start and end apart: 9, of which 6 were waited for; matrix products, arithmetic and copies ran while one was open for 0% of the time, Pallas kernels for 10%

profile of v11, /device:TPU:102, one launch (start us, length us, event | category | flops | bytes accessed | tf_op | source)
XLA Modules:
  0.0 33.9 jit_solution(10343352407876998776)
XLA Ops:
  0.6 1.2 %copy-done.3 = f32[2,2,2,32,8,32]{5,4,3,2,1,0:T(8,128)S(1)} copy-done((f32[2,2,2,32,8,32]{5,4,3,2,1,0:T(8,128)S(1)}, f32[2,2,2,32,8,32]{5,4,3,2,1,0:T(8,128)}, u32[]{:S(2)}) %copy-start.3) | copy-done | bytes 262168
  1.9 0.3 pack_vias.1
  2.2 0.9 %collective-permute-start = (f32[33,8,128]{2,1,0:T(8,128)S(1)}, f32[33,8,128]{2,1,0:T(8,128)S(1)}, u32[]{:S(2)}, u32[]{:S(2)}) collective-permute-start(f32[33,8,128]{2,1,0:T(8,128)S(1)} %get-tuple-element.32.send_ref), channel_id=1, source_target_pairs={{0,128},{128,0},{1,129},{129,1},{2,130},{130,2},{3,131},{131,3},{4... | collective-permute-start | bytes 405512 | tf_op jit(solution)/shard_map/ppermute | solution.py:671
  3.1 0.1 pack_base.1.base_ref
  3.2 0.0 copy-start.2
  3.2 0.1 collective-permute-start.1
  3.3 0.7 %spread_cells.1 = (f32[4,32,8,128]{3,2,1,0:T(8,128)S(1)}, f32[4,8,128]{2,1,0:T(8,128)S(1)}, f32[4,4,8,128]{3,2,1,0:T(8,128)S(1)}, bf16[256,1024]{1,0:T(8,128)(2,1)S(1)}, f32[4,64,128]{2,1,0:T(8,128)S(1)}) custom-call(s32[2,32,8,32]{3,2,1,0:T(8,128)S(1)} %copy-done.4, s32[2,8,32]{2,1,0:T(8,128)S(1)} %copy-done.6, f32[2,2,2,8,32]{4,3,2,1,0:T(8,128)S(1)} %copy-done.5), custom_call_target="tpu_custom_call" | custom-call | tf_op jit(solution)/shard_map/spread_cells/pallas_call | solution.py:677
  4.1 0.4 %collective-permute-done.1.got_ref.first_ref = f32[32,128]{1,0:T(8,128)S(1)} collective-permute-done((f32[32,128]{1,0:T(8,128)S(1)}, f32[32,128]{1,0:T(8,128)S(1)}, u32[]{:S(2)}, u32[]{:S(2)}) %collective-permute-start.1) | collective-permute-done | bytes 16416 | tf_op jit(solution)/shard_map/ppermute | solution.py:662
  4.5 3.4 %collective-permute-start.3 = (f32[352,128]{1,0:T(8,128)S(1)}, f32[352,128]{1,0:T(8,128)S(1)}, u32[]{:S(2)}, u32[]{:S(2)}) collective-permute-start(f32[352,128]{1,0:T(8,128)S(1)} %get-tuple-element.40), channel_id=1, source_target_pairs={{0,128},{8,16},{16,8},{24,32},{32,24},{40,48},{48,40},{56,64},{64,... | collective-permute-start | bytes 540680 | tf_op jit(solution)/shard_map/ppermute | solution.py:662
  8.0 2.0 %place_vias.1 = (f32[4,4,64,128]{3,2,1,0:T(8,128)S(1)}, f32[416,128]{1,0:T(8,128)S(1)}, f32[128,128]{1,0:T(8,128)S(1)}, f32[8,128]{1,0:T(8,128)S(1)}) custom-call(f32[2,32,8,128]{3,2,1,0:T(8,128)S(1)} %get-tuple-element.31.packed_ref, f32[33,8,128]{2,1,0:T(8,128)S(1)} %get-tuple-element.32.send_ref, f32[33,8,128]{2,1,0:T(8,128)S(1)} %collective-permute-done.got_ref, ...), custom_call_target="tpu_custom_call" | custom-call | flops 1000000000 | bytes 10000000 | tf_op jit(solution)/shard_map/place_vias/pallas_call | solution.py:686
  10.0 0.1 collective-permute-start.2
  10.1 3.6 %collective-permute-start.4 = (f32[128,128]{1,0:T(8,128)S(1)}, f32[128,128]{1,0:T(8,128)S(1)}, u32[]{:S(2)}, u32[]{:S(2)}) collective-permute-start(f32[128,128]{1,0:T(8,128)S(1)} %get-tuple-element.41), channel_id=1, source_target_pairs={{0,128},{8,16},{16,8},{24,32},{32,24},{40,48},{48,40},{56,64},{64,... | collective-permute-start | bytes 196616 | tf_op jit(solution)/shard_map/ppermute | solution.py:662
  13.7 0.1 collective-permute-start.5
  13.8 1.2 %collective-permute-done.5.relayed_ref = f32[32,128]{1,0:T(8,128)S(1)} collective-permute-done((f32[32,128]{1,0:T(8,128)S(1)}, f32[32,128]{1,0:T(8,128)S(1)}, u32[]{:S(2)}, u32[]{:S(2)}) %collective-permute-start.5) | collective-permute-done | bytes 16416 | tf_op jit(solution)/shard_map/ppermute | solution.py:662
  15.0 0.6 %collective-permute-start.6 = (f32[32,128]{1,0:T(8,128)S(1)}, f32[32,128]{1,0:T(8,128)S(1)}, u32[]{:S(2)}, u32[]{:S(2)}) collective-permute-start(f32[32,128]{1,0:T(8,128)S(1)} %pack_shares.1), channel_id=1, source_target_pairs={{0,128},{128,0},{1,129},{129,1},{2,130},{130,2},{3,131},{131,3},{4... | collective-permute-start | bytes 49160 | tf_op jit(solution)/shard_map/ppermute | solution.py:696
  15.5 1.9 %collective-permute-done.4.late_ref = f32[128,128]{1,0:T(8,128)S(1)} collective-permute-done((f32[128,128]{1,0:T(8,128)S(1)}, f32[128,128]{1,0:T(8,128)S(1)}, u32[]{:S(2)}, u32[]{:S(2)}) %collective-permute-start.4) | collective-permute-done | bytes 65568 | tf_op jit(solution)/shard_map/ppermute | solution.py:662
  17.5 1.2 %collective-permute-done.6.shares_ref = f32[32,128]{1,0:T(8,128)S(1)} collective-permute-done((f32[32,128]{1,0:T(8,128)S(1)}, f32[32,128]{1,0:T(8,128)S(1)}, u32[]{:S(2)}, u32[]{:S(2)}) %collective-permute-start.6) | collective-permute-done | bytes 16416 | tf_op jit(solution)/shard_map/ppermute | solution.py:696
  18.7 0.6 %column_strips.1 = (f32[224,128]{1,0:T(8,128)S(1)}, f32[224,128]{1,0:T(8,128)S(1)}, f32[200,128]{1,0:T(8,128)S(1)}) custom-call(f32[2,2,64,256]{3,2,1,0:T(8,128)S(1)} %copy-done, f32[2,64,256]{2,1,0:T(8,128)S(1)} %copy-done.2, f32[2,2,64,256]{3,2,1,0:T(8,128)S(1)} %copy-done.1, f32[4,64,128]{2,1,0:T(8,128)S(1)} %get-tuple-element.30.counts_ref, ...), custom_call_target="tpu_custom_call" | custom-call | tf_op jit(solution)/shard_map/column_strips/pallas_call | solution.py:698
  19.3 0.2 collective-permute-start.7
  19.5 4.0 %collective-permute-start.8 = (f32[224,128]{1,0:T(8,128)S(1)}, f32[224,128]{1,0:T(8,128)S(1)}, u32[]{:S(2)}, u32[]{:S(2)}) collective-permute-start(f32[224,128]{1,0:T(8,128)S(1)} %get-tuple-element.57), channel_id=1, source_target_pairs={{0,128},{1,2},{2,1},{3,4},{4,3},{5,6},{6,5},{7,135},{128,0},{129,1... | collective-permute-start | bytes 344072 | tf_op jit(solution)/shard_map/ppermute | solution.py:662
  23.6 0.5 %assemble.1 = (f32[4,88,256]{2,1,0:T(8,128)S(1)}, f32[4,88,256]{2,1,0:T(8,128)S(1)}, f32[2,88,256]{2,1,0:T(8,128)S(1)}, f32[2,88,256]{2,1,0:T(8,128)S(1)}, f32[4...) custom-call(f32[2,2,64,256]{3,2,1,0:T(8,128)S(1)} %copy-done, ...), custom_call_target="tpu_custom_call" | custom-call | tf_op jit(solution)/shard_map/assemble/pallas_call | solution.py:705
  24.1 0.1 collective-permute-done.7.even_ref
  24.2 2.1 %collective-permute-done.8.odd_ref = f32[224,128]{1,0:T(8,128)S(1)} collective-permute-done((f32[224,128]{1,0:T(8,128)S(1)}, f32[224,128]{1,0:T(8,128)S(1)}, u32[]{:S(2)}, u32[]{:S(2)}) %collective-permute-start.8) | collective-permute-done | bytes 114720 | tf_op jit(solution)/shard_map/ppermute | solution.py:662
  26.3 7.6 %solve.1 = (f32[2,2,64,256]{3,2,1,0:T(8,128)}, f32[2,8,32]{2,1,0:T(8,128)}) custom-call(f32[4,88,256]{2,1,0:T(8,128)S(1)} %get-tuple-element.42.s_ref, f32[4,88,256]{2,1,0:T(8,128)S(1)} %get-tuple-element.43.x_ref, f32[2,88,256]{2,1,0:T(8,128)S(1)} %get-tuple-element.44.c_ref, f32[2,88,256]{2,1,0:T(8,128)S(1)} %get-tuple-element.45.k_ref, ...), custom_call_target="tpu_custom_call" | custom-call | tf_op jit(solution)/shard_map/solve/pallas_call | solution.py:712
  (24 shorter events, 0.1 us)
Async XLA Ops:
  0.6 1.2 %copy-start.3 = (f32[2,2,2,32,8,32]{5,4,3,2,1,0:T(8,128)S(1)}, f32[2,2,2,32,8,32]{5,4,3,2,1,0:T(8,128)}, u32[]{:S(2)}) copy-start(f32[2,2,2,32,8,32]{5,4,3,2,1,0:T(8,128)} %via_ref.1) | copy-start | bytes 786436
  1.9 1.2 %copy-start.7 = (f32[2,8,32]{2,1,0:T(8,128)S(1)}, f32[2,8,32]{2,1,0:T(8,128)}, u32[]{:S(2)}) copy-start(f32[2,8,32]{2,1,0:T(8,128)} %sheet_ref.4) | copy-start | bytes 6148
  1.9 1.2 %copy-start.8 = (f32[2,8,32]{2,1,0:T(8,128)S(1)}, f32[2,8,32]{2,1,0:T(8,128)}, u32[]{:S(2)}) copy-start(f32[2,8,32]{2,1,0:T(8,128)} %start_ref.1) | copy-start | bytes 6148
  1.9 1.2 %copy-start.9 = (s32[1,4]{1,0:T(1,128)S(1)}, s32[1,4]{1,0:T(1,128)}, u32[]{:S(2)}) copy-start(s32[1,4]{1,0:T(1,128)} %bump_ref.1) | copy-start | bytes 52
  1.9 1.4 %copy-start.4 = (s32[2,32,8,32]{3,2,1,0:T(8,128)S(1)}, s32[2,32,8,32]{3,2,1,0:T(8,128)}, u32[]{:S(2)}) copy-start(s32[2,32,8,32]{3,2,1,0:T(8,128)} %cell_ref.1) | copy-start | bytes 196612
  1.9 1.4 %copy-start.5 = (f32[2,2,2,8,32]{4,3,2,1,0:T(8,128)S(1)}, f32[2,2,2,8,32]{4,3,2,1,0:T(8,128)}, u32[]{:S(2)}) copy-start(f32[2,2,2,8,32]{4,3,2,1,0:T(8,128)} %load_ref.1) | copy-start | bytes 24580
  1.9 1.4 %copy-start.6 = (s32[2,8,32]{2,1,0:T(8,128)S(1)}, s32[2,8,32]{2,1,0:T(8,128)}, u32[]{:S(2)}) copy-start(s32[2,8,32]{2,1,0:T(8,128)} %load_cell_ref.1) | copy-start | bytes 6148
  1.9 2.6 %copy-start.1 = (f32[2,2,64,256]{3,2,1,0:T(8,128)S(1)}, f32[2,2,64,256]{3,2,1,0:T(8,128)}, u32[]{:S(2)}) copy-start(f32[2,2,64,256]{3,2,1,0:T(8,128)} %drop_ref.5) | copy-start | bytes 786436
  2.2 2.3 %copy-start = (f32[2,2,64,256]{3,2,1,0:T(8,128)S(1)}, f32[2,2,64,256]{3,2,1,0:T(8,128)}, u32[]{:S(2)}) copy-start(f32[2,2,64,256]{3,2,1,0:T(8,128)} %sheet_ref.7) | copy-start | bytes 786436
  2.2 5.8 %collective-permute-start = (f32[33,8,128]{2,1,0:T(8,128)S(1)}, f32[33,8,128]{2,1,0:T(8,128)S(1)}, u32[]{:S(2)}, u32[]{:S(2)}) collective-permute-start(f32[33,8,128]{2,1,0:T(8,128)S(1)} %get-tuple-element.32.send_ref), channel_id=1, source_target_pairs={{0,128},{128,0},{1,129},{129,1},{2,130},{130,2},{3,131},{131,3},{4... | collective-permute-start | bytes 405512 | tf_op jit(solution)/shard_map/ppermute | solution.py:671
  3.2 1.3 %copy-start.2 = (f32[2,64,256]{2,1,0:T(8,128)S(1)}, f32[2,64,256]{2,1,0:T(8,128)}, u32[]{:S(2)}) copy-start(f32[2,64,256]{2,1,0:T(8,128)} %cap_ref.5) | copy-start | bytes 393220
  3.2 1.3 %collective-permute-start.1 = (f32[32,128]{1,0:T(8,128)S(1)}, f32[32,128]{1,0:T(8,128)S(1)}, u32[]{:S(2)}, u32[]{:S(2)}) collective-permute-start(f32[32,128]{1,0:T(8,128)S(1)} %pack_base.1.base_ref), channel_id=1, source_target_pairs={{0,8},{8,0},{16,24},{24,16},{32,40},{40,32},{48,56},{56,48},{64,72... | collective-permute-start | bytes 49160 | tf_op jit(solution)/shard_map/ppermute | solution.py:662
  4.5 9.2 %collective-permute-start.3 = (f32[352,128]{1,0:T(8,128)S(1)}, f32[352,128]{1,0:T(8,128)S(1)}, u32[]{:S(2)}, u32[]{:S(2)}) collective-permute-start(f32[352,128]{1,0:T(8,128)S(1)} %get-tuple-element.40), channel_id=1, source_target_pairs={{0,128},{8,16},{16,8},{24,32},{32,24},{40,48},{48,40},{56,64},{64,... | collective-permute-start | bytes 540680 | tf_op jit(solution)/shard_map/ppermute | solution.py:662
  10.0 8.7 %collective-permute-start.2 = (f32[416,128]{1,0:T(8,128)S(1)}, f32[416,128]{1,0:T(8,128)S(1)}, u32[]{:S(2)}, u32[]{:S(2)}) collective-permute-start(f32[416,128]{1,0:T(8,128)S(1)} %get-tuple-element.39), channel_id=1, source_target_pairs={{0,8},{8,0},{16,24},{24,16},{32,40},{40,32},{48,56},{56,48},{64,72... | collective-permute-start | bytes 638984 | tf_op jit(solution)/shard_map/ppermute | solution.py:662
  10.1 7.4 %collective-permute-start.4 = (f32[128,128]{1,0:T(8,128)S(1)}, f32[128,128]{1,0:T(8,128)S(1)}, u32[]{:S(2)}, u32[]{:S(2)}) collective-permute-start(f32[128,128]{1,0:T(8,128)S(1)} %get-tuple-element.41), channel_id=1, source_target_pairs={{0,128},{8,16},{16,8},{24,32},{32,24},{40,48},{48,40},{56,64},{64,... | collective-permute-start | bytes 196616 | tf_op jit(solution)/shard_map/ppermute | solution.py:662
  13.7 1.3 %collective-permute-start.5 = (f32[32,128]{1,0:T(8,128)S(1)}, f32[32,128]{1,0:T(8,128)S(1)}, u32[]{:S(2)}, u32[]{:S(2)}) collective-permute-start(f32[32,128]{1,0:T(8,128)S(1)} %pack_relay.1), channel_id=1, source_target_pairs={{0,8},{8,0},{16,24},{24,16},{32,40},{40,32},{48,56},{56,48},{64,72... | collective-permute-start | bytes 49160 | tf_op jit(solution)/shard_map/ppermute | solution.py:662
  15.0 3.7 %collective-permute-start.6 = (f32[32,128]{1,0:T(8,128)S(1)}, f32[32,128]{1,0:T(8,128)S(1)}, u32[]{:S(2)}, u32[]{:S(2)}) collective-permute-start(f32[32,128]{1,0:T(8,128)S(1)} %pack_shares.1), channel_id=1, source_target_pairs={{0,128},{128,0},{1,129},{129,1},{2,130},{130,2},{3,131},{131,3},{4... | collective-permute-start | bytes 49160 | tf_op jit(solution)/shard_map/ppermute | solution.py:696
  19.3 4.9 %collective-permute-start.7 = (f32[224,128]{1,0:T(8,128)S(1)}, f32[224,128]{1,0:T(8,128)S(1)}, u32[]{:S(2)}, u32[]{:S(2)}) collective-permute-start(f32[224,128]{1,0:T(8,128)S(1)} %get-tuple-element.56), channel_id=1, source_target_pairs={{0,1},{1,0},{2,3},{3,2},{4,5},{5,4},{6,7},{7,6},{128,129},{129,128... | collective-permute-start | bytes 344072 | tf_op jit(solution)/shard_map/ppermute | solution.py:662
  19.5 6.8 %collective-permute-start.8 = (f32[224,128]{1,0:T(8,128)S(1)}, f32[224,128]{1,0:T(8,128)S(1)}, u32[]{:S(2)}, u32[]{:S(2)}) collective-permute-start(f32[224,128]{1,0:T(8,128)S(1)} %get-tuple-element.57), channel_id=1, source_target_pairs={{0,128},{1,2},{2,1},{3,4},{4,3},{5,6},{6,5},{7,135},{128,0},{129,1... | collective-permute-start | bytes 344072 | tf_op jit(solution)/shard_map/ppermute | solution.py:662

commit v12 on v11

--- a/solution.py
+++ b/solution.py
@@ -287,7 +287,7 @@
 
 def strip_kernel(
     sheet_ref, cap_ref, drop_ref, counts_ref, field_ref, base_ref, arriving_ref, first_ref, between_ref,
-    within_ref, late_ref, relayed_ref, shares_ref, even_ref, odd_ref, wide_ref,
+    within_ref, late_ref, relayed_ref, shares_ref, odd_ref, even_ref, wide_ref,
 ):
     lane = lane_iota()
     within = lane % 16
@@ -492,7 +492,7 @@
 
 def solve_kernel(
     s_ref, x_ref, c_ref, k_ref, one_ref, two_ref, up_ref, down_ref, left_ref, right_ref, diag_ref, spread_ref,
-    wide_ref, even_ref, odd_ref, out_ref, base_out_ref,
+    wide_ref, odd_ref, even_ref, out_ref, base_out_ref,
     c_ext, k_ext, f_ext, bound, link_up, link_down, link_left, link_right, inv_ext, src, state, alt,
 ):
     lane = lane_iota()
@@ -695,11 +695,11 @@
     shares = call(shares_kernel, "pack_shares", (buffer(4),), spec(3))(first, between, relayed)[0]
     shares = lax.ppermute(shares, "die", others)
 
-    even, odd, wide = call(
+    odd, even, wide = call(
         strip_kernel, "column_strips", (buffer(COL_GROUPS), buffer(COL_GROUPS), arr(200, 128)), spec(13)
     )(sheet_res, capacity, drop_start, counts, field, base, arriving, first, between, within, late, relayed, shares)
+    odd = swap(odd, "col", 1)
     even = swap(even, "col", 0)
-    odd = swap(odd, "col", 1)
 
     image, pair = arr(4, 8 * GROUPS, 256), arr(2, 8 * GROUPS, 256)
     parts = call(
@@ -710,7 +710,7 @@
     ext = pltpu.VMEM((8 * GROUPS, 384), F32)
     scratch = [ext, ext, pltpu.VMEM((2, 8 * GROUPS, 384), F32), pltpu.VMEM((4, 40, 384), F32)] + [ext] * 8
     return call(solve_kernel, "solve", (arr(2, 2, 64, 256), arr(2, 8, 32)), spec(15), scratch)(
-        *parts, wide, even, odd
+        *parts, wide, odd, even
     )
 
 

time: 34.1 us -> 35 us (1.026)
  waiting for transfers between devices: 7 us -> 9.02 us
  starting transfers between devices: 13 us -> 12 us
    ppermute x7, waiting for transfers between devices: 5.76 us -> 7.78 us  [swap(): lax.ppermute(value, ('die', axis), swaps(lax.axis_size(axis), offset))]
    ppermute x7, starting transfers between devices: 11.5 us -> 10.5 us  [swap(): lax.ppermute(value, ('die', axis), swaps(lax.axis_size(axis), offset))]
where the time goes in v12:
time: 35 us; the launch traced here: 34.9 us
  starting transfers between devices  12 us (34%)
  Pallas kernels  11.8 us (34%)
  waiting for transfers between devices  9.02 us (26%)
  local copies, waits for them, and re-layouts  1.26 us (4%)
  between operations  0.79 us (2%)
    ppermute x7, starting transfers between devices, swap(): lax.ppermute(value, ('die', axis), swaps(lax.axis_size(axis), offset))  10.5 us
    ppermute x7, waiting for transfers between devices, swap(): lax.ppermute(value, ('die', axis), swaps(lax.axis_size(axis), offset))  7.78 us
    pallas_call x1, Pallas kernels, per_device(): call(solve_kernel, 'solve', (arr(2, 2, 64, 256), arr(2, 8, 32)), spec(15)...  7.55 us
    pallas_call x1, Pallas kernels, per_device(): call(place_kernel, 'place_vias', (arr(4, 4, 64, 128), buffer(LATE + EARLY...  2.04 us
    unnamed x20, local copies, waits for them, and re-layouts  1.26 us
    ppermute x1, waiting for transfers between devices, per_device(): shares = lax.ppermute(shares, 'die', others)  1.24 us
    ppermute x1, starting transfers between devices, per_device(): got = lax.ppermute(send, 'die', others)  0.91 us
    pallas_call x1, Pallas kernels, per_device(): call(prepare_kernel, 'spread_cells', (arr(4, VIAS, 8, 128), arr(4, 8, 128...  0.74 us
  transfers between devices with their start and end apart: 9, of which 6 were waited for; matrix products, arithmetic and copies ran while one was open for 0% of the time, Pallas kernels for 10%

profile of v12, /device:TPU:102, one launch (start us, length us, event | category | flops | bytes accessed | tf_op | source)
XLA Modules:
  0.0 34.9 jit_solution(16834476495041069698)
XLA Ops:
  0.6 1.2 %copy-done.3 = f32[2,2,2,32,8,32]{5,4,3,2,1,0:T(8,128)S(1)} copy-done((f32[2,2,2,32,8,32]{5,4,3,2,1,0:T(8,128)S(1)}, f32[2,2,2,32,8,32]{5,4,3,2,1,0:T(8,128)}, u32[]{:S(2)}) %copy-start.3) | copy-done | bytes 262168
  1.9 0.3 pack_vias.1
  2.2 0.0 copy-start
  2.2 0.9 %collective-permute-start = (f32[33,8,128]{2,1,0:T(8,128)S(1)}, f32[33,8,128]{2,1,0:T(8,128)S(1)}, u32[]{:S(2)}, u32[]{:S(2)}) collective-permute-start(f32[33,8,128]{2,1,0:T(8,128)S(1)} %get-tuple-element.32.send_ref), channel_id=1, source_target_pairs={{0,128},{128,0},{1,129},{129,1},{2,130},{130,2},{3,131},{131,3},{4... | collective-permute-start | bytes 405512 | tf_op jit(solution)/shard_map/ppermute | solution.py:671
  3.1 0.1 pack_base.1.base_ref
  3.2 0.0 copy-start.2
  3.2 0.1 collective-permute-start.1
  3.3 0.7 %spread_cells.1 = (f32[4,32,8,128]{3,2,1,0:T(8,128)S(1)}, f32[4,8,128]{2,1,0:T(8,128)S(1)}, f32[4,4,8,128]{3,2,1,0:T(8,128)S(1)}, bf16[256,1024]{1,0:T(8,128)(2,1)S(1)}, f32[4,64,128]{2,1,0:T(8,128)S(1)}) custom-call(s32[2,32,8,32]{3,2,1,0:T(8,128)S(1)} %copy-done.4, s32[2,8,32]{2,1,0:T(8,128)S(1)} %copy-done.6, f32[2,2,2,8,32]{4,3,2,1,0:T(8,128)S(1)} %copy-done.5), custom_call_target="tpu_custom_call" | custom-call | tf_op jit(solution)/shard_map/spread_cells/pallas_call | solution.py:677
  4.1 0.4 %collective-permute-done.1.got_ref.first_ref = f32[32,128]{1,0:T(8,128)S(1)} collective-permute-done((f32[32,128]{1,0:T(8,128)S(1)}, f32[32,128]{1,0:T(8,128)S(1)}, u32[]{:S(2)}, u32[]{:S(2)}) %collective-permute-start.1) | collective-permute-done | bytes 16416 | tf_op jit(solution)/shard_map/ppermute | solution.py:662
  4.5 3.4 %collective-permute-start.3 = (f32[352,128]{1,0:T(8,128)S(1)}, f32[352,128]{1,0:T(8,128)S(1)}, u32[]{:S(2)}, u32[]{:S(2)}) collective-permute-start(f32[352,128]{1,0:T(8,128)S(1)} %get-tuple-element.40), channel_id=1, source_target_pairs={{0,128},{8,16},{16,8},{24,32},{32,24},{40,48},{48,40},{56,64},{64,... | collective-permute-start | bytes 540680 | tf_op jit(solution)/shard_map/ppermute | solution.py:662
  8.0 2.0 %place_vias.1 = (f32[4,4,64,128]{3,2,1,0:T(8,128)S(1)}, f32[416,128]{1,0:T(8,128)S(1)}, f32[128,128]{1,0:T(8,128)S(1)}, f32[8,128]{1,0:T(8,128)S(1)}) custom-call(f32[2,32,8,128]{3,2,1,0:T(8,128)S(1)} %get-tuple-element.31.packed_ref, f32[33,8,128]{2,1,0:T(8,128)S(1)} %get-tuple-element.32.send_ref, f32[33,8,128]{2,1,0:T(8,128)S(1)} %collective-permute-done.got_ref, ...), custom_call_target="tpu_custom_call" | custom-call | flops 1000000000 | bytes 10000000 | tf_op jit(solution)/shard_map/place_vias/pallas_call | solution.py:686
  10.0 0.1 collective-permute-start.2
  10.1 3.6 %collective-permute-start.4 = (f32[128,128]{1,0:T(8,128)S(1)}, f32[128,128]{1,0:T(8,128)S(1)}, u32[]{:S(2)}, u32[]{:S(2)}) collective-permute-start(f32[128,128]{1,0:T(8,128)S(1)} %get-tuple-element.41), channel_id=1, source_target_pairs={{0,128},{8,16},{16,8},{24,32},{32,24},{40,48},{48,40},{56,64},{64,... | collective-permute-start | bytes 196616 | tf_op jit(solution)/shard_map/ppermute | solution.py:662
  13.7 0.1 collective-permute-start.5
  13.8 1.2 %collective-permute-done.5.relayed_ref = f32[32,128]{1,0:T(8,128)S(1)} collective-permute-done((f32[32,128]{1,0:T(8,128)S(1)}, f32[32,128]{1,0:T(8,128)S(1)}, u32[]{:S(2)}, u32[]{:S(2)}) %collective-permute-start.5) | collective-permute-done | bytes 16416 | tf_op jit(solution)/shard_map/ppermute | solution.py:662
  15.0 0.6 %collective-permute-start.6 = (f32[32,128]{1,0:T(8,128)S(1)}, f32[32,128]{1,0:T(8,128)S(1)}, u32[]{:S(2)}, u32[]{:S(2)}) collective-permute-start(f32[32,128]{1,0:T(8,128)S(1)} %pack_shares.1), channel_id=1, source_target_pairs={{0,128},{128,0},{1,129},{129,1},{2,130},{130,2},{3,131},{131,3},{4... | collective-permute-start | bytes 49160 | tf_op jit(solution)/shard_map/ppermute | solution.py:696
  15.5 1.9 %collective-permute-done.4.late_ref = f32[128,128]{1,0:T(8,128)S(1)} collective-permute-done((f32[128,128]{1,0:T(8,128)S(1)}, f32[128,128]{1,0:T(8,128)S(1)}, u32[]{:S(2)}, u32[]{:S(2)}) %collective-permute-start.4) | collective-permute-done | bytes 65568 | tf_op jit(solution)/shard_map/ppermute | solution.py:662
  17.5 1.2 %collective-permute-done.6.shares_ref = f32[32,128]{1,0:T(8,128)S(1)} collective-permute-done((f32[32,128]{1,0:T(8,128)S(1)}, f32[32,128]{1,0:T(8,128)S(1)}, u32[]{:S(2)}, u32[]{:S(2)}) %collective-permute-start.6) | collective-permute-done | bytes 16416 | tf_op jit(solution)/shard_map/ppermute | solution.py:696
  18.7 0.6 %column_strips.1 = (f32[224,128]{1,0:T(8,128)S(1)}, f32[224,128]{1,0:T(8,128)S(1)}, f32[200,128]{1,0:T(8,128)S(1)}) custom-call(f32[2,2,64,256]{3,2,1,0:T(8,128)S(1)} %copy-done, f32[2,64,256]{2,1,0:T(8,128)S(1)} %copy-done.2, f32[2,2,64,256]{3,2,1,0:T(8,128)S(1)} %copy-done.1, f32[4,64,128]{2,1,0:T(8,128)S(1)} %get-tuple-element.30.counts_ref, ...), custom_call_target="tpu_custom_call" | custom-call | tf_op jit(solution)/shard_map/column_strips/pallas_call | solution.py:698
  19.3 3.2 %collective-permute-start.7 = (f32[224,128]{1,0:T(8,128)S(1)}, f32[224,128]{1,0:T(8,128)S(1)}, u32[]{:S(2)}, u32[]{:S(2)}) collective-permute-start(f32[224,128]{1,0:T(8,128)S(1)} %get-tuple-element.56), channel_id=1, source_target_pairs={{0,128},{1,2},{2,1},{3,4},{4,3},{5,6},{6,5},{7,135},{128,0},{129,1... | collective-permute-start | bytes 344072 | tf_op jit(solution)/shard_map/ppermute | solution.py:662
  22.5 0.5 %assemble.1 = (f32[4,88,256]{2,1,0:T(8,128)S(1)}, f32[4,88,256]{2,1,0:T(8,128)S(1)}, f32[2,88,256]{2,1,0:T(8,128)S(1)}, f32[2,88,256]{2,1,0:T(8,128)S(1)}, f32[4...) custom-call(f32[2,2,64,256]{3,2,1,0:T(8,128)S(1)} %copy-done, ...), custom_call_target="tpu_custom_call" | custom-call | tf_op jit(solution)/shard_map/assemble/pallas_call | solution.py:705
  23.1 2.3 %collective-permute-done.7.odd_ref = f32[224,128]{1,0:T(8,128)S(1)} collective-permute-done((f32[224,128]{1,0:T(8,128)S(1)}, f32[224,128]{1,0:T(8,128)S(1)}, u32[]{:S(2)}, u32[]{:S(2)}) %collective-permute-start.7) | collective-permute-done | bytes 114720 | tf_op jit(solution)/shard_map/ppermute | solution.py:662
  25.4 1.9 %collective-permute-done.8.even_ref = f32[224,128]{1,0:T(8,128)S(1)} collective-permute-done((f32[224,128]{1,0:T(8,128)S(1)}, f32[224,128]{1,0:T(8,128)S(1)}, u32[]{:S(2)}, u32[]{:S(2)}) %collective-permute-start.8) | collective-permute-done | bytes 114720 | tf_op jit(solution)/shard_map/ppermute | solution.py:662
  27.3 7.6 %solve.1 = (f32[2,2,64,256]{3,2,1,0:T(8,128)}, f32[2,8,32]{2,1,0:T(8,128)}) custom-call(f32[4,88,256]{2,1,0:T(8,128)S(1)} %get-tuple-element.42.s_ref, f32[4,88,256]{2,1,0:T(8,128)S(1)} %get-tuple-element.43.x_ref, f32[2,88,256]{2,1,0:T(8,128)S(1)} %get-tuple-element.44.c_ref, f32[2,88,256]{2,1,0:T(8,128)S(1)} %get-tuple-element.45.k_ref, ...), custom_call_target="tpu_custom_call" | custom-call | tf_op jit(solution)/shard_map/solve/pallas_call | solution.py:712
  (24 shorter events, 0.1 us)
Async XLA Ops:
  0.6 1.2 %copy-start.3 = (f32[2,2,2,32,8,32]{5,4,3,2,1,0:T(8,128)S(1)}, f32[2,2,2,32,8,32]{5,4,3,2,1,0:T(8,128)}, u32[]{:S(2)}) copy-start(f32[2,2,2,32,8,32]{5,4,3,2,1,0:T(8,128)} %via_ref.1) | copy-start | bytes 786436
  1.9 1.2 %copy-start.7 = (f32[2,8,32]{2,1,0:T(8,128)S(1)}, f32[2,8,32]{2,1,0:T(8,128)}, u32[]{:S(2)}) copy-start(f32[2,8,32]{2,1,0:T(8,128)} %sheet_ref.4) | copy-start | bytes 6148
  1.9 1.2 %copy-start.8 = (f32[2,8,32]{2,1,0:T(8,128)S(1)}, f32[2,8,32]{2,1,0:T(8,128)}, u32[]{:S(2)}) copy-start(f32[2,8,32]{2,1,0:T(8,128)} %start_ref.1) | copy-start | bytes 6148
  1.9 1.2 %copy-start.9 = (s32[1,4]{1,0:T(1,128)S(1)}, s32[1,4]{1,0:T(1,128)}, u32[]{:S(2)}) copy-start(s32[1,4]{1,0:T(1,128)} %bump_ref.1) | copy-start | bytes 52
  1.9 1.4 %copy-start.4 = (s32[2,32,8,32]{3,2,1,0:T(8,128)S(1)}, s32[2,32,8,32]{3,2,1,0:T(8,128)}, u32[]{:S(2)}) copy-start(s32[2,32,8,32]{3,2,1,0:T(8,128)} %cell_ref.1) | copy-start | bytes 196612
  1.9 1.4 %copy-start.5 = (f32[2,2,2,8,32]{4,3,2,1,0:T(8,128)S(1)}, f32[2,2,2,8,32]{4,3,2,1,0:T(8,128)}, u32[]{:S(2)}) copy-start(f32[2,2,2,8,32]{4,3,2,1,0:T(8,128)} %load_ref.1) | copy-start | bytes 24580
  1.9 1.4 %copy-start.6 = (s32[2,8,32]{2,1,0:T(8,128)S(1)}, s32[2,8,32]{2,1,0:T(8,128)}, u32[]{:S(2)}) copy-start(s32[2,8,32]{2,1,0:T(8,128)} %load_cell_ref.1) | copy-start | bytes 6148
  1.9 2.6 %copy-start.1 = (f32[2,2,64,256]{3,2,1,0:T(8,128)S(1)}, f32[2,2,64,256]{3,2,1,0:T(8,128)}, u32[]{:S(2)}) copy-start(f32[2,2,64,256]{3,2,1,0:T(8,128)} %drop_ref.5) | copy-start | bytes 786436
  2.2 2.3 %copy-start = (f32[2,2,64,256]{3,2,1,0:T(8,128)S(1)}, f32[2,2,64,256]{3,2,1,0:T(8,128)}, u32[]{:S(2)}) copy-start(f32[2,2,64,256]{3,2,1,0:T(8,128)} %sheet_ref.7) | copy-start | bytes 786436
  2.2 5.8 %collective-permute-start = (f32[33,8,128]{2,1,0:T(8,128)S(1)}, f32[33,8,128]{2,1,0:T(8,128)S(1)}, u32[]{:S(2)}, u32[]{:S(2)}) collective-permute-start(f32[33,8,128]{2,1,0:T(8,128)S(1)} %get-tuple-element.32.send_ref), channel_id=1, source_target_pairs={{0,128},{128,0},{1,129},{129,1},{2,130},{130,2},{3,131},{131,3},{4... | collective-permute-start | bytes 405512 | tf_op jit(solution)/shard_map/ppermute | solution.py:671
  3.2 1.3 %copy-start.2 = (f32[2,64,256]{2,1,0:T(8,128)S(1)}, f32[2,64,256]{2,1,0:T(8,128)}, u32[]{:S(2)}) copy-start(f32[2,64,256]{2,1,0:T(8,128)} %cap_ref.5) | copy-start | bytes 393220
  3.2 1.3 %collective-permute-start.1 = (f32[32,128]{1,0:T(8,128)S(1)}, f32[32,128]{1,0:T(8,128)S(1)}, u32[]{:S(2)}, u32[]{:S(2)}) collective-permute-start(f32[32,128]{1,0:T(8,128)S(1)} %pack_base.1.base_ref), channel_id=1, source_target_pairs={{0,8},{8,0},{16,24},{24,16},{32,40},{40,32},{48,56},{56,48},{64,72... | collective-permute-start | bytes 49160 | tf_op jit(solution)/shard_map/ppermute | solution.py:662
  4.5 9.2 %collective-permute-start.3 = (f32[352,128]{1,0:T(8,128)S(1)}, f32[352,128]{1,0:T(8,128)S(1)}, u32[]{:S(2)}, u32[]{:S(2)}) collective-permute-start(f32[352,128]{1,0:T(8,128)S(1)} %get-tuple-element.40), channel_id=1, source_target_pairs={{0,128},{8,16},{16,8},{24,32},{32,24},{40,48},{48,40},{56,64},{64,... | collective-permute-start | bytes 540680 | tf_op jit(solution)/shard_map/ppermute | solution.py:662
  10.0 8.7 %collective-permute-start.2 = (f32[416,128]{1,0:T(8,128)S(1)}, f32[416,128]{1,0:T(8,128)S(1)}, u32[]{:S(2)}, u32[]{:S(2)}) collective-permute-start(f32[416,128]{1,0:T(8,128)S(1)} %get-tuple-element.39), channel_id=1, source_target_pairs={{0,8},{8,0},{16,24},{24,16},{32,40},{40,32},{48,56},{56,48},{64,72... | collective-permute-start | bytes 638984 | tf_op jit(solution)/shard_map/ppermute | solution.py:662
  10.1 7.4 %collective-permute-start.4 = (f32[128,128]{1,0:T(8,128)S(1)}, f32[128,128]{1,0:T(8,128)S(1)}, u32[]{:S(2)}, u32[]{:S(2)}) collective-permute-start(f32[128,128]{1,0:T(8,128)S(1)} %get-tuple-element.41), channel_id=1, source_target_pairs={{0,128},{8,16},{16,8},{24,32},{32,24},{40,48},{48,40},{56,64},{64,... | collective-permute-start | bytes 196616 | tf_op jit(solution)/shard_map/ppermute | solution.py:662
  13.7 1.3 %collective-permute-start.5 = (f32[32,128]{1,0:T(8,128)S(1)}, f32[32,128]{1,0:T(8,128)S(1)}, u32[]{:S(2)}, u32[]{:S(2)}) collective-permute-start(f32[32,128]{1,0:T(8,128)S(1)} %pack_relay.1), channel_id=1, source_target_pairs={{0,8},{8,0},{16,24},{24,16},{32,40},{40,32},{48,56},{56,48},{64,72... | collective-permute-start | bytes 49160 | tf_op jit(solution)/shard_map/ppermute | solution.py:662
  15.0 3.7 %collective-permute-start.6 = (f32[32,128]{1,0:T(8,128)S(1)}, f32[32,128]{1,0:T(8,128)S(1)}, u32[]{:S(2)}, u32[]{:S(2)}) collective-permute-start(f32[32,128]{1,0:T(8,128)S(1)} %pack_shares.1), channel_id=1, source_target_pairs={{0,128},{128,0},{1,129},{129,1},{2,130},{130,2},{3,131},{131,3},{4... | collective-permute-start | bytes 49160 | tf_op jit(solution)/shard_map/ppermute | solution.py:696
  19.3 6.1 %collective-permute-start.7 = (f32[224,128]{1,0:T(8,128)S(1)}, f32[224,128]{1,0:T(8,128)S(1)}, u32[]{:S(2)}, u32[]{:S(2)}) collective-permute-start(f32[224,128]{1,0:T(8,128)S(1)} %get-tuple-element.56), channel_id=1, source_target_pairs={{0,128},{1,2},{2,1},{3,4},{4,3},{5,6},{6,5},{7,135},{128,0},{129,1... | collective-permute-start | bytes 344072 | tf_op jit(solution)/shard_map/ppermute | solution.py:662
  22.5 4.8 %collective-permute-start.8 = (f32[224,128]{1,0:T(8,128)S(1)}, f32[224,128]{1,0:T(8,128)S(1)}, u32[]{:S(2)}, u32[]{:S(2)}) collective-permute-start(f32[224,128]{1,0:T(8,128)S(1)} %get-tuple-element.57), channel_id=1, source_target_pairs={{0,1},{1,0},{2,3},{3,2},{4,5},{5,4},{6,7},{7,6},{128,129},{129,128... | collective-permute-start | bytes 344072 | tf_op jit(solution)/shard_map/ppermute | solution.py:662

commit v13 on v11

--- a/solution.py
+++ b/solution.py
@@ -523,14 +523,6 @@
             value = jnp.where(take_right, right, wide_ref[rows(5 * field + g), :])
             out.append(jnp.where(take_left, left, value))
         fields.append(jnp.concatenate(out, axis=0))
-    solved = base_solve((fields[0], fields[1], (fields[2], fields[3]), fields[4]))
-    for t in range(STEPS):
-        pieces = halves(solved[t])
-        for n in range(2):
-            bound[2 * t + n] = jnp.dot(pieces, spread_ref[n], preferred_element_type=F32)
-    for n in range(2):
-        base_out_ref[n] = roll(solved[1][0:8], -(64 * n + 16), 1)[:, 0:32]
-
     sub, sub3 = sub_iota(), sub_iota(384)
     last = lax.axis_size("row") - 1
 
@@ -561,6 +553,15 @@
                 k_ext[rows(g), :] = wide(k_ref, g, third(1, 2 + d, g), d)
         @pl.when(row >= 0)
         def _():
+            if i == 0:
+                solved = base_solve((fields[0], fields[1], (fields[2], fields[3]), fields[4]))
+                for t in range(STEPS):
+                    pieces = halves(solved[t])
+                    for n in range(2):
+                        bound[2 * t + n] = jnp.dot(pieces, spread_ref[n], preferred_element_type=F32)
+                for n in range(2):
+                    base_out_ref[n] = roll(solved[1][0:8], -(64 * n + 16), 1)[:, 0:32]
+
             sheets = [third(0, i, g) for g in range(GROUPS)]
             for g in range(GROUPS):
                 here = sheets[g]

time: 34.1 us -> 33.8 us (level)
    pallas_call x1, Pallas kernels: 7.56 us -> 7.2 us  [per_device(): call(solve_kernel, 'solve', (arr(2, 2, 64, 256), arr(2, 8, 32)), spec(15)...]
where the time goes in v13:
time: 33.8 us; the launch traced here: 33.5 us
  starting transfers between devices  13 us (38%)
  Pallas kernels  11.5 us (34%)
  waiting for transfers between devices  7 us (21%)
  local copies, waits for them, and re-layouts  1.26 us (4%)
  between operations  0.79 us (2%)
    ppermute x7, starting transfers between devices, swap(): lax.ppermute(value, ('die', axis), swaps(lax.axis_size(axis), offset))  11.5 us
    pallas_call x1, Pallas kernels, per_device(): call(solve_kernel, 'solve', (arr(2, 2, 64, 256), arr(2, 8, 32)), spec(15)...  7.2 us
    ppermute x7, waiting for transfers between devices, swap(): lax.ppermute(value, ('die', axis), swaps(lax.axis_size(axis), offset))  5.77 us
    pallas_call x1, Pallas kernels, per_device(): call(place_kernel, 'place_vias', (arr(4, 4, 64, 128), buffer(LATE + EARLY...  2.04 us
    unnamed x20, local copies, waits for them, and re-layouts  1.26 us
    ppermute x1, waiting for transfers between devices, per_device(): shares = lax.ppermute(shares, 'die', others)  1.23 us
    ppermute x1, starting transfers between devices, per_device(): got = lax.ppermute(send, 'die', others)  0.91 us
    pallas_call x1, Pallas kernels, per_device(): call(prepare_kernel, 'spread_cells', (arr(4, VIAS, 8, 128), arr(4, 8, 128...  0.73 us
  transfers between devices with their start and end apart: 9, of which 6 were waited for; matrix products, arithmetic and copies ran while one was open for 0% of the time, Pallas kernels for 10%

profile of v13, /device:TPU:102, one launch (start us, length us, event | category | flops | bytes accessed | tf_op | source)
XLA Modules:
  0.0 33.5 jit_solution(5138000620760285712)
XLA Ops:
  0.6 1.2 %copy-done.3 = f32[2,2,2,32,8,32]{5,4,3,2,1,0:T(8,128)S(1)} copy-done((f32[2,2,2,32,8,32]{5,4,3,2,1,0:T(8,128)S(1)}, f32[2,2,2,32,8,32]{5,4,3,2,1,0:T(8,128)}, u32[]{:S(2)}) %copy-start.3) | copy-done | bytes 262168
  1.9 0.3 pack_vias.1
  2.2 0.0 copy-start
  2.2 0.9 %collective-permute-start = (f32[33,8,128]{2,1,0:T(8,128)S(1)}, f32[33,8,128]{2,1,0:T(8,128)S(1)}, u32[]{:S(2)}, u32[]{:S(2)}) collective-permute-start(f32[33,8,128]{2,1,0:T(8,128)S(1)} %get-tuple-element.32.send_ref), channel_id=1, source_target_pairs={{0,128},{128,0},{1,129},{129,1},{2,130},{130,2},{3,131},{131,3},{4... | collective-permute-start | bytes 405512 | tf_op jit(solution)/shard_map/ppermute | solution.py:672
  3.1 0.1 pack_base.1.base_ref
  3.2 0.1 collective-permute-start.1
  3.3 0.7 %spread_cells.1 = (f32[4,32,8,128]{3,2,1,0:T(8,128)S(1)}, f32[4,8,128]{2,1,0:T(8,128)S(1)}, f32[4,4,8,128]{3,2,1,0:T(8,128)S(1)}, bf16[256,1024]{1,0:T(8,128)(2,1)S(1)}, f32[4,64,128]{2,1,0:T(8,128)S(1)}) custom-call(s32[2,32,8,32]{3,2,1,0:T(8,128)S(1)} %copy-done.4, s32[2,8,32]{2,1,0:T(8,128)S(1)} %copy-done.6, f32[2,2,2,8,32]{4,3,2,1,0:T(8,128)S(1)} %copy-done.5), custom_call_target="tpu_custom_call" | custom-call | tf_op jit(solution)/shard_map/spread_cells/pallas_call | solution.py:678
  4.1 0.4 %collective-permute-done.1.got_ref.first_ref = f32[32,128]{1,0:T(8,128)S(1)} collective-permute-done((f32[32,128]{1,0:T(8,128)S(1)}, f32[32,128]{1,0:T(8,128)S(1)}, u32[]{:S(2)}, u32[]{:S(2)}) %collective-permute-start.1) | collective-permute-done | bytes 16416 | tf_op jit(solution)/shard_map/ppermute | solution.py:663
  4.5 3.4 %collective-permute-start.3 = (f32[352,128]{1,0:T(8,128)S(1)}, f32[352,128]{1,0:T(8,128)S(1)}, u32[]{:S(2)}, u32[]{:S(2)}) collective-permute-start(f32[352,128]{1,0:T(8,128)S(1)} %get-tuple-element.40), channel_id=1, source_target_pairs={{0,128},{8,16},{16,8},{24,32},{32,24},{40,48},{48,40},{56,64},{64,... | collective-permute-start | bytes 540680 | tf_op jit(solution)/shard_map/ppermute | solution.py:663
  8.0 2.0 %place_vias.1 = (f32[4,4,64,128]{3,2,1,0:T(8,128)S(1)}, f32[416,128]{1,0:T(8,128)S(1)}, f32[128,128]{1,0:T(8,128)S(1)}, f32[8,128]{1,0:T(8,128)S(1)}) custom-call(f32[2,32,8,128]{3,2,1,0:T(8,128)S(1)} %get-tuple-element.31.packed_ref, f32[33,8,128]{2,1,0:T(8,128)S(1)} %get-tuple-element.32.send_ref, f32[33,8,128]{2,1,0:T(8,128)S(1)} %collective-permute-done.got_ref, ...), custom_call_target="tpu_custom_call" | custom-call | flops 1000000000 | bytes 10000000 | tf_op jit(solution)/shard_map/place_vias/pallas_call | solution.py:687
  10.0 0.1 collective-permute-start.2
  10.1 3.6 %collective-permute-start.4 = (f32[128,128]{1,0:T(8,128)S(1)}, f32[128,128]{1,0:T(8,128)S(1)}, u32[]{:S(2)}, u32[]{:S(2)}) collective-permute-start(f32[128,128]{1,0:T(8,128)S(1)} %get-tuple-element.41), channel_id=1, source_target_pairs={{0,128},{8,16},{16,8},{24,32},{32,24},{40,48},{48,40},{56,64},{64,... | collective-permute-start | bytes 196616 | tf_op jit(solution)/shard_map/ppermute | solution.py:663
  13.7 0.1 collective-permute-start.5
  13.8 1.2 %collective-permute-done.5.relayed_ref = f32[32,128]{1,0:T(8,128)S(1)} collective-permute-done((f32[32,128]{1,0:T(8,128)S(1)}, f32[32,128]{1,0:T(8,128)S(1)}, u32[]{:S(2)}, u32[]{:S(2)}) %collective-permute-start.5) | collective-permute-done | bytes 16416 | tf_op jit(solution)/shard_map/ppermute | solution.py:663
  15.0 0.6 %collective-permute-start.6 = (f32[32,128]{1,0:T(8,128)S(1)}, f32[32,128]{1,0:T(8,128)S(1)}, u32[]{:S(2)}, u32[]{:S(2)}) collective-permute-start(f32[32,128]{1,0:T(8,128)S(1)} %pack_shares.1), channel_id=1, source_target_pairs={{0,128},{128,0},{1,129},{129,1},{2,130},{130,2},{3,131},{131,3},{4... | collective-permute-start | bytes 49160 | tf_op jit(solution)/shard_map/ppermute | solution.py:697
  15.5 1.9 %collective-permute-done.4.late_ref = f32[128,128]{1,0:T(8,128)S(1)} collective-permute-done((f32[128,128]{1,0:T(8,128)S(1)}, f32[128,128]{1,0:T(8,128)S(1)}, u32[]{:S(2)}, u32[]{:S(2)}) %collective-permute-start.4) | collective-permute-done | bytes 65568 | tf_op jit(solution)/shard_map/ppermute | solution.py:663
  17.5 1.2 %collective-permute-done.6.shares_ref = f32[32,128]{1,0:T(8,128)S(1)} collective-permute-done((f32[32,128]{1,0:T(8,128)S(1)}, f32[32,128]{1,0:T(8,128)S(1)}, u32[]{:S(2)}, u32[]{:S(2)}) %collective-permute-start.6) | collective-permute-done | bytes 16416 | tf_op jit(solution)/shard_map/ppermute | solution.py:697
  18.7 0.6 %column_strips.1 = (f32[224,128]{1,0:T(8,128)S(1)}, f32[224,128]{1,0:T(8,128)S(1)}, f32[200,128]{1,0:T(8,128)S(1)}) custom-call(f32[2,2,64,256]{3,2,1,0:T(8,128)S(1)} %copy-done, f32[2,64,256]{2,1,0:T(8,128)S(1)} %copy-done.2, f32[2,2,64,256]{3,2,1,0:T(8,128)S(1)} %copy-done.1, f32[4,64,128]{2,1,0:T(8,128)S(1)} %get-tuple-element.30.counts_ref, ...), custom_call_target="tpu_custom_call" | custom-call | tf_op jit(solution)/shard_map/column_strips/pallas_call | solution.py:699
  19.3 0.2 collective-permute-start.7
  19.5 4.0 %collective-permute-start.8 = (f32[224,128]{1,0:T(8,128)S(1)}, f32[224,128]{1,0:T(8,128)S(1)}, u32[]{:S(2)}, u32[]{:S(2)}) collective-permute-start(f32[224,128]{1,0:T(8,128)S(1)} %get-tuple-element.57), channel_id=1, source_target_pairs={{0,128},{1,2},{2,1},{3,4},{4,3},{5,6},{6,5},{7,135},{128,0},{129,1... | collective-permute-start | bytes 344072 | tf_op jit(solution)/shard_map/ppermute | solution.py:663
  23.6 0.5 %assemble.1 = (f32[4,88,256]{2,1,0:T(8,128)S(1)}, f32[4,88,256]{2,1,0:T(8,128)S(1)}, f32[2,88,256]{2,1,0:T(8,128)S(1)}, f32[2,88,256]{2,1,0:T(8,128)S(1)}, f32[4...) custom-call(f32[2,2,64,256]{3,2,1,0:T(8,128)S(1)} %copy-done, ...), custom_call_target="tpu_custom_call" | custom-call | tf_op jit(solution)/shard_map/assemble/pallas_call | solution.py:706
  24.1 0.1 collective-permute-done.7.even_ref
  24.2 2.1 %collective-permute-done.8.odd_ref = f32[224,128]{1,0:T(8,128)S(1)} collective-permute-done((f32[224,128]{1,0:T(8,128)S(1)}, f32[224,128]{1,0:T(8,128)S(1)}, u32[]{:S(2)}, u32[]{:S(2)}) %collective-permute-start.8) | collective-permute-done | bytes 114720 | tf_op jit(solution)/shard_map/ppermute | solution.py:663
  26.3 7.2 %solve.1 = (f32[2,2,64,256]{3,2,1,0:T(8,128)}, f32[2,8,32]{2,1,0:T(8,128)}) custom-call(f32[4,88,256]{2,1,0:T(8,128)S(1)} %get-tuple-element.42.s_ref, f32[4,88,256]{2,1,0:T(8,128)S(1)} %get-tuple-element.43.x_ref, f32[2,88,256]{2,1,0:T(8,128)S(1)} %get-tuple-element.44.c_ref, f32[2,88,256]{2,1,0:T(8,128)S(1)} %get-tuple-element.45.k_ref, ...), custom_call_target="tpu_custom_call" | custom-call | tf_op jit(solution)/shard_map/solve/pallas_call | solution.py:713
  (24 shorter events, 0.1 us)
Async XLA Ops:
  0.6 1.2 %copy-start.3 = (f32[2,2,2,32,8,32]{5,4,3,2,1,0:T(8,128)S(1)}, f32[2,2,2,32,8,32]{5,4,3,2,1,0:T(8,128)}, u32[]{:S(2)}) copy-start(f32[2,2,2,32,8,32]{5,4,3,2,1,0:T(8,128)} %via_ref.1) | copy-start | bytes 786436
  1.9 1.2 %copy-start.7 = (f32[2,8,32]{2,1,0:T(8,128)S(1)}, f32[2,8,32]{2,1,0:T(8,128)}, u32[]{:S(2)}) copy-start(f32[2,8,32]{2,1,0:T(8,128)} %sheet_ref.4) | copy-start | bytes 6148
  1.9 1.2 %copy-start.8 = (f32[2,8,32]{2,1,0:T(8,128)S(1)}, f32[2,8,32]{2,1,0:T(8,128)}, u32[]{:S(2)}) copy-start(f32[2,8,32]{2,1,0:T(8,128)} %start_ref.1) | copy-start | bytes 6148
  1.9 1.2 %copy-start.9 = (s32[1,4]{1,0:T(1,128)S(1)}, s32[1,4]{1,0:T(1,128)}, u32[]{:S(2)}) copy-start(s32[1,4]{1,0:T(1,128)} %bump_ref.1) | copy-start | bytes 52
  1.9 1.4 %copy-start.4 = (s32[2,32,8,32]{3,2,1,0:T(8,128)S(1)}, s32[2,32,8,32]{3,2,1,0:T(8,128)}, u32[]{:S(2)}) copy-start(s32[2,32,8,32]{3,2,1,0:T(8,128)} %cell_ref.1) | copy-start | bytes 196612
  1.9 1.4 %copy-start.5 = (f32[2,2,2,8,32]{4,3,2,1,0:T(8,128)S(1)}, f32[2,2,2,8,32]{4,3,2,1,0:T(8,128)}, u32[]{:S(2)}) copy-start(f32[2,2,2,8,32]{4,3,2,1,0:T(8,128)} %load_ref.1) | copy-start | bytes 24580
  1.9 1.4 %copy-start.6 = (s32[2,8,32]{2,1,0:T(8,128)S(1)}, s32[2,8,32]{2,1,0:T(8,128)}, u32[]{:S(2)}) copy-start(s32[2,8,32]{2,1,0:T(8,128)} %load_cell_ref.1) | copy-start | bytes 6148
  1.9 2.6 %copy-start.1 = (f32[2,2,64,256]{3,2,1,0:T(8,128)S(1)}, f32[2,2,64,256]{3,2,1,0:T(8,128)}, u32[]{:S(2)}) copy-start(f32[2,2,64,256]{3,2,1,0:T(8,128)} %drop_ref.5) | copy-start | bytes 786436
  2.2 2.3 %copy-start = (f32[2,2,64,256]{3,2,1,0:T(8,128)S(1)}, f32[2,2,64,256]{3,2,1,0:T(8,128)}, u32[]{:S(2)}) copy-start(f32[2,2,64,256]{3,2,1,0:T(8,128)} %sheet_ref.7) | copy-start | bytes 786436
  2.2 5.8 %collective-permute-start = (f32[33,8,128]{2,1,0:T(8,128)S(1)}, f32[33,8,128]{2,1,0:T(8,128)S(1)}, u32[]{:S(2)}, u32[]{:S(2)}) collective-permute-start(f32[33,8,128]{2,1,0:T(8,128)S(1)} %get-tuple-element.32.send_ref), channel_id=1, source_target_pairs={{0,128},{128,0},{1,129},{129,1},{2,130},{130,2},{3,131},{131,3},{4... | collective-permute-start | bytes 405512 | tf_op jit(solution)/shard_map/ppermute | solution.py:672
  3.2 1.3 %copy-start.2 = (f32[2,64,256]{2,1,0:T(8,128)S(1)}, f32[2,64,256]{2,1,0:T(8,128)}, u32[]{:S(2)}) copy-start(f32[2,64,256]{2,1,0:T(8,128)} %cap_ref.5) | copy-start | bytes 393220
  3.2 1.3 %collective-permute-start.1 = (f32[32,128]{1,0:T(8,128)S(1)}, f32[32,128]{1,0:T(8,128)S(1)}, u32[]{:S(2)}, u32[]{:S(2)}) collective-permute-start(f32[32,128]{1,0:T(8,128)S(1)} %pack_base.1.base_ref), channel_id=1, source_target_pairs={{0,8},{8,0},{16,24},{24,16},{32,40},{40,32},{48,56},{56,48},{64,72... | collective-permute-start | bytes 49160 | tf_op jit(solution)/shard_map/ppermute | solution.py:663
  4.5 9.2 %collective-permute-start.3 = (f32[352,128]{1,0:T(8,128)S(1)}, f32[352,128]{1,0:T(8,128)S(1)}, u32[]{:S(2)}, u32[]{:S(2)}) collective-permute-start(f32[352,128]{1,0:T(8,128)S(1)} %get-tuple-element.40), channel_id=1, source_target_pairs={{0,128},{8,16},{16,8},{24,32},{32,24},{40,48},{48,40},{56,64},{64,... | collective-permute-start | bytes 540680 | tf_op jit(solution)/shard_map/ppermute | solution.py:663
  10.0 8.7 %collective-permute-start.2 = (f32[416,128]{1,0:T(8,128)S(1)}, f32[416,128]{1,0:T(8,128)S(1)}, u32[]{:S(2)}, u32[]{:S(2)}) collective-permute-start(f32[416,128]{1,0:T(8,128)S(1)} %get-tuple-element.39), channel_id=1, source_target_pairs={{0,8},{8,0},{16,24},{24,16},{32,40},{40,32},{48,56},{56,48},{64,72... | collective-permute-start | bytes 638984 | tf_op jit(solution)/shard_map/ppermute | solution.py:663
  10.1 7.4 %collective-permute-start.4 = (f32[128,128]{1,0:T(8,128)S(1)}, f32[128,128]{1,0:T(8,128)S(1)}, u32[]{:S(2)}, u32[]{:S(2)}) collective-permute-start(f32[128,128]{1,0:T(8,128)S(1)} %get-tuple-element.41), channel_id=1, source_target_pairs={{0,128},{8,16},{16,8},{24,32},{32,24},{40,48},{48,40},{56,64},{64,... | collective-permute-start | bytes 196616 | tf_op jit(solution)/shard_map/ppermute | solution.py:663
  13.7 1.3 %collective-permute-start.5 = (f32[32,128]{1,0:T(8,128)S(1)}, f32[32,128]{1,0:T(8,128)S(1)}, u32[]{:S(2)}, u32[]{:S(2)}) collective-permute-start(f32[32,128]{1,0:T(8,128)S(1)} %pack_relay.1), channel_id=1, source_target_pairs={{0,8},{8,0},{16,24},{24,16},{32,40},{40,32},{48,56},{56,48},{64,72... | collective-permute-start | bytes 49160 | tf_op jit(solution)/shard_map/ppermute | solution.py:663
  15.0 3.7 %collective-permute-start.6 = (f32[32,128]{1,0:T(8,128)S(1)}, f32[32,128]{1,0:T(8,128)S(1)}, u32[]{:S(2)}, u32[]{:S(2)}) collective-permute-start(f32[32,128]{1,0:T(8,128)S(1)} %pack_shares.1), channel_id=1, source_target_pairs={{0,128},{128,0},{1,129},{129,1},{2,130},{130,2},{3,131},{131,3},{4... | collective-permute-start | bytes 49160 | tf_op jit(solution)/shard_map/ppermute | solution.py:697
  19.3 4.9 %collective-permute-start.7 = (f32[224,128]{1,0:T(8,128)S(1)}, f32[224,128]{1,0:T(8,128)S(1)}, u32[]{:S(2)}, u32[]{:S(2)}) collective-permute-start(f32[224,128]{1,0:T(8,128)S(1)} %get-tuple-element.56), channel_id=1, source_target_pairs={{0,1},{1,0},{2,3},{3,2},{4,5},{5,4},{6,7},{7,6},{128,129},{129,128... | collective-permute-start | bytes 344072 | tf_op jit(solution)/shard_map/ppermute | solution.py:663
  19.5 6.8 %collective-permute-start.8 = (f32[224,128]{1,0:T(8,128)S(1)}, f32[224,128]{1,0:T(8,128)S(1)}, u32[]{:S(2)}, u32[]{:S(2)}) collective-permute-start(f32[224,128]{1,0:T(8,128)S(1)} %get-tuple-element.57), channel_id=1, source_target_pairs={{0,128},{1,2},{2,1},{3,4},{4,3},{5,6},{6,5},{7,135},{128,0},{129,1... | collective-permute-start | bytes 344072 | tf_op jit(solution)/shard_map/ppermute | solution.py:663
